TPU v7x, 32 devices: a whole 2x2x4 slice. The times are simulated.
32 devices in a mesh: groups: 2 (over y), dp: 4 (over z), block: 2 (over x), cores: 2 (over core).
Axes of the slice: x: 2, y: 2, z: 4, core: 2. Of those that a mesh axis runs over, the one named last changes fastest.
Arguments:
- activations: bfloat16 [16, 128, 5120], P(('groups', 'dp'), None, ('block', 'cores')), parts along dimension 0, may hold values from -6 to 6
- gradients: bfloat16 [16, 128, 27648], P(('groups', 'dp'), None, ('block', 'cores')), parts along dimension 0, may hold values from -0.5 to 0.5
- token_counts: int32 [16], P(('groups', 'dp')), parts along dimension 0, may hold values from 1 to 128, 768 in all
- basis_act: bfloat16 [5120, 1536], P(('block', 'cores')), may hold values from -0.078125 to 0.078125
- basis_store: bfloat16 [4, 27648, 128], P('dp', ('block', 'cores')), may hold values from -0.0390625 to 0.0390625
- owner_slot: int32 [4], replicated, may hold values from 0 to 3, each once
- reader_blocks: int32 [4, 2], P(('block', 'cores')), may hold values from 0 to 2, all different within a row
Outputs:
- eigenvalues: float32 [2048, 512], P(('groups', 'dp'), ('block', 'cores')), parts along dimension 0
There are 2 independent parts, one for each index of `groups`. A program takes and returns all parts, laid end to end along the dimension named above; an argument that names none is the same for every part. Nothing has to cross between parts.
Inputs may be any that keep to these rules, and one draw needn't show every extreme that they name: `owner_slot`: each number of 0 to 3 appears once. `reader_blocks`: the 2 numbers of a row differ; every input-side block appears in some row. `token_counts`: within each part they sum to 768 and some sequence uses all 128 slots.
All inputs are finite; a program needn't handle non-finite values. No bound on the sum of `token_counts` on one device may be relied on, other than what follows from the above.
Results may differ from a plain program's by a relative error of at most 0.0017.
Values may be sent and summed in bfloat16 or wider, within the bound.
No kernel may reach another device: no remote copies, remote signals or barrier semaphores. Data moves between devices by JAX's collectives and lax.ppermute only.
A program may use at most 64 MiB of HBM per device.

v0:
```python
import jax
import jax.numpy as jnp
from jax import lax
from jax.sharding import PartitionSpec as P

BW = 512
RL = 2
LEN = 128


def from_root(block, axis, source):
    block = jnp.where(lax.axis_index(axis) == source, block, jnp.zeros_like(block))
    return lax.psum(block, axis)


def on_device(
    activations, gradients, token_counts, basis_act, basis_store, owner_slot, reader_blocks
):
    seq_local = activations.shape[0]
    slots = seq_local * LEN
    positions = jnp.arange(LEN, dtype=jnp.int32)
    in_range = (positions[None, :] < token_counts[:, None]).astype(jnp.bfloat16)
    flat_acts = activations.reshape(slots, activations.shape[2])
    masked = (gradients * in_range[:, :, None]).reshape(slots, gradients.shape[2])
    partial_value = lax.dot_general(
        basis_act, flat_acts, (((0,), (1,)), ((), ())), preferred_element_type=jnp.float32
    )
    act_rot_t = lax.psum(partial_value, ("block", "cores")).astype(jnp.bfloat16)
    pieces = owner_slot.shape[0]
    slots_dev = basis_store.shape[0]

    def send_piece(piece_index, totals):
        slot = owner_slot[piece_index]
        local = lax.dynamic_index_in_dim(basis_store, slot % slots_dev, 0, keepdims=False)
        piece = from_root(local, "dp", slot // slots_dev)
        term = jnp.dot(masked, piece, preferred_element_type=jnp.float32)
        return lax.dynamic_update_index_in_dim(totals, term, piece_index, 0)

    empty = jnp.zeros((pieces, slots, basis_store.shape[2]), jnp.float32)
    totals = lax.fori_loop(0, pieces, send_piece, empty)
    mine = lax.psum_scatter(totals, ("block", "cores"), scatter_dimension=0, tiled=True)
    grad_rot = mine[0].astype(jnp.bfloat16).reshape(seq_local, LEN, basis_store.shape[2])
    blocks = reader_blocks[0]
    chosen = jnp.concatenate(
        [lax.dynamic_slice_in_dim(act_rot_t, blocks[r] * BW, BW, 0) for r in range(RL)], axis=0
    )
    chosen = chosen.reshape(RL * BW, seq_local, LEN)
    products = jnp.einsum("rsl,slc->src", chosen, grad_rot, preferred_element_type=jnp.float32)
    partial_sq = jnp.sum(products * products, axis=0)
    summed = lax.psum_scatter(partial_sq, "dp", scatter_dimension=0, tiled=True)
    return summed / (seq_local * lax.axis_size("dp"))


def solution(mesh):
    in_specs = (
        P(("groups", "dp"), None, ("block", "cores")),
        P(("groups", "dp"), None, ("block", "cores")),
        P(("groups", "dp")),
        P(("block", "cores"), None),
        P("dp", ("block", "cores"), None),
        P(),
        P(("block", "cores"), None),
    )
    out_specs = P(("groups", "dp"), ("block", "cores"))
    return jax.shard_map(
        on_device, mesh=mesh, in_specs=in_specs, out_specs=out_specs, check_vma=False
    )
```

profile of v0, /device:TPU:0, one launch (start us, length us, event | category | flops | bytes accessed | tf_op | source)
XLA Modules:
  0.0 417.9 jit_solution(16161415520159982069)
XLA Ops:
  7.4 0.0 copy-start
  7.4 0.8 compare_convert_fusion
  8.2 0.0 copy-start.1
  8.2 0.0 copy-start.3
  8.2 4.2 broadcast_multiply_fusion
  12.3 0.0 copy-done.1
  12.3 0.0 copy-done.3
  12.3 0.0 copy-start.2
  12.3 333.1 %while.15 = (s32[]{:T(128)}, f32[4,256,128]{1,2,0:T(8,128)}, s32[4]{0:T(128)S(1)}, bf16[1,6912,128]{2,1,0:T(8,128)(2,1)S(1)}, bf16[256,6912]{1,0:T(8,128)(2,1)}, /*index=5*/s32[]{:T(128)}, u32[]{:T(128)}, u32[]{:T(128)}) while((s32[]{:T(128)}, f32[4,256,128]{1,2,0:T(8,128)}, s32[4]{0:T(128)S(1)}, bf16[1,6912,128]{2,1,0:T(8,128)(2,1)S(1)}, ...), condition=%wide.region_3.4_spmd, body=%wide.region_1.3_spmd.sunk | while | flops 454754304 | bytes 19595456 | solution.py:40
  12.4 0.0 all-reduce.3.cloned.1.call-start
  12.4 0.6 dynamic_slice.25
  13.7 1.4 select_bitcast_fusion.2
  15.0 0.0 all-reduce.3.cloned.1.call-update
  15.0 78.9 %all-reduce.3.cloned.1.call-done = bf16[6912,128]{1,0:T(8,128)(2,1)} async-done(((bf16[6912,128]{1,0:T(8,128)(2,1)}), bf16[6912,128]{1,0:T(8,128)(2,1)}) %all-reduce.3.cloned.1.call-update) | async-done | bytes 1769488 | tf_op jit(solution)/shard_map/while/body/eval_jaxpr/psum | solution.py:13
  94.0 4.5 %fusion.16 = f32[4,256,128]{1,2,0:T(8,128)} fusion(f32[4,256,128]{1,2,0:T(8,128)} %get-tuple-element.194, s32[]{:T(128)S(6)} %copy.20, bf16[6912,128]{1,0:T(8,128)(2,1)} %all-reduce.3.cloned.1.call-done, bf16[256,6912]{1,0:T(8,128)(2,1)} %get-tuple-element.205), kind=kOutput, calls=%fused_computation.2.clone.1 | convolution fusion | flops 452984832 | bytes 5439492 | tf_op jit(solution)/shard_map/while/body/eval_jaxpr/dot_general | solution.py:36
  98.5 0.0 all-reduce.3.cloned.1.call-start
  98.5 0.6 dynamic_slice.25
  99.7 1.4 select_bitcast_fusion.2
  101.1 0.0 all-reduce.3.cloned.1.call-update
  101.1 75.3 %all-reduce.3.cloned.1.call-done = bf16[6912,128]{1,0:T(8,128)(2,1)} async-done(((bf16[6912,128]{1,0:T(8,128)(2,1)}), bf16[6912,128]{1,0:T(8,128)(2,1)}) %all-reduce.3.cloned.1.call-update) | async-done | bytes 1769488 | tf_op jit(solution)/shard_map/while/body/eval_jaxpr/psum | solution.py:13
  176.4 4.5 %fusion.16 = f32[4,256,128]{1,2,0:T(8,128)} fusion(f32[4,256,128]{1,2,0:T(8,128)} %get-tuple-element.194, s32[]{:T(128)S(6)} %copy.20, bf16[6912,128]{1,0:T(8,128)(2,1)} %all-reduce.3.cloned.1.call-done, bf16[256,6912]{1,0:T(8,128)(2,1)} %get-tuple-element.205), kind=kOutput, calls=%fused_computation.2.clone.1 | convolution fusion | flops 452984832 | bytes 5439492 | tf_op jit(solution)/shard_map/while/body/eval_jaxpr/dot_general | solution.py:36
  180.9 0.0 all-reduce.3.cloned.1.call-start
  180.9 0.6 dynamic_slice.25
  182.1 1.4 select_bitcast_fusion.2
  183.5 0.0 all-reduce.3.cloned.1.call-update
  183.5 75.3 %all-reduce.3.cloned.1.call-done = bf16[6912,128]{1,0:T(8,128)(2,1)} async-done(((bf16[6912,128]{1,0:T(8,128)(2,1)}), bf16[6912,128]{1,0:T(8,128)(2,1)}) %all-reduce.3.cloned.1.call-update) | async-done | bytes 1769488 | tf_op jit(solution)/shard_map/while/body/eval_jaxpr/psum | solution.py:13
  258.8 4.5 %fusion.16 = f32[4,256,128]{1,2,0:T(8,128)} fusion(f32[4,256,128]{1,2,0:T(8,128)} %get-tuple-element.194, s32[]{:T(128)S(6)} %copy.20, bf16[6912,128]{1,0:T(8,128)(2,1)} %all-reduce.3.cloned.1.call-done, bf16[256,6912]{1,0:T(8,128)(2,1)} %get-tuple-element.205), kind=kOutput, calls=%fused_computation.2.clone.1 | convolution fusion | flops 452984832 | bytes 5439492 | tf_op jit(solution)/shard_map/while/body/eval_jaxpr/dot_general | solution.py:36
  263.3 0.0 all-reduce.3.cloned.1.call-start
  263.3 0.6 dynamic_slice.25
  264.6 1.4 select_bitcast_fusion.2
  265.9 0.0 all-reduce.3.cloned.1.call-update
  265.9 75.0 %all-reduce.3.cloned.1.call-done = bf16[6912,128]{1,0:T(8,128)(2,1)} async-done(((bf16[6912,128]{1,0:T(8,128)(2,1)}), bf16[6912,128]{1,0:T(8,128)(2,1)}) %all-reduce.3.cloned.1.call-update) | async-done | bytes 1769488 | tf_op jit(solution)/shard_map/while/body/eval_jaxpr/psum | solution.py:13
  340.9 4.5 %fusion.16 = f32[4,256,128]{1,2,0:T(8,128)} fusion(f32[4,256,128]{1,2,0:T(8,128)} %get-tuple-element.194, s32[]{:T(128)S(6)} %copy.20, bf16[6912,128]{1,0:T(8,128)(2,1)} %all-reduce.3.cloned.1.call-done, bf16[256,6912]{1,0:T(8,128)(2,1)} %get-tuple-element.205), kind=kOutput, calls=%fused_computation.2.clone.1 | convolution fusion | flops 452984832 | bytes 5439492 | tf_op jit(solution)/shard_map/while/body/eval_jaxpr/dot_general | solution.py:36
  345.4 0.0 reduce-scatter.3.cloned.1.call-start
  345.4 0.6 reduce-scatter.3.cloned.1.call-update
  346.0 0.0 reduce-scatter.5.cloned.1.call-start
  346.0 0.0 copy-done.2
  346.0 0.6 fusion.4
  348.0 0.0 copy-done
  348.0 3.3 fusion.5
  351.3 35.2 %all-reduce.4 = bf16[1536,256]{1,0:T(8,128)(2,1)S(1)} all-reduce(f32[1536,256]{1,0:T(8,128)S(1)} %fusion.5), channel_id=1, replica_groups=mesh['groups'=2,'dp'=4,'block'=2,'cores'=2] {'block','cores'}, use_global_device_ids=true, to_apply=%region_0.0 | all-reduce | flops 393216 | bytes 2359296 | tf_op jit(solution)/shard_map/psum | solution.py:28
  386.6 0.0 reduce-scatter.3.cloned.1.call-done
  386.7 0.9 convert_element_type.19
  387.6 0.1 copy.10
  387.7 1.1 fusion.1
  388.8 0.0 reduce-scatter.5.cloned.1.call-update
  388.8 20.4 %reduce-scatter.5.cloned.1.call-done = f32[256,128]{1,0:T(8,128)} async-done(((f32[1024,128]{1,0:T(8,128)}), f32[256,128]{1,0:T(8,128)}) %reduce-scatter.5.cloned.1.call-update) | async-done | bytes 131088 | tf_op jit(solution)/shard_map/reduce_scatter | solution.py:50
  409.2 1.6 broadcast_multiply_fusion.1
  (2 shorter events, 0.0 us)
Async XLA Ops:
  7.4 340.6 %copy-start = (bf16[2,128,1280]{2,1,0:T(8,128)(2,1)S(1)}, bf16[2,128,1280]{2,1,0:T(8,128)(2,1)}, u32[]{:S(2)}) copy-start(bf16[2,128,1280]{2,1,0:T(8,128)(2,1)} %param.9) | copy-start | bytes 1966084
  8.2 4.2 %copy-start.1 = (bf16[1,6912,128]{2,1,0:T(8,128)(2,1)S(1)}, bf16[1,6912,128]{2,1,0:T(8,128)(2,1)}, u32[]{:S(2)}) copy-start(bf16[1,6912,128]{2,1,0:T(8,128)(2,1)} %param.13) | copy-start | bytes 5308420
  8.2 4.2 %copy-start.3 = (s32[4]{0:T(128)S(1)}, s32[4]{0:T(128)}, u32[]{:S(2)}) copy-start(s32[4]{0:T(128)} %param.14) | copy-start | bytes 52
  12.3 333.7 %copy-start.2 = (s32[1,2]{1,0:T(1,128)S(1)}, s32[1,2]{1,0:T(1,128)}, u32[]{:S(2)}) copy-start(s32[1,2]{1,0:T(1,128)} %param.15) | copy-start | bytes 28
  12.4 81.6 %all-reduce.3.cloned.1.call-start = ((), (), s32[]{:S(2)}) async-start(), calls=%async_computation.4 | async-start | bytes 3538944 | tf_op jit(solution)/shard_map/while/body/eval_jaxpr/psum | solution.py:13
  98.5 77.9 %all-reduce.3.cloned.1.call-start = ((), (), s32[]{:S(2)}) async-start(), calls=%async_computation.4 | async-start | bytes 3538944 | tf_op jit(solution)/shard_map/while/body/eval_jaxpr/psum | solution.py:13
  180.9 77.9 %all-reduce.3.cloned.1.call-start = ((), (), s32[]{:S(2)}) async-start(), calls=%async_computation.4 | async-start | bytes 3538944 | tf_op jit(solution)/shard_map/while/body/eval_jaxpr/psum | solution.py:13
  263.3 77.6 %all-reduce.3.cloned.1.call-start = ((), (), s32[]{:S(2)}) async-start(), calls=%async_computation.4 | async-start | bytes 3538944 | tf_op jit(solution)/shard_map/while/body/eval_jaxpr/psum | solution.py:13
  345.4 41.3 %reduce-scatter.3.cloned.1.call-start = ((), (), s32[]{:S(2)}) async-start(), calls=%async_computation.2 | async-start | bytes 655360 | tf_op jit(solution)/shard_map/reduce_scatter | solution.py:41
  346.0 63.2 %reduce-scatter.5.cloned.1.call-start = ((), (), s32[]{:S(2)}) async-start(), calls=%async_computation.3 | async-start | bytes 655360 | tf_op jit(solution)/shard_map/reduce_scatter | solution.py:50
Sparse Core Ops, SparseCore 0:
  15.7 78.2 all-reduce.2
  101.8 74.5 all-reduce.2
  184.2 74.5 all-reduce.2
  266.4 74.5 all-reduce.2
Sparse Core Ops, SparseCore 1:
  348.4 23.5 reduce-scatter.2
  388.9 20.3 reduce-scatter.4
where the time goes:
time: 418 us
  waiting for transfers between devices  326 us (78%)
  blocking collectives  35.2 us (8%)
  matrix products  22.4 us (5%)
  between operations  15.9 us (4%)
  other arithmetic  12.9 us (3%)
    psum x4, waiting for transfers between devices, from_root(): return lax.psum(block, axis)  305 us
    psum x1, blocking collectives, on_device(): act_rot_t = lax.psum(partial_value, ('block', 'cores')).astype(jnp.bfloat16)  35.2 us
    reduce_scatter x1, waiting for transfers between devices, on_device(): summed = lax.psum_scatter(partial_sq, 'dp', scatter_dimension=0, tiled=True)  20.4 us
    dot_general x4, matrix products, send_piece(): term = jnp.dot(masked, piece, preferred_element_type=jnp.float32)  17.9 us
  transfers between devices with their start and end apart: 6, of which 5 were waited for; matrix products, arithmetic and copies ran while one was open for 1% of the time, Pallas kernels for 0%

commit v1 on v0

v1 whole, which is shorter than its diff:
```python
import jax
import jax.numpy as jnp
from jax import lax
from jax.sharding import PartitionSpec as P

BW = 512
LEN = 128
F32 = jnp.float32
BF16 = jnp.bfloat16


def shift(value, axis, step):
    size = lax.axis_size(axis)
    return lax.ppermute(value, axis, [(i, (i + step) % size) for i in range(size)])


def block_of(value, index):
    return lax.dynamic_index_in_dim(value, index, 0, keepdims=False)


def reduce_scatter(blocks, axis, wire=F32):
    size, me = lax.axis_size(axis), lax.axis_index(axis)
    total = block_of(blocks, me)
    for step in range(1, size):
        term = block_of(blocks, (me + step) % size).astype(wire)
        total = total + shift(term, axis, step).astype(F32)
    return total


def gather(block, axis):
    size, me = lax.axis_size(axis), lax.axis_index(axis)
    out = jnp.zeros((size,) + block.shape, block.dtype)
    out = lax.dynamic_update_index_in_dim(out, block, me, 0)
    for step in range(1, size):
        came = shift(block, axis, step)
        out = lax.dynamic_update_index_in_dim(out, came, (me - step) % size, 0)
    return out


def on_device(
    activations, gradients, token_counts, basis_act, basis_store, owner_slot, reader_blocks
):
    seq_local = activations.shape[0]
    slots = seq_local * LEN
    groups, dp = lax.axis_size("groups"), lax.axis_size("dp")
    cores, blocks = lax.axis_size("cores"), lax.axis_size("block")
    group, row = lax.axis_index("groups"), lax.axis_index("dp")
    pieces = owner_slot.shape[0]
    per_row, features, width = basis_store.shape
    part_features = features // groups

    flat_grads = gradients.reshape(slots, features)

    def share(index):
        return lax.dynamic_slice_in_dim(flat_grads, index * part_features, part_features, 1)

    rows = [share(group)]
    for step in range(1, groups):
        rows.append(shift(share((group + step) % groups), "groups", step))
    rows = jnp.concatenate(rows, axis=0)

    flat_acts = activations.reshape(slots, activations.shape[2])
    partial_act = lax.dot_general(
        basis_act, flat_acts, (((0,), (1,)), ((), ())), preferred_element_type=F32
    )
    window = partial_act.shape[0]
    act = reduce_scatter(partial_act.reshape(cores, window // cores, slots), "cores")
    act = reduce_scatter(act.reshape(blocks, -1, slots), "block").astype(BF16)
    act = gather(act, "block").reshape(-1, slots)
    act_rot_t = gather(act, "cores").reshape(window, slots)

    held = lax.dynamic_slice_in_dim(basis_store, group * part_features, part_features, 1)
    piece_of_slot = jnp.zeros((pieces,), jnp.int32).at[owner_slot].set(
        jnp.arange(pieces, dtype=jnp.int32)
    )
    totals = jnp.zeros((pieces, groups * slots, width), F32)
    for step in range(dp):
        source = (row - step) % dp
        for local in range(per_row):
            term = jnp.dot(rows, held[local], preferred_element_type=F32)
            index = piece_of_slot[source * per_row + local]
            totals = lax.dynamic_update_index_in_dim(totals, term, index, 0)
        if step < dp - 1:
            held = shift(held, "dp", 1)

    by_block = totals.reshape(blocks, cores, groups, slots, width)
    mine = reduce_scatter(jnp.moveaxis(by_block, 1, 0), "cores")
    mine = reduce_scatter(mine, "block")
    total = mine[0]
    for step in range(1, groups):
        total = total + shift(mine[step], "groups", -step)
    positions = jnp.arange(LEN, dtype=jnp.int32)
    in_range = (positions[None, :] < token_counts[:, None]).astype(F32)
    grad_rot = total.reshape(seq_local, LEN, width) * in_range[:, :, None]
    grad_rot = grad_rot.astype(BF16)

    wanted = reader_blocks[0]
    chosen = jnp.concatenate(
        [
            lax.dynamic_slice_in_dim(act_rot_t, wanted[r] * BW, BW, 0)
            for r in range(wanted.shape[0])
        ],
        axis=0,
    )
    chosen = chosen.reshape(-1, seq_local, LEN)
    products = jnp.einsum("rsl,slc->src", chosen, grad_rot, preferred_element_type=F32)
    partial_sq = jnp.sum(products * products, axis=0)
    summed = reduce_scatter(partial_sq.reshape(dp, -1, width), "dp", BF16)
    return summed / (seq_local * dp)


def solution(mesh):
    in_specs = (
        P(("groups", "dp"), None, ("block", "cores")),
        P(("groups", "dp"), None, ("block", "cores")),
        P(("groups", "dp")),
        P(("block", "cores"), None),
        P("dp", ("block", "cores"), None),
        P(),
        P(("block", "cores"), None),
    )
    out_specs = P(("groups", "dp"), ("block", "cores"))
    return jax.shard_map(
        on_device, mesh=mesh, in_specs=in_specs, out_specs=out_specs, check_vma=False
    )
```

time: 418 us -> 127 us (0.30)
  waiting for transfers between devices: 326 us -> 43.7 us
  local copies, waits for them, and re-layouts: 3.14 us -> 40.3 us
  blocking collectives: 35.2 us -> 0 us
  starting transfers between devices: 0.09 us -> 13.5 us
  other arithmetic: 12.9 us -> 4.25 us
  between operations: 15.9 us -> 8.96 us
  matrix products: 22.4 us -> 15.5 us
    psum x4 -> x0, waiting for transfers between devices: 305 us -> none  [from_root(): return lax.psum(block, axis)]
    ppermute x0 -> x14, waiting for transfers between devices: none -> 43.7 us  [shift(): lax.ppermute(value, axis, [(i, (i + step) % size) for i in range(size)])]
    psum x1 -> x0, blocking collectives: 35.2 us -> none  [on_device(): act_rot_t = lax.psum(partial_value, ('block', 'cores')).astype(jnp.bfloat16)]
    reduce_scatter x2 -> x0, waiting for transfers between devices: 20.4 us -> none  [the longest x1 20.4 us: on_device(): summed = lax.psum_scatter(partial_sq, 'dp', scatter_dimension=0, tiled=True)]
    dynamic_update_slice x0 -> x3, local copies, waits for them, and re-layouts: none -> 15.6 us  [the longest x2 8.15 us: gather(): out = lax.dynamic_update_index_in_dim(out, came, (me - step) % size, 0)]
    ppermute x0 -> x14, starting transfers between devices: none -> 13.5 us  [shift(): lax.ppermute(value, axis, [(i, (i + step) % size) for i in range(size)])]
    dot_general x5, matrix products: 19 us -> 12 us  [the longest x4 11.6 us: on_device(): term = jnp.dot(rows, held[local], preferred_element_type=F32)]
    dot_general x0 -> x1, local copies, waits for them, and re-layouts: none -> 6.28 us  [on_device(): lax.dot_general(basis_act, flat_acts, (((0,), (1,)), ((), ())), preferred...]
  transfers between devices with their start and end apart: 6 -> 14, of which waited for: 5 -> 7; matrix products, arithmetic and copies ran while one was open for 1% -> 42% of each run, Pallas kernels for 0% -> 0%
where the time goes in v1:
time: 127 us; the launch traced here: 126 us
  waiting for transfers between devices  43.7 us (34%)
  local copies, waits for them, and re-layouts  40.3 us (32%)
  matrix products  15.5 us (12%)
  starting transfers between devices  13.5 us (11%)
  between operations  8.96 us (7%)
  other arithmetic  4.25 us (3%)
    ppermute x14, waiting for transfers between devices, shift(): lax.ppermute(value, axis, [(i, (i + step) % size) for i in range(size)])  43.7 us
    ppermute x14, starting transfers between devices, shift(): lax.ppermute(value, axis, [(i, (i + step) % size) for i in range(size)])  13.5 us
    dot_general x4, matrix products, on_device(): term = jnp.dot(rows, held[local], preferred_element_type=F32)  11.6 us
    dynamic_update_slice x2, local copies, waits for them, and re-layouts, gather(): out = lax.dynamic_update_index_in_dim(out, came, (me - step) % size, 0)  8.15 us
    dynamic_update_slice x1, local copies, waits for them, and re-layouts, gather(): out = lax.dynamic_update_index_in_dim(out, block, me, 0)  7.46 us
    dot_general x1, local copies, waits for them, and re-layouts, on_device(): lax.dot_general(basis_act, flat_acts, (((0,), (1,)), ((), ())), preferred...  6.28 us
    dot_general x1, matrix products, on_device(): lax.dot_general(basis_act, flat_acts, (((0,), (1,)), ((), ())), preferred...  3.52 us
    unnamed x15, local copies, waits for them, and re-layouts  3.52 us
  transfers between devices with their start and end apart: 14, of which 7 were waited for; matrix products, arithmetic and copies ran while one was open for 42% of the time, Pallas kernels for 0%

profile of v1, /device:TPU:0, one launch (start us, length us, event | category | flops | bytes accessed | tf_op | source)
XLA Modules:
  0.0 126.3 jit_solution(13923429008212331190)
XLA Ops:
  0.0 1.5 %copy-done = bf16[1,6912,128]{2,1,0:T(8,128)(2,1)S(1)} copy-done((bf16[1,6912,128]{2,1,0:T(8,128)(2,1)S(1)}, bf16[1,6912,128]{2,1,0:T(8,128)(2,1)}, u32[]{:S(2)}) %copy-start) | copy-done | bytes 1769496
  1.5 1.0 constant_dynamic-slice_fusion
  2.5 3.0 %collective-permute-start.5 = (bf16[1,3456,128]{2,1,0:T(8,128)(2,1)}, bf16[1,3456,128]{2,1,0:T(8,128)(2,1)}, u32[]{:S(2)}, u32[]{:S(2)}) collective-permute-start(bf16[1,3456,128]{2,1,0:T(8,128)(2,1)} %constant_dynamic-slice_fusion), channel_id=1, source_target_pairs={{0,4},{4,8},{8,12},{12,0},{1,5},{5,9},{9,13},{13,1},{2,6},{6,10},{... | collective-permute-start | bytes 2654216 | tf_op jit(solution)/shard_map/ppermute | solution.py:14
  5.5 3.5 %constant_dynamic-slice_fusion.2 = (bf16[256,3456]{1,0:T(8,128)(2,1)}, bf16[256,3456]{1,0:T(8,128)(2,1)S(1)}) fusion(bf16[256,6912]{1,0:T(8,128)(2,1)} %bitcast.102, s32[]{:T(128)S(6)} %select_n.151, s32[]{:T(128)S(6)} %select_n.153), kind=kLoop, calls=%fused_computation.45 | loop fusion | bytes 7077896 | tf_op jit(solution)/shard_map/dynamic_slice | solution.py:55
  9.0 1.5 %collective-permute-start.4 = (bf16[256,3456]{1,0:T(8,128)(2,1)S(1)}, bf16[256,3456]{1,0:T(8,128)(2,1)}, u32[]{:S(2)}, u32[]{:S(2)}) collective-permute-start(bf16[256,3456]{1,0:T(8,128)(2,1)S(1)} %get-tuple-element.8), channel_id=1, source_target_pairs={{0,16},{16,0},{1,17},{17,1},{2,18},{18,2},{3,19},{19,3},{4,20},{20... | collective-permute-start | bytes 5308424 | tf_op jit(solution)/shard_map/ppermute | solution.py:14
  10.5 6.3 %copy.17 = bf16[1536,1280]{1,0:T(8,128)(2,1)} copy(bf16[1536,1280]{0,1:T(8,128)(2,1)} %bitcast.100) | data formatting | bytes 7864320 | tf_op jit(solution)/shard_map/dot_general | solution.py:63
  16.8 3.5 %fusion.23 = f32[2,768,256]{2,1,0:T(8,128)S(1)} fusion(bf16[2,768,1280]{2,1,0:T(8,128)(2,1)} %bitcast.101, bf16[256,1280,1]{1,0,2:T(8,128)(2,1)} %bitcast.111), kind=kOutput, calls=%fused_computation.54 | convolution fusion | flops 1006632960 | bytes 6160384 | tf_op jit(solution)/shard_map/dot_general | solution.py:63
  20.3 1.1 copy-done.3
  21.5 1.0 dynamic-slice_bitcast_fusion
  22.5 0.0 collective-permute-start
  22.5 5.0 %collective-permute-done.5 = bf16[1,3456,128]{2,1,0:T(8,128)(2,1)} collective-permute-done((bf16[1,3456,128]{2,1,0:T(8,128)(2,1)}, bf16[1,3456,128]{2,1,0:T(8,128)(2,1)}, u32[]{:S(2)}, u32[]{:S(2)}) %collective-permute-start.5) | collective-permute-done | bytes 884768 | tf_op jit(solution)/shard_map/ppermute | solution.py:14
  27.5 0.0 collective-permute-start.6
  27.5 0.6 scatter_custom_fusion
  28.1 0.7 fusion.21
  36.0 0.0 collective-permute-done
  36.1 1.5 %bitcast_add_fusion = f32[768,256]{1,0:T(8,128)S(1)} fusion(f32[768,256]{1,0:T(8,128)} %collective-permute-done, f32[2,768,256]{2,1,0:T(8,128)} %copy-done.3, s32[]{:T(128)S(6)} %select_n.139), kind=kLoop, calls=%fused_computation.16 | loop fusion | flops 196608 | bytes 2359300 | tf_op jit(solution)/shard_map/add | solution.py:26
  37.6 1.6 %collective-permute-start.1 = (f32[384,256]{1,0:T(8,128)S(1)}, f32[384,256]{1,0:T(8,128)S(1)}, u32[]{:S(2)}, u32[]{:S(2)}) collective-permute-start(f32[384,256]{1,0:T(8,128)S(1)} %dynamic-slice_bitcast_fusion.2), channel_id=1, source_target_pairs={{0,2},{2,0},{1,3},{3,1},{4,6},{6,4},{5,7},{7,5},{8,10},{10,8},{9,1... | collective-permute-start | bytes 1179656 | tf_op jit(solution)/shard_map/ppermute | solution.py:14
  39.1 11.3 %collective-permute-done.6 = bf16[1,3456,128]{2,1,0:T(8,128)(2,1)} collective-permute-done((bf16[1,3456,128]{2,1,0:T(8,128)(2,1)}, bf16[1,3456,128]{2,1,0:T(8,128)(2,1)}, u32[]{:S(2)}, u32[]{:S(2)}) %collective-permute-start.6) | collective-permute-done | bytes 884768 | tf_op jit(solution)/shard_map/ppermute | solution.py:14
  50.4 0.0 collective-permute-start.7
  50.4 0.0 collective-permute-done.4
  50.4 0.1 broadcast_in_dim.48
  50.5 3.4 %fusion.4 = f32[4,512,128]{2,1,0:T(8,128)S(1)} fusion(f32[4,512,128]{2,1,0:T(8,128)S(1)} %broadcast_in_dim.48, s32[]{:T(128)S(6)} %select_n.157, bf16[1,3456,128]{2,1,0:T(8,128)(2,1)} %constant_dynamic-slice_fusion, bf16[256,3456]{1,0:T(8,128)(2,1)} %collective-permute-done.4, bf16[256,3456]{1,0:T(8,128)(2,1)} %get-tuple-element.7), kind=kOutput, calls=%fused_computation.11 | convolution fusion | flops 460062720 | bytes 4685828 | tf_op jit(solution)/shard_map/dot_general | solution.py:80
  54.0 2.8 %fusion.3 = f32[4,512,128]{2,1,0:T(8,128)S(1)} fusion(f32[4,512,128]{2,1,0:T(8,128)S(1)} %fusion.4, s32[]{:T(128)S(6)} %select_n.160, bf16[1,3456,128]{2,1,0:T(8,128)(2,1)} %collective-permute-done.5, bf16[256,3456]{1,0:T(8,128)(2,1)} %collective-permute-done.4, bf16[256,3456]{1,0:T(8,128)(2,1)S(1)} %copy-done.2), kind=kOutput, calls=%fused_computation.9 | convolution fusion | flops 460062720 | bytes 4685828 | tf_op jit(solution)/shard_map/dot_general | solution.py:80
  56.8 2.8 %fusion.2 = f32[4,512,128]{2,1,0:T(8,128)S(1)} fusion(f32[4,512,128]{2,1,0:T(8,128)S(1)} %fusion.3, s32[]{:T(128)S(6)} %select_n.163, bf16[1,3456,128]{2,1,0:T(8,128)(2,1)} %collective-permute-done.6, bf16[256,3456]{1,0:T(8,128)(2,1)} %collective-permute-done.4, bf16[256,3456]{1,0:T(8,128)(2,1)S(1)} %copy-done.2), kind=kOutput, calls=%fused_computation.7 | convolution fusion | flops 460062720 | bytes 4685828 | tf_op jit(solution)/shard_map/dot_general | solution.py:80
  59.6 12.8 %collective-permute-done.7 = bf16[1,3456,128]{2,1,0:T(8,128)(2,1)S(1)} collective-permute-done((bf16[1,3456,128]{2,1,0:T(8,128)(2,1)}, bf16[1,3456,128]{2,1,0:T(8,128)(2,1)S(1)}, u32[]{:S(2)}, u32[]{:S(2)}) %collective-permute-start.7) | collective-permute-done | bytes 884768 | tf_op jit(solution)/shard_map/ppermute | solution.py:14
  72.3 2.6 %fusion.1 = f32[4,512,128]{2,1,0:T(8,128)S(1)} fusion(f32[4,512,128]{2,1,0:T(8,128)S(1)} %fusion.2, s32[]{:T(128)S(6)} %select_n.166, bf16[1,3456,128]{2,1,0:T(8,128)(2,1)S(1)} %collective-permute-done.7, bf16[256,3456]{1,0:T(8,128)(2,1)} %collective-permute-done.4, bf16[256,3456]{1,0:T(8,128)(2,1)S(1)} %copy-done.2), kind=kOutput, calls=%fused_computation.5 | convolution fusion | flops 460062720 | bytes 4685828 | tf_op jit(solution)/shard_map/dot_general | solution.py:80
  74.9 0.0 copy-start.4
  74.9 0.0 copy-start.6
  74.9 0.8 dynamic-slice_bitcast_fusion.1
  75.8 0.0 collective-permute-start.8
  75.8 0.0 collective-permute-done.1
  75.8 0.8 broadcast_in_dim.43
  76.6 0.8 bitcast_dynamic-update-slice_fusion.1
  77.4 1.0 collective-permute-start.2
  78.4 6.5 %collective-permute-done.2 = bf16[384,256]{1,0:T(8,128)(2,1)S(1)} collective-permute-done((bf16[384,256]{1,0:T(8,128)(2,1)}, bf16[384,256]{1,0:T(8,128)(2,1)S(1)}, u32[]{:S(2)}, u32[]{:S(2)}) %collective-permute-start.2) | collective-permute-done | bytes 196640 | tf_op jit(solution)/shard_map/ppermute | solution.py:14
  84.9 0.7 bitcast_dynamic-update-slice_fusion
  85.6 0.0 collective-permute-start.3
  85.6 0.0 collective-permute-done.8
  85.6 0.1 bitcast_add_fusion.1
  85.7 0.8 copy-done.1
  86.5 0.7 dynamic-slice_bitcast_fusion.3
  87.2 1.0 collective-permute-start.9
  88.2 0.6 fusion.22
  90.2 0.1 compare_convert_fusion
  90.3 2.3 %copy.13 = bf16[1,768,256]{1,0,2:T(2,128)(2,1)S(1)} copy(bf16[1,768,256]{2,1,0:T(8,128)(2,1)} %bitcast.11) | data formatting | bytes 786432 | tf_op jit(solution)/shard_map/jit(dynamic_update_index_in_dim)/broadcast_in_dim | solution.py:33
  92.6 0.4 broadcast_in_dim.42
  93.0 7.5 %dynamic_update_slice.29 = bf16[2,768,256]{1,0,2:T(2,128)(2,1)S(1)} dynamic-update-slice(bf16[2,768,256]{1,0,2:T(2,128)(2,1)S(1)} %broadcast_in_dim.42, bf16[1,768,256]{1,0,2:T(2,128)(2,1)S(1)} %copy.13, s32[]{:T(128)S(6)} %select_n.139, s32[]{:T(128)} %constant.153.clone.1, s32[]{:T(128)} %constant.153.clone.1) | dynamic-update-slice | bytes 786436 | tf_op jit(solution)/shard_map/jit(dynamic_update_index_in_dim)/dynamic_update_slice | solution.py:33
  100.5 0.0 collective-permute-done.3
  100.5 2.3 %copy.14 = bf16[1,768,256]{1,0,2:T(2,128)(2,1)S(1)} copy(bf16[1,768,256]{2,1,0:T(8,128)(2,1)} %bitcast.13) | data formatting | bytes 786432 | tf_op jit(solution)/shard_map/jit(dynamic_update_index_in_dim)/broadcast_in_dim | solution.py:36
  102.8 7.5 %dynamic_update_slice.30 = bf16[2,768,256]{1,0,2:T(2,128)(2,1)S(1)} dynamic-update-slice(bf16[2,768,256]{1,0,2:T(2,128)(2,1)S(1)} %dynamic_update_slice.29, bf16[1,768,256]{1,0,2:T(2,128)(2,1)S(1)} %copy.14, s32[]{:T(128)S(6)} %select_n.148, s32[]{:T(128)} %constant.153.clone.1, s32[]{:T(128)} %constant.153.clone.1) | dynamic-update-slice | bytes 786436 | tf_op jit(solution)/shard_map/jit(dynamic_update_index_in_dim)/dynamic_update_slice | solution.py:36
  110.3 0.1 copy.18
  110.4 0.0 collective-permute-done.9
  110.4 1.1 bitcast_add_fusion.3
  111.5 1.6 %collective-permute-start.10 = (f32[256,128]{1,0:T(8,128)S(1)}, f32[256,128]{1,0:T(8,128)S(1)}, u32[]{:S(2)}, u32[]{:S(2)}) collective-permute-start(f32[256,128]{1,0:T(8,128)S(1)} %slice_bitcast_fusion), channel_id=1, source_target_pairs={{0,16},{16,0},{1,17},{17,1},{2,18},{18,2},{3,19},{19,3},{4,20},{20... | collective-permute-start | bytes 393224 | tf_op jit(solution)/shard_map/ppermute | solution.py:14
  113.1 0.1 pad_maximum_fusion.1
  113.1 4.0 %collective-permute-done.10 = f32[256,128]{1,0:T(8,128)S(1)} collective-permute-done((f32[256,128]{1,0:T(8,128)S(1)}, f32[256,128]{1,0:T(8,128)S(1)}, u32[]{:S(2)}, u32[]{:S(2)}) %collective-permute-start.10) | collective-permute-done | bytes 131104 | tf_op jit(solution)/shard_map/ppermute | solution.py:14
  117.2 0.4 fusion
  117.6 0.1 collective-permute-start.11
  117.7 0.2 collective-permute-start.12
  117.9 3.6 %collective-permute-start.13 = (bf16[256,128]{1,0:T(8,128)(2,1)S(1)}, bf16[256,128]{1,0:T(8,128)(2,1)S(1)}, u32[]{:S(2)}, u32[]{:S(2)}) collective-permute-start(bf16[256,128]{1,0:T(8,128)(2,1)S(1)} %get-tuple-element.12), channel_id=1, source_target_pairs={{0,12},{4,0},{8,4},{12,8},{1,13},{5,1},{9,5},{13,9},{2,14},{6,2},{... | collective-permute-start | bytes 196616 | tf_op jit(solution)/shard_map/ppermute | solution.py:14
  121.5 2.8 %collective-permute-done.11 = bf16[256,128]{1,0:T(8,128)(2,1)S(1)} collective-permute-done((bf16[256,128]{1,0:T(8,128)(2,1)S(1)}, bf16[256,128]{1,0:T(8,128)(2,1)S(1)}, u32[]{:S(2)}, u32[]{:S(2)}) %collective-permute-start.11) | collective-permute-done | bytes 65568 | tf_op jit(solution)/shard_map/ppermute | solution.py:14
  124.3 1.3 %collective-permute-done.12 = bf16[256,128]{1,0:T(8,128)(2,1)S(1)} collective-permute-done((bf16[256,128]{1,0:T(8,128)(2,1)S(1)}, bf16[256,128]{1,0:T(8,128)(2,1)S(1)}, u32[]{:S(2)}, u32[]{:S(2)}) %collective-permute-start.12) | collective-permute-done | bytes 65568 | tf_op jit(solution)/shard_map/ppermute | solution.py:14
  125.6 0.0 collective-permute-done.13
  125.6 0.7 fusion.13
  (16 shorter events, 0.2 us)
Async XLA Ops:
  0.0 1.5 %copy-start = (bf16[1,6912,128]{2,1,0:T(8,128)(2,1)S(1)}, bf16[1,6912,128]{2,1,0:T(8,128)(2,1)}, u32[]{:S(2)}) copy-start(bf16[1,6912,128]{2,1,0:T(8,128)(2,1)} %param.11) | copy-start | bytes 5308420
  2.5 25.0 %collective-permute-start.5 = (bf16[1,3456,128]{2,1,0:T(8,128)(2,1)}, bf16[1,3456,128]{2,1,0:T(8,128)(2,1)}, u32[]{:S(2)}, u32[]{:S(2)}) collective-permute-start(bf16[1,3456,128]{2,1,0:T(8,128)(2,1)} %constant_dynamic-slice_fusion), channel_id=1, source_target_pairs={{0,4},{4,8},{8,12},{12,0},{1,5},{5,9},{9,13},{13,1},{2,6},{6,10},{... | collective-permute-start | bytes 2654216 | tf_op jit(solution)/shard_map/ppermute | solution.py:14
  9.0 41.4 %collective-permute-start.4 = (bf16[256,3456]{1,0:T(8,128)(2,1)S(1)}, bf16[256,3456]{1,0:T(8,128)(2,1)}, u32[]{:S(2)}, u32[]{:S(2)}) collective-permute-start(bf16[256,3456]{1,0:T(8,128)(2,1)S(1)} %get-tuple-element.8), channel_id=1, source_target_pairs={{0,16},{16,0},{1,17},{17,1},{2,18},{18,2},{3,19},{19,3},{4,20},{20... | collective-permute-start | bytes 5308424 | tf_op jit(solution)/shard_map/ppermute | solution.py:14
  16.8 10.7 %copy-start.5 = (s32[4]{0:T(128)S(1)}, s32[4]{0:T(128)}, u32[]{:S(2)}) copy-start(s32[4]{0:T(128)} %param.12) | copy-start | bytes 52
  20.3 1.1 copy-start.3
  22.5 13.6 %collective-permute-start = (f32[768,256]{1,0:T(8,128)}, f32[768,256]{1,0:T(8,128)}, u32[]{:S(2)}, u32[]{:S(2)}) collective-permute-start(f32[768,256]{1,0:T(8,128)} %dynamic-slice_bitcast_fusion), channel_id=1, source_target_pairs={{0,1},{1,0},{2,3},{3,2},{4,5},{5,4},{6,7},{7,6},{8,9},{9,8},{10,11... | collective-permute-start | bytes 2359304 | tf_op jit(solution)/shard_map/ppermute | solution.py:14
  27.5 22.9 %collective-permute-start.6 = (bf16[1,3456,128]{2,1,0:T(8,128)(2,1)}, bf16[1,3456,128]{2,1,0:T(8,128)(2,1)}, u32[]{:S(2)}, u32[]{:S(2)}) collective-permute-start(bf16[1,3456,128]{2,1,0:T(8,128)(2,1)} %collective-permute-done.5), channel_id=1, source_target_pairs={{0,4},{4,8},{8,12},{12,0},{1,5},{5,9},{9,13},{13,1},{2,6},{6,10},{... | collective-permute-start | bytes 2654216 | tf_op jit(solution)/shard_map/ppermute | solution.py:14
  37.6 38.2 %collective-permute-start.1 = (f32[384,256]{1,0:T(8,128)S(1)}, f32[384,256]{1,0:T(8,128)S(1)}, u32[]{:S(2)}, u32[]{:S(2)}) collective-permute-start(f32[384,256]{1,0:T(8,128)S(1)} %dynamic-slice_bitcast_fusion.2), channel_id=1, source_target_pairs={{0,2},{2,0},{1,3},{3,1},{4,6},{6,4},{5,7},{7,5},{8,10},{10,8},{9,1... | collective-permute-start | bytes 1179656 | tf_op jit(solution)/shard_map/ppermute | solution.py:14
  50.4 21.9 %collective-permute-start.7 = (bf16[1,3456,128]{2,1,0:T(8,128)(2,1)}, bf16[1,3456,128]{2,1,0:T(8,128)(2,1)S(1)}, u32[]{:S(2)}, u32[]{:S(2)}) collective-permute-start(bf16[1,3456,128]{2,1,0:T(8,128)(2,1)} %collective-permute-done.6), channel_id=1, source_target_pairs={{0,4},{4,8},{8,12},{12,0},{1,5},{5,9},{9,13},{13,1},{2,6},{6,10},{... | collective-permute-start | bytes 2654216 | tf_op jit(solution)/shard_map/ppermute | solution.py:14
  50.5 3.5 %copy-start.2 = (bf16[256,3456]{1,0:T(8,128)(2,1)S(1)}, bf16[256,3456]{1,0:T(8,128)(2,1)}, u32[]{:S(2)}) copy-start(bf16[256,3456]{1,0:T(8,128)(2,1)} %get-tuple-element.7) | copy-start | bytes 5308420
  74.9 13.3 %copy-start.4 = (s32[1,2]{1,0:T(1,128)S(1)}, s32[1,2]{1,0:T(1,128)}, u32[]{:S(2)}) copy-start(s32[1,2]{1,0:T(1,128)} %param.13) | copy-start | bytes 28
  74.9 15.3 %copy-start.6 = (s32[2]{0:T(128)S(1)}, s32[2]{0:T(128)}, u32[]{:S(2)}) copy-start(s32[2]{0:T(128)} %param.9) | copy-start | bytes 28
  75.8 9.8 %collective-permute-start.8 = (f32[2,2,256,128]{3,2,1,0:T(8,128)}, f32[2,2,256,128]{3,2,1,0:T(8,128)S(1)}, u32[]{:S(2)}, u32[]{:S(2)}) collective-permute-start(f32[2,2,256,128]{3,2,1,0:T(8,128)} %dynamic-slice_bitcast_fusion.1), channel_id=1, source_target_pairs={{0,1},{1,0},{2,3},{3,2},{4,5},{5,4},{6,7},{7,6},{8,9},{9,8},{10,11... | collective-permute-start | bytes 1572872 | tf_op jit(solution)/shard_map/ppermute | solution.py:14
  77.4 7.5 %collective-permute-start.2 = (bf16[384,256]{1,0:T(8,128)(2,1)}, bf16[384,256]{1,0:T(8,128)(2,1)S(1)}, u32[]{:S(2)}, u32[]{:S(2)}) collective-permute-start(bf16[384,256]{1,0:T(8,128)(2,1)} %get-tuple-element.6), channel_id=1, source_target_pairs={{0,2},{2,0},{1,3},{3,1},{4,6},{6,4},{5,7},{7,5},{8,10},{10,8},{9,1... | collective-permute-start | bytes 589832 | tf_op jit(solution)/shard_map/ppermute | solution.py:14
  85.6 14.9 %collective-permute-start.3 = (bf16[768,256]{1,0:T(8,128)(2,1)}, bf16[768,256]{1,0:T(8,128)(2,1)}, u32[]{:S(2)}, u32[]{:S(2)}) collective-permute-start(bf16[768,256]{1,0:T(8,128)(2,1)} %bitcast.12), channel_id=1, source_target_pairs={{0,1},{1,0},{2,3},{3,2},{4,5},{5,4},{6,7},{7,6},{8,9},{9,8},{10,11... | collective-permute-start | bytes 1179656 | tf_op jit(solution)/shard_map/ppermute | solution.py:14
  85.7 0.8 copy-start.1
  87.2 23.2 %collective-permute-start.9 = (f32[2,256,128]{2,1,0:T(8,128)}, f32[2,256,128]{2,1,0:T(8,128)}, u32[]{:S(2)}, u32[]{:S(2)}) collective-permute-start(f32[2,256,128]{2,1,0:T(8,128)} %dynamic-slice_bitcast_fusion.3), channel_id=1, source_target_pairs={{0,2},{2,0},{1,3},{3,1},{4,6},{6,4},{5,7},{7,5},{8,10},{10,8},{9,1... | collective-permute-start | bytes 786440 | tf_op jit(solution)/shard_map/ppermute | solution.py:14
  111.5 5.7 %collective-permute-start.10 = (f32[256,128]{1,0:T(8,128)S(1)}, f32[256,128]{1,0:T(8,128)S(1)}, u32[]{:S(2)}, u32[]{:S(2)}) collective-permute-start(f32[256,128]{1,0:T(8,128)S(1)} %slice_bitcast_fusion), channel_id=1, source_target_pairs={{0,16},{16,0},{1,17},{17,1},{2,18},{18,2},{3,19},{19,3},{4,20},{20... | collective-permute-start | bytes 393224 | tf_op jit(solution)/shard_map/ppermute | solution.py:14
  117.6 6.7 %collective-permute-start.11 = (bf16[256,128]{1,0:T(8,128)(2,1)S(1)}, bf16[256,128]{1,0:T(8,128)(2,1)S(1)}, u32[]{:S(2)}, u32[]{:S(2)}) collective-permute-start(bf16[256,128]{1,0:T(8,128)(2,1)S(1)} %get-tuple-element.11), channel_id=1, source_target_pairs={{0,4},{4,8},{8,12},{12,0},{1,5},{5,9},{9,13},{13,1},{2,6},{6,10},{... | collective-permute-start | bytes 196616 | tf_op jit(solution)/shard_map/ppermute | solution.py:14
  117.7 7.9 %collective-permute-start.12 = (bf16[256,128]{1,0:T(8,128)(2,1)S(1)}, bf16[256,128]{1,0:T(8,128)(2,1)S(1)}, u32[]{:S(2)}, u32[]{:S(2)}) collective-permute-start(bf16[256,128]{1,0:T(8,128)(2,1)S(1)} %get-tuple-element.13), channel_id=1, source_target_pairs={{0,8},{4,12},{8,0},{12,4},{1,9},{5,13},{9,1},{13,5},{2,10},{6,14},... | collective-permute-start | bytes 196616 | tf_op jit(solution)/shard_map/ppermute | solution.py:14
  117.9 7.7 %collective-permute-start.13 = (bf16[256,128]{1,0:T(8,128)(2,1)S(1)}, bf16[256,128]{1,0:T(8,128)(2,1)S(1)}, u32[]{:S(2)}, u32[]{:S(2)}) collective-permute-start(bf16[256,128]{1,0:T(8,128)(2,1)S(1)} %get-tuple-element.12), channel_id=1, source_target_pairs={{0,12},{4,0},{8,4},{12,8},{1,13},{5,1},{9,5},{13,9},{2,14},{6,2},{... | collective-permute-start | bytes 196616 | tf_op jit(solution)/shard_map/ppermute | solution.py:14

commit v2 on v1

--- a/solution.py
+++ b/solution.py
@@ -81,14 +81,24 @@
             index = piece_of_slot[source * per_row + local]
             totals = lax.dynamic_update_index_in_dim(totals, term, index, 0)
         if step < dp - 1:
+            if step == dp - 2:
+                held, act_rot_t = lax.optimization_barrier((held, act_rot_t))
             held = shift(held, "dp", 1)
 
     by_block = totals.reshape(blocks, cores, groups, slots, width)
     mine = reduce_scatter(jnp.moveaxis(by_block, 1, 0), "cores")
-    mine = reduce_scatter(mine, "block")
-    total = mine[0]
-    for step in range(1, groups):
-        total = total + shift(mine[step], "groups", -step)
+    block = lax.axis_index("block")
+    total = block_of(mine, block)[0]
+    for far in range(blocks):
+        toward = block_of(mine, (block + far) % blocks)
+        for back in range(groups):
+            if far or back:
+                pairs = [
+                    (g * blocks + b, ((g - back) % groups) * blocks + (b + far) % blocks)
+                    for g in range(groups)
+                    for b in range(blocks)
+                ]
+                total = total + lax.ppermute(toward[back], ("groups", "block"), pairs)
     positions = jnp.arange(LEN, dtype=jnp.int32)
     in_range = (positions[None, :] < token_counts[:, None]).astype(F32)
     grad_rot = total.reshape(seq_local, LEN, width) * in_range[:, :, None]

time: 127 us -> 126 us (level)
  local copies, waits for them, and re-layouts: 40.3 us -> 38.8 us
    ppermute x0 -> x3, waiting for transfers between devices: none -> 4.91 us  [on_device(): total = total + lax.ppermute(toward[back], ('groups', 'block'), pairs)]
    ppermute x14 -> x12, waiting for transfers between devices: 43.7 us -> 39.9 us  [shift(): lax.ppermute(value, axis, [(i, (i + step) % size) for i in range(size)])]
    ppermute x0 -> x3, starting transfers between devices: none -> 3.55 us  [on_device(): total = total + lax.ppermute(toward[back], ('groups', 'block'), pairs)]
    ppermute x14 -> x12, starting transfers between devices: 13.5 us -> 10.9 us  [shift(): lax.ppermute(value, axis, [(i, (i + step) % size) for i in range(size)])]
    unnamed x15 -> x13, local copies, waits for them, and re-layouts: 3.52 us -> 1.04 us
    add x3 -> x2, other arithmetic: 2.6 us -> 1.53 us  [reduce_scatter(): total = total + shift(term, axis, step).astype(F32)]
    squeeze x4 -> x3, local copies, waits for them, and re-layouts: 2.61 us -> 1.9 us  [block_of(): return lax.dynamic_index_in_dim(value, index, 0, keepdims=False)]
  transfers between devices with their start and end apart: 14 -> 15, of which waited for: 7 -> 8; matrix products, arithmetic and copies ran while one was open for 42% -> 33% of each run, Pallas kernels for 0% -> 0%
where the time goes in v2:
time: 126 us
  waiting for transfers between devices  44.8 us (36%)
  local copies, waits for them, and re-layouts  38.8 us (31%)
  matrix products  15.5 us (12%)
  starting transfers between devices  14.4 us (11%)
  between operations  8.93 us (7%)
  other arithmetic  3.1 us (2%)
    ppermute x12, waiting for transfers between devices, shift(): lax.ppermute(value, axis, [(i, (i + step) % size) for i in range(size)])  39.9 us
    dot_general x4, matrix products, on_device(): term = jnp.dot(rows, held[local], preferred_element_type=F32)  11.6 us
    ppermute x12, starting transfers between devices, shift(): lax.ppermute(value, axis, [(i, (i + step) % size) for i in range(size)])  10.9 us
    dynamic_update_slice x2, local copies, waits for them, and re-layouts, gather(): out = lax.dynamic_update_index_in_dim(out, came, (me - step) % size, 0)  8.16 us
    dynamic_update_slice x1, local copies, waits for them, and re-layouts, gather(): out = lax.dynamic_update_index_in_dim(out, block, me, 0)  7.46 us
    dot_general x1, local copies, waits for them, and re-layouts, on_device(): lax.dot_general(basis_act, flat_acts, (((0,), (1,)), ((), ())), preferred...  6.24 us
    ppermute x3, waiting for transfers between devices, on_device(): total = total + lax.ppermute(toward[back], ('groups', 'block'), pairs)  4.91 us
    dynamic_slice x1, local copies, waits for them, and re-layouts, share(): lax.dynamic_slice_in_dim(flat_grads, index * part_features, part_features...  4.08 us
  transfers between devices with their start and end apart: 15, of which 8 were waited for; matrix products, arithmetic and copies ran while one was open for 33% of the time, Pallas kernels for 0%

profile of v2, /device:TPU:0, one launch (start us, length us, event | category | flops | bytes accessed | tf_op | source)
XLA Modules:
  0.0 125.6 jit_solution(11602685796227475153)
XLA Ops:
  0.0 0.0 copy-start
  0.0 6.2 %copy.17 = bf16[1536,1280]{1,0:T(8,128)(2,1)} copy(bf16[1536,1280]{0,1:T(8,128)(2,1)} %bitcast.104) | data formatting | bytes 7864320 | tf_op jit(solution)/shard_map/dot_general | solution.py:63
  6.2 3.5 %fusion.25 = f32[2,768,256]{2,1,0:T(8,128)S(1)} fusion(bf16[2,768,1280]{2,1,0:T(8,128)(2,1)} %bitcast.105, bf16[256,1280,1]{1,0,2:T(8,128)(2,1)} %bitcast.115), kind=kOutput, calls=%fused_computation.56 | convolution fusion | flops 1006632960 | bytes 6160384 | tf_op jit(solution)/shard_map/dot_general | solution.py:63
  9.7 1.0 dynamic-slice_bitcast_fusion
  10.8 0.5 collective-permute-start.2
  11.2 1.1 constant_dynamic-slice_fusion.4
  12.3 2.6 %collective-permute-start = (bf16[1,3456,128]{2,1,0:T(8,128)(2,1)}, bf16[1,3456,128]{2,1,0:T(8,128)(2,1)}, u32[]{:S(2)}, u32[]{:S(2)}) collective-permute-start(bf16[1,3456,128]{2,1,0:T(8,128)(2,1)} %constant_dynamic-slice_fusion.4), channel_id=1, source_target_pairs={{0,4},{4,8},{8,12},{12,0},{1,5},{5,9},{9,13},{13,1},{2,6},{6,10},{... | collective-permute-start | bytes 2654216 | tf_op jit(solution)/shard_map/ppermute | solution.py:14
  14.9 4.1 %constant_dynamic-slice_fusion.1 = (bf16[256,3456]{1,0:T(8,128)(2,1)}, bf16[256,3456]{1,0:T(8,128)(2,1)}) fusion(bf16[256,6912]{1,0:T(8,128)(2,1)} %bitcast.106, s32[]{:T(128)S(6)} %select_n.146, s32[]{:T(128)S(6)} %select_n.160), kind=kLoop, calls=%fused_computation.46 | loop fusion | bytes 7077896 | tf_op jit(solution)/shard_map/dynamic_slice | solution.py:55
  19.0 1.5 %collective-permute-start.6 = (bf16[256,3456]{1,0:T(8,128)(2,1)}, bf16[256,3456]{1,0:T(8,128)(2,1)}, u32[]{:S(2)}, u32[]{:S(2)}) collective-permute-start(bf16[256,3456]{1,0:T(8,128)(2,1)} %get-tuple-element.12), channel_id=1, source_target_pairs={{0,16},{16,0},{1,17},{17,1},{2,18},{18,2},{3,19},{19,3},{4,20},{20... | collective-permute-start | bytes 5308424 | tf_op jit(solution)/shard_map/ppermute | solution.py:14
  20.5 0.0 collective-permute-done.2
  20.5 1.5 %bitcast_add_fusion = f32[768,256]{1,0:T(8,128)S(1)} fusion(f32[768,256]{1,0:T(8,128)} %collective-permute-done.2, f32[2,768,256]{2,1,0:T(8,128)} %copy-done.2, s32[]{:T(128)S(6)} %select_n.147), kind=kLoop, calls=%fused_computation.16 | loop fusion | flops 196608 | bytes 2359300 | tf_op jit(solution)/shard_map/add | solution.py:26
  22.0 1.5 %collective-permute-start.3 = (f32[384,256]{1,0:T(8,128)S(1)}, f32[384,256]{1,0:T(8,128)S(1)}, u32[]{:S(2)}, u32[]{:S(2)}) collective-permute-start(f32[384,256]{1,0:T(8,128)S(1)} %dynamic-slice_bitcast_fusion.2), channel_id=1, source_target_pairs={{0,2},{2,0},{1,3},{3,1},{4,6},{6,4},{5,7},{7,5},{8,10},{10,8},{9,1... | collective-permute-start | bytes 1179656 | tf_op jit(solution)/shard_map/ppermute | solution.py:14
  23.5 14.0 %collective-permute-done = bf16[1,3456,128]{2,1,0:T(8,128)(2,1)} collective-permute-done((bf16[1,3456,128]{2,1,0:T(8,128)(2,1)}, bf16[1,3456,128]{2,1,0:T(8,128)(2,1)}, u32[]{:S(2)}, u32[]{:S(2)}) %collective-permute-start) | collective-permute-done | bytes 884768 | tf_op jit(solution)/shard_map/ppermute | solution.py:14
  37.5 0.0 collective-permute-start.1
  37.5 0.0 collective-permute-done.3
  37.5 0.8 broadcast_in_dim.43
  38.4 0.7 bitcast_dynamic-update-slice_fusion.1
  39.1 1.5 %collective-permute-start.4 = (bf16[384,256]{1,0:T(8,128)(2,1)S(1)}, bf16[384,256]{1,0:T(8,128)(2,1)S(1)}, u32[]{:S(2)}, u32[]{:S(2)}) collective-permute-start(bf16[384,256]{1,0:T(8,128)(2,1)S(1)} %get-tuple-element.10), channel_id=1, source_target_pairs={{0,2},{2,0},{1,3},{3,1},{4,6},{6,4},{5,7},{7,5},{8,10},{10,8},{9,1... | collective-permute-start | bytes 589832 | tf_op jit(solution)/shard_map/ppermute | solution.py:14
  40.6 5.2 %collective-permute-done.4 = bf16[384,256]{1,0:T(8,128)(2,1)S(1)} collective-permute-done((bf16[384,256]{1,0:T(8,128)(2,1)S(1)}, bf16[384,256]{1,0:T(8,128)(2,1)S(1)}, u32[]{:S(2)}, u32[]{:S(2)}) %collective-permute-start.4) | collective-permute-done | bytes 196640 | tf_op jit(solution)/shard_map/ppermute | solution.py:14
  45.8 0.7 bitcast_dynamic-update-slice_fusion
  46.5 0.0 collective-permute-start.5
  46.5 0.6 scatter_custom_fusion
  47.2 0.7 fusion.23
  55.2 2.3 %copy.13 = bf16[1,768,256]{1,0,2:T(2,128)(2,1)S(1)} copy(bf16[1,768,256]{2,1,0:T(8,128)(2,1)} %bitcast.11) | data formatting | bytes 786432 | tf_op jit(solution)/shard_map/jit(dynamic_update_index_in_dim)/broadcast_in_dim | solution.py:33
  57.5 0.4 broadcast_in_dim.42
  57.9 7.5 %dynamic_update_slice.29 = bf16[2,768,256]{1,0,2:T(2,128)(2,1)S(1)} dynamic-update-slice(bf16[2,768,256]{1,0,2:T(2,128)(2,1)S(1)} %broadcast_in_dim.42, bf16[1,768,256]{1,0,2:T(2,128)(2,1)S(1)} %copy.13, s32[]{:T(128)S(6)} %select_n.147, s32[]{:T(128)} %constant.157.clone.1, s32[]{:T(128)} %constant.157.clone.1) | dynamic-update-slice | bytes 786436 | tf_op jit(solution)/shard_map/jit(dynamic_update_index_in_dim)/dynamic_update_slice | solution.py:33
  65.4 0.0 collective-permute-done.5
  65.4 2.3 %copy.14 = bf16[1,768,256]{1,0,2:T(2,128)(2,1)S(1)} copy(bf16[1,768,256]{2,1,0:T(8,128)(2,1)} %bitcast.13) | data formatting | bytes 786432 | tf_op jit(solution)/shard_map/jit(dynamic_update_index_in_dim)/broadcast_in_dim | solution.py:36
  67.7 7.5 %dynamic_update_slice.30 = bf16[2,768,256]{1,0,2:T(2,128)(2,1)S(1)} dynamic-update-slice(bf16[2,768,256]{1,0,2:T(2,128)(2,1)S(1)} %dynamic_update_slice.29, bf16[1,768,256]{1,0,2:T(2,128)(2,1)S(1)} %copy.14, s32[]{:T(128)S(6)} %select_n.156, s32[]{:T(128)} %constant.157.clone.1, s32[]{:T(128)} %constant.157.clone.1) | dynamic-update-slice | bytes 786436 | tf_op jit(solution)/shard_map/jit(dynamic_update_index_in_dim)/dynamic_update_slice | solution.py:36
  75.2 1.0 copy.18
  76.2 0.0 collective-permute-done.1
  76.2 0.8 collective-permute-start.7
  77.0 0.0 collective-permute-done.6
  77.0 0.1 broadcast_in_dim.48
  77.1 3.4 %fusion.4 = f32[4,512,128]{2,1,0:T(8,128)S(1)} fusion(f32[4,512,128]{2,1,0:T(8,128)S(1)} %broadcast_in_dim.48, s32[]{:T(128)S(6)} %select_n.164, bf16[1,3456,128]{2,1,0:T(8,128)(2,1)} %constant_dynamic-slice_fusion.4, bf16[256,3456]{1,0:T(8,128)(2,1)} %collective-permute-done.6, bf16[256,3456]{1,0:T(8,128)(2,1)} %get-tuple-element.11), kind=kOutput, calls=%fused_computation.11 | convolution fusion | flops 460062720 | bytes 4685828 | tf_op jit(solution)/shard_map/dot_general | solution.py:80
  80.5 0.0 copy-done.1
  80.5 2.8 %fusion.3 = f32[4,512,128]{2,1,0:T(8,128)S(1)} fusion(f32[4,512,128]{2,1,0:T(8,128)S(1)} %fusion.4, s32[]{:T(128)S(6)} %select_n.167, bf16[1,3456,128]{2,1,0:T(8,128)(2,1)} %collective-permute-done, bf16[256,3456]{1,0:T(8,128)(2,1)} %collective-permute-done.6, bf16[256,3456]{1,0:T(8,128)(2,1)S(1)} %copy-done.1), kind=kOutput, calls=%fused_computation.9 | convolution fusion | flops 460062720 | bytes 4685828 | tf_op jit(solution)/shard_map/dot_general | solution.py:80
  83.3 2.8 %fusion.2 = f32[4,512,128]{2,1,0:T(8,128)S(1)} fusion(f32[4,512,128]{2,1,0:T(8,128)S(1)} %fusion.3, s32[]{:T(128)S(6)} %select_n.170, bf16[1,3456,128]{2,1,0:T(8,128)(2,1)} %collective-permute-done.1, bf16[256,3456]{1,0:T(8,128)(2,1)} %collective-permute-done.6, bf16[256,3456]{1,0:T(8,128)(2,1)S(1)} %copy-done.1), kind=kOutput, calls=%fused_computation.7 | convolution fusion | flops 460062720 | bytes 4685828 | tf_op jit(solution)/shard_map/dot_general | solution.py:80
  86.1 0.0 copy-start.3
  86.2 0.0 copy-start.5
  86.2 14.1 %collective-permute-done.7 = bf16[1,3456,128]{2,1,0:T(8,128)(2,1)S(1)} collective-permute-done((bf16[1,3456,128]{2,1,0:T(8,128)(2,1)}, bf16[1,3456,128]{2,1,0:T(8,128)(2,1)S(1)}, u32[]{:S(2)}, u32[]{:S(2)}) %collective-permute-start.7) | collective-permute-done | bytes 884768 | tf_op jit(solution)/shard_map/ppermute | solution.py:14
  100.2 2.6 %fusion.1 = f32[4,512,128]{2,1,0:T(8,128)S(1)} fusion(f32[4,512,128]{2,1,0:T(8,128)S(1)} %fusion.2, s32[]{:T(128)S(6)} %select_n.173, bf16[1,3456,128]{2,1,0:T(8,128)(2,1)S(1)} %collective-permute-done.7, bf16[256,3456]{1,0:T(8,128)(2,1)} %collective-permute-done.6, bf16[256,3456]{1,0:T(8,128)(2,1)S(1)} %copy-done.1), kind=kOutput, calls=%fused_computation.5 | convolution fusion | flops 460062720 | bytes 4685828 | tf_op jit(solution)/shard_map/dot_general | solution.py:80
  102.8 0.8 dynamic-slice_bitcast_fusion.1
  103.7 0.0 collective-permute-start.8
  103.7 0.6 fusion.24
  105.6 0.1 compare_convert_fusion
  105.7 0.1 collective-permute-done.8
  105.8 0.1 bitcast_add_fusion.1
  105.9 2.4 %collective-permute-start.11 = (f32[256,128]{1,0:T(8,128)S(1)}, f32[256,128]{1,0:T(8,128)S(1)}, u32[]{:S(2)}, u32[]{:S(2)}) collective-permute-start(f32[256,128]{1,0:T(8,128)S(1)} %get-tuple-element.20), channel_id=1, source_target_pairs={{0,18},{2,16},{16,2},{18,0},{1,19},{3,17},{17,3},{19,1},{4,22},{6,... | collective-permute-start | bytes 393224 | tf_op jit(solution)/shard_map/ppermute | solution.py:101
  108.3 0.5 collective-permute-start.10
  108.8 0.6 collective-permute-start.9
  109.4 1.1 constant_dynamic-slice_fusion.3
  110.5 0.1 pad_maximum_fusion.1
  110.6 2.6 %collective-permute-done.11 = f32[256,128]{1,0:T(8,128)S(1)} collective-permute-done((f32[256,128]{1,0:T(8,128)S(1)}, f32[256,128]{1,0:T(8,128)S(1)}, u32[]{:S(2)}, u32[]{:S(2)}) %collective-permute-start.11) | collective-permute-done | bytes 131104 | tf_op jit(solution)/shard_map/ppermute | solution.py:101
  113.1 2.3 %collective-permute-done.10 = f32[256,128]{1,0:T(8,128)S(1)} collective-permute-done((f32[256,128]{1,0:T(8,128)S(1)}, f32[256,128]{1,0:T(8,128)S(1)}, u32[]{:S(2)}, u32[]{:S(2)}) %collective-permute-start.10) | collective-permute-done | bytes 131104 | tf_op jit(solution)/shard_map/ppermute | solution.py:101
  115.4 0.0 collective-permute-done.9
  115.5 0.4 fusion
  116.0 1.8 %collective-permute-start.14 = (bf16[256,128]{1,0:T(8,128)(2,1)S(1)}, bf16[256,128]{1,0:T(8,128)(2,1)S(1)}, u32[]{:S(2)}, u32[]{:S(2)}) collective-permute-start(bf16[256,128]{1,0:T(8,128)(2,1)S(1)} %get-tuple-element.16), channel_id=1, source_target_pairs={{0,12},{4,0},{8,4},{12,8},{1,13},{5,1},{9,5},{13,9},{2,14},{6,2},{... | collective-permute-start | bytes 196616 | tf_op jit(solution)/shard_map/ppermute | solution.py:14
  117.8 0.0 collective-permute-start.13
  117.8 0.6 collective-permute-start.12
  118.4 1.9 %collective-permute-done.14 = bf16[256,128]{1,0:T(8,128)(2,1)S(1)} collective-permute-done((bf16[256,128]{1,0:T(8,128)(2,1)S(1)}, bf16[256,128]{1,0:T(8,128)(2,1)S(1)}, u32[]{:S(2)}, u32[]{:S(2)}) %collective-permute-start.14) | collective-permute-done | bytes 65568 | tf_op jit(solution)/shard_map/ppermute | solution.py:14
  120.3 4.6 %collective-permute-done.13 = bf16[256,128]{1,0:T(8,128)(2,1)S(1)} collective-permute-done((bf16[256,128]{1,0:T(8,128)(2,1)S(1)}, bf16[256,128]{1,0:T(8,128)(2,1)S(1)}, u32[]{:S(2)}, u32[]{:S(2)}) %collective-permute-start.13) | collective-permute-done | bytes 65568 | tf_op jit(solution)/shard_map/ppermute | solution.py:14
  124.9 0.0 collective-permute-done.12
  124.9 0.7 fusion.15
  (14 shorter events, 0.2 us)
Async XLA Ops:
  0.0 11.2 %copy-start = (bf16[1,6912,128]{2,1,0:T(8,128)(2,1)S(1)}, bf16[1,6912,128]{2,1,0:T(8,128)(2,1)}, u32[]{:S(2)}) copy-start(bf16[1,6912,128]{2,1,0:T(8,128)(2,1)} %param.11) | copy-start | bytes 5308420
  9.7 9.2 %copy-start.2 = (f32[2,768,256]{2,1,0:T(8,128)}, f32[2,768,256]{2,1,0:T(8,128)S(1)}, u32[]{:S(2)}) copy-start(f32[2,768,256]{2,1,0:T(8,128)S(1)} %fusion.25) | copy-start | bytes 4718596
  10.8 9.7 %collective-permute-start.2 = (f32[768,256]{1,0:T(8,128)}, f32[768,256]{1,0:T(8,128)}, u32[]{:S(2)}, u32[]{:S(2)}) collective-permute-start(f32[768,256]{1,0:T(8,128)} %dynamic-slice_bitcast_fusion), channel_id=1, source_target_pairs={{0,1},{1,0},{2,3},{3,2},{4,5},{5,4},{6,7},{7,6},{8,9},{9,8},{10,11... | collective-permute-start | bytes 2359304 | tf_op jit(solution)/shard_map/ppermute | solution.py:14
  12.3 25.2 %collective-permute-start = (bf16[1,3456,128]{2,1,0:T(8,128)(2,1)}, bf16[1,3456,128]{2,1,0:T(8,128)(2,1)}, u32[]{:S(2)}, u32[]{:S(2)}) collective-permute-start(bf16[1,3456,128]{2,1,0:T(8,128)(2,1)} %constant_dynamic-slice_fusion.4), channel_id=1, source_target_pairs={{0,4},{4,8},{8,12},{12,0},{1,5},{5,9},{9,13},{13,1},{2,6},{6,10},{... | collective-permute-start | bytes 2654216 | tf_op jit(solution)/shard_map/ppermute | solution.py:14
  19.0 27.6 %copy-start.4 = (s32[4]{0:T(128)S(1)}, s32[4]{0:T(128)}, u32[]{:S(2)}) copy-start(s32[4]{0:T(128)} %param.12) | copy-start | bytes 52
  19.0 58.0 %collective-permute-start.6 = (bf16[256,3456]{1,0:T(8,128)(2,1)}, bf16[256,3456]{1,0:T(8,128)(2,1)}, u32[]{:S(2)}, u32[]{:S(2)}) collective-permute-start(bf16[256,3456]{1,0:T(8,128)(2,1)} %get-tuple-element.12), channel_id=1, source_target_pairs={{0,16},{16,0},{1,17},{17,1},{2,18},{18,2},{3,19},{19,3},{4,20},{20... | collective-permute-start | bytes 5308424 | tf_op jit(solution)/shard_map/ppermute | solution.py:14
  22.0 15.5 %collective-permute-start.3 = (f32[384,256]{1,0:T(8,128)S(1)}, f32[384,256]{1,0:T(8,128)S(1)}, u32[]{:S(2)}, u32[]{:S(2)}) collective-permute-start(f32[384,256]{1,0:T(8,128)S(1)} %dynamic-slice_bitcast_fusion.2), channel_id=1, source_target_pairs={{0,2},{2,0},{1,3},{3,1},{4,6},{6,4},{5,7},{7,5},{8,10},{10,8},{9,1... | collective-permute-start | bytes 1179656 | tf_op jit(solution)/shard_map/ppermute | solution.py:14
  37.5 38.6 %collective-permute-start.1 = (bf16[1,3456,128]{2,1,0:T(8,128)(2,1)}, bf16[1,3456,128]{2,1,0:T(8,128)(2,1)}, u32[]{:S(2)}, u32[]{:S(2)}) collective-permute-start(bf16[1,3456,128]{2,1,0:T(8,128)(2,1)} %collective-permute-done), channel_id=1, source_target_pairs={{0,4},{4,8},{8,12},{12,0},{1,5},{5,9},{9,13},{13,1},{2,6},{6,10},{... | collective-permute-start | bytes 2654216 | tf_op jit(solution)/shard_map/ppermute | solution.py:14
  39.1 6.7 %collective-permute-start.4 = (bf16[384,256]{1,0:T(8,128)(2,1)S(1)}, bf16[384,256]{1,0:T(8,128)(2,1)S(1)}, u32[]{:S(2)}, u32[]{:S(2)}) collective-permute-start(bf16[384,256]{1,0:T(8,128)(2,1)S(1)} %get-tuple-element.10), channel_id=1, source_target_pairs={{0,2},{2,0},{1,3},{3,1},{4,6},{6,4},{5,7},{7,5},{8,10},{10,8},{9,1... | collective-permute-start | bytes 589832 | tf_op jit(solution)/shard_map/ppermute | solution.py:14
  46.5 18.8 %collective-permute-start.5 = (bf16[768,256]{1,0:T(8,128)(2,1)}, bf16[768,256]{1,0:T(8,128)(2,1)}, u32[]{:S(2)}, u32[]{:S(2)}) collective-permute-start(bf16[768,256]{1,0:T(8,128)(2,1)} %bitcast.12), channel_id=1, source_target_pairs={{0,1},{1,0},{2,3},{3,2},{4,5},{5,4},{6,7},{7,6},{8,9},{9,8},{10,11... | collective-permute-start | bytes 1179656 | tf_op jit(solution)/shard_map/ppermute | solution.py:14
  76.2 24.1 %collective-permute-start.7 = (bf16[1,3456,128]{2,1,0:T(8,128)(2,1)}, bf16[1,3456,128]{2,1,0:T(8,128)(2,1)S(1)}, u32[]{:S(2)}, u32[]{:S(2)}) collective-permute-start(bf16[1,3456,128]{2,1,0:T(8,128)(2,1)} %collective-permute-done.1), channel_id=1, source_target_pairs={{0,4},{4,8},{8,12},{12,0},{1,5},{5,9},{9,13},{13,1},{2,6},{6,10},{... | collective-permute-start | bytes 2654216 | tf_op jit(solution)/shard_map/ppermute | solution.py:14
  77.1 3.5 %copy-start.1 = (bf16[256,3456]{1,0:T(8,128)(2,1)S(1)}, bf16[256,3456]{1,0:T(8,128)(2,1)}, u32[]{:S(2)}) copy-start(bf16[256,3456]{1,0:T(8,128)(2,1)} %get-tuple-element.11) | copy-start | bytes 5308420
  86.1 17.5 %copy-start.3 = (s32[1,2]{1,0:T(1,128)S(1)}, s32[1,2]{1,0:T(1,128)}, u32[]{:S(2)}) copy-start(s32[1,2]{1,0:T(1,128)} %param.13) | copy-start | bytes 28
  86.2 19.4 %copy-start.5 = (s32[2]{0:T(128)S(1)}, s32[2]{0:T(128)}, u32[]{:S(2)}) copy-start(s32[2]{0:T(128)} %param.9) | copy-start | bytes 28
  103.7 2.1 %collective-permute-start.8 = (f32[2,2,256,128]{3,2,1,0:T(8,128)}, f32[2,2,256,128]{3,2,1,0:T(8,128)S(1)}, u32[]{:S(2)}, u32[]{:S(2)}) collective-permute-start(f32[2,2,256,128]{3,2,1,0:T(8,128)} %dynamic-slice_bitcast_fusion.1), channel_id=1, source_target_pairs={{0,1},{1,0},{2,3},{3,2},{4,5},{5,4},{6,7},{7,6},{8,9},{9,8},{10,11... | collective-permute-start | bytes 1572872 | tf_op jit(solution)/shard_map/ppermute | solution.py:14
  105.9 7.3 %collective-permute-start.11 = (f32[256,128]{1,0:T(8,128)S(1)}, f32[256,128]{1,0:T(8,128)S(1)}, u32[]{:S(2)}, u32[]{:S(2)}) collective-permute-start(f32[256,128]{1,0:T(8,128)S(1)} %get-tuple-element.20), channel_id=1, source_target_pairs={{0,18},{2,16},{16,2},{18,0},{1,19},{3,17},{17,3},{19,1},{4,22},{6,... | collective-permute-start | bytes 393224 | tf_op jit(solution)/shard_map/ppermute | solution.py:101
  108.3 7.2 %collective-permute-start.10 = (f32[256,128]{1,0:T(8,128)S(1)}, f32[256,128]{1,0:T(8,128)S(1)}, u32[]{:S(2)}, u32[]{:S(2)}) collective-permute-start(f32[256,128]{1,0:T(8,128)S(1)} %get-tuple-element.19), channel_id=1, source_target_pairs={{0,2},{2,0},{16,18},{18,16},{1,3},{3,1},{17,19},{19,17},{4,6},{6,4... | collective-permute-start | bytes 393224 | tf_op jit(solution)/shard_map/ppermute | solution.py:101
  108.8 6.7 %collective-permute-start.9 = (f32[256,128]{1,0:T(8,128)S(1)}, f32[256,128]{1,0:T(8,128)S(1)}, u32[]{:S(2)}, u32[]{:S(2)}) collective-permute-start(f32[256,128]{1,0:T(8,128)S(1)} %get-tuple-element.18), channel_id=1, source_target_pairs={{0,16},{2,18},{16,0},{18,2},{1,17},{3,19},{17,1},{19,3},{4,20},{6,... | collective-permute-start | bytes 393224 | tf_op jit(solution)/shard_map/ppermute | solution.py:101
  116.0 4.3 %collective-permute-start.14 = (bf16[256,128]{1,0:T(8,128)(2,1)S(1)}, bf16[256,128]{1,0:T(8,128)(2,1)S(1)}, u32[]{:S(2)}, u32[]{:S(2)}) collective-permute-start(bf16[256,128]{1,0:T(8,128)(2,1)S(1)} %get-tuple-element.16), channel_id=1, source_target_pairs={{0,12},{4,0},{8,4},{12,8},{1,13},{5,1},{9,5},{13,9},{2,14},{6,2},{... | collective-permute-start | bytes 196616 | tf_op jit(solution)/shard_map/ppermute | solution.py:14
  117.8 7.2 %collective-permute-start.13 = (bf16[256,128]{1,0:T(8,128)(2,1)S(1)}, bf16[256,128]{1,0:T(8,128)(2,1)S(1)}, u32[]{:S(2)}, u32[]{:S(2)}) collective-permute-start(bf16[256,128]{1,0:T(8,128)(2,1)S(1)} %get-tuple-element.17), channel_id=1, source_target_pairs={{0,8},{4,12},{8,0},{12,4},{1,9},{5,13},{9,1},{13,5},{2,10},{6,14},... | collective-permute-start | bytes 196616 | tf_op jit(solution)/shard_map/ppermute | solution.py:14
  117.8 7.2 %collective-permute-start.12 = (bf16[256,128]{1,0:T(8,128)(2,1)S(1)}, bf16[256,128]{1,0:T(8,128)(2,1)S(1)}, u32[]{:S(2)}, u32[]{:S(2)}) collective-permute-start(bf16[256,128]{1,0:T(8,128)(2,1)S(1)} %get-tuple-element.15), channel_id=1, source_target_pairs={{0,4},{4,8},{8,12},{12,0},{1,5},{5,9},{9,13},{13,1},{2,6},{6,10},{... | collective-permute-start | bytes 196616 | tf_op jit(solution)/shard_map/ppermute | solution.py:14

commit v3 on v2

v3 whole, which is shorter than its diff:
```python
import functools

import jax
import jax.numpy as jnp
from jax import lax
from jax.experimental import pallas as pl
from jax.experimental.pallas import tpu as pltpu
from jax.sharding import PartitionSpec as P

BW = 512
LEN = 128
F32 = jnp.float32
BF16 = jnp.bfloat16
VMEM_LIMIT = 40 * 1024 * 1024
VMEM = pl.BlockSpec(memory_space=pltpu.VMEM)
SMEM = pl.BlockSpec(memory_space=pltpu.SMEM)


def shift(value, axis, step):
    size = lax.axis_size(axis)
    return lax.ppermute(value, axis, [(i, (i + step) % size) for i in range(size)])


def block_of(value, index):
    return lax.dynamic_index_in_dim(value, index, 0, keepdims=False)


def reduce_scatter(blocks, axis):
    size, me = lax.axis_size(axis), lax.axis_index(axis)
    total = block_of(blocks, me)
    for step in range(1, size):
        total = total + shift(block_of(blocks, (me + step) % size), axis, step)
    return total


def gather(block, axis):
    size, me = lax.axis_size(axis), lax.axis_index(axis)
    out = jnp.zeros((size,) + block.shape, block.dtype)
    out = lax.dynamic_update_index_in_dim(out, block, me, 0)
    for step in range(1, size):
        came = shift(block, axis, step)
        out = lax.dynamic_update_index_in_dim(out, came, (me - step) % size, 0)
    return out


def rotate_kernel(cores, place, acts, basis, keep, send):
    height = keep.shape[0]
    for step in range(cores):
        share = lax.rem(place[1] + step, cores)
        columns = pl.ds(pl.multiple_of(share * height, height), height)
        term = jnp.dot(acts[...], basis[:, columns], preferred_element_type=F32)
        if step == 0:
            keep[...] = term.T
        else:
            send[step - 1] = term.T


def rotate(place, acts, basis, cores):
    height, width = basis.shape[1] // cores, acts.shape[0]
    return pl.pallas_call(
        functools.partial(rotate_kernel, cores),
        out_shape=(
            jax.ShapeDtypeStruct((height, width), F32),
            jax.ShapeDtypeStruct((cores - 1, height, width), F32),
        ),
        in_specs=[SMEM, VMEM, VMEM],
        out_specs=(VMEM, VMEM),
        compiler_params=pltpu.CompilerParams(vmem_limit_bytes=VMEM_LIMIT),
    )(place, acts, basis)


def pack_kernel(dp, cores, owner, place, rows, held, early, keep, send, last):
    row, core = place[0], place[1]
    last[...] = jnp.dot(rows[...], held[...], preferred_element_type=F32)
    for block in range(keep.shape[0]):
        for step in range(cores):
            piece = block * cores + lax.rem(core + step, cores)
            position = lax.rem(row - owner[piece] + dp, dp)
            target = keep.at[block] if step == 0 else send.at[step - 1, block]

            @pl.when(position == dp - 1)
            def _():
                target[...] = last[...]

            @pl.when(position < dp - 1)
            def _():
                target[...] = early[position]


def pack(owner_slot, place, rows, held, early, blocks, cores, dp):
    shape = (rows.shape[0], held.shape[1])
    return pl.pallas_call(
        functools.partial(pack_kernel, dp, cores),
        out_shape=(
            jax.ShapeDtypeStruct((blocks,) + shape, F32),
            jax.ShapeDtypeStruct((cores - 1, blocks) + shape, F32),
        ),
        in_specs=[SMEM, SMEM, VMEM, VMEM, VMEM],
        out_specs=(VMEM, VMEM),
        scratch_shapes=[pltpu.VMEM(shape, F32)],
        compiler_params=pltpu.CompilerParams(vmem_limit_bytes=VMEM_LIMIT),
    )(owner_slot, place, rows, held, early)


def square_kernel(dp, terms, counts, wanted, place, act, *refs):
    parts, outs = refs[:terms], refs[terms:]
    row = place[0]
    total = parts[0][...]
    for part in parts[1:]:
        total = total + part[...]
    sequences = total.shape[0] // LEN
    rotated = []
    for s in range(sequences):
        position = lax.broadcasted_iota(jnp.int32, (LEN, total.shape[1]), 0)
        used = jnp.where(position < counts[s], total[s * LEN : (s + 1) * LEN], 0.0)
        rotated.append(used.astype(BF16))
    height = outs[0].shape[0]
    for step in range(dp):
        start = lax.rem(row + step, dp) * height
        first = wanted[0, start // BW] * BW + lax.rem(start, BW)
        rows = pl.ds(pl.multiple_of(first, height), height)
        square = None
        for s in range(sequences):
            product = jnp.dot(
                act[rows, s * LEN : (s + 1) * LEN], rotated[s], preferred_element_type=F32
            )
            square = product * product if square is None else square + product * product
        outs[step][...] = square.astype(outs[step].dtype)


def squares(counts, wanted, place, act, parts, height, dp):
    width = parts[0].shape[1]
    return pl.pallas_call(
        functools.partial(square_kernel, dp, len(parts)),
        out_shape=tuple(
            jax.ShapeDtypeStruct((height, width), F32 if step == 0 else BF16)
            for step in range(dp)
        ),
        in_specs=[SMEM, SMEM, SMEM, VMEM] + [VMEM] * len(parts),
        out_specs=(VMEM,) * dp,
        compiler_params=pltpu.CompilerParams(vmem_limit_bytes=VMEM_LIMIT),
    )(counts, wanted, place, act, *parts)


def on_device(
    activations, gradients, token_counts, basis_act, basis_store, owner_slot, reader_blocks
):
    seq_local = activations.shape[0]
    slots = seq_local * LEN
    groups, dp = lax.axis_size("groups"), lax.axis_size("dp")
    cores, blocks = lax.axis_size("cores"), lax.axis_size("block")
    group, row = lax.axis_index("groups"), lax.axis_index("dp")
    block, core = lax.axis_index("block"), lax.axis_index("cores")
    _, features, width = basis_store.shape
    part_features = features // groups
    place = jnp.stack([row, core])

    held = lax.dynamic_slice_in_dim(basis_store[0], group * part_features, part_features, 0)
    flat_grads = gradients.reshape(slots, features)

    def share(index):
        return lax.dynamic_slice_in_dim(flat_grads, index * part_features, part_features, 1)

    away = [share((group + step) % groups) for step in range(1, groups)]
    pieces = [held]
    for step in range(1, dp):
        pieces.append(shift(pieces[-1], "dp", 1))
        if step == 1:
            pieces[1], activations = lax.optimization_barrier((pieces[1], activations))
    rows = [share(group)]
    for step in range(1, groups):
        rows.append(shift(away[step - 1], "groups", step))
    rows = jnp.concatenate(rows, axis=0)

    flat_acts = activations.reshape(slots, activations.shape[2])
    window = basis_act.shape[1]
    act, away = rotate(place, flat_acts, basis_act, cores)
    for step in range(1, cores):
        act = act + shift(away[step - 1], "cores", step)
    act = reduce_scatter(act.reshape(blocks, -1, slots), "block").astype(BF16)
    act = gather(act, "block").reshape(-1, slots)
    act_rot_t = gather(act, "cores").reshape(window, slots)

    early = [jnp.dot(rows, piece, preferred_element_type=F32) for piece in pieces[:-1]]
    held, act_rot_t = lax.optimization_barrier((pieces[-1], act_rot_t))
    keep, send = pack(
        owner_slot, place, rows, held, jnp.stack(early), blocks, cores, dp
    )
    for step in range(1, cores):
        keep = keep + shift(send[step - 1], "cores", step)

    mine = keep.reshape(blocks, groups, slots, width)
    parts = [block_of(mine, block)[0]]
    for far in range(blocks):
        toward = block_of(mine, (block + far) % blocks)
        for back in range(groups):
            if far or back:
                pairs = [
                    (g * blocks + b, ((g - back) % groups) * blocks + (b + far) % blocks)
                    for g in range(groups)
                    for b in range(blocks)
                ]
                parts.append(lax.ppermute(toward[back], ("groups", "block"), pairs))

    height = reader_blocks.shape[1] * BW // dp
    own, *others = squares(
        token_counts, reader_blocks, place, act_rot_t, parts, height, dp
    )
    for step in range(1, dp):
        own = own + shift(others[step - 1], "dp", step).astype(F32)
    return own / (seq_local * dp)


def solution(mesh):
    in_specs = (
        P(("groups", "dp"), None, ("block", "cores")),
        P(("groups", "dp"), None, ("block", "cores")),
        P(("groups", "dp")),
        P(("block", "cores"), None),
        P("dp", ("block", "cores"), None),
        P(),
        P(("block", "cores"), None),
    )
    out_specs = P(("groups", "dp"), ("block", "cores"))
    return jax.shard_map(
        on_device, mesh=mesh, in_specs=in_specs, out_specs=out_specs, check_vma=False
    )
```

time: 126 us -> 106 us (0.84)
  local copies, waits for them, and re-layouts: 38.8 us -> 8.97 us
  waiting for transfers between devices: 44.8 us -> 63.2 us
  between operations: 8.93 us -> 0.17 us
  matrix products: 15.5 us -> 8.39 us
  Pallas kernels: 0 us -> 6.2 us
    ppermute x12, waiting for transfers between devices: 39.9 us -> 55.9 us  [shift(): lax.ppermute(value, axis, [(i, (i + step) % size) for i in range(size)])]
    dynamic_update_slice x2, local copies, waits for them, and re-layouts: 8.16 us -> 0.05 us  [gather(): out = lax.dynamic_update_index_in_dim(out, came, (me - step) % size, 0)]
    dynamic_update_slice x1, local copies, waits for them, and re-layouts: 7.46 us -> 0.03 us  [gather(): out = lax.dynamic_update_index_in_dim(out, block, me, 0)]
    dot_general x6 -> x3, matrix products: 15.5 us -> 8.39 us  [on_device(): jnp.dot(rows, piece, preferred_element_type=F32)]
    dot_general x1 -> x0, local copies, waits for them, and re-layouts: 6.24 us -> none  [on_device(): lax.dot_general(basis_act, flat_acts, (((0,), (1,)), ((), ())), preferred...]
    pallas_call x0 -> x3, Pallas kernels: none -> 6.2 us  [the longest x1 2.8 us: rotate(): pl.pallas_call(functools.partial(rotate_kernel, cores), out_shape=(jax.Sh...]
    broadcast_in_dim x3 -> x0, local copies, waits for them, and re-layouts: 4.67 us -> none  [the longest x1 2.3 us: gather(): out = lax.dynamic_update_index_in_dim(out, block, me, 0)]
    unnamed x13 -> x14, local copies, waits for them, and re-layouts: 1.04 us -> 3.61 us
  transfers between devices with their start and end apart: 15 -> 15, of which waited for: 8 -> 11; matrix products, arithmetic and copies ran while one was open for 33% -> 14% of each run, Pallas kernels for 0% -> 3%
where the time goes in v3:
time: 106 us
  waiting for transfers between devices  63.2 us (60%)
  starting transfers between devices  15.2 us (14%)
  local copies, waits for them, and re-layouts  8.97 us (8%)
  matrix products  8.39 us (8%)
  Pallas kernels  6.2 us (6%)
  other arithmetic  3.78 us (4%)
    ppermute x12, waiting for transfers between devices, shift(): lax.ppermute(value, axis, [(i, (i + step) % size) for i in range(size)])  55.9 us
    ppermute x12, starting transfers between devices, shift(): lax.ppermute(value, axis, [(i, (i + step) % size) for i in range(size)])  11.6 us
    dot_general x3, matrix products, on_device(): jnp.dot(rows, piece, preferred_element_type=F32)  8.39 us
    ppermute x3, waiting for transfers between devices, on_device(): parts.append(lax.ppermute(toward[back], ('groups', 'block'), pairs))  7.28 us
    dynamic_slice x1, local copies, waits for them, and re-layouts, share(): lax.dynamic_slice_in_dim(flat_grads, index * part_features, part_features...  4.13 us
    unnamed x14, local copies, waits for them, and re-layouts  3.61 us
    ppermute x3, starting transfers between devices, on_device(): parts.append(lax.ppermute(toward[back], ('groups', 'block'), pairs))  3.55 us
    pallas_call x1, Pallas kernels, rotate(): pl.pallas_call(functools.partial(rotate_kernel, cores), out_shape=(jax.Sh...  2.8 us
  transfers between devices with their start and end apart: 15, of which 11 were waited for; matrix products, arithmetic and copies ran while one was open for 14% of the time, Pallas kernels for 3%

profile of v3, /device:TPU:0, one launch (start us, length us, event | category | flops | bytes accessed | tf_op | source)
XLA Modules:
  0.0 105.9 jit_solution(10421714062142402777)
XLA Ops:
  0.0 0.0 copy-start
  0.0 1.5 %copy-done = bf16[1,6912,128]{2,1,0:T(8,128)(2,1)S(1)} copy-done((bf16[1,6912,128]{2,1,0:T(8,128)(2,1)S(1)}, bf16[1,6912,128]{2,1,0:T(8,128)(2,1)}, u32[]{:S(2)}) %copy-start) | copy-done | bytes 1769496
  1.5 1.0 dynamic-slice_bitcast_fusion
  2.5 3.0 %collective-permute-start = (bf16[3456,128]{1,0:T(8,128)(2,1)}, bf16[3456,128]{1,0:T(8,128)(2,1)}, u32[]{:S(2)}, u32[]{:S(2)}) collective-permute-start(bf16[3456,128]{1,0:T(8,128)(2,1)} %dynamic-slice_bitcast_fusion), channel_id=1, source_target_pairs={{0,4},{4,8},{8,12},{12,0},{1,5},{5,9},{9,13},{13,1},{2,6},{6,10},{... | collective-permute-start | bytes 2654216 | tf_op jit(solution)/shard_map/ppermute | solution.py:21
  5.5 0.0 copy-start.2
  5.5 4.1 %constant_dynamic-slice_fusion.1 = (bf16[256,3456]{1,0:T(8,128)(2,1)}, bf16[256,3456]{1,0:T(8,128)(2,1)}) fusion(bf16[256,6912]{1,0:T(8,128)(2,1)} %bitcast.47, s32[]{:T(128)S(6)} %select_n.57, s32[]{:T(128)S(6)} %select_n.67), kind=kLoop, calls=%fused_computation.19 | loop fusion | bytes 7077896 | tf_op jit(solution)/shard_map/dynamic_slice | solution.py:162
  9.6 1.5 %collective-permute-start.7 = (bf16[256,3456]{1,0:T(8,128)(2,1)}, bf16[256,3456]{1,0:T(8,128)(2,1)}, u32[]{:S(2)}, u32[]{:S(2)}) collective-permute-start(bf16[256,3456]{1,0:T(8,128)(2,1)} %get-tuple-element.32), channel_id=1, source_target_pairs={{0,16},{16,0},{1,17},{17,1},{2,18},{18,2},{3,19},{19,3},{4,20},{20... | collective-permute-start | bytes 5308424 | tf_op jit(solution)/shard_map/ppermute | solution.py:21
  11.1 0.1 pad_add_fusion.place
  11.2 16.3 %collective-permute-done = bf16[3456,128]{1,0:T(8,128)(2,1)} collective-permute-done((bf16[3456,128]{1,0:T(8,128)(2,1)}, bf16[3456,128]{1,0:T(8,128)(2,1)}, u32[]{:S(2)}, u32[]{:S(2)}) %collective-permute-start) | collective-permute-done | bytes 884768 | tf_op jit(solution)/shard_map/ppermute | solution.py:21
  27.5 0.0 copy-done.2
  27.5 0.0 copy-start.1
  27.5 2.1 %copy-done.1 = bf16[1280,1536]{1,0:T(8,128)(2,1)S(1)} copy-done((bf16[1280,1536]{1,0:T(8,128)(2,1)S(1)}, bf16[1280,1536]{1,0:T(8,128)(2,1)}, u32[]{:S(2)}) %copy-start.1) | copy-done | bytes 3932184
  29.6 2.8 %shard_map.73 = (f32[768,256]{1,0:T(8,128)S(1)}, f32[1,768,256]{2,1,0:T(8,128)}) custom-call(s32[2]{0:T(128)S(1)} %pad_add_fusion.place, bf16[256,1280]{1,0:T(8,128)(2,1)S(1)} %bitcast.46, bf16[1280,1536]{1,0:T(8,128)(2,1)S(1)} %copy-done.1), custom_call_target="tpu_custom_call" | custom-call | tf_op jit(solution)/shard_map/pallas_call | solution.py:60
  32.4 0.0 collective-permute-start.3
  32.4 0.0 collective-permute-start.1
  32.4 0.0 copy-start.6
  32.4 2.5 %collective-permute-done.3 = f32[768,256]{1,0:T(8,128)S(1)} collective-permute-done((f32[768,256]{1,0:T(8,128)}, f32[768,256]{1,0:T(8,128)S(1)}, u32[]{:S(2)}, u32[]{:S(2)}) %collective-permute-start.3) | collective-permute-done | bytes 786464 | tf_op jit(solution)/shard_map/ppermute | solution.py:21
  34.9 0.1 add.77
  35.0 1.6 %collective-permute-start.4 = (f32[384,256]{1,0:T(8,128)S(1)}, f32[384,256]{1,0:T(8,128)S(1)}, u32[]{:S(2)}, u32[]{:S(2)}) collective-permute-start(f32[384,256]{1,0:T(8,128)S(1)} %dynamic-slice_bitcast_fusion.1), channel_id=1, source_target_pairs={{0,2},{2,0},{1,3},{3,1},{4,6},{6,4},{5,7},{7,5},{8,10},{10,8},{9,1... | collective-permute-start | bytes 1179656 | tf_op jit(solution)/shard_map/ppermute | solution.py:21
  36.6 20.0 %collective-permute-done.1 = bf16[3456,128]{1,0:T(8,128)(2,1)} collective-permute-done((bf16[3456,128]{1,0:T(8,128)(2,1)}, bf16[3456,128]{1,0:T(8,128)(2,1)}, u32[]{:S(2)}, u32[]{:S(2)}) %collective-permute-start.1) | collective-permute-done | bytes 884768 | tf_op jit(solution)/shard_map/ppermute | solution.py:21
  56.6 0.0 collective-permute-start.2
  56.6 0.0 collective-permute-done.7
  56.6 0.0 copy-done.6
  56.6 1.7 %pad_maximum_fusion.rows = bf16[512,3456]{1,0:T(8,128)(2,1)S(1)} fusion(bf16[256,3456]{1,0:T(8,128)(2,1)} %collective-permute-done.7, bf16[256,3456]{1,0:T(8,128)(2,1)S(1)} %copy-done.6), kind=kLoop, calls=%fused_computation | loop fusion | flops 7077888 | bytes 7077888 | tf_op jit(solution)/shard_map/concatenate | solution.py:173
  58.3 2.8 %convolution_bitcast_fusion = f32[1,512,128]{2,1,0:T(8,128)S(1)} fusion(bf16[3456,128]{1,0:T(8,128)(2,1)} %collective-permute-done.1, bf16[256,3456]{1,0:T(8,128)(2,1)} %collective-permute-done.7, bf16[256,3456]{1,0:T(8,128)(2,1)S(1)} %copy-done.6), kind=kOutput, calls=%fused_computation.1 | convolution fusion | flops 460062720 | bytes 4685824 | tf_op jit(solution)/shard_map/dot_general | solution.py:184
  61.1 0.0 collective-permute-done.4
  61.2 1.6 %collective-permute-start.5 = (bf16[384,256]{1,0:T(8,128)(2,1)S(1)}, bf16[384,256]{1,0:T(8,128)(2,1)S(1)}, u32[]{:S(2)}, u32[]{:S(2)}) collective-permute-start(bf16[384,256]{1,0:T(8,128)(2,1)S(1)} %get-tuple-element.30), channel_id=1, source_target_pairs={{0,2},{2,0},{1,3},{3,1},{4,6},{6,4},{5,7},{7,5},{8,10},{10,8},{9,1... | collective-permute-start | bytes 589832 | tf_op jit(solution)/shard_map/ppermute | solution.py:21
  62.8 2.8 %convolution_bitcast_fusion.1 = f32[1,512,128]{2,1,0:T(8,128)S(1)} fusion(bf16[3456,128]{1,0:T(8,128)(2,1)} %collective-permute-done, bf16[256,3456]{1,0:T(8,128)(2,1)} %collective-permute-done.7, bf16[256,3456]{1,0:T(8,128)(2,1)S(1)} %copy-done.6), kind=kOutput, calls=%fused_computation.2 | convolution fusion | flops 460062720 | bytes 4685824 | tf_op jit(solution)/shard_map/dot_general | solution.py:184
  65.6 2.2 %collective-permute-done.5 = bf16[384,256]{1,0:T(8,128)(2,1)S(1)} collective-permute-done((bf16[384,256]{1,0:T(8,128)(2,1)S(1)}, bf16[384,256]{1,0:T(8,128)(2,1)S(1)}, u32[]{:S(2)}, u32[]{:S(2)}) %collective-permute-start.5) | collective-permute-done | bytes 196640 | tf_op jit(solution)/shard_map/ppermute | solution.py:21
  67.8 0.1 collective-permute-start.6
  67.9 2.8 %convolution_bitcast_fusion.2 = f32[1,512,128]{2,1,0:T(8,128)S(1)} fusion(bf16[3456,128]{1,0:T(8,128)(2,1)} %dynamic-slice_bitcast_fusion, bf16[256,3456]{1,0:T(8,128)(2,1)} %collective-permute-done.7, bf16[256,3456]{1,0:T(8,128)(2,1)S(1)} %copy-done.6), kind=kOutput, calls=%fused_computation.3 | convolution fusion | flops 460062720 | bytes 4685824 | tf_op jit(solution)/shard_map/dot_general | solution.py:184
  70.7 0.0 copy-start.3
  70.7 0.1 pad_maximum_fusion.1.early
  70.8 0.1 broadcast_in_dim.20
  70.9 0.0 collective-permute-done.6
  70.9 8.9 %collective-permute-done.2.held = bf16[3456,128]{1,0:T(8,128)(2,1)S(1)} collective-permute-done((bf16[3456,128]{1,0:T(8,128)(2,1)}, bf16[3456,128]{1,0:T(8,128)(2,1)S(1)}, u32[]{:S(2)}, u32[]{:S(2)}) %collective-permute-start.2) | collective-permute-done | bytes 884768 | tf_op jit(solution)/shard_map/ppermute | solution.py:21
  79.8 0.0 copy-done.3
  79.9 0.0 copy-start.4
  79.9 0.0 copy-start.5
  79.9 2.5 %shard_map.74 = (f32[2,512,128]{2,1,0:T(8,128)S(1)}, f32[1,2,512,128]{3,2,1,0:T(8,128)}) custom-call(s32[4]{0:T(128)S(1)} %copy-done.3, s32[2]{0:T(128)S(1)} %pad_add_fusion.place, bf16[512,3456]{1,0:T(8,128)(2,1)S(1)} %pad_maximum_fusion.rows, bf16[3456,128]{1,0:T(8,128)(2,1)S(1)} %collective-permute-done.2.held, f32[3,512,128]{2,1,0:T(8,128)S(1)} %pad_maximum_fusion.1.early), custom_call_target="tpu_custom_call" | custom-call | tf_op jit(solution)/shard_map/pallas_call | solution.py:92
  82.4 0.0 collective-permute-start.8
  82.4 2.2 %collective-permute-done.8 = f32[2,512,128]{2,1,0:T(8,128)} collective-permute-done((f32[2,512,128]{2,1,0:T(8,128)}, f32[2,512,128]{2,1,0:T(8,128)}, u32[]{:S(2)}, u32[]{:S(2)}) %collective-permute-start.8) | collective-permute-done | bytes 524320 | tf_op jit(solution)/shard_map/ppermute | solution.py:21
  84.7 1.1 %add.91 = f32[2,512,128]{2,1,0:T(8,128)S(1)} add(f32[2,512,128]{2,1,0:T(8,128)S(1)} %get-tuple-element.23, f32[2,512,128]{2,1,0:T(8,128)} %collective-permute-done.8) | non-fusion elementwise | flops 131072 | bytes 1572864 | tf_op jit(solution)/shard_map/add | solution.py:190
  85.8 1.6 %collective-permute-start.10 = (f32[256,128]{1,0:T(8,128)S(1)}, f32[256,128]{1,0:T(8,128)S(1)}, u32[]{:S(2)}, u32[]{:S(2)}) collective-permute-start(f32[256,128]{1,0:T(8,128)S(1)} %get-tuple-element.34), channel_id=1, source_target_pairs={{0,2},{2,0},{16,18},{18,16},{1,3},{3,1},{17,19},{19,17},{4,6},{6,4... | collective-permute-start | bytes 393224 | tf_op jit(solution)/shard_map/ppermute | solution.py:203
  87.4 1.5 %collective-permute-start.11 = (f32[256,128]{1,0:T(8,128)S(1)}, f32[256,128]{1,0:T(8,128)S(1)}, u32[]{:S(2)}, u32[]{:S(2)}) collective-permute-start(f32[256,128]{1,0:T(8,128)S(1)} %get-tuple-element.33), channel_id=1, source_target_pairs={{0,18},{2,16},{16,2},{18,0},{1,19},{3,17},{17,3},{19,1},{4,22},{6,... | collective-permute-start | bytes 393224 | tf_op jit(solution)/shard_map/ppermute | solution.py:203
  88.9 0.5 collective-permute-start.9
  89.4 2.6 %collective-permute-done.10.refs_2_ = f32[256,128]{1,0:T(8,128)S(1)} collective-permute-done((f32[256,128]{1,0:T(8,128)S(1)}, f32[256,128]{1,0:T(8,128)S(1)}, u32[]{:S(2)}, u32[]{:S(2)}) %collective-permute-start.10) | collective-permute-done | bytes 131104 | tf_op jit(solution)/shard_map/ppermute | solution.py:203
  92.0 3.3 %collective-permute-done.11.refs_3_ = f32[256,128]{1,0:T(8,128)S(1)} collective-permute-done((f32[256,128]{1,0:T(8,128)S(1)}, f32[256,128]{1,0:T(8,128)S(1)}, u32[]{:S(2)}, u32[]{:S(2)}) %collective-permute-start.11) | collective-permute-done | bytes 131104 | tf_op jit(solution)/shard_map/ppermute | solution.py:203
  95.3 1.4 %collective-permute-done.9.refs_1_ = f32[256,128]{1,0:T(8,128)S(1)} collective-permute-done((f32[256,128]{1,0:T(8,128)S(1)}, f32[256,128]{1,0:T(8,128)S(1)}, u32[]{:S(2)}, u32[]{:S(2)}) %collective-permute-start.9) | collective-permute-done | bytes 131104 | tf_op jit(solution)/shard_map/ppermute | solution.py:203
  96.6 0.0 copy-done.4
  96.6 0.0 copy-done.5
  96.7 0.9 shard_map.75
  97.5 0.1 collective-permute-start.12
  97.6 0.2 collective-permute-start.13
  97.8 3.6 %collective-permute-start.14 = (bf16[256,128]{1,0:T(8,128)(2,1)S(1)}, bf16[256,128]{1,0:T(8,128)(2,1)S(1)}, u32[]{:S(2)}, u32[]{:S(2)}) collective-permute-start(bf16[256,128]{1,0:T(8,128)(2,1)S(1)} %get-tuple-element.28), channel_id=1, source_target_pairs={{0,12},{4,0},{8,4},{12,8},{1,13},{5,1},{9,5},{13,9},{2,14},{6,2},{... | collective-permute-start | bytes 196616 | tf_op jit(solution)/shard_map/ppermute | solution.py:21
  101.4 2.6 %collective-permute-done.12 = bf16[256,128]{1,0:T(8,128)(2,1)S(1)} collective-permute-done((bf16[256,128]{1,0:T(8,128)(2,1)S(1)}, bf16[256,128]{1,0:T(8,128)(2,1)S(1)}, u32[]{:S(2)}, u32[]{:S(2)}) %collective-permute-start.12) | collective-permute-done | bytes 65568 | tf_op jit(solution)/shard_map/ppermute | solution.py:21
  104.0 1.2 %collective-permute-done.13 = bf16[256,128]{1,0:T(8,128)(2,1)S(1)} collective-permute-done((bf16[256,128]{1,0:T(8,128)(2,1)S(1)}, bf16[256,128]{1,0:T(8,128)(2,1)S(1)}, u32[]{:S(2)}, u32[]{:S(2)}) %collective-permute-start.13) | collective-permute-done | bytes 65568 | tf_op jit(solution)/shard_map/ppermute | solution.py:21
  105.2 0.0 collective-permute-done.14
  105.2 0.7 add_multiply_fusion
  (7 shorter events, 0.2 us)
Async XLA Ops:
  0.0 1.5 %copy-start = (bf16[1,6912,128]{2,1,0:T(8,128)(2,1)S(1)}, bf16[1,6912,128]{2,1,0:T(8,128)(2,1)}, u32[]{:S(2)}) copy-start(bf16[1,6912,128]{2,1,0:T(8,128)(2,1)} %param.11) | copy-start | bytes 5308420
  2.5 25.0 %collective-permute-start = (bf16[3456,128]{1,0:T(8,128)(2,1)}, bf16[3456,128]{1,0:T(8,128)(2,1)}, u32[]{:S(2)}, u32[]{:S(2)}) collective-permute-start(bf16[3456,128]{1,0:T(8,128)(2,1)} %dynamic-slice_bitcast_fusion), channel_id=1, source_target_pairs={{0,4},{4,8},{8,12},{12,0},{1,5},{5,9},{9,13},{13,1},{2,6},{6,10},{... | collective-permute-start | bytes 2654216 | tf_op jit(solution)/shard_map/ppermute | solution.py:21
  5.5 22.0 %copy-start.2 = (bf16[2,128,1280]{2,1,0:T(8,128)(2,1)S(1)}, bf16[2,128,1280]{2,1,0:T(8,128)(2,1)}, u32[]{:S(2)}) copy-start(bf16[2,128,1280]{2,1,0:T(8,128)(2,1)} %param.7) | copy-start | bytes 1966084
  9.6 47.0 %collective-permute-start.7 = (bf16[256,3456]{1,0:T(8,128)(2,1)}, bf16[256,3456]{1,0:T(8,128)(2,1)}, u32[]{:S(2)}, u32[]{:S(2)}) collective-permute-start(bf16[256,3456]{1,0:T(8,128)(2,1)} %get-tuple-element.32), channel_id=1, source_target_pairs={{0,16},{16,0},{1,17},{17,1},{2,18},{18,2},{3,19},{19,3},{4,20},{20... | collective-permute-start | bytes 5308424 | tf_op jit(solution)/shard_map/ppermute | solution.py:21
  27.5 2.1 %copy-start.1 = (bf16[1280,1536]{1,0:T(8,128)(2,1)S(1)}, bf16[1280,1536]{1,0:T(8,128)(2,1)}, u32[]{:S(2)}) copy-start(bf16[1280,1536]{1,0:T(8,128)(2,1)} %basis.1) | copy-start | bytes 11796484
  32.4 2.5 %collective-permute-start.3 = (f32[768,256]{1,0:T(8,128)}, f32[768,256]{1,0:T(8,128)S(1)}, u32[]{:S(2)}, u32[]{:S(2)}) collective-permute-start(f32[768,256]{1,0:T(8,128)} %bitcast.4), channel_id=1, source_target_pairs={{0,1},{1,0},{2,3},{3,2},{4,5},{5,4},{6,7},{7,6},{8,9},{9,8},{10,11... | collective-permute-start | bytes 2359304 | tf_op jit(solution)/shard_map/ppermute | solution.py:21
  32.4 24.2 %collective-permute-start.1 = (bf16[3456,128]{1,0:T(8,128)(2,1)}, bf16[3456,128]{1,0:T(8,128)(2,1)}, u32[]{:S(2)}, u32[]{:S(2)}) collective-permute-start(bf16[3456,128]{1,0:T(8,128)(2,1)} %collective-permute-done), channel_id=1, source_target_pairs={{0,4},{4,8},{8,12},{12,0},{1,5},{5,9},{9,13},{13,1},{2,6},{6,10},{... | collective-permute-start | bytes 2654216 | tf_op jit(solution)/shard_map/ppermute | solution.py:21
  32.4 24.2 %copy-start.6 = (bf16[256,3456]{1,0:T(8,128)(2,1)S(1)}, bf16[256,3456]{1,0:T(8,128)(2,1)}, u32[]{:S(2)}) copy-start(bf16[256,3456]{1,0:T(8,128)(2,1)} %get-tuple-element.31) | copy-start | bytes 5308420
  35.0 26.1 %collective-permute-start.4 = (f32[384,256]{1,0:T(8,128)S(1)}, f32[384,256]{1,0:T(8,128)S(1)}, u32[]{:S(2)}, u32[]{:S(2)}) collective-permute-start(f32[384,256]{1,0:T(8,128)S(1)} %dynamic-slice_bitcast_fusion.1), channel_id=1, source_target_pairs={{0,2},{2,0},{1,3},{3,1},{4,6},{6,4},{5,7},{7,5},{8,10},{10,8},{9,1... | collective-permute-start | bytes 1179656 | tf_op jit(solution)/shard_map/ppermute | solution.py:21
  56.6 23.3 %collective-permute-start.2 = (bf16[3456,128]{1,0:T(8,128)(2,1)}, bf16[3456,128]{1,0:T(8,128)(2,1)S(1)}, u32[]{:S(2)}, u32[]{:S(2)}) collective-permute-start(bf16[3456,128]{1,0:T(8,128)(2,1)} %collective-permute-done.1), channel_id=1, source_target_pairs={{0,4},{4,8},{8,12},{12,0},{1,5},{5,9},{9,13},{13,1},{2,6},{6,10},{... | collective-permute-start | bytes 2654216 | tf_op jit(solution)/shard_map/ppermute | solution.py:21
  61.2 6.6 %collective-permute-start.5 = (bf16[384,256]{1,0:T(8,128)(2,1)S(1)}, bf16[384,256]{1,0:T(8,128)(2,1)S(1)}, u32[]{:S(2)}, u32[]{:S(2)}) collective-permute-start(bf16[384,256]{1,0:T(8,128)(2,1)S(1)} %get-tuple-element.30), channel_id=1, source_target_pairs={{0,2},{2,0},{1,3},{3,1},{4,6},{6,4},{5,7},{7,5},{8,10},{10,8},{9,1... | collective-permute-start | bytes 589832 | tf_op jit(solution)/shard_map/ppermute | solution.py:21
  67.8 3.1 %collective-permute-start.6 = (bf16[768,256]{1,0:T(8,128)(2,1)S(1)}, bf16[768,256]{1,0:T(8,128)(2,1)S(1)}, u32[]{:S(2)}, u32[]{:S(2)}) collective-permute-start(bf16[768,256]{1,0:T(8,128)(2,1)S(1)} %bitcast.51), channel_id=1, source_target_pairs={{0,1},{1,0},{2,3},{3,2},{4,5},{5,4},{6,7},{7,6},{8,9},{9,8},{10,11... | collective-permute-start | bytes 1179656 | tf_op jit(solution)/shard_map/ppermute | solution.py:21
  70.7 9.1 %copy-start.3 = (s32[4]{0:T(128)S(1)}, s32[4]{0:T(128)}, u32[]{:S(2)}) copy-start(s32[4]{0:T(128)} %owner.1) | copy-start | bytes 52
  79.9 16.8 %copy-start.4 = (s32[2]{0:T(128)S(1)}, s32[2]{0:T(128)}, u32[]{:S(2)}) copy-start(s32[2]{0:T(128)} %counts.1) | copy-start | bytes 28
  79.9 16.8 %copy-start.5 = (s32[1,2]{1,0:T(1,128)S(1)}, s32[1,2]{1,0:T(1,128)}, u32[]{:S(2)}) copy-start(s32[1,2]{1,0:T(1,128)} %wanted.1) | copy-start | bytes 28
  82.4 2.3 %collective-permute-start.8 = (f32[2,512,128]{2,1,0:T(8,128)}, f32[2,512,128]{2,1,0:T(8,128)}, u32[]{:S(2)}, u32[]{:S(2)}) collective-permute-start(f32[2,512,128]{2,1,0:T(8,128)} %bitcast.18), channel_id=1, source_target_pairs={{0,1},{1,0},{2,3},{3,2},{4,5},{5,4},{6,7},{7,6},{8,9},{9,8},{10,11... | collective-permute-start | bytes 1572872 | tf_op jit(solution)/shard_map/ppermute | solution.py:21
  85.8 6.2 %collective-permute-start.10 = (f32[256,128]{1,0:T(8,128)S(1)}, f32[256,128]{1,0:T(8,128)S(1)}, u32[]{:S(2)}, u32[]{:S(2)}) collective-permute-start(f32[256,128]{1,0:T(8,128)S(1)} %get-tuple-element.34), channel_id=1, source_target_pairs={{0,2},{2,0},{16,18},{18,16},{1,3},{3,1},{17,19},{19,17},{4,6},{6,4... | collective-permute-start | bytes 393224 | tf_op jit(solution)/shard_map/ppermute | solution.py:203
  87.4 7.9 %collective-permute-start.11 = (f32[256,128]{1,0:T(8,128)S(1)}, f32[256,128]{1,0:T(8,128)S(1)}, u32[]{:S(2)}, u32[]{:S(2)}) collective-permute-start(f32[256,128]{1,0:T(8,128)S(1)} %get-tuple-element.33), channel_id=1, source_target_pairs={{0,18},{2,16},{16,2},{18,0},{1,19},{3,17},{17,3},{19,1},{4,22},{6,... | collective-permute-start | bytes 393224 | tf_op jit(solution)/shard_map/ppermute | solution.py:203
  88.9 7.8 %collective-permute-start.9 = (f32[256,128]{1,0:T(8,128)S(1)}, f32[256,128]{1,0:T(8,128)S(1)}, u32[]{:S(2)}, u32[]{:S(2)}) collective-permute-start(f32[256,128]{1,0:T(8,128)S(1)} %get-tuple-element.35), channel_id=1, source_target_pairs={{0,16},{2,18},{16,0},{18,2},{1,17},{3,19},{17,1},{19,3},{4,20},{6,... | collective-permute-start | bytes 393224 | tf_op jit(solution)/shard_map/ppermute | solution.py:203
  97.5 6.5 %collective-permute-start.12 = (bf16[256,128]{1,0:T(8,128)(2,1)S(1)}, bf16[256,128]{1,0:T(8,128)(2,1)S(1)}, u32[]{:S(2)}, u32[]{:S(2)}) collective-permute-start(bf16[256,128]{1,0:T(8,128)(2,1)S(1)} %get-tuple-element.26), channel_id=1, source_target_pairs={{0,4},{4,8},{8,12},{12,0},{1,5},{5,9},{9,13},{13,1},{2,6},{6,10},{... | collective-permute-start | bytes 196616 | tf_op jit(solution)/shard_map/ppermute | solution.py:21
  97.6 7.6 %collective-permute-start.13 = (bf16[256,128]{1,0:T(8,128)(2,1)S(1)}, bf16[256,128]{1,0:T(8,128)(2,1)S(1)}, u32[]{:S(2)}, u32[]{:S(2)}) collective-permute-start(bf16[256,128]{1,0:T(8,128)(2,1)S(1)} %get-tuple-element.27), channel_id=1, source_target_pairs={{0,8},{4,12},{8,0},{12,4},{1,9},{5,13},{9,1},{13,5},{2,10},{6,14},... | collective-permute-start | bytes 196616 | tf_op jit(solution)/shard_map/ppermute | solution.py:21
  97.8 7.4 %collective-permute-start.14 = (bf16[256,128]{1,0:T(8,128)(2,1)S(1)}, bf16[256,128]{1,0:T(8,128)(2,1)S(1)}, u32[]{:S(2)}, u32[]{:S(2)}) collective-permute-start(bf16[256,128]{1,0:T(8,128)(2,1)S(1)} %get-tuple-element.28), channel_id=1, source_target_pairs={{0,12},{4,0},{8,4},{12,8},{1,13},{5,1},{9,5},{13,9},{2,14},{6,2},{... | collective-permute-start | bytes 196616 | tf_op jit(solution)/shard_map/ppermute | solution.py:21

commit v4 on v3

v4 whole, which is shorter than its diff:
```python
import functools

import jax
import jax.numpy as jnp
from jax import lax
from jax.experimental import pallas as pl
from jax.experimental.pallas import tpu as pltpu
from jax.sharding import PartitionSpec as P

BW = 512
LEN = 128
FLOPS_SCALE = 1
F32 = jnp.float32
BF16 = jnp.bfloat16
VMEM_LIMIT = 40 * 1024 * 1024
VMEM = pl.BlockSpec(memory_space=pltpu.VMEM)
SMEM = pl.BlockSpec(memory_space=pltpu.SMEM)


def after(value, *gates):
    return lax.optimization_barrier((value,) + gates)[0]


def shift(value, axis, step):
    size = lax.axis_size(axis)
    return lax.ppermute(value, axis, [(i, (i + step) % size) for i in range(size)])


def block_of(value, index):
    return lax.dynamic_index_in_dim(value, index, 0, keepdims=False)


def to_neighbour(value, far, step):
    cores, blocks = lax.axis_size("cores"), lax.axis_size("block")
    pairs = [
        (b * cores + c, (b + far) % blocks * cores + (c + step) % cores)
        for b in range(blocks)
        for c in range(cores)
    ]
    return lax.ppermute(value, ("block", "cores"), pairs)


def gather_act(act):
    cores, blocks = lax.axis_size("cores"), lax.axis_size("block")
    core, block = lax.axis_index("cores"), lax.axis_index("block")
    out = jnp.zeros((cores, blocks) + act.shape, act.dtype)
    for far in range(blocks):
        for step in range(cores):
            came = to_neighbour(act, far, step) if far or step else act
            source = ((core - step) % cores, (block - far) % blocks, 0, 0)
            out = lax.dynamic_update_slice(out, came[None, None], source)
    return out.reshape(-1, act.shape[-1])


def rotate_kernel(blocks, cores, place, acts, basis, *outs):
    height = outs[0].shape[0]
    for core_step in range(cores):
        core = lax.rem(place[1] + core_step, cores)
        span = blocks * height
        columns = pl.ds(pl.multiple_of(core * span, span), span)
        term = jnp.dot(acts[...], basis[:, columns], preferred_element_type=F32)
        for share in range(blocks):
            step = lax.rem(share - place[2] + blocks, blocks)
            part = term[:, share * height : (share + 1) * height].T
            for i in range(blocks):

                @pl.when(step == i)
                def _():
                    outs[i * cores + core_step][...] = part


def rotate(place, acts, basis, blocks, cores):
    shape = (basis.shape[1] // (blocks * cores), acts.shape[0])
    return pl.pallas_call(
        functools.partial(rotate_kernel, blocks, cores),
        out_shape=(jax.ShapeDtypeStruct(shape, F32),) * (blocks * cores),
        in_specs=[SMEM, VMEM, VMEM],
        out_specs=(VMEM,) * (blocks * cores),
        compiler_params=pltpu.CompilerParams(vmem_limit_bytes=VMEM_LIMIT),
    )(place, acts, basis)


def product(rows, piece, start):
    total, first = None, 0
    for part in rows:
        last = first + part.shape[1]
        low, high = max(first, start), min(last, start + piece.shape[0])
        if low < high:
            term = jnp.dot(
                part[:, low - first : high - first],
                piece[low - start : high - start],
                preferred_element_type=F32,
            )
            total = term if total is None else total + term
        first = last
    return total


def early_kernel(parts, shares, *refs):
    rows, pieces, out = refs[:parts], refs[parts:-1], refs[-1]
    for position in range(out.shape[0]):
        total = None
        for share, start in enumerate(shares):
            i = position * len(shares) + share
            if i < len(pieces):
                term = product(rows, pieces[i], start)
                total = term if total is None else total + term
        out[position] = total


def early_products(rows, pieces, shares):
    positions = -(-len(pieces) // len(shares))
    height, width = rows[0].shape[0], pieces[0].shape[1]
    flops = 2 * height * width * sum(piece.shape[0] for piece in pieces)
    return pl.pallas_call(
        functools.partial(early_kernel, len(rows), shares),
        out_shape=jax.ShapeDtypeStruct((positions, height, width), F32),
        in_specs=[VMEM] * (len(rows) + len(pieces)),
        out_specs=VMEM,
        compiler_params=pltpu.CompilerParams(vmem_limit_bytes=VMEM_LIMIT),
        cost_estimate=pl.CostEstimate(
            flops=FLOPS_SCALE * flops, bytes_accessed=flops // width, transcendentals=0
        ),
    )(*rows, *pieces)


def pack_kernel(dp, cores, parts, start, owner, place, held, *refs):
    row, core = place[0], place[1]
    groups, refs = len(parts), list(refs)
    rows = [[refs.pop(0) for _ in range(cuts)] for cuts in parts]
    early = [refs.pop(0) for _ in parts]
    almost = [refs.pop(0) for _ in parts]
    last, height = refs.pop(), early[0].shape[1]
    spans = [pl.ds(g * height, height) for g in range(groups)]
    for g in range(groups):
        last[spans[g]] = almost[g][0] + product(rows[g], held, start)
    for block in range(refs[0].shape[0]):
        for step in range(cores):
            piece = block * cores + lax.rem(core + step, cores)
            position = lax.rem(row - owner[piece] + dp, dp)
            target = refs[step].at[block]

            @pl.when(position == dp - 1)
            def _():
                target[...] = last[...]

            @pl.when(position < dp - 1)
            def _():
                for g in range(groups):
                    target[spans[g]] = early[g][position]


def pack(owner_slot, place, rows, held, start, early, almost, blocks, cores):
    positions, height, width = early[0].shape
    shape = (len(rows) * height, width)
    parts = tuple(len(part) for part in rows)
    return pl.pallas_call(
        functools.partial(pack_kernel, positions + 1, cores, parts, start),
        out_shape=(jax.ShapeDtypeStruct((blocks,) + shape, F32),) * cores,
        in_specs=[SMEM, SMEM] + [VMEM] * (1 + sum(parts) + 2 * len(rows)),
        out_specs=(VMEM,) * cores,
        scratch_shapes=[pltpu.VMEM(shape, F32)],
        compiler_params=pltpu.CompilerParams(vmem_limit_bytes=VMEM_LIMIT),
    )(owner_slot, place, held, *[cut for part in rows for cut in part], *early, *almost)


def square_kernel(dp, terms, counts, wanted, place, act, *refs):
    parts, outs = refs[:terms], refs[terms:]
    row = place[0]
    total = parts[0][...]
    for part in parts[1:]:
        total = total + part[...]
    sequences = total.shape[0] // LEN
    rotated = []
    for s in range(sequences):
        position = lax.broadcasted_iota(jnp.int32, (LEN, total.shape[1]), 0)
        used = jnp.where(position < counts[s], total[s * LEN : (s + 1) * LEN], 0.0)
        rotated.append(used.astype(BF16))
    height = outs[0].shape[0]
    for step in range(dp):
        start = lax.rem(row + step, dp) * height
        first = wanted[0, start // BW] * BW + lax.rem(start, BW)
        rows = pl.ds(pl.multiple_of(first, height), height)
        square = None
        for s in range(sequences):
            product = jnp.dot(
                act[rows, s * LEN : (s + 1) * LEN], rotated[s], preferred_element_type=F32
            )
            square = product * product if square is None else square + product * product
        outs[step][...] = square.astype(outs[step].dtype)


def squares(counts, wanted, place, act, parts, height, dp):
    width = parts[0].shape[1]
    return pl.pallas_call(
        functools.partial(square_kernel, dp, len(parts)),
        out_shape=tuple(
            jax.ShapeDtypeStruct((height, width), F32 if step == 0 else BF16)
            for step in range(dp)
        ),
        in_specs=[SMEM, SMEM, SMEM, VMEM] + [VMEM] * len(parts),
        out_specs=(VMEM,) * dp,
        compiler_params=pltpu.CompilerParams(vmem_limit_bytes=VMEM_LIMIT),
    )(counts, wanted, place, act, *parts)


def on_device(
    activations, gradients, token_counts, basis_act, basis_store, owner_slot, reader_blocks
):
    seq_local = activations.shape[0]
    slots = seq_local * LEN
    groups, dp = lax.axis_size("groups"), lax.axis_size("dp")
    cores, blocks = lax.axis_size("cores"), lax.axis_size("block")
    group, row = lax.axis_index("groups"), lax.axis_index("dp")
    block, core = lax.axis_index("block"), lax.axis_index("cores")
    _, features, width = basis_store.shape
    part_features = features // groups
    place = jnp.stack([row, core, block])

    cut = -(-part_features // 256) * 128
    shares = (0, cut)
    rings = [
        [lax.dynamic_slice_in_dim(basis_store[0], group * part_features + start, size, 0)]
        for start, size in zip(shares, (cut, part_features - cut))
    ]
    flat_grads = after(gradients.reshape(slots, features), rings[0][0], rings[1][0])

    def share(index, start, size):
        return lax.dynamic_slice_in_dim(flat_grads, index * part_features + start, size, 1)

    rows, first = [[share(group, 0, part_features)]], part_features * 7 // 10 // 128 * 128
    for step in range(1, groups):
        rows.append(
            [
                shift(share((group + step) % groups, start, size), "groups", step)
                for start, size in ((0, first), (first, part_features - first))
            ]
        )

    flat_acts = activations.reshape(slots, activations.shape[2])
    act, *away = rotate(place, flat_acts, basis_act, blocks, cores)
    for step in range(1, dp):
        for ring in rings:
            ring.append(shift(ring[-1], "dp", 1))
    away = [to_neighbour(part, i // cores, i % cores) for i, part in enumerate(away, 1)]
    for part in away:
        act = act + part
    act_rot_t = gather_act(act.astype(BF16))

    pieces = [ring[step] for step in range(dp) for ring in rings]
    early = [early_products(part, pieces[:-2], shares) for part in rows]
    almost = [early_products(part, pieces[-2:-1], shares[:1]) for part in rows]
    last, *almost = lax.optimization_barrier((pieces[-1], *almost))
    keep, *send = pack(
        owner_slot, place, rows, last, cut, early, almost, blocks, cores
    )
    for step in range(1, cores):
        keep = keep + shift(send[step - 1], "cores", step)
    keep, act_rot_t = lax.optimization_barrier((keep, act_rot_t))

    mine = keep.reshape(blocks, groups, slots, width)
    parts = [block_of(mine, block)[0]]
    for far in range(blocks):
        toward = block_of(mine, (block + far) % blocks)
        for back in range(groups):
            if far or back:
                pairs = [
                    (g * blocks + b, ((g - back) % groups) * blocks + (b + far) % blocks)
                    for g in range(groups)
                    for b in range(blocks)
                ]
                parts.append(lax.ppermute(toward[back], ("groups", "block"), pairs))

    height = reader_blocks.shape[1] * BW // dp
    own, *others = squares(
        token_counts, reader_blocks, place, act_rot_t, parts, height, dp
    )
    for step in range(1, dp):
        own = own + shift(others[step - 1], "dp", step).astype(F32)
    return own / (seq_local * dp)


def solution(mesh):
    in_specs = (
        P(("groups", "dp"), None, ("block", "cores")),
        P(("groups", "dp"), None, ("block", "cores")),
        P(("groups", "dp")),
        P(("block", "cores"), None),
        P("dp", ("block", "cores"), None),
        P(),
        P(("block", "cores"), None),
    )
    out_specs = P(("groups", "dp"), ("block", "cores"))
    return jax.shard_map(
        on_device, mesh=mesh, in_specs=in_specs, out_specs=out_specs, check_vma=False
    )
```

time: 106 us -> 103 us (0.972)
  waiting for transfers between devices: 63.2 us -> 42.4 us
  Pallas kernels: 6.2 us -> 17.4 us
  local copies, waits for them, and re-layouts: 8.97 us -> 18.1 us
  matrix products: 8.39 us -> 0 us
  starting transfers between devices: 15.2 us -> 21.2 us
    ppermute x12, waiting for transfers between devices: 55.9 us -> 29.6 us  [shift(): lax.ppermute(value, axis, [(i, (i + step) % size) for i in range(size)])]
    pallas_call x2 -> x6, Pallas kernels: 5.35 us -> 16 us  [the longest x4 10.3 us: early_products(): pl.pallas_call(functools.partial(early_kernel, len(rows), shares), out_sh...]
    dot_general x3 -> x0, matrix products: 8.39 us -> none  [on_device(): jnp.dot(rows, piece, preferred_element_type=F32)]
    ppermute x0 -> x6, waiting for transfers between devices: none -> 6.96 us  [to_neighbour(): return lax.ppermute(value, ('block', 'cores'), pairs)]
    ppermute x12, starting transfers between devices: 11.6 us -> 15.2 us  [shift(): lax.ppermute(value, axis, [(i, (i + step) % size) for i in range(size)])]
    unnamed x14 -> x24, local copies, waits for them, and re-layouts: 3.61 us -> 6.94 us
    dynamic_update_slice x3, local copies, waits for them, and re-layouts: 0.08 us -> 3.01 us  [gather_act(): out = lax.dynamic_update_slice(out, came[None, None], source)]
    ppermute x0 -> x6, starting transfers between devices: none -> 2.5 us  [to_neighbour(): return lax.ppermute(value, ('block', 'cores'), pairs)]
  transfers between devices with their start and end apart: 15 -> 21, of which waited for: 11 -> 11; matrix products, arithmetic and copies ran while one was open for 14% -> 11% of each run, Pallas kernels for 3% -> 16%
where the time goes in v4:
time: 103 us; the launch traced here: 102 us
  waiting for transfers between devices  42.4 us (41%)
  starting transfers between devices  21.2 us (21%)
  local copies, waits for them, and re-layouts  18.1 us (18%)
  Pallas kernels  17.4 us (17%)
  other arithmetic  2.92 us (3%)
    ppermute x12, waiting for transfers between devices, shift(): lax.ppermute(value, axis, [(i, (i + step) % size) for i in range(size)])  29.6 us
    ppermute x12, starting transfers between devices, shift(): lax.ppermute(value, axis, [(i, (i + step) % size) for i in range(size)])  15.2 us
    pallas_call x4, Pallas kernels, early_products(): pl.pallas_call(functools.partial(early_kernel, len(rows), shares), out_sh...  10.3 us
    ppermute x6, waiting for transfers between devices, to_neighbour(): return lax.ppermute(value, ('block', 'cores'), pairs)  6.96 us
    unnamed x24, local copies, waits for them, and re-layouts  6.94 us
    ppermute x3, waiting for transfers between devices, on_device(): parts.append(lax.ppermute(toward[back], ('groups', 'block'), pairs))  5.91 us
    dynamic_slice x2, local copies, waits for them, and re-layouts, on_device(): lax.dynamic_slice_in_dim(basis_store[0], group * part_features + start, s...  3.79 us
    ppermute x3, starting transfers between devices, on_device(): parts.append(lax.ppermute(toward[back], ('groups', 'block'), pairs))  3.55 us
  transfers between devices with their start and end apart: 21, of which 11 were waited for; matrix products, arithmetic and copies ran while one was open for 11% of the time, Pallas kernels for 16%

profile of v4, /device:TPU:0, one launch (start us, length us, event | category | flops | bytes accessed | tf_op | source)
XLA Modules:
  0.0 102.2 jit_solution(9731756785486078510)
XLA Ops:
  0.0 2.0 %dynamic-slice_bitcast_fusion.1.refs_2_.refs_3_ = bf16[1664,128]{1,0:T(8,128)(2,1)} fusion(bf16[1,6912,128]{2,1,0:T(8,128)(2,1)} %param.11, s32[]{:T(128)S(6)} %select_n.76), kind=kLoop, calls=%fused_computation.1 | loop fusion | bytes 851972 | tf_op jit(solution)/shard_map/dynamic_slice | solution.py:223
  2.0 3.0 %collective-permute-start = (bf16[1664,128]{1,0:T(8,128)(2,1)}, bf16[1664,128]{1,0:T(8,128)(2,1)}, u32[]{:S(2)}, u32[]{:S(2)}) collective-permute-start(bf16[1664,128]{1,0:T(8,128)(2,1)} %dynamic-slice_bitcast_fusion.1.refs_2_.refs_3_), channel_id=1, source_target_pairs={{0,4},{4,8},{8,12},{12,0},{1,5},{5,9},{9,13},{13,1},{2,6},{6,10},{... | collective-permute-start | bytes 1277960 | tf_op jit(solution)/shard_map/ppermute | solution.py:26
  5.0 0.1 pad_add_fusion.place
  5.1 2.1 %copy-done.3 = bf16[1280,1536]{1,0:T(8,128)(2,1)S(1)} copy-done((bf16[1280,1536]{1,0:T(8,128)(2,1)S(1)}, bf16[1280,1536]{1,0:T(8,128)(2,1)}, u32[]{:S(2)}) %copy-start.3) | copy-done | bytes 3932184
  7.2 1.1 %copy-done.4 = bf16[2,128,1280]{2,1,0:T(8,128)(2,1)S(1)} copy-done((bf16[2,128,1280]{2,1,0:T(8,128)(2,1)S(1)}, bf16[2,128,1280]{2,1,0:T(8,128)(2,1)}, u32[]{:S(2)}) %copy-start.4) | copy-done | bytes 655384
  8.3 3.4 %shard_map.78 = (f32[384,256]{1,0:T(8,128)S(1)}, f32[384,256]{1,0:T(8,128)S(1)}, f32[384,256]{1,0:T(8,128)S(1)}, f32[384,256]{1,0:T(8,128)}) custom-call(s32[3]{0:T(128)S(1)} %pad_add_fusion.place, bf16[256,1280]{1,0:T(8,128)(2,1)S(1)} %bitcast.30, bf16[1280,1536]{1,0:T(8,128)(2,1)S(1)} %copy-done.3), custom_call_target="tpu_custom_call" | custom-call | tf_op jit(solution)/shard_map/pallas_call | solution.py:74
  11.7 0.7 copy-done.5
  12.4 0.7 copy-done.10
  13.2 0.8 copy-done.11
  13.9 0.6 collective-permute-start.11
  14.6 1.8 %dynamic-slice_bitcast_fusion.refs_1_.refs_2_ = bf16[1792,128]{1,0:T(8,128)(2,1)} fusion(bf16[1,6912,128]{2,1,0:T(8,128)(2,1)} %param.11, s32[]{:T(128)S(6)} %select_n.77), kind=kLoop, calls=%fused_computation | loop fusion | bytes 917508 | tf_op jit(solution)/shard_map/dynamic_slice | solution.py:223
  16.4 1.6 %collective-permute-start.3 = (bf16[1792,128]{1,0:T(8,128)(2,1)}, bf16[1792,128]{1,0:T(8,128)(2,1)}, u32[]{:S(2)}, u32[]{:S(2)}) collective-permute-start(bf16[1792,128]{1,0:T(8,128)(2,1)} %dynamic-slice_bitcast_fusion.refs_1_.refs_2_), channel_id=1, source_target_pairs={{0,4},{4,8},{8,12},{12,0},{1,5},{5,9},{9,13},{13,1},{2,6},{6,10},{... | collective-permute-start | bytes 1376264 | tf_op jit(solution)/shard_map/ppermute | solution.py:26
  17.9 0.9 collective-permute-start.10
  18.8 0.1 collective-permute-start.9
  18.9 1.1 %constant_dynamic-slice_fusion.1 = bf16[256,2304]{1,0:T(8,128)(2,1)} fusion(bf16[256,6912]{1,0:T(8,128)(2,1)S(1)} %bitcast.29, s32[]{:T(128)S(6)} %select_n.79), kind=kLoop, calls=%fused_computation.13 | loop fusion | bytes 2359300 | tf_op jit(solution)/shard_map/dynamic_slice | solution.py:229
  20.0 5.6 %collective-permute-done.11 = f32[384,256]{1,0:T(8,128)} collective-permute-done((f32[384,256]{1,0:T(8,128)}, f32[384,256]{1,0:T(8,128)}, u32[]{:S(2)}, u32[]{:S(2)}) %collective-permute-start.11) | collective-permute-done | bytes 393248 | tf_op jit(solution)/shard_map/ppermute | solution.py:40
  25.6 1.5 %collective-permute-start.6 = (bf16[256,2304]{1,0:T(8,128)(2,1)}, bf16[256,2304]{1,0:T(8,128)(2,1)}, u32[]{:S(2)}, u32[]{:S(2)}) collective-permute-start(bf16[256,2304]{1,0:T(8,128)(2,1)} %constant_dynamic-slice_fusion.1), channel_id=1, source_target_pairs={{0,16},{16,0},{1,17},{17,1},{2,18},{18,2},{3,19},{19,3},{4,20},{20... | collective-permute-start | bytes 3538952 | tf_op jit(solution)/shard_map/ppermute | solution.py:26
  27.1 0.0 collective-permute-done.refs_4_.refs_5_
  27.1 1.6 %collective-permute-start.1 = (bf16[1664,128]{1,0:T(8,128)(2,1)}, bf16[1664,128]{1,0:T(8,128)(2,1)}, u32[]{:S(2)}, u32[]{:S(2)}) collective-permute-start(bf16[1664,128]{1,0:T(8,128)(2,1)} %collective-permute-done.refs_4_.refs_5_), channel_id=1, source_target_pairs={{0,4},{4,8},{8,12},{12,0},{1,5},{5,9},{9,13},{13,1},{2,6},{6,10},{... | collective-permute-start | bytes 1277960 | tf_op jit(solution)/shard_map/ppermute | solution.py:26
  28.7 3.2 %collective-permute-done.3.refs_3_.refs_4_ = bf16[1792,128]{1,0:T(8,128)(2,1)} collective-permute-done((bf16[1792,128]{1,0:T(8,128)(2,1)}, bf16[1792,128]{1,0:T(8,128)(2,1)}, u32[]{:S(2)}, u32[]{:S(2)}) %collective-permute-start.3) | collective-permute-done | bytes 458784 | tf_op jit(solution)/shard_map/ppermute | solution.py:26
  31.9 0.0 collective-permute-start.4
  31.9 0.9 constant_dynamic-slice_fusion
  32.8 1.3 %collective-permute-done.10 = f32[384,256]{1,0:T(8,128)} collective-permute-done((f32[384,256]{1,0:T(8,128)}, f32[384,256]{1,0:T(8,128)}, u32[]{:S(2)}, u32[]{:S(2)}) %collective-permute-start.10) | collective-permute-done | bytes 393248 | tf_op jit(solution)/shard_map/ppermute | solution.py:40
  34.1 1.5 %collective-permute-start.7 = (bf16[256,1152]{1,0:T(8,128)(2,1)}, bf16[256,1152]{1,0:T(8,128)(2,1)}, u32[]{:S(2)}, u32[]{:S(2)}) collective-permute-start(bf16[256,1152]{1,0:T(8,128)(2,1)} %constant_dynamic-slice_fusion), channel_id=1, source_target_pairs={{0,16},{16,0},{1,17},{17,1},{2,18},{18,2},{3,19},{19,3},{4,20},{20... | collective-permute-start | bytes 1769480 | tf_op jit(solution)/shard_map/ppermute | solution.py:26
  35.6 0.0 collective-permute-done.9
  35.6 0.9 broadcast_in_dim.15
  36.5 2.1 %bitcast_dynamic-update-slice_fusion.3 = (bf16[2,2,384,256]{3,2,1,0:T(8,128)(2,1)}, bf16[384,256]{1,0:T(8,128)(2,1)}) fusion(bf16[2,2,384,256]{3,2,1,0:T(8,128)(2,1)} %broadcast_in_dim.15, s32[]{:T(128)S(6)} %select_n.82, s32[]{:T(128)S(6)} %select_n.84, f32[384,256]{1,0:T(8,128)} %collective-permute-done.11, f32[384,256]{1,0:T(8,128)} %collective-permute-done.10, ...), kind=kLoop, calls=%fused_computation.6 | loop fusion | flops 393216 | bytes 1966088 | tf_op jit(solution)/shard_map/dynamic_update_slice | solution.py:51
  38.6 0.0 collective-permute-start.12
  38.6 3.4 %collective-permute-done.1.refs_6_.refs_7_ = bf16[1664,128]{1,0:T(8,128)(2,1)} collective-permute-done((bf16[1664,128]{1,0:T(8,128)(2,1)}, bf16[1664,128]{1,0:T(8,128)(2,1)}, u32[]{:S(2)}, u32[]{:S(2)}) %collective-permute-start.1) | collective-permute-done | bytes 426016 | tf_op jit(solution)/shard_map/ppermute | solution.py:26
  42.0 0.0 collective-permute-start.2
  42.0 9.8 %collective-permute-done.4.refs_5_.refs_6_ = bf16[1792,128]{1,0:T(8,128)(2,1)} collective-permute-done((bf16[1792,128]{1,0:T(8,128)(2,1)}, bf16[1792,128]{1,0:T(8,128)(2,1)}, u32[]{:S(2)}, u32[]{:S(2)}) %collective-permute-start.4) | collective-permute-done | bytes 458784 | tf_op jit(solution)/shard_map/ppermute | solution.py:26
  51.8 1.4 %constant_dynamic-slice_fusion.2.refs_0_ = bf16[256,3456]{1,0:T(8,128)(2,1)} fusion(bf16[256,6912]{1,0:T(8,128)(2,1)S(1)} %bitcast.28, s32[]{:T(128)S(6)} %select_n.77), kind=kLoop, calls=%fused_computation.14 | loop fusion | bytes 3538948 | tf_op jit(solution)/shard_map/dynamic_slice | solution.py:229
  53.2 1.5 %copy-done.1 = bf16[256,3456]{1,0:T(8,128)(2,1)S(1)} copy-done((bf16[256,3456]{1,0:T(8,128)(2,1)S(1)}, bf16[256,3456]{1,0:T(8,128)(2,1)}, u32[]{:S(2)}) %copy-start.1) | copy-done | bytes 1769496
  54.7 3.2 %shard_map.75.refs_3_ = f32[3,256,128]{2,1,0:T(8,128)S(1)} custom-call(bf16[256,3456]{1,0:T(8,128)(2,1)S(1)} %copy-done.1, bf16[1792,128]{1,0:T(8,128)(2,1)} %dynamic-slice_bitcast_fusion.refs_1_.refs_2_, bf16[1664,128]{1,0:T(8,128)(2,1)} %dynamic-slice_bitcast_fusion.1.refs_2_.refs_3_, bf16[1792,128]{1,0:T(8,128)(2,1)} %collective-permute-done.3.refs_3_.refs_4_, ...), custom_call_target="tpu_custom_call" | custom-call | flops 679477248 | bytes 5308416 | tf_op jit(solution)/shard_map/pallas_call | solution.py:115
  57.9 8.7 %collective-permute-done.7.refs_1_.refs_2_ = bf16[256,1152]{1,0:T(8,128)(2,1)} collective-permute-done((bf16[256,1152]{1,0:T(8,128)(2,1)}, bf16[256,1152]{1,0:T(8,128)(2,1)}, u32[]{:S(2)}, u32[]{:S(2)}) %collective-permute-start.7) | collective-permute-done | bytes 589856 | tf_op jit(solution)/shard_map/ppermute | solution.py:26
  66.6 0.9 collective-permute-start.13
  67.5 3.7 %shard_map.76.refs_4_ = f32[3,256,128]{2,1,0:T(8,128)S(1)} custom-call(bf16[256,2304]{1,0:T(8,128)(2,1)} %collective-permute-done.6.refs_0_.refs_1_, bf16[256,1152]{1,0:T(8,128)(2,1)} %collective-permute-done.7.refs_1_.refs_2_, bf16[1792,128]{1,0:T(8,128)(2,1)} %dynamic-slice_bitcast_fusion.refs_1_.refs_2_, ...), custom_call_target="tpu_custom_call" | custom-call | flops 679477248 | bytes 5308416 | tf_op jit(solution)/shard_map/pallas_call | solution.py:115
  71.3 1.4 %shard_map.73.refs_5_ = f32[1,256,128]{2,1,0:T(8,128)S(1)} custom-call(bf16[256,3456]{1,0:T(8,128)(2,1)S(1)} %copy-done.2, bf16[1792,128]{1,0:T(8,128)(2,1)} %collective-permute-done.5.refs_1_.refs_2_), custom_call_target="tpu_custom_call" | custom-call | flops 117440512 | bytes 917504 | tf_op jit(solution)/shard_map/pallas_call | solution.py:115
  72.7 0.0 copy-start.7
  72.7 1.9 %shard_map.74.refs_6_ = f32[1,256,128]{2,1,0:T(8,128)S(1)} custom-call(bf16[256,2304]{1,0:T(8,128)(2,1)} %collective-permute-done.6.refs_0_.refs_1_, bf16[256,1152]{1,0:T(8,128)(2,1)} %collective-permute-done.7.refs_1_.refs_2_, bf16[1792,128]{1,0:T(8,128)(2,1)} %collective-permute-done.5.refs_1_.refs_2_), custom_call_target="tpu_custom_call" | custom-call | flops 117440512 | bytes 917504 | tf_op jit(solution)/shard_map/pallas_call | solution.py:115
  74.7 0.0 collective-permute-done.2.held
  74.7 2.3 %shard_map.77 = (f32[2,512,128]{2,1,0:T(8,128)S(1)}, f32[2,512,128]{2,1,0:T(8,128)S(1)}) custom-call(s32[4]{0:T(128)S(1)} %copy-done.7, s32[3]{0:T(128)S(1)} %pad_add_fusion.place, bf16[1664,128]{1,0:T(8,128)(2,1)} %collective-permute-done.2.held, bf16[256,3456]{1,0:T(8,128)(2,1)S(1)} %copy-done.2, bf16[256,2304]{1,0:T(8,128)(2,1)} %collective-permute-done.6.refs_0_.refs_1_, ...), custom_call_target="tpu_custom_call" | custom-call | tf_op jit(solution)/shard_map/pallas_call | solution.py:157
  77.0 1.3 %collective-permute-start.8 = (f32[2,512,128]{2,1,0:T(8,128)S(1)}, f32[2,512,128]{2,1,0:T(8,128)S(1)}, u32[]{:S(2)}, u32[]{:S(2)}) collective-permute-start(f32[2,512,128]{2,1,0:T(8,128)S(1)} %get-tuple-element.26), channel_id=1, source_target_pairs={{0,1},{1,0},{2,3},{3,2},{4,5},{5,4},{6,7},{7,6},{8,9},{9,8},{10,11... | collective-permute-start | bytes 1572872 | tf_op jit(solution)/shard_map/ppermute | solution.py:26
  78.3 0.0 collective-permute-done.12
  78.3 1.6 %bitcast_dynamic-update-slice_fusion.2 = bf16[2,2,384,256]{3,2,1,0:T(8,128)(2,1)} fusion(bf16[2,2,384,256]{3,2,1,0:T(8,128)(2,1)} %get-tuple-element.37, s32[]{:T(128)S(6)} %select_n.86, s32[]{:T(128)S(6)} %select_n.84, bf16[384,256]{1,0:T(8,128)(2,1)} %collective-permute-done.12), kind=kLoop, calls=%fused_computation.5 | loop fusion | bytes 393224 | tf_op jit(solution)/shard_map/dynamic_update_slice | solution.py:51
  79.9 0.7 bitcast_dynamic-update-slice_fusion.1
  80.6 0.0 collective-permute-done.14
  80.6 0.7 bitcast_dynamic-update-slice_fusion
  81.3 0.0 collective-permute-done.8
  81.3 0.1 add.110
  81.4 1.6 %collective-permute-start.15 = (f32[256,128]{1,0:T(8,128)S(1)}, f32[256,128]{1,0:T(8,128)S(1)}, u32[]{:S(2)}, u32[]{:S(2)}) collective-permute-start(f32[256,128]{1,0:T(8,128)S(1)} %get-tuple-element.41), channel_id=1, source_target_pairs={{0,16},{2,18},{16,0},{18,2},{1,17},{3,19},{17,1},{19,3},{4,20},{6,... | collective-permute-start | bytes 393224 | tf_op jit(solution)/shard_map/ppermute | solution.py:272
  83.0 0.9 collective-permute-start.16
  83.9 1.1 %collective-permute-start.17 = (f32[256,128]{1,0:T(8,128)S(1)}, f32[256,128]{1,0:T(8,128)S(1)}, u32[]{:S(2)}, u32[]{:S(2)}) collective-permute-start(f32[256,128]{1,0:T(8,128)S(1)} %get-tuple-element.39), channel_id=1, source_target_pairs={{0,18},{2,16},{16,2},{18,0},{1,19},{3,17},{17,3},{19,1},{4,22},{6,... | collective-permute-start | bytes 393224 | tf_op jit(solution)/shard_map/ppermute | solution.py:272
  85.0 1.9 %collective-permute-done.15.refs_1_ = f32[256,128]{1,0:T(8,128)S(1)} collective-permute-done((f32[256,128]{1,0:T(8,128)S(1)}, f32[256,128]{1,0:T(8,128)S(1)}, u32[]{:S(2)}, u32[]{:S(2)}) %collective-permute-start.15) | collective-permute-done | bytes 131104 | tf_op jit(solution)/shard_map/ppermute | solution.py:272
  86.9 2.5 %collective-permute-done.16.refs_2_ = f32[256,128]{1,0:T(8,128)S(1)} collective-permute-done((f32[256,128]{1,0:T(8,128)S(1)}, f32[256,128]{1,0:T(8,128)S(1)}, u32[]{:S(2)}, u32[]{:S(2)}) %collective-permute-start.16) | collective-permute-done | bytes 131104 | tf_op jit(solution)/shard_map/ppermute | solution.py:272
  89.4 1.5 %collective-permute-done.17.refs_3_ = f32[256,128]{1,0:T(8,128)S(1)} collective-permute-done((f32[256,128]{1,0:T(8,128)S(1)}, f32[256,128]{1,0:T(8,128)S(1)}, u32[]{:S(2)}, u32[]{:S(2)}) %collective-permute-start.17) | collective-permute-done | bytes 131104 | tf_op jit(solution)/shard_map/ppermute | solution.py:272
  90.9 1.4 %shard_map.79 = (f32[256,128]{1,0:T(8,128)S(1)}, bf16[256,128]{1,0:T(8,128)(2,1)S(1)}, bf16[256,128]{1,0:T(8,128)(2,1)S(1)}, bf16[256,128]{1,0:T(8,128)(2,1)S(1)}) custom-call(s32[2]{0:T(128)S(1)} %copy-done.8, s32[1,2]{1,0:T(1,128)S(1)} %copy-done.9, s32[3]{0:T(128)S(1)} %pad_add_fusion.place, bf16[1536,256]{1,0:T(8,128)(2,1)} %bitcast.11.act, ...), custom_call_target="tpu_custom_call" | custom-call | tf_op jit(solution)/shard_map/pallas_call | solution.py:195
  92.4 2.3 %collective-permute-start.20 = (bf16[256,128]{1,0:T(8,128)(2,1)S(1)}, bf16[256,128]{1,0:T(8,128)(2,1)S(1)}, u32[]{:S(2)}, u32[]{:S(2)}) collective-permute-start(bf16[256,128]{1,0:T(8,128)(2,1)S(1)} %get-tuple-element.36), channel_id=1, source_target_pairs={{0,12},{4,0},{8,4},{12,8},{1,13},{5,1},{9,5},{13,9},{2,14},{6,2},{... | collective-permute-start | bytes 196616 | tf_op jit(solution)/shard_map/ppermute | solution.py:26
  94.7 0.8 collective-permute-start.19
  95.5 1.6 %collective-permute-start.18 = (bf16[256,128]{1,0:T(8,128)(2,1)S(1)}, bf16[256,128]{1,0:T(8,128)(2,1)S(1)}, u32[]{:S(2)}, u32[]{:S(2)}) collective-permute-start(bf16[256,128]{1,0:T(8,128)(2,1)S(1)} %get-tuple-element.34), channel_id=1, source_target_pairs={{0,4},{4,8},{8,12},{12,0},{1,5},{5,9},{9,13},{13,1},{2,6},{6,10},{... | collective-permute-start | bytes 196616 | tf_op jit(solution)/shard_map/ppermute | solution.py:26
  97.0 0.0 collective-permute-done.20
  97.0 3.8 %collective-permute-done.19 = bf16[256,128]{1,0:T(8,128)(2,1)S(1)} collective-permute-done((bf16[256,128]{1,0:T(8,128)(2,1)S(1)}, bf16[256,128]{1,0:T(8,128)(2,1)S(1)}, u32[]{:S(2)}, u32[]{:S(2)}) %collective-permute-start.19) | collective-permute-done | bytes 65568 | tf_op jit(solution)/shard_map/ppermute | solution.py:26
  100.9 0.7 collective-permute-done.18
  101.5 0.7 add_multiply_fusion
  (23 shorter events, 0.1 us)
Async XLA Ops:
  0.0 18.9 %copy-start = (bf16[2,128,6912]{2,1,0:T(8,128)(2,1)S(1)}, bf16[2,128,6912]{2,1,0:T(8,128)(2,1)}, u32[]{:S(2)}) copy-start(bf16[2,128,6912]{2,1,0:T(8,128)(2,1)} %param.8) | copy-start | bytes 10616836
  2.0 25.2 %collective-permute-start = (bf16[1664,128]{1,0:T(8,128)(2,1)}, bf16[1664,128]{1,0:T(8,128)(2,1)}, u32[]{:S(2)}, u32[]{:S(2)}) collective-permute-start(bf16[1664,128]{1,0:T(8,128)(2,1)} %dynamic-slice_bitcast_fusion.1.refs_2_.refs_3_), channel_id=1, source_target_pairs={{0,4},{4,8},{8,12},{12,0},{1,5},{5,9},{9,13},{13,1},{2,6},{6,10},{... | collective-permute-start | bytes 1277960 | tf_op jit(solution)/shard_map/ppermute | solution.py:26
  5.1 2.1 %copy-start.3 = (bf16[1280,1536]{1,0:T(8,128)(2,1)S(1)}, bf16[1280,1536]{1,0:T(8,128)(2,1)}, u32[]{:S(2)}) copy-start(bf16[1280,1536]{1,0:T(8,128)(2,1)} %basis.1) | copy-start | bytes 11796484
  7.2 1.1 %copy-start.4 = (bf16[2,128,1280]{2,1,0:T(8,128)(2,1)S(1)}, bf16[2,128,1280]{2,1,0:T(8,128)(2,1)}, u32[]{:S(2)}) copy-start(bf16[2,128,1280]{2,1,0:T(8,128)(2,1)} %param.7) | copy-start | bytes 1966084
  11.7 0.7 copy-start.5
  12.4 0.7 copy-start.10
  13.2 0.8 copy-start.11
  13.9 11.7 %collective-permute-start.11 = (f32[384,256]{1,0:T(8,128)}, f32[384,256]{1,0:T(8,128)}, u32[]{:S(2)}, u32[]{:S(2)}) collective-permute-start(f32[384,256]{1,0:T(8,128)} %get-tuple-element.30), channel_id=1, source_target_pairs={{0,3},{1,2},{2,1},{3,0},{4,7},{5,6},{6,5},{7,4},{8,11},{9,10},{10,... | collective-permute-start | bytes 1179656 | tf_op jit(solution)/shard_map/ppermute | solution.py:40
  16.4 15.5 %collective-permute-start.3 = (bf16[1792,128]{1,0:T(8,128)(2,1)}, bf16[1792,128]{1,0:T(8,128)(2,1)}, u32[]{:S(2)}, u32[]{:S(2)}) collective-permute-start(bf16[1792,128]{1,0:T(8,128)(2,1)} %dynamic-slice_bitcast_fusion.refs_1_.refs_2_), channel_id=1, source_target_pairs={{0,4},{4,8},{8,12},{12,0},{1,5},{5,9},{9,13},{13,1},{2,6},{6,10},{... | collective-permute-start | bytes 1376264 | tf_op jit(solution)/shard_map/ppermute | solution.py:26
  17.9 16.1 %collective-permute-start.10 = (f32[384,256]{1,0:T(8,128)}, f32[384,256]{1,0:T(8,128)}, u32[]{:S(2)}, u32[]{:S(2)}) collective-permute-start(f32[384,256]{1,0:T(8,128)} %copy-done.11), channel_id=1, source_target_pairs={{0,2},{1,3},{2,0},{3,1},{4,6},{5,7},{6,4},{7,5},{8,10},{9,11},{10,... | collective-permute-start | bytes 1179656 | tf_op jit(solution)/shard_map/ppermute | solution.py:40
  18.8 16.8 %collective-permute-start.9 = (f32[384,256]{1,0:T(8,128)}, f32[384,256]{1,0:T(8,128)}, u32[]{:S(2)}, u32[]{:S(2)}) collective-permute-start(f32[384,256]{1,0:T(8,128)} %copy-done.10), channel_id=1, source_target_pairs={{0,1},{1,0},{2,3},{3,2},{4,5},{5,4},{6,7},{7,6},{8,9},{9,8},{10,11... | collective-permute-start | bytes 1179656 | tf_op jit(solution)/shard_map/ppermute | solution.py:40
  25.6 41.9 %collective-permute-start.6 = (bf16[256,2304]{1,0:T(8,128)(2,1)}, bf16[256,2304]{1,0:T(8,128)(2,1)}, u32[]{:S(2)}, u32[]{:S(2)}) collective-permute-start(bf16[256,2304]{1,0:T(8,128)(2,1)} %constant_dynamic-slice_fusion.1), channel_id=1, source_target_pairs={{0,16},{16,0},{1,17},{17,1},{2,18},{18,2},{3,19},{19,3},{4,20},{20... | collective-permute-start | bytes 3538952 | tf_op jit(solution)/shard_map/ppermute | solution.py:26
  27.1 9.4 %copy-start.6 = (f32[384,256]{1,0:T(8,128)S(1)}, f32[384,256]{1,0:T(8,128)}, u32[]{:S(2)}) copy-start(f32[384,256]{1,0:T(8,128)} %copy-done.5) | copy-start | bytes 1179652
  27.1 14.9 %collective-permute-start.1 = (bf16[1664,128]{1,0:T(8,128)(2,1)}, bf16[1664,128]{1,0:T(8,128)(2,1)}, u32[]{:S(2)}, u32[]{:S(2)}) collective-permute-start(bf16[1664,128]{1,0:T(8,128)(2,1)} %collective-permute-done.refs_4_.refs_5_), channel_id=1, source_target_pairs={{0,4},{4,8},{8,12},{12,0},{1,5},{5,9},{9,13},{13,1},{2,6},{6,10},{... | collective-permute-start | bytes 1277960 | tf_op jit(solution)/shard_map/ppermute | solution.py:26
  31.9 20.0 %collective-permute-start.4 = (bf16[1792,128]{1,0:T(8,128)(2,1)}, bf16[1792,128]{1,0:T(8,128)(2,1)}, u32[]{:S(2)}, u32[]{:S(2)}) collective-permute-start(bf16[1792,128]{1,0:T(8,128)(2,1)} %collective-permute-done.3.refs_3_.refs_4_), channel_id=1, source_target_pairs={{0,4},{4,8},{8,12},{12,0},{1,5},{5,9},{9,13},{13,1},{2,6},{6,10},{... | collective-permute-start | bytes 1376264 | tf_op jit(solution)/shard_map/ppermute | solution.py:26
  34.1 32.5 %collective-permute-start.7 = (bf16[256,1152]{1,0:T(8,128)(2,1)}, bf16[256,1152]{1,0:T(8,128)(2,1)}, u32[]{:S(2)}, u32[]{:S(2)}) collective-permute-start(bf16[256,1152]{1,0:T(8,128)(2,1)} %constant_dynamic-slice_fusion), channel_id=1, source_target_pairs={{0,16},{16,0},{1,17},{17,1},{2,18},{18,2},{3,19},{19,3},{4,20},{20... | collective-permute-start | bytes 1769480 | tf_op jit(solution)/shard_map/ppermute | solution.py:26
  38.6 39.6 %collective-permute-start.12 = (bf16[384,256]{1,0:T(8,128)(2,1)}, bf16[384,256]{1,0:T(8,128)(2,1)}, u32[]{:S(2)}, u32[]{:S(2)}) collective-permute-start(bf16[384,256]{1,0:T(8,128)(2,1)} %get-tuple-element.38), channel_id=1, source_target_pairs={{0,1},{1,0},{2,3},{3,2},{4,5},{5,4},{6,7},{7,6},{8,9},{9,8},{10,11... | collective-permute-start | bytes 589832 | tf_op jit(solution)/shard_map/ppermute | solution.py:40
  42.0 32.7 %collective-permute-start.2 = (bf16[1664,128]{1,0:T(8,128)(2,1)}, bf16[1664,128]{1,0:T(8,128)(2,1)}, u32[]{:S(2)}, u32[]{:S(2)}) collective-permute-start(bf16[1664,128]{1,0:T(8,128)(2,1)} %collective-permute-done.1.refs_6_.refs_7_), channel_id=1, source_target_pairs={{0,4},{4,8},{8,12},{12,0},{1,5},{5,9},{9,13},{13,1},{2,6},{6,10},{... | collective-permute-start | bytes 1277960 | tf_op jit(solution)/shard_map/ppermute | solution.py:26
  51.8 19.5 %collective-permute-start.5 = (bf16[1792,128]{1,0:T(8,128)(2,1)}, bf16[1792,128]{1,0:T(8,128)(2,1)}, u32[]{:S(2)}, u32[]{:S(2)}) collective-permute-start(bf16[1792,128]{1,0:T(8,128)(2,1)} %collective-permute-done.4.refs_5_.refs_6_), channel_id=1, source_target_pairs={{0,4},{4,8},{8,12},{12,0},{1,5},{5,9},{9,13},{13,1},{2,6},{6,10},{... | collective-permute-start | bytes 1376264 | tf_op jit(solution)/shard_map/ppermute | solution.py:26
  53.2 1.5 %copy-start.1 = (bf16[256,3456]{1,0:T(8,128)(2,1)S(1)}, bf16[256,3456]{1,0:T(8,128)(2,1)}, u32[]{:S(2)}) copy-start(bf16[256,3456]{1,0:T(8,128)(2,1)} %constant_dynamic-slice_fusion.2.refs_0_) | copy-start | bytes 5308420
  57.9 13.4 %copy-start.2 = (bf16[256,3456]{1,0:T(8,128)(2,1)S(1)}, bf16[256,3456]{1,0:T(8,128)(2,1)}, u32[]{:S(2)}) copy-start(bf16[256,3456]{1,0:T(8,128)(2,1)} %constant_dynamic-slice_fusion.2.refs_0_) | copy-start | bytes 5308420
  66.6 13.3 %collective-permute-start.13 = (bf16[384,256]{1,0:T(8,128)(2,1)}, bf16[384,256]{1,0:T(8,128)(2,1)S(1)}, u32[]{:S(2)}, u32[]{:S(2)}) collective-permute-start(bf16[384,256]{1,0:T(8,128)(2,1)} %get-tuple-element.38), channel_id=1, source_target_pairs={{0,2},{1,3},{2,0},{3,1},{4,6},{5,7},{6,4},{7,5},{8,10},{9,11},{10,... | collective-permute-start | bytes 589832 | tf_op jit(solution)/shard_map/ppermute | solution.py:40
  67.5 13.1 %collective-permute-start.14 = (bf16[384,256]{1,0:T(8,128)(2,1)}, bf16[384,256]{1,0:T(8,128)(2,1)S(1)}, u32[]{:S(2)}, u32[]{:S(2)}) collective-permute-start(bf16[384,256]{1,0:T(8,128)(2,1)} %get-tuple-element.38), channel_id=1, source_target_pairs={{0,3},{1,2},{2,1},{3,0},{4,7},{5,6},{6,5},{7,4},{8,11},{9,10},{10,... | collective-permute-start | bytes 589832 | tf_op jit(solution)/shard_map/ppermute | solution.py:40
  72.7 2.0 %copy-start.7 = (s32[4]{0:T(128)S(1)}, s32[4]{0:T(128)}, u32[]{:S(2)}) copy-start(s32[4]{0:T(128)} %owner.1) | copy-start | bytes 52
  77.0 4.3 %collective-permute-start.8 = (f32[2,512,128]{2,1,0:T(8,128)S(1)}, f32[2,512,128]{2,1,0:T(8,128)S(1)}, u32[]{:S(2)}, u32[]{:S(2)}) collective-permute-start(f32[2,512,128]{2,1,0:T(8,128)S(1)} %get-tuple-element.26), channel_id=1, source_target_pairs={{0,1},{1,0},{2,3},{3,2},{4,5},{5,4},{6,7},{7,6},{8,9},{9,8},{10,11... | collective-permute-start | bytes 1572872 | tf_op jit(solution)/shard_map/ppermute | solution.py:26
  79.9 11.0 %copy-start.8 = (s32[2]{0:T(128)S(1)}, s32[2]{0:T(128)}, u32[]{:S(2)}) copy-start(s32[2]{0:T(128)} %counts.1) | copy-start | bytes 28
  79.9 11.0 %copy-start.9 = (s32[1,2]{1,0:T(1,128)S(1)}, s32[1,2]{1,0:T(1,128)}, u32[]{:S(2)}) copy-start(s32[1,2]{1,0:T(1,128)} %wanted.1) | copy-start | bytes 28
  81.4 5.5 %collective-permute-start.15 = (f32[256,128]{1,0:T(8,128)S(1)}, f32[256,128]{1,0:T(8,128)S(1)}, u32[]{:S(2)}, u32[]{:S(2)}) collective-permute-start(f32[256,128]{1,0:T(8,128)S(1)} %get-tuple-element.41), channel_id=1, source_target_pairs={{0,16},{2,18},{16,0},{18,2},{1,17},{3,19},{17,1},{19,3},{4,20},{6,... | collective-permute-start | bytes 393224 | tf_op jit(solution)/shard_map/ppermute | solution.py:272
  83.0 6.4 %collective-permute-start.16 = (f32[256,128]{1,0:T(8,128)S(1)}, f32[256,128]{1,0:T(8,128)S(1)}, u32[]{:S(2)}, u32[]{:S(2)}) collective-permute-start(f32[256,128]{1,0:T(8,128)S(1)} %get-tuple-element.40), channel_id=1, source_target_pairs={{0,2},{2,0},{16,18},{18,16},{1,3},{3,1},{17,19},{19,17},{4,6},{6,4... | collective-permute-start | bytes 393224 | tf_op jit(solution)/shard_map/ppermute | solution.py:272
  83.9 7.0 %collective-permute-start.17 = (f32[256,128]{1,0:T(8,128)S(1)}, f32[256,128]{1,0:T(8,128)S(1)}, u32[]{:S(2)}, u32[]{:S(2)}) collective-permute-start(f32[256,128]{1,0:T(8,128)S(1)} %get-tuple-element.39), channel_id=1, source_target_pairs={{0,18},{2,16},{16,2},{18,0},{1,19},{3,17},{17,3},{19,1},{4,22},{6,... | collective-permute-start | bytes 393224 | tf_op jit(solution)/shard_map/ppermute | solution.py:272
  92.4 4.7 %collective-permute-start.20 = (bf16[256,128]{1,0:T(8,128)(2,1)S(1)}, bf16[256,128]{1,0:T(8,128)(2,1)S(1)}, u32[]{:S(2)}, u32[]{:S(2)}) collective-permute-start(bf16[256,128]{1,0:T(8,128)(2,1)S(1)} %get-tuple-element.36), channel_id=1, source_target_pairs={{0,12},{4,0},{8,4},{12,8},{1,13},{5,1},{9,5},{13,9},{2,14},{6,2},{... | collective-permute-start | bytes 196616 | tf_op jit(solution)/shard_map/ppermute | solution.py:26
  94.7 6.2 %collective-permute-start.19 = (bf16[256,128]{1,0:T(8,128)(2,1)S(1)}, bf16[256,128]{1,0:T(8,128)(2,1)S(1)}, u32[]{:S(2)}, u32[]{:S(2)}) collective-permute-start(bf16[256,128]{1,0:T(8,128)(2,1)S(1)} %get-tuple-element.35), channel_id=1, source_target_pairs={{0,8},{4,12},{8,0},{12,4},{1,9},{5,13},{9,1},{13,5},{2,10},{6,14},... | collective-permute-start | bytes 196616 | tf_op jit(solution)/shard_map/ppermute | solution.py:26
  95.5 6.1 %collective-permute-start.18 = (bf16[256,128]{1,0:T(8,128)(2,1)S(1)}, bf16[256,128]{1,0:T(8,128)(2,1)S(1)}, u32[]{:S(2)}, u32[]{:S(2)}) collective-permute-start(bf16[256,128]{1,0:T(8,128)(2,1)S(1)} %get-tuple-element.34), channel_id=1, source_target_pairs={{0,4},{4,8},{8,12},{12,0},{1,5},{5,9},{9,13},{13,1},{2,6},{6,10},{... | collective-permute-start | bytes 196616 | tf_op jit(solution)/shard_map/ppermute | solution.py:26

commit v5 on v4

--- a/solution.py
+++ b/solution.py
@@ -124,44 +124,71 @@
     )(*rows, *pieces)
 
 
-def pack_kernel(dp, cores, parts, start, owner, place, held, *refs):
+def total_of(position, early, last, group):
+    positions = early[0].shape[0]
+    height = early[0].shape[1]
+    at_last = last[pl.ds(group * height, height)]
+    before = early[group][jnp.minimum(position, positions - 1)]
+    return jnp.where(position == positions, at_last, before)
+
+
+def pack_kernel(dp, cores, parts, owner, place, held, *refs):
     row, core = place[0], place[1]
-    groups, refs = len(parts), list(refs)
+    refs = list(refs)
     rows = [[refs.pop(0) for _ in range(cuts)] for cuts in parts]
     early = [refs.pop(0) for _ in parts]
-    almost = [refs.pop(0) for _ in parts]
-    last, height = refs.pop(), early[0].shape[1]
-    spans = [pl.ds(g * height, height) for g in range(groups)]
-    for g in range(groups):
-        last[spans[g]] = almost[g][0] + product(rows[g], held, start)
-    for block in range(refs[0].shape[0]):
-        for step in range(cores):
+    last, sends = refs[0], refs[1:]
+    height = early[0].shape[1]
+    for g in range(len(parts)):
+        last[g * height : (g + 1) * height] = product(rows[g], held, 0)
+    for step in range(1, cores):
+        for block in range(sends[0].shape[0]):
             piece = block * cores + lax.rem(core + step, cores)
             position = lax.rem(row - owner[piece] + dp, dp)
-            target = refs[step].at[block]
-
-            @pl.when(position == dp - 1)
-            def _():
-                target[...] = last[...]
-
-            @pl.when(position < dp - 1)
-            def _():
-                for g in range(groups):
-                    target[spans[g]] = early[g][position]
-
-
-def pack(owner_slot, place, rows, held, start, early, almost, blocks, cores):
+            for g in range(len(parts)):
+                sends[step - 1][block, g * height : (g + 1) * height] = total_of(
+                    position, early, last, g
+                )
+
+
+def pack(owner_slot, place, rows, held, early, blocks, cores):
     positions, height, width = early[0].shape
     shape = (len(rows) * height, width)
     parts = tuple(len(part) for part in rows)
     return pl.pallas_call(
-        functools.partial(pack_kernel, positions + 1, cores, parts, start),
-        out_shape=(jax.ShapeDtypeStruct((blocks,) + shape, F32),) * cores,
-        in_specs=[SMEM, SMEM] + [VMEM] * (1 + sum(parts) + 2 * len(rows)),
+        functools.partial(pack_kernel, positions + 1, cores, parts),
+        out_shape=(jax.ShapeDtypeStruct(shape, F32),)
+        + (jax.ShapeDtypeStruct((blocks,) + shape, F32),) * (cores - 1),
+        in_specs=[SMEM, SMEM] + [VMEM] * (1 + sum(parts) + len(rows)),
         out_specs=(VMEM,) * cores,
-        scratch_shapes=[pltpu.VMEM(shape, F32)],
-        compiler_params=pltpu.CompilerParams(vmem_limit_bytes=VMEM_LIMIT),
-    )(owner_slot, place, held, *[cut for part in rows for cut in part], *early, *almost)
+        compiler_params=pltpu.CompilerParams(vmem_limit_bytes=VMEM_LIMIT),
+    )(owner_slot, place, held, *[cut for part in rows for cut in part], *early)
+
+
+def join_kernel(dp, cores, groups, blocks, owner, place, last, *refs):
+    row, core, me = place[0], place[1], place[2]
+    early, came, outs = refs[:groups], refs[groups : groups + cores - 1], refs[groups + cores - 1 :]
+    height = early[0].shape[1]
+    for far in range(blocks):
+        block = lax.rem(me + far, blocks)
+        position = lax.rem(row - owner[block * cores + core] + dp, dp)
+        for g in range(groups):
+            total = total_of(position, early, last, g)
+            for other in came:
+                total = total + other[block, g * height : (g + 1) * height]
+            outs[far * groups + g][...] = total
+
+
+def join(owner_slot, place, last, early, came, blocks, cores):
+    positions, height, width = early[0].shape
+    groups = len(early)
+    return pl.pallas_call(
+        functools.partial(join_kernel, positions + 1, cores, groups, blocks),
+        out_shape=(jax.ShapeDtypeStruct((height, width), F32),) * (blocks * groups),
+        in_specs=[SMEM, SMEM] + [VMEM] * (1 + groups + len(came)),
+        out_specs=(VMEM,) * (blocks * groups),
+        compiler_params=pltpu.CompilerParams(vmem_limit_bytes=VMEM_LIMIT),
+    )(owner_slot, place, last, *early, *came)
 
 
 def square_kernel(dp, terms, counts, wanted, place, act, *refs):
@@ -217,51 +244,42 @@
     part_features = features // groups
     place = jnp.stack([row, core, block])
 
-    cut = -(-part_features // 256) * 128
-    shares = (0, cut)
-    rings = [
-        [lax.dynamic_slice_in_dim(basis_store[0], group * part_features + start, size, 0)]
-        for start, size in zip(shares, (cut, part_features - cut))
+    ring = [
+        lax.dynamic_slice_in_dim(basis_store[0], group * part_features, part_features, 0)
     ]
-    flat_grads = after(gradients.reshape(slots, features), rings[0][0], rings[1][0])
-
-    def share(index, start, size):
-        return lax.dynamic_slice_in_dim(flat_grads, index * part_features + start, size, 1)
-
-    rows, first = [[share(group, 0, part_features)]], part_features * 7 // 10 // 128 * 128
-    for step in range(1, groups):
-        rows.append(
-            [
-                shift(share((group + step) % groups, start, size), "groups", step)
-                for start, size in ((0, first), (first, part_features - first))
-            ]
-        )
+    flat_grads = after(gradients.reshape(slots, features), ring[0])
+
+    def share(index):
+        return lax.dynamic_slice_in_dim(flat_grads, index * part_features, part_features, 1)
+
+    away = [share((group + step) % groups) for step in range(1, groups)]
+    others = [[shift(rows, "groups", step)] for step, rows in enumerate(away, 1)]
 
     flat_acts = activations.reshape(slots, activations.shape[2])
-    act, *away = rotate(place, flat_acts, basis_act, blocks, cores)
+    act, *away_act = rotate(place, flat_acts, basis_act, blocks, cores)
+    act_rot_t = None
     for step in range(1, dp):
-        for ring in rings:
-            ring.append(shift(ring[-1], "dp", 1))
-    away = [to_neighbour(part, i // cores, i % cores) for i, part in enumerate(away, 1)]
-    for part in away:
-        act = act + part
-    act_rot_t = gather_act(act.astype(BF16))
-
-    pieces = [ring[step] for step in range(dp) for ring in rings]
-    early = [early_products(part, pieces[:-2], shares) for part in rows]
-    almost = [early_products(part, pieces[-2:-1], shares[:1]) for part in rows]
-    last, *almost = lax.optimization_barrier((pieces[-1], *almost))
-    keep, *send = pack(
-        owner_slot, place, rows, last, cut, early, almost, blocks, cores
-    )
-    for step in range(1, cores):
-        keep = keep + shift(send[step - 1], "cores", step)
-    keep, act_rot_t = lax.optimization_barrier((keep, act_rot_t))
-
-    mine = keep.reshape(blocks, groups, slots, width)
-    parts = [block_of(mine, block)[0]]
+        came = shift(ring[-1], "dp", 1)
+        if step == 1:
+            came, act, flat_grads, *away_act = lax.optimization_barrier(
+                (came, act, flat_grads, *away_act)
+            )
+            for i, part in enumerate(away_act, 1):
+                act = act + to_neighbour(part, i // cores, i % cores)
+            rows = [[share(group)]] + others
+        if step == 2:
+            came, act = lax.optimization_barrier((came, act))
+            act_rot_t = gather_act(act.astype(BF16))
+        ring.append(came)
+
+    early = [early_products(part, ring[:-1], (0,)) for part in rows]
+    last, act_rot_t, *early = lax.optimization_barrier((ring[-1], act_rot_t, *early))
+    last, *sends = pack(owner_slot, place, rows, last, early, blocks, cores)
+    came = [shift(send, "cores", step) for step, send in enumerate(sends, 1)]
+    parts = join(owner_slot, place, last, early, came, blocks, cores)
+
+    parts = list(parts)
     for far in range(blocks):
-        toward = block_of(mine, (block + far) % blocks)
         for back in range(groups):
             if far or back:
                 pairs = [
@@ -269,7 +287,8 @@
                     for g in range(groups)
                     for b in range(blocks)
                 ]
-                parts.append(lax.ppermute(toward[back], ("groups", "block"), pairs))
+                i = far * groups + back
+                parts[i] = lax.ppermute(parts[i], ("groups", "block"), pairs)
 
     height = reader_blocks.shape[1] * BW // dp
     own, *others = squares(

time: 103 us -> 100 us (0.971)
  waiting for transfers between devices: 42.4 us -> 59.5 us
  local copies, waits for them, and re-layouts: 18.1 us -> 10.1 us
  starting transfers between devices: 21.2 us -> 15.8 us
  Pallas kernels: 17.4 us -> 13.8 us
  other arithmetic: 2.92 us -> 0.89 us
    ppermute x6, waiting for transfers between devices: 6.96 us -> 19.8 us  [to_neighbour(): return lax.ppermute(value, ('block', 'cores'), pairs)]
    ppermute x12 -> x8, starting transfers between devices: 15.2 us -> 8.49 us  [shift(): lax.ppermute(value, axis, [(i, (i + step) % size) for i in range(size)])]
    ppermute x12 -> x8, waiting for transfers between devices: 29.6 us -> 33.7 us  [shift(): lax.ppermute(value, axis, [(i, (i + step) % size) for i in range(size)])]
    dynamic_slice x5 -> x3, local copies, waits for them, and re-layouts: 7.11 us -> 3.73 us  [the longest x1 2.28 us: on_device(): lax.dynamic_slice_in_dim(basis_store[0], group * part_features, part_feat...]
    pallas_call x4 -> x2, Pallas kernels: 10.3 us -> 7.02 us  [early_products(): pl.pallas_call(functools.partial(early_kernel, len(rows), shares), out_sh...]
    dynamic_update_slice x3 -> x4, local copies, waits for them, and re-layouts: 3.01 us -> 0.08 us  [gather_act(): out = lax.dynamic_update_slice(out, came[None, None], source)]
    dynamic_update_slice x1 -> x0, other arithmetic: 2.09 us -> none  [gather_act(): out = lax.dynamic_update_slice(out, came[None, None], source)]
    ppermute x6, starting transfers between devices: 2.5 us -> 3.72 us  [to_neighbour(): return lax.ppermute(value, ('block', 'cores'), pairs)]
  transfers between devices with their start and end apart: 21 -> 17, of which waited for: 11 -> 12; matrix products, arithmetic and copies ran while one was open for 11% -> 2% of each run, Pallas kernels for 16% -> 10%
where the time goes in v5:
time: 100 us
  waiting for transfers between devices  59.5 us (60%)
  starting transfers between devices  15.8 us (16%)
  Pallas kernels  13.8 us (14%)
  local copies, waits for them, and re-layouts  10.1 us (10%)
    ppermute x8, waiting for transfers between devices, shift(): lax.ppermute(value, axis, [(i, (i + step) % size) for i in range(size)])  33.7 us
    ppermute x6, waiting for transfers between devices, to_neighbour(): return lax.ppermute(value, ('block', 'cores'), pairs)  19.8 us
    ppermute x8, starting transfers between devices, shift(): lax.ppermute(value, axis, [(i, (i + step) % size) for i in range(size)])  8.49 us
    pallas_call x2, Pallas kernels, early_products(): pl.pallas_call(functools.partial(early_kernel, len(rows), shares), out_sh...  7.02 us
    unnamed x22, local copies, waits for them, and re-layouts  6.22 us
    ppermute x3, waiting for transfers between devices, on_device(): parts[i] = lax.ppermute(parts[i], ('groups', 'block'), pairs)  6.04 us
    ppermute x6, starting transfers between devices, to_neighbour(): return lax.ppermute(value, ('block', 'cores'), pairs)  3.72 us
    ppermute x3, starting transfers between devices, on_device(): parts[i] = lax.ppermute(parts[i], ('groups', 'block'), pairs)  3.55 us
  transfers between devices with their start and end apart: 17, of which 12 were waited for; matrix products, arithmetic and copies ran while one was open for 2% of the time, Pallas kernels for 10%

profile of v5, /device:TPU:0, one launch (start us, length us, event | category | flops | bytes accessed | tf_op | source)
XLA Modules:
  0.0 100.2 jit_solution(11584759876152560050)
XLA Ops:
  0.0 0.0 copy-start
  0.0 2.3 %dynamic-slice_bitcast_fusion.refs_1_ = bf16[3456,128]{1,0:T(8,128)(2,1)} fusion(bf16[1,6912,128]{2,1,0:T(8,128)(2,1)} %param.11, s32[]{:T(128)S(6)} %select_n.54), kind=kLoop, calls=%fused_computation | loop fusion | bytes 1769476 | tf_op jit(solution)/shard_map/dynamic_slice | solution.py:248
  2.3 3.0 %collective-permute-start = (bf16[3456,128]{1,0:T(8,128)(2,1)}, bf16[3456,128]{1,0:T(8,128)(2,1)}, u32[]{:S(2)}, u32[]{:S(2)}) collective-permute-start(bf16[3456,128]{1,0:T(8,128)(2,1)} %dynamic-slice_bitcast_fusion.refs_1_), channel_id=1, source_target_pairs={{0,4},{4,8},{8,12},{12,0},{1,5},{5,9},{9,13},{13,1},{2,6},{6,10},{... | collective-permute-start | bytes 2654216 | tf_op jit(solution)/shard_map/ppermute | solution.py:26
  5.3 0.0 copy-done
  5.3 1.3 %constant_dynamic-slice_fusion = bf16[256,3456]{1,0:T(8,128)(2,1)} fusion(bf16[256,6912]{1,0:T(8,128)(2,1)S(1)} %bitcast.16, s32[]{:T(128)S(6)} %select_n.64), kind=kLoop, calls=%fused_computation.7 | loop fusion | bytes 3538948 | tf_op jit(solution)/shard_map/dynamic_slice | solution.py:253
  6.6 1.5 %collective-permute-start.9 = (bf16[256,3456]{1,0:T(8,128)(2,1)}, bf16[256,3456]{1,0:T(8,128)(2,1)}, u32[]{:S(2)}, u32[]{:S(2)}) collective-permute-start(bf16[256,3456]{1,0:T(8,128)(2,1)} %constant_dynamic-slice_fusion), channel_id=1, source_target_pairs={{0,16},{16,0},{1,17},{17,1},{2,18},{18,2},{3,19},{19,3},{4,20},{20... | collective-permute-start | bytes 5308424 | tf_op jit(solution)/shard_map/ppermute | solution.py:26
  8.2 0.1 pad_add_fusion.place
  8.2 0.0 copy-start.1
  8.2 2.1 %copy-done.1 = bf16[1280,1536]{1,0:T(8,128)(2,1)S(1)} copy-done((bf16[1280,1536]{1,0:T(8,128)(2,1)S(1)}, bf16[1280,1536]{1,0:T(8,128)(2,1)}, u32[]{:S(2)}) %copy-start.1) | copy-done | bytes 3932184
  10.3 0.0 copy-start.2
  10.4 1.1 %copy-done.2 = bf16[2,128,1280]{2,1,0:T(8,128)(2,1)S(1)} copy-done((bf16[2,128,1280]{2,1,0:T(8,128)(2,1)S(1)}, bf16[2,128,1280]{2,1,0:T(8,128)(2,1)}, u32[]{:S(2)}) %copy-start.2) | copy-done | bytes 655384
  11.4 2.6 %shard_map.73 = (f32[384,256]{1,0:T(8,128)S(1)}, f32[384,256]{1,0:T(8,128)S(1)}, f32[384,256]{1,0:T(8,128)S(1)}, f32[384,256]{1,0:T(8,128)S(1)}) custom-call(s32[3]{0:T(128)S(1)} %pad_add_fusion.place, bf16[256,1280]{1,0:T(8,128)(2,1)S(1)} %bitcast.19, bf16[1280,1536]{1,0:T(8,128)(2,1)S(1)} %copy-done.1), custom_call_target="tpu_custom_call" | custom-call | tf_op jit(solution)/shard_map/pallas_call | solution.py:74
  14.1 0.0 copy-start.3
  14.1 0.8 copy-done.3
  14.9 0.0 copy-start.8
  14.9 0.8 copy-done.8
  15.6 0.7 copy-done.9
  16.3 0.7 copy-done.10
  17.1 10.2 %collective-permute-done.refs_2_ = bf16[3456,128]{1,0:T(8,128)(2,1)} collective-permute-done((bf16[3456,128]{1,0:T(8,128)(2,1)}, bf16[3456,128]{1,0:T(8,128)(2,1)}, u32[]{:S(2)}, u32[]{:S(2)}) %collective-permute-start) | collective-permute-done | bytes 884768 | tf_op jit(solution)/shard_map/ppermute | solution.py:26
  27.3 0.0 collective-permute-start.1
  27.3 0.0 collective-permute-start.2
  27.3 1.6 %collective-permute-start.3 = (f32[384,256]{1,0:T(8,128)}, f32[384,256]{1,0:T(8,128)S(1)}, u32[]{:S(2)}, u32[]{:S(2)}) collective-permute-start(f32[384,256]{1,0:T(8,128)} %copy-done.9), channel_id=1, source_target_pairs={{0,2},{1,3},{2,0},{3,1},{4,6},{5,7},{6,4},{7,5},{8,10},{9,11},{10,... | collective-permute-start | bytes 1179656 | tf_op jit(solution)/shard_map/ppermute | solution.py:40
  28.9 0.3 collective-permute-start.4
  29.2 0.1 constant_dynamic-slice_fusion.1.refs_0_
  29.3 0.0 collective-permute-done.2
  29.3 10.2 %collective-permute-done.3 = f32[384,256]{1,0:T(8,128)S(1)} collective-permute-done((f32[384,256]{1,0:T(8,128)}, f32[384,256]{1,0:T(8,128)S(1)}, u32[]{:S(2)}, u32[]{:S(2)}) %collective-permute-start.3) | collective-permute-done | bytes 393248 | tf_op jit(solution)/shard_map/ppermute | solution.py:40
  39.5 7.5 %collective-permute-done.4 = f32[384,256]{1,0:T(8,128)S(1)} collective-permute-done((f32[384,256]{1,0:T(8,128)}, f32[384,256]{1,0:T(8,128)S(1)}, u32[]{:S(2)}, u32[]{:S(2)}) %collective-permute-start.4) | collective-permute-done | bytes 393248 | tf_op jit(solution)/shard_map/ppermute | solution.py:40
  47.0 0.0 copy-done.4
  47.0 0.1 add_add_fusion
  47.1 3.1 %collective-permute-done.1.refs_3_ = bf16[3456,128]{1,0:T(8,128)(2,1)} collective-permute-done((bf16[3456,128]{1,0:T(8,128)(2,1)}, bf16[3456,128]{1,0:T(8,128)(2,1)}, u32[]{:S(2)}, u32[]{:S(2)}) %collective-permute-start.1) | collective-permute-done | bytes 884768 | tf_op jit(solution)/shard_map/ppermute | solution.py:26
  50.2 0.0 collective-permute-start.6
  50.2 1.2 %collective-permute-start.7 = (bf16[384,256]{1,0:T(8,128)(2,1)S(1)}, bf16[384,256]{1,0:T(8,128)(2,1)S(1)}, u32[]{:S(2)}, u32[]{:S(2)}) collective-permute-start(bf16[384,256]{1,0:T(8,128)(2,1)S(1)} %add_add_fusion), channel_id=1, source_target_pairs={{0,2},{1,3},{2,0},{3,1},{4,6},{5,7},{6,4},{7,5},{8,10},{9,11},{10,... | collective-permute-start | bytes 589832 | tf_op jit(solution)/shard_map/ppermute | solution.py:40
  51.5 0.6 collective-permute-start.8
  52.1 0.0 collective-permute-start.5
  52.1 3.3 %shard_map.74.refs_2_.refs_0_ = f32[3,256,128]{2,1,0:T(8,128)S(1)} custom-call(bf16[256,3456]{1,0:T(8,128)(2,1)S(1)} %constant_dynamic-slice_fusion.1.refs_0_, bf16[3456,128]{1,0:T(8,128)(2,1)} %dynamic-slice_bitcast_fusion.refs_1_, bf16[3456,128]{1,0:T(8,128)(2,1)} %collective-permute-done.refs_2_, bf16[3456,128]{1,0:T(8,128)(2,1)} %collective-permute-done.1.refs_3_), custom_call_target="tpu_custom_call" | custom-call | flops 679477248 | bytes 5308416 | tf_op jit(solution)/shard_map/pallas_call | solution.py:115
  55.4 0.0 collective-permute-done.9.refs_0_.refs_1_
  55.4 3.8 %shard_map.75.refs_3_.refs_1_ = f32[3,256,128]{2,1,0:T(8,128)S(1)} custom-call(bf16[256,3456]{1,0:T(8,128)(2,1)} %collective-permute-done.9.refs_0_.refs_1_, bf16[3456,128]{1,0:T(8,128)(2,1)} %dynamic-slice_bitcast_fusion.refs_1_, bf16[3456,128]{1,0:T(8,128)(2,1)} %collective-permute-done.refs_2_, bf16[3456,128]{1,0:T(8,128)(2,1)} %collective-permute-done.1.refs_3_), custom_call_target="tpu_custom_call" | custom-call | flops 679477248 | bytes 5308416 | tf_op jit(solution)/shard_map/pallas_call | solution.py:115
  59.2 0.0 copy-start.5
  59.2 0.1 broadcast_in_dim.15
  59.3 0.0 collective-permute-done.6
  59.3 0.0 collective-permute-done.7
  59.3 2.0 %collective-permute-done.8 = bf16[384,256]{1,0:T(8,128)(2,1)S(1)} collective-permute-done((bf16[384,256]{1,0:T(8,128)(2,1)S(1)}, bf16[384,256]{1,0:T(8,128)(2,1)S(1)}, u32[]{:S(2)}, u32[]{:S(2)}) %collective-permute-start.8) | collective-permute-done | bytes 196640 | tf_op jit(solution)/shard_map/ppermute | solution.py:40
  61.4 14.5 %collective-permute-done.5.held = bf16[3456,128]{1,0:T(8,128)(2,1)S(1)} collective-permute-done((bf16[3456,128]{1,0:T(8,128)(2,1)}, bf16[3456,128]{1,0:T(8,128)(2,1)S(1)}, u32[]{:S(2)}, u32[]{:S(2)}) %collective-permute-start.5) | collective-permute-done | bytes 884768 | tf_op jit(solution)/shard_map/ppermute | solution.py:26
  76.0 0.0 copy-done.5
  76.0 2.6 %shard_map.76 = (f32[512,128]{1,0:T(8,128)S(1)}, f32[2,512,128]{2,1,0:T(8,128)S(1)}) custom-call(s32[4]{0:T(128)S(1)} %copy-done.5, s32[3]{0:T(128)S(1)} %pad_add_fusion.place, bf16[3456,128]{1,0:T(8,128)(2,1)S(1)} %collective-permute-done.5.held, bf16[256,3456]{1,0:T(8,128)(2,1)S(1)} %constant_dynamic-slice_fusion.1.refs_0_, ...), custom_call_target="tpu_custom_call" | custom-call | tf_op jit(solution)/shard_map/pallas_call | solution.py:158
  78.6 0.1 collective-permute-start.10
  78.6 1.9 %collective-permute-done.10.refs_2_ = f32[2,512,128]{2,1,0:T(8,128)S(1)} collective-permute-done((f32[2,512,128]{2,1,0:T(8,128)S(1)}, f32[2,512,128]{2,1,0:T(8,128)S(1)}, u32[]{:S(2)}, u32[]{:S(2)}) %collective-permute-start.10) | collective-permute-done | bytes 524320 | tf_op jit(solution)/shard_map/ppermute | solution.py:26
  80.5 0.7 shard_map.77
  81.2 1.3 %collective-permute-start.11 = (f32[256,128]{1,0:T(8,128)S(1)}, f32[256,128]{1,0:T(8,128)S(1)}, u32[]{:S(2)}, u32[]{:S(2)}) collective-permute-start(f32[256,128]{1,0:T(8,128)S(1)} %get-tuple-element.52), channel_id=1, source_target_pairs={{0,16},{2,18},{16,0},{18,2},{1,17},{3,19},{17,1},{19,3},{4,20},{6,... | collective-permute-start | bytes 393224 | tf_op jit(solution)/shard_map/ppermute | solution.py:291
  82.5 1.5 %collective-permute-start.12 = (f32[256,128]{1,0:T(8,128)S(1)}, f32[256,128]{1,0:T(8,128)S(1)}, u32[]{:S(2)}, u32[]{:S(2)}) collective-permute-start(f32[256,128]{1,0:T(8,128)S(1)} %get-tuple-element.53), channel_id=1, source_target_pairs={{0,2},{2,0},{16,18},{18,16},{1,3},{3,1},{17,19},{19,17},{4,6},{6,4... | collective-permute-start | bytes 393224 | tf_op jit(solution)/shard_map/ppermute | solution.py:291
  84.0 0.7 collective-permute-start.13
  84.8 2.0 %collective-permute-done.11.refs_1_ = f32[256,128]{1,0:T(8,128)S(1)} collective-permute-done((f32[256,128]{1,0:T(8,128)S(1)}, f32[256,128]{1,0:T(8,128)S(1)}, u32[]{:S(2)}, u32[]{:S(2)}) %collective-permute-start.11) | collective-permute-done | bytes 131104 | tf_op jit(solution)/shard_map/ppermute | solution.py:291
  86.8 2.1 %collective-permute-done.12.refs_2_ = f32[256,128]{1,0:T(8,128)S(1)} collective-permute-done((f32[256,128]{1,0:T(8,128)S(1)}, f32[256,128]{1,0:T(8,128)S(1)}, u32[]{:S(2)}, u32[]{:S(2)}) %collective-permute-start.12) | collective-permute-done | bytes 131104 | tf_op jit(solution)/shard_map/ppermute | solution.py:291
  88.9 1.9 %collective-permute-done.13.refs_3_ = f32[256,128]{1,0:T(8,128)S(1)} collective-permute-done((f32[256,128]{1,0:T(8,128)S(1)}, f32[256,128]{1,0:T(8,128)S(1)}, u32[]{:S(2)}, u32[]{:S(2)}) %collective-permute-start.13) | collective-permute-done | bytes 131104 | tf_op jit(solution)/shard_map/ppermute | solution.py:291
  90.8 0.0 copy-done.6
  90.8 0.0 copy-done.7
  90.8 0.9 shard_map.78
  91.7 0.1 collective-permute-start.14
  91.7 0.2 collective-permute-start.15
  91.9 3.6 %collective-permute-start.16 = (bf16[256,128]{1,0:T(8,128)(2,1)S(1)}, bf16[256,128]{1,0:T(8,128)(2,1)S(1)}, u32[]{:S(2)}, u32[]{:S(2)}) collective-permute-start(bf16[256,128]{1,0:T(8,128)(2,1)S(1)} %get-tuple-element.58), channel_id=1, source_target_pairs={{0,12},{4,0},{8,4},{12,8},{1,13},{5,1},{9,5},{13,9},{2,14},{6,2},{... | collective-permute-start | bytes 196616 | tf_op jit(solution)/shard_map/ppermute | solution.py:26
  95.6 2.6 %collective-permute-done.14 = bf16[256,128]{1,0:T(8,128)(2,1)S(1)} collective-permute-done((bf16[256,128]{1,0:T(8,128)(2,1)S(1)}, bf16[256,128]{1,0:T(8,128)(2,1)S(1)}, u32[]{:S(2)}, u32[]{:S(2)}) %collective-permute-start.14) | collective-permute-done | bytes 65568 | tf_op jit(solution)/shard_map/ppermute | solution.py:26
  98.2 1.3 %collective-permute-done.15 = bf16[256,128]{1,0:T(8,128)(2,1)S(1)} collective-permute-done((bf16[256,128]{1,0:T(8,128)(2,1)S(1)}, bf16[256,128]{1,0:T(8,128)(2,1)S(1)}, u32[]{:S(2)}, u32[]{:S(2)}) %collective-permute-start.15) | collective-permute-done | bytes 65568 | tf_op jit(solution)/shard_map/ppermute | solution.py:26
  99.5 0.0 collective-permute-done.16
  99.5 0.7 add_multiply_fusion
  (9 shorter events, 0.1 us)
Async XLA Ops:
  0.0 5.3 %copy-start = (bf16[2,128,6912]{2,1,0:T(8,128)(2,1)S(1)}, bf16[2,128,6912]{2,1,0:T(8,128)(2,1)}, u32[]{:S(2)}) copy-start(bf16[2,128,6912]{2,1,0:T(8,128)(2,1)} %param.8) | copy-start | bytes 10616836
  2.3 25.0 %collective-permute-start = (bf16[3456,128]{1,0:T(8,128)(2,1)}, bf16[3456,128]{1,0:T(8,128)(2,1)}, u32[]{:S(2)}, u32[]{:S(2)}) collective-permute-start(bf16[3456,128]{1,0:T(8,128)(2,1)} %dynamic-slice_bitcast_fusion.refs_1_), channel_id=1, source_target_pairs={{0,4},{4,8},{8,12},{12,0},{1,5},{5,9},{9,13},{13,1},{2,6},{6,10},{... | collective-permute-start | bytes 2654216 | tf_op jit(solution)/shard_map/ppermute | solution.py:26
  6.6 48.7 %collective-permute-start.9 = (bf16[256,3456]{1,0:T(8,128)(2,1)}, bf16[256,3456]{1,0:T(8,128)(2,1)}, u32[]{:S(2)}, u32[]{:S(2)}) collective-permute-start(bf16[256,3456]{1,0:T(8,128)(2,1)} %constant_dynamic-slice_fusion), channel_id=1, source_target_pairs={{0,16},{16,0},{1,17},{17,1},{2,18},{18,2},{3,19},{19,3},{4,20},{20... | collective-permute-start | bytes 5308424 | tf_op jit(solution)/shard_map/ppermute | solution.py:26
  8.2 2.1 %copy-start.1 = (bf16[1280,1536]{1,0:T(8,128)(2,1)S(1)}, bf16[1280,1536]{1,0:T(8,128)(2,1)}, u32[]{:S(2)}) copy-start(bf16[1280,1536]{1,0:T(8,128)(2,1)} %basis.1) | copy-start | bytes 11796484
  10.3 1.1 %copy-start.2 = (bf16[2,128,1280]{2,1,0:T(8,128)(2,1)S(1)}, bf16[2,128,1280]{2,1,0:T(8,128)(2,1)}, u32[]{:S(2)}) copy-start(bf16[2,128,1280]{2,1,0:T(8,128)(2,1)} %param.7) | copy-start | bytes 1966084
  14.1 0.8 copy-start.3
  14.9 0.8 copy-start.8
  15.6 0.7 copy-start.9
  16.3 0.7 copy-start.10
  27.3 22.9 %collective-permute-start.1 = (bf16[3456,128]{1,0:T(8,128)(2,1)}, bf16[3456,128]{1,0:T(8,128)(2,1)}, u32[]{:S(2)}, u32[]{:S(2)}) collective-permute-start(bf16[3456,128]{1,0:T(8,128)(2,1)} %collective-permute-done.refs_2_), channel_id=1, source_target_pairs={{0,4},{4,8},{8,12},{12,0},{1,5},{5,9},{9,13},{13,1},{2,6},{6,10},{... | collective-permute-start | bytes 2654216 | tf_op jit(solution)/shard_map/ppermute | solution.py:26
  27.3 19.7 %copy-start.4 = (f32[384,256]{1,0:T(8,128)S(1)}, f32[384,256]{1,0:T(8,128)}, u32[]{:S(2)}) copy-start(f32[384,256]{1,0:T(8,128)} %copy-done.3) | copy-start | bytes 1179652
  27.3 2.0 %collective-permute-start.2 = (f32[384,256]{1,0:T(8,128)}, f32[384,256]{1,0:T(8,128)S(1)}, u32[]{:S(2)}, u32[]{:S(2)}) collective-permute-start(f32[384,256]{1,0:T(8,128)} %copy-done.10), channel_id=1, source_target_pairs={{0,1},{1,0},{2,3},{3,2},{4,5},{5,4},{6,7},{7,6},{8,9},{9,8},{10,11... | collective-permute-start | bytes 1179656 | tf_op jit(solution)/shard_map/ppermute | solution.py:40
  27.3 12.2 %collective-permute-start.3 = (f32[384,256]{1,0:T(8,128)}, f32[384,256]{1,0:T(8,128)S(1)}, u32[]{:S(2)}, u32[]{:S(2)}) collective-permute-start(f32[384,256]{1,0:T(8,128)} %copy-done.9), channel_id=1, source_target_pairs={{0,2},{1,3},{2,0},{3,1},{4,6},{5,7},{6,4},{7,5},{8,10},{9,11},{10,... | collective-permute-start | bytes 1179656 | tf_op jit(solution)/shard_map/ppermute | solution.py:40
  28.9 18.1 %collective-permute-start.4 = (f32[384,256]{1,0:T(8,128)}, f32[384,256]{1,0:T(8,128)S(1)}, u32[]{:S(2)}, u32[]{:S(2)}) collective-permute-start(f32[384,256]{1,0:T(8,128)} %copy-done.8), channel_id=1, source_target_pairs={{0,3},{1,2},{2,1},{3,0},{4,7},{5,6},{6,5},{7,4},{8,11},{9,10},{10,... | collective-permute-start | bytes 1179656 | tf_op jit(solution)/shard_map/ppermute | solution.py:40
  50.2 9.0 %collective-permute-start.6 = (bf16[384,256]{1,0:T(8,128)(2,1)S(1)}, bf16[384,256]{1,0:T(8,128)(2,1)S(1)}, u32[]{:S(2)}, u32[]{:S(2)}) collective-permute-start(bf16[384,256]{1,0:T(8,128)(2,1)S(1)} %add_add_fusion), channel_id=1, source_target_pairs={{0,1},{1,0},{2,3},{3,2},{4,5},{5,4},{6,7},{7,6},{8,9},{9,8},{10,11... | collective-permute-start | bytes 589832 | tf_op jit(solution)/shard_map/ppermute | solution.py:40
  50.2 9.1 %collective-permute-start.7 = (bf16[384,256]{1,0:T(8,128)(2,1)S(1)}, bf16[384,256]{1,0:T(8,128)(2,1)S(1)}, u32[]{:S(2)}, u32[]{:S(2)}) collective-permute-start(bf16[384,256]{1,0:T(8,128)(2,1)S(1)} %add_add_fusion), channel_id=1, source_target_pairs={{0,2},{1,3},{2,0},{3,1},{4,6},{5,7},{6,4},{7,5},{8,10},{9,11},{10,... | collective-permute-start | bytes 589832 | tf_op jit(solution)/shard_map/ppermute | solution.py:40
  51.5 9.9 %collective-permute-start.8 = (bf16[384,256]{1,0:T(8,128)(2,1)S(1)}, bf16[384,256]{1,0:T(8,128)(2,1)S(1)}, u32[]{:S(2)}, u32[]{:S(2)}) collective-permute-start(bf16[384,256]{1,0:T(8,128)(2,1)S(1)} %add_add_fusion), channel_id=1, source_target_pairs={{0,3},{1,2},{2,1},{3,0},{4,7},{5,6},{6,5},{7,4},{8,11},{9,10},{10,... | collective-permute-start | bytes 589832 | tf_op jit(solution)/shard_map/ppermute | solution.py:40
  52.1 23.8 %collective-permute-start.5 = (bf16[3456,128]{1,0:T(8,128)(2,1)}, bf16[3456,128]{1,0:T(8,128)(2,1)S(1)}, u32[]{:S(2)}, u32[]{:S(2)}) collective-permute-start(bf16[3456,128]{1,0:T(8,128)(2,1)} %collective-permute-done.1.refs_3_), channel_id=1, source_target_pairs={{0,4},{4,8},{8,12},{12,0},{1,5},{5,9},{9,13},{13,1},{2,6},{6,10},{... | collective-permute-start | bytes 2654216 | tf_op jit(solution)/shard_map/ppermute | solution.py:26
  59.2 16.8 %copy-start.5 = (s32[4]{0:T(128)S(1)}, s32[4]{0:T(128)}, u32[]{:S(2)}) copy-start(s32[4]{0:T(128)} %owner.3) | copy-start | bytes 52
  76.0 14.8 %copy-start.6 = (s32[2]{0:T(128)S(1)}, s32[2]{0:T(128)}, u32[]{:S(2)}) copy-start(s32[2]{0:T(128)} %counts.1) | copy-start | bytes 28
  76.0 14.8 %copy-start.7 = (s32[1,2]{1,0:T(1,128)S(1)}, s32[1,2]{1,0:T(1,128)}, u32[]{:S(2)}) copy-start(s32[1,2]{1,0:T(1,128)} %wanted.1) | copy-start | bytes 28
  78.6 2.0 %collective-permute-start.10 = (f32[2,512,128]{2,1,0:T(8,128)S(1)}, f32[2,512,128]{2,1,0:T(8,128)S(1)}, u32[]{:S(2)}, u32[]{:S(2)}) collective-permute-start(f32[2,512,128]{2,1,0:T(8,128)S(1)} %get-tuple-element.50), channel_id=1, source_target_pairs={{0,1},{1,0},{2,3},{3,2},{4,5},{5,4},{6,7},{7,6},{8,9},{9,8},{10,11... | collective-permute-start | bytes 1572872 | tf_op jit(solution)/shard_map/ppermute | solution.py:26
  81.2 5.6 %collective-permute-start.11 = (f32[256,128]{1,0:T(8,128)S(1)}, f32[256,128]{1,0:T(8,128)S(1)}, u32[]{:S(2)}, u32[]{:S(2)}) collective-permute-start(f32[256,128]{1,0:T(8,128)S(1)} %get-tuple-element.52), channel_id=1, source_target_pairs={{0,16},{2,18},{16,0},{18,2},{1,17},{3,19},{17,1},{19,3},{4,20},{6,... | collective-permute-start | bytes 393224 | tf_op jit(solution)/shard_map/ppermute | solution.py:291
  82.5 6.4 %collective-permute-start.12 = (f32[256,128]{1,0:T(8,128)S(1)}, f32[256,128]{1,0:T(8,128)S(1)}, u32[]{:S(2)}, u32[]{:S(2)}) collective-permute-start(f32[256,128]{1,0:T(8,128)S(1)} %get-tuple-element.53), channel_id=1, source_target_pairs={{0,2},{2,0},{16,18},{18,16},{1,3},{3,1},{17,19},{19,17},{4,6},{6,4... | collective-permute-start | bytes 393224 | tf_op jit(solution)/shard_map/ppermute | solution.py:291
  84.0 6.8 %collective-permute-start.13 = (f32[256,128]{1,0:T(8,128)S(1)}, f32[256,128]{1,0:T(8,128)S(1)}, u32[]{:S(2)}, u32[]{:S(2)}) collective-permute-start(f32[256,128]{1,0:T(8,128)S(1)} %get-tuple-element.54), channel_id=1, source_target_pairs={{0,18},{2,16},{16,2},{18,0},{1,19},{3,17},{17,3},{19,1},{4,22},{6,... | collective-permute-start | bytes 393224 | tf_op jit(solution)/shard_map/ppermute | solution.py:291
  91.7 6.5 %collective-permute-start.14 = (bf16[256,128]{1,0:T(8,128)(2,1)S(1)}, bf16[256,128]{1,0:T(8,128)(2,1)S(1)}, u32[]{:S(2)}, u32[]{:S(2)}) collective-permute-start(bf16[256,128]{1,0:T(8,128)(2,1)S(1)} %get-tuple-element.56), channel_id=1, source_target_pairs={{0,4},{4,8},{8,12},{12,0},{1,5},{5,9},{9,13},{13,1},{2,6},{6,10},{... | collective-permute-start | bytes 196616 | tf_op jit(solution)/shard_map/ppermute | solution.py:26
  91.7 7.7 %collective-permute-start.15 = (bf16[256,128]{1,0:T(8,128)(2,1)S(1)}, bf16[256,128]{1,0:T(8,128)(2,1)S(1)}, u32[]{:S(2)}, u32[]{:S(2)}) collective-permute-start(bf16[256,128]{1,0:T(8,128)(2,1)S(1)} %get-tuple-element.57), channel_id=1, source_target_pairs={{0,8},{4,12},{8,0},{12,4},{1,9},{5,13},{9,1},{13,5},{2,10},{6,14},... | collective-permute-start | bytes 196616 | tf_op jit(solution)/shard_map/ppermute | solution.py:26
  91.9 7.5 %collective-permute-start.16 = (bf16[256,128]{1,0:T(8,128)(2,1)S(1)}, bf16[256,128]{1,0:T(8,128)(2,1)S(1)}, u32[]{:S(2)}, u32[]{:S(2)}) collective-permute-start(bf16[256,128]{1,0:T(8,128)(2,1)S(1)} %get-tuple-element.58), channel_id=1, source_target_pairs={{0,12},{4,0},{8,4},{12,8},{1,13},{5,1},{9,5},{13,9},{2,14},{6,2},{... | collective-permute-start | bytes 196616 | tf_op jit(solution)/shard_map/ppermute | solution.py:26

commit v6 on v5

--- a/solution.py
+++ b/solution.py
@@ -9,7 +9,6 @@
 
 BW = 512
 LEN = 128
-FLOPS_SCALE = 1
 F32 = jnp.float32
 BF16 = jnp.bfloat16
 VMEM_LIMIT = 40 * 1024 * 1024
@@ -40,16 +39,27 @@
     return lax.ppermute(value, ("block", "cores"), pairs)
 
 
-def gather_act(act):
+def assemble_kernel(blocks, cores, place, *refs):
+    parts, out = refs[:-1], refs[-1]
+    height = parts[0].shape[0]
+    for i, part in enumerate(parts):
+        core = lax.rem(place[1] - i % cores + cores, cores)
+        block = lax.rem(place[2] - i // cores + blocks, blocks)
+        start = pl.multiple_of((core * blocks + block) * height, height)
+        out[pl.ds(start, height)] = part[...]
+
+
+def gather_act(place, act):
     cores, blocks = lax.axis_size("cores"), lax.axis_size("block")
-    core, block = lax.axis_index("cores"), lax.axis_index("block")
-    out = jnp.zeros((cores, blocks) + act.shape, act.dtype)
-    for far in range(blocks):
-        for step in range(cores):
-            came = to_neighbour(act, far, step) if far or step else act
-            source = ((core - step) % cores, (block - far) % blocks, 0, 0)
-            out = lax.dynamic_update_slice(out, came[None, None], source)
-    return out.reshape(-1, act.shape[-1])
+    parts = [act] + [to_neighbour(act, i // cores, i % cores) for i in range(1, blocks * cores)]
+    shape = (len(parts) * act.shape[0], act.shape[1])
+    return pl.pallas_call(
+        functools.partial(assemble_kernel, blocks, cores),
+        out_shape=jax.ShapeDtypeStruct(shape, act.dtype),
+        in_specs=[SMEM] + [VMEM] * len(parts),
+        out_specs=VMEM,
+        compiler_params=pltpu.CompilerParams(vmem_limit_bytes=VMEM_LIMIT),
+    )(place, *parts)
 
 
 def rotate_kernel(blocks, cores, place, acts, basis, *outs):
@@ -119,7 +129,7 @@
         out_specs=VMEM,
         compiler_params=pltpu.CompilerParams(vmem_limit_bytes=VMEM_LIMIT),
         cost_estimate=pl.CostEstimate(
-            flops=FLOPS_SCALE * flops, bytes_accessed=flops // width, transcendentals=0
+            flops=flops, bytes_accessed=flops // width, transcendentals=0
         ),
     )(*rows, *pieces)
 
@@ -132,15 +142,16 @@
     return jnp.where(position == positions, at_last, before)
 
 
-def pack_kernel(dp, cores, parts, owner, place, held, *refs):
+def pack_kernel(dp, cores, parts, start, owner, place, held, *refs):
     row, core = place[0], place[1]
     refs = list(refs)
     rows = [[refs.pop(0) for _ in range(cuts)] for cuts in parts]
     early = [refs.pop(0) for _ in parts]
+    almost = [refs.pop(0) for _ in parts]
     last, sends = refs[0], refs[1:]
     height = early[0].shape[1]
     for g in range(len(parts)):
-        last[g * height : (g + 1) * height] = product(rows[g], held, 0)
+        last[g * height : (g + 1) * height] = almost[g][0] + product(rows[g], held, start)
     for step in range(1, cores):
         for block in range(sends[0].shape[0]):
             piece = block * cores + lax.rem(core + step, cores)
@@ -151,18 +162,18 @@
                 )
 
 
-def pack(owner_slot, place, rows, held, early, blocks, cores):
+def pack(owner_slot, place, rows, held, start, early, almost, blocks, cores):
     positions, height, width = early[0].shape
     shape = (len(rows) * height, width)
     parts = tuple(len(part) for part in rows)
     return pl.pallas_call(
-        functools.partial(pack_kernel, positions + 1, cores, parts),
+        functools.partial(pack_kernel, positions + 1, cores, parts, start),
         out_shape=(jax.ShapeDtypeStruct(shape, F32),)
         + (jax.ShapeDtypeStruct((blocks,) + shape, F32),) * (cores - 1),
-        in_specs=[SMEM, SMEM] + [VMEM] * (1 + sum(parts) + len(rows)),
+        in_specs=[SMEM, SMEM] + [VMEM] * (1 + sum(parts) + 2 * len(rows)),
         out_specs=(VMEM,) * cores,
         compiler_params=pltpu.CompilerParams(vmem_limit_bytes=VMEM_LIMIT),
-    )(owner_slot, place, held, *[cut for part in rows for cut in part], *early)
+    )(owner_slot, place, held, *[cut for part in rows for cut in part], *early, *almost)
 
 
 def join_kernel(dp, cores, groups, blocks, owner, place, last, *refs):
@@ -244,10 +255,13 @@
     part_features = features // groups
     place = jnp.stack([row, core, block])
 
-    ring = [
-        lax.dynamic_slice_in_dim(basis_store[0], group * part_features, part_features, 0)
+    cut = part_features // 256 * 128
+    shares = (0, cut)
+    first, second = [
+        [lax.dynamic_slice_in_dim(basis_store[0], group * part_features + start, size, 0)]
+        for start, size in zip(shares, (cut, part_features - cut))
     ]
-    flat_grads = after(gradients.reshape(slots, features), ring[0])
+    flat_grads = after(gradients.reshape(slots, features), first[0], second[0])
 
     def share(index):
         return lax.dynamic_slice_in_dim(flat_grads, index * part_features, part_features, 1)
@@ -257,25 +271,30 @@
 
     flat_acts = activations.reshape(slots, activations.shape[2])
     act, *away_act = rotate(place, flat_acts, basis_act, blocks, cores)
-    act_rot_t = None
     for step in range(1, dp):
-        came = shift(ring[-1], "dp", 1)
+        first.append(shift(first[-1], "dp", 1))
+        second.append(shift(second[-1], "dp", 1))
         if step == 1:
-            came, act, flat_grads, *away_act = lax.optimization_barrier(
-                (came, act, flat_grads, *away_act)
+            first[1], act, flat_grads, *away_act = lax.optimization_barrier(
+                (first[1], act, flat_grads, *away_act)
             )
-            for i, part in enumerate(away_act, 1):
-                act = act + to_neighbour(part, i // cores, i % cores)
+            away_act = [
+                to_neighbour(part, i // cores, i % cores) for i, part in enumerate(away_act, 1)
+            ]
             rows = [[share(group)]] + others
-        if step == 2:
-            came, act = lax.optimization_barrier((came, act))
-            act_rot_t = gather_act(act.astype(BF16))
-        ring.append(came)
-
-    early = [early_products(part, ring[:-1], (0,)) for part in rows]
-    last, act_rot_t, *early = lax.optimization_barrier((ring[-1], act_rot_t, *early))
-    last, *sends = pack(owner_slot, place, rows, last, early, blocks, cores)
+    act = after(act, second[2])
+    for part in away_act:
+        act = act + part
+    act_rot_t = gather_act(place, act.astype(BF16))
+
+    pieces = [piece for pair in zip(first, second) for piece in pair]
+    early = [early_products(part, pieces[:-2], shares) for part in rows]
+    pieces[-2], *early = lax.optimization_barrier((pieces[-2], *early))
+    almost = [early_products(part, pieces[-2:-1], shares[:1]) for part in rows]
+    last, *almost = lax.optimization_barrier((pieces[-1], *almost))
+    last, *sends = pack(owner_slot, place, rows, last, cut, early, almost, blocks, cores)
     came = [shift(send, "cores", step) for step, send in enumerate(sends, 1)]
+    came[0], act_rot_t = lax.optimization_barrier((came[0], act_rot_t))
     parts = join(owner_slot, place, last, early, came, blocks, cores)
 
     parts = list(parts)

time: 100 us -> 108 us (1.080)
  starting transfers between devices: 15.8 us -> 20 us
  waiting for transfers between devices: 59.5 us -> 62.8 us
  Pallas kernels: 13.8 us -> 15.6 us
  local copies, waits for them, and re-layouts: 10.1 us -> 8.43 us
    ppermute x8 -> x11, waiting for transfers between devices: 33.7 us -> 47.4 us  [shift(): lax.ppermute(value, axis, [(i, (i + step) % size) for i in range(size)])]
    ppermute x6, waiting for transfers between devices: 19.8 us -> 8.8 us  [to_neighbour(): return lax.ppermute(value, ('block', 'cores'), pairs)]
    unnamed x22 -> x12, local copies, waits for them, and re-layouts: 6.22 us -> 3.23 us
    ppermute x8 -> x11, starting transfers between devices: 8.49 us -> 11.4 us  [shift(): lax.ppermute(value, axis, [(i, (i + step) % size) for i in range(size)])]
    pallas_call x2 -> x4, Pallas kernels: 7.02 us -> 8.68 us  [early_products(): pl.pallas_call(functools.partial(early_kernel, len(rows), shares), out_sh...]
    dynamic_slice x1 -> x2, local copies, waits for them, and re-layouts: 2.28 us -> 3.77 us  [on_device(): lax.dynamic_slice_in_dim(basis_store[0], group * part_features + start, s...]
    ppermute x6, starting transfers between devices: 3.72 us -> 5.07 us  [to_neighbour(): return lax.ppermute(value, ('block', 'cores'), pairs)]
  transfers between devices with their start and end apart: 17 -> 20, of which waited for: 12 -> 12; matrix products, arithmetic and copies ran while one was open for 2% -> 0% of each run, Pallas kernels for 10% -> 13%
where the time goes in v6:
time: 108 us
  waiting for transfers between devices  62.8 us (58%)
  starting transfers between devices  20 us (19%)
  Pallas kernels  15.6 us (14%)
  local copies, waits for them, and re-layouts  8.43 us (8%)
    ppermute x11, waiting for transfers between devices, shift(): lax.ppermute(value, axis, [(i, (i + step) % size) for i in range(size)])  47.4 us
    ppermute x11, starting transfers between devices, shift(): lax.ppermute(value, axis, [(i, (i + step) % size) for i in range(size)])  11.4 us
    ppermute x6, waiting for transfers between devices, to_neighbour(): return lax.ppermute(value, ('block', 'cores'), pairs)  8.8 us
    pallas_call x4, Pallas kernels, early_products(): pl.pallas_call(functools.partial(early_kernel, len(rows), shares), out_sh...  8.68 us
    ppermute x3, waiting for transfers between devices, on_device(): parts[i] = lax.ppermute(parts[i], ('groups', 'block'), pairs)  6.62 us
    ppermute x6, starting transfers between devices, to_neighbour(): return lax.ppermute(value, ('block', 'cores'), pairs)  5.07 us
    dynamic_slice x2, local copies, waits for them, and re-layouts, on_device(): lax.dynamic_slice_in_dim(basis_store[0], group * part_features + start, s...  3.77 us
    ppermute x3, starting transfers between devices, on_device(): parts[i] = lax.ppermute(parts[i], ('groups', 'block'), pairs)  3.55 us
  transfers between devices with their start and end apart: 20, of which 12 were waited for; matrix products, arithmetic and copies ran while one was open for 0% of the time, Pallas kernels for 13%

profile of v6, /device:TPU:0, one launch (start us, length us, event | category | flops | bytes accessed | tf_op | source)
XLA Modules:
  0.0 107.8 jit_solution(15102806312770131459)
XLA Ops:
  0.0 0.0 copy-start
  0.0 2.0 %dynamic-slice_bitcast_fusion.refs_2_ = bf16[1792,128]{1,0:T(8,128)(2,1)} fusion(bf16[1,6912,128]{2,1,0:T(8,128)(2,1)} %param.11, s32[]{:T(128)S(6)} %select_n.17), kind=kLoop, calls=%fused_computation | loop fusion | bytes 917508 | tf_op jit(solution)/shard_map/dynamic_slice | solution.py:261
  2.0 1.8 %dynamic-slice_bitcast_fusion.1.refs_1_ = bf16[1664,128]{1,0:T(8,128)(2,1)} fusion(bf16[1,6912,128]{2,1,0:T(8,128)(2,1)} %param.11, s32[]{:T(128)S(6)} %select_n.18), kind=kLoop, calls=%fused_computation.1 | loop fusion | bytes 851972 | tf_op jit(solution)/shard_map/dynamic_slice | solution.py:261
  3.8 0.0 copy-done
  3.8 1.3 %constant_dynamic-slice_fusion = bf16[256,3456]{1,0:T(8,128)(2,1)} fusion(bf16[256,6912]{1,0:T(8,128)(2,1)S(1)} %bitcast.9, s32[]{:T(128)S(6)} %select_n.20), kind=kLoop, calls=%fused_computation.4 | loop fusion | bytes 3538948 | tf_op jit(solution)/shard_map/dynamic_slice | solution.py:267
  5.1 3.0 %collective-permute-start.6 = (bf16[256,3456]{1,0:T(8,128)(2,1)}, bf16[256,3456]{1,0:T(8,128)(2,1)}, u32[]{:S(2)}, u32[]{:S(2)}) collective-permute-start(bf16[256,3456]{1,0:T(8,128)(2,1)} %constant_dynamic-slice_fusion), channel_id=1, source_target_pairs={{0,16},{16,0},{1,17},{17,1},{2,18},{18,2},{3,19},{19,3},{4,20},{20... | collective-permute-start | bytes 5308424 | tf_op jit(solution)/shard_map/ppermute | solution.py:25
  8.1 1.6 %collective-permute-start = (bf16[1792,128]{1,0:T(8,128)(2,1)}, bf16[1792,128]{1,0:T(8,128)(2,1)}, u32[]{:S(2)}, u32[]{:S(2)}) collective-permute-start(bf16[1792,128]{1,0:T(8,128)(2,1)} %dynamic-slice_bitcast_fusion.refs_2_), channel_id=1, source_target_pairs={{0,4},{4,8},{8,12},{12,0},{1,5},{5,9},{9,13},{13,1},{2,6},{6,10},{... | collective-permute-start | bytes 1376264 | tf_op jit(solution)/shard_map/ppermute | solution.py:25
  9.6 1.6 %collective-permute-start.3 = (bf16[1664,128]{1,0:T(8,128)(2,1)}, bf16[1664,128]{1,0:T(8,128)(2,1)}, u32[]{:S(2)}, u32[]{:S(2)}) collective-permute-start(bf16[1664,128]{1,0:T(8,128)(2,1)} %dynamic-slice_bitcast_fusion.1.refs_1_), channel_id=1, source_target_pairs={{0,4},{4,8},{8,12},{12,0},{1,5},{5,9},{9,13},{13,1},{2,6},{6,10},{... | collective-permute-start | bytes 1277960 | tf_op jit(solution)/shard_map/ppermute | solution.py:25
  11.2 12.4 %collective-permute-done.refs_4_ = bf16[1792,128]{1,0:T(8,128)(2,1)} collective-permute-done((bf16[1792,128]{1,0:T(8,128)(2,1)}, bf16[1792,128]{1,0:T(8,128)(2,1)}, u32[]{:S(2)}, u32[]{:S(2)}) %collective-permute-start) | collective-permute-done | bytes 458784 | tf_op jit(solution)/shard_map/ppermute | solution.py:25
  23.6 0.0 collective-permute-start.1
  23.6 0.1 pad_add_fusion.place
  23.7 2.1 %copy-done.1 = bf16[1280,1536]{1,0:T(8,128)(2,1)S(1)} copy-done((bf16[1280,1536]{1,0:T(8,128)(2,1)S(1)}, bf16[1280,1536]{1,0:T(8,128)(2,1)}, u32[]{:S(2)}) %copy-start.1) | copy-done | bytes 3932184
  25.8 1.1 %copy-done.2 = bf16[2,128,1280]{2,1,0:T(8,128)(2,1)S(1)} copy-done((bf16[2,128,1280]{2,1,0:T(8,128)(2,1)S(1)}, bf16[2,128,1280]{2,1,0:T(8,128)(2,1)}, u32[]{:S(2)}) %copy-start.2) | copy-done | bytes 655384
  26.9 2.6 %shard_map.73 = (f32[384,256]{1,0:T(8,128)S(1)}, f32[384,256]{1,0:T(8,128)S(1)}, f32[384,256]{1,0:T(8,128)S(1)}, f32[384,256]{1,0:T(8,128)S(1)}) custom-call(s32[3]{0:T(128)S(1)} %pad_add_fusion.place, bf16[256,1280]{1,0:T(8,128)(2,1)S(1)} %bitcast.11, bf16[1280,1536]{1,0:T(8,128)(2,1)S(1)} %copy-done.1), custom_call_target="tpu_custom_call" | custom-call | tf_op jit(solution)/shard_map/pallas_call | solution.py:84
  29.5 3.2 %collective-permute-done.3.refs_3_ = bf16[1664,128]{1,0:T(8,128)(2,1)} collective-permute-done((bf16[1664,128]{1,0:T(8,128)(2,1)}, bf16[1664,128]{1,0:T(8,128)(2,1)}, u32[]{:S(2)}, u32[]{:S(2)}) %collective-permute-start.3) | collective-permute-done | bytes 426016 | tf_op jit(solution)/shard_map/ppermute | solution.py:25
  32.7 0.0 collective-permute-start.4
  32.7 0.0 collective-permute-start.10
  32.7 1.6 %collective-permute-start.8 = (f32[384,256]{1,0:T(8,128)S(1)}, f32[384,256]{1,0:T(8,128)S(1)}, u32[]{:S(2)}, u32[]{:S(2)}) collective-permute-start(f32[384,256]{1,0:T(8,128)S(1)} %get-tuple-element.51), channel_id=1, source_target_pairs={{0,1},{1,0},{2,3},{3,2},{4,5},{5,4},{6,7},{7,6},{8,9},{9,8},{10,11... | collective-permute-start | bytes 1179656 | tf_op jit(solution)/shard_map/ppermute | solution.py:39
  34.3 15.8 %collective-permute-done.4.refs_5_ = bf16[1664,128]{1,0:T(8,128)(2,1)S(1)} collective-permute-done((bf16[1664,128]{1,0:T(8,128)(2,1)}, bf16[1664,128]{1,0:T(8,128)(2,1)S(1)}, u32[]{:S(2)}, u32[]{:S(2)}) %collective-permute-start.4) | collective-permute-done | bytes 426016 | tf_op jit(solution)/shard_map/ppermute | solution.py:25
  50.2 1.5 %collective-permute-start.9 = (f32[384,256]{1,0:T(8,128)S(1)}, f32[384,256]{1,0:T(8,128)S(1)}, u32[]{:S(2)}, u32[]{:S(2)}) collective-permute-start(f32[384,256]{1,0:T(8,128)S(1)} %get-tuple-element.52), channel_id=1, source_target_pairs={{0,2},{1,3},{2,0},{3,1},{4,6},{5,7},{6,4},{7,5},{8,10},{9,11},{10,... | collective-permute-start | bytes 1179656 | tf_op jit(solution)/shard_map/ppermute | solution.py:39
  51.7 0.0 collective-permute-done.1.refs_6_
  51.7 0.0 collective-permute-start.5
  51.7 0.0 collective-permute-done.6.refs_0_.refs_1_
  51.7 1.3 %collective-permute-start.2 = (bf16[1792,128]{1,0:T(8,128)(2,1)S(1)}, bf16[1792,128]{1,0:T(8,128)(2,1)S(1)}, u32[]{:S(2)}, u32[]{:S(2)}) collective-permute-start(bf16[1792,128]{1,0:T(8,128)(2,1)S(1)} %collective-permute-done.1.refs_6_), channel_id=1, source_target_pairs={{0,4},{4,8},{8,12},{12,0},{1,5},{5,9},{9,13},{13,1},{2,6},{6,10},{... | collective-permute-start | bytes 1376264 | tf_op jit(solution)/shard_map/ppermute | solution.py:25
  53.0 0.1 constant_dynamic-slice_fusion.1.refs_0_
  53.1 3.0 %shard_map.74.refs_2_.refs_0_ = f32[3,256,128]{2,1,0:T(8,128)S(1)} custom-call(bf16[256,3456]{1,0:T(8,128)(2,1)S(1)} %constant_dynamic-slice_fusion.1.refs_0_, bf16[1664,128]{1,0:T(8,128)(2,1)} %dynamic-slice_bitcast_fusion.1.refs_1_, bf16[1792,128]{1,0:T(8,128)(2,1)} %dynamic-slice_bitcast_fusion.refs_2_, bf16[1664,128]{1,0:T(8,128)(2,1)} %collective-permute-done.3.refs_3_, ...), custom_call_target="tpu_custom_call" | custom-call | flops 679477248 | bytes 5308416 | tf_op jit(solution)/shard_map/pallas_call | solution.py:125
  56.1 3.5 %shard_map.75.refs_3_.refs_1_ = f32[3,256,128]{2,1,0:T(8,128)S(1)} custom-call(bf16[256,3456]{1,0:T(8,128)(2,1)} %collective-permute-done.6.refs_0_.refs_1_, bf16[1664,128]{1,0:T(8,128)(2,1)} %dynamic-slice_bitcast_fusion.1.refs_1_, bf16[1792,128]{1,0:T(8,128)(2,1)} %dynamic-slice_bitcast_fusion.refs_2_, bf16[1664,128]{1,0:T(8,128)(2,1)} %collective-permute-done.3.refs_3_, ...), custom_call_target="tpu_custom_call" | custom-call | flops 679477248 | bytes 5308416 | tf_op jit(solution)/shard_map/pallas_call | solution.py:125
  59.6 0.0 copy-start.3
  59.6 6.6 %collective-permute-done.5.refs_1_ = bf16[1664,128]{1,0:T(8,128)(2,1)S(1)} collective-permute-done((bf16[1664,128]{1,0:T(8,128)(2,1)S(1)}, bf16[1664,128]{1,0:T(8,128)(2,1)S(1)}, u32[]{:S(2)}, u32[]{:S(2)}) %collective-permute-start.5) | collective-permute-done | bytes 426016 | tf_op jit(solution)/shard_map/ppermute | solution.py:25
  66.2 0.4 shard_map.76.refs_4_
  66.6 1.9 %shard_map.77.refs_5_ = f32[1,256,128]{2,1,0:T(8,128)S(1)} custom-call(bf16[256,3456]{1,0:T(8,128)(2,1)} %collective-permute-done.6.refs_0_.refs_1_, bf16[1664,128]{1,0:T(8,128)(2,1)S(1)} %collective-permute-done.5.refs_1_), custom_call_target="tpu_custom_call" | custom-call | flops 109051904 | bytes 851968 | tf_op jit(solution)/shard_map/pallas_call | solution.py:125
  68.5 5.0 %collective-permute-done.2.held = bf16[1792,128]{1,0:T(8,128)(2,1)S(1)} collective-permute-done((bf16[1792,128]{1,0:T(8,128)(2,1)S(1)}, bf16[1792,128]{1,0:T(8,128)(2,1)S(1)}, u32[]{:S(2)}, u32[]{:S(2)}) %collective-permute-start.2) | collective-permute-done | bytes 458784 | tf_op jit(solution)/shard_map/ppermute | solution.py:25
  73.5 2.1 %shard_map.78 = (f32[512,128]{1,0:T(8,128)S(1)}, f32[2,512,128]{2,1,0:T(8,128)S(1)}) custom-call(s32[4]{0:T(128)S(1)} %copy-done.3, s32[3]{0:T(128)S(1)} %pad_add_fusion.place, bf16[1792,128]{1,0:T(8,128)(2,1)S(1)} %collective-permute-done.2.held, bf16[256,3456]{1,0:T(8,128)(2,1)S(1)} %constant_dynamic-slice_fusion.1.refs_0_, ...), custom_call_target="tpu_custom_call" | custom-call | tf_op jit(solution)/shard_map/pallas_call | solution.py:169
  75.6 0.1 collective-permute-start.7
  75.7 0.0 collective-permute-done.10
  75.7 0.0 collective-permute-done.8
  75.7 0.0 collective-permute-done.9
  75.7 0.1 add_convert_fusion.refs_0_
  75.8 0.0 copy-start.4
  75.8 0.0 copy-start.5
  75.8 0.5 collective-permute-start.11
  76.4 0.5 collective-permute-start.12
  76.9 0.9 collective-permute-start.13
  77.8 0.0 collective-permute-done.11.refs_1_
  77.9 6.3 %collective-permute-done.12.refs_2_ = bf16[384,256]{1,0:T(8,128)(2,1)S(1)} collective-permute-done((bf16[384,256]{1,0:T(8,128)(2,1)S(1)}, bf16[384,256]{1,0:T(8,128)(2,1)S(1)}, u32[]{:S(2)}, u32[]{:S(2)}) %collective-permute-start.12) | collective-permute-done | bytes 196640 | tf_op jit(solution)/shard_map/ppermute | solution.py:39
  84.1 2.5 %collective-permute-done.13.refs_3_ = bf16[384,256]{1,0:T(8,128)(2,1)S(1)} collective-permute-done((bf16[384,256]{1,0:T(8,128)(2,1)S(1)}, bf16[384,256]{1,0:T(8,128)(2,1)S(1)}, u32[]{:S(2)}, u32[]{:S(2)}) %collective-permute-start.13) | collective-permute-done | bytes 196640 | tf_op jit(solution)/shard_map/ppermute | solution.py:39
  86.6 0.6 shard_map.79.act
  87.2 0.0 collective-permute-done.7.refs_2_
  87.2 0.7 shard_map.80
  87.9 0.6 collective-permute-start.14
  88.5 0.8 collective-permute-start.15
  89.2 2.2 %collective-permute-start.16 = (f32[256,128]{1,0:T(8,128)S(1)}, f32[256,128]{1,0:T(8,128)S(1)}, u32[]{:S(2)}, u32[]{:S(2)}) collective-permute-start(f32[256,128]{1,0:T(8,128)S(1)} %get-tuple-element.60), channel_id=1, source_target_pairs={{0,18},{2,16},{16,2},{18,0},{1,19},{3,17},{17,3},{19,1},{4,22},{6,... | collective-permute-start | bytes 393224 | tf_op jit(solution)/shard_map/ppermute | solution.py:310
  91.4 2.6 %collective-permute-done.14.refs_1_ = f32[256,128]{1,0:T(8,128)S(1)} collective-permute-done((f32[256,128]{1,0:T(8,128)S(1)}, f32[256,128]{1,0:T(8,128)S(1)}, u32[]{:S(2)}, u32[]{:S(2)}) %collective-permute-start.14) | collective-permute-done | bytes 131104 | tf_op jit(solution)/shard_map/ppermute | solution.py:310
  94.1 0.7 collective-permute-done.15.refs_2_
  94.8 3.3 %collective-permute-done.16.refs_3_ = f32[256,128]{1,0:T(8,128)S(1)} collective-permute-done((f32[256,128]{1,0:T(8,128)S(1)}, f32[256,128]{1,0:T(8,128)S(1)}, u32[]{:S(2)}, u32[]{:S(2)}) %collective-permute-start.16) | collective-permute-done | bytes 131104 | tf_op jit(solution)/shard_map/ppermute | solution.py:310
  98.1 0.0 copy-done.5
  98.1 0.9 shard_map.81
  98.9 0.1 collective-permute-start.17
  99.0 0.5 collective-permute-start.18
  99.5 3.3 %collective-permute-start.19 = (bf16[256,128]{1,0:T(8,128)(2,1)S(1)}, bf16[256,128]{1,0:T(8,128)(2,1)S(1)}, u32[]{:S(2)}, u32[]{:S(2)}) collective-permute-start(bf16[256,128]{1,0:T(8,128)(2,1)S(1)} %get-tuple-element.64), channel_id=1, source_target_pairs={{0,12},{4,0},{8,4},{12,8},{1,13},{5,1},{9,5},{13,9},{2,14},{6,2},{... | collective-permute-start | bytes 196616 | tf_op jit(solution)/shard_map/ppermute | solution.py:25
  102.8 3.0 %collective-permute-done.17 = bf16[256,128]{1,0:T(8,128)(2,1)S(1)} collective-permute-done((bf16[256,128]{1,0:T(8,128)(2,1)S(1)}, bf16[256,128]{1,0:T(8,128)(2,1)S(1)}, u32[]{:S(2)}, u32[]{:S(2)}) %collective-permute-start.17) | collective-permute-done | bytes 65568 | tf_op jit(solution)/shard_map/ppermute | solution.py:25
  105.8 1.3 %collective-permute-done.18 = bf16[256,128]{1,0:T(8,128)(2,1)S(1)} collective-permute-done((bf16[256,128]{1,0:T(8,128)(2,1)S(1)}, bf16[256,128]{1,0:T(8,128)(2,1)S(1)}, u32[]{:S(2)}, u32[]{:S(2)}) %collective-permute-start.18) | collective-permute-done | bytes 65568 | tf_op jit(solution)/shard_map/ppermute | solution.py:25
  107.1 0.0 collective-permute-done.19
  107.2 0.7 add_multiply_fusion
  (4 shorter events, 0.0 us)
Async XLA Ops:
  0.0 3.8 %copy-start = (bf16[2,128,6912]{2,1,0:T(8,128)(2,1)S(1)}, bf16[2,128,6912]{2,1,0:T(8,128)(2,1)}, u32[]{:S(2)}) copy-start(bf16[2,128,6912]{2,1,0:T(8,128)(2,1)} %param.8) | copy-start | bytes 10616836
  5.1 46.6 %collective-permute-start.6 = (bf16[256,3456]{1,0:T(8,128)(2,1)}, bf16[256,3456]{1,0:T(8,128)(2,1)}, u32[]{:S(2)}, u32[]{:S(2)}) collective-permute-start(bf16[256,3456]{1,0:T(8,128)(2,1)} %constant_dynamic-slice_fusion), channel_id=1, source_target_pairs={{0,16},{16,0},{1,17},{17,1},{2,18},{18,2},{3,19},{19,3},{4,20},{20... | collective-permute-start | bytes 5308424 | tf_op jit(solution)/shard_map/ppermute | solution.py:25
  8.1 15.6 %collective-permute-start = (bf16[1792,128]{1,0:T(8,128)(2,1)}, bf16[1792,128]{1,0:T(8,128)(2,1)}, u32[]{:S(2)}, u32[]{:S(2)}) collective-permute-start(bf16[1792,128]{1,0:T(8,128)(2,1)} %dynamic-slice_bitcast_fusion.refs_2_), channel_id=1, source_target_pairs={{0,4},{4,8},{8,12},{12,0},{1,5},{5,9},{9,13},{13,1},{2,6},{6,10},{... | collective-permute-start | bytes 1376264 | tf_op jit(solution)/shard_map/ppermute | solution.py:25
  9.6 23.1 %collective-permute-start.3 = (bf16[1664,128]{1,0:T(8,128)(2,1)}, bf16[1664,128]{1,0:T(8,128)(2,1)}, u32[]{:S(2)}, u32[]{:S(2)}) collective-permute-start(bf16[1664,128]{1,0:T(8,128)(2,1)} %dynamic-slice_bitcast_fusion.1.refs_1_), channel_id=1, source_target_pairs={{0,4},{4,8},{8,12},{12,0},{1,5},{5,9},{9,13},{13,1},{2,6},{6,10},{... | collective-permute-start | bytes 1277960 | tf_op jit(solution)/shard_map/ppermute | solution.py:25
  23.6 28.1 %collective-permute-start.1 = (bf16[1792,128]{1,0:T(8,128)(2,1)}, bf16[1792,128]{1,0:T(8,128)(2,1)S(1)}, u32[]{:S(2)}, u32[]{:S(2)}) collective-permute-start(bf16[1792,128]{1,0:T(8,128)(2,1)} %collective-permute-done.refs_4_), channel_id=1, source_target_pairs={{0,4},{4,8},{8,12},{12,0},{1,5},{5,9},{9,13},{13,1},{2,6},{6,10},{... | collective-permute-start | bytes 1376264 | tf_op jit(solution)/shard_map/ppermute | solution.py:25
  23.7 2.1 %copy-start.1 = (bf16[1280,1536]{1,0:T(8,128)(2,1)S(1)}, bf16[1280,1536]{1,0:T(8,128)(2,1)}, u32[]{:S(2)}) copy-start(bf16[1280,1536]{1,0:T(8,128)(2,1)} %basis.1) | copy-start | bytes 11796484
  25.8 1.1 %copy-start.2 = (bf16[2,128,1280]{2,1,0:T(8,128)(2,1)S(1)}, bf16[2,128,1280]{2,1,0:T(8,128)(2,1)}, u32[]{:S(2)}) copy-start(bf16[2,128,1280]{2,1,0:T(8,128)(2,1)} %param.7) | copy-start | bytes 1966084
  32.7 17.5 %collective-permute-start.4 = (bf16[1664,128]{1,0:T(8,128)(2,1)}, bf16[1664,128]{1,0:T(8,128)(2,1)S(1)}, u32[]{:S(2)}, u32[]{:S(2)}) collective-permute-start(bf16[1664,128]{1,0:T(8,128)(2,1)} %collective-permute-done.3.refs_3_), channel_id=1, source_target_pairs={{0,4},{4,8},{8,12},{12,0},{1,5},{5,9},{9,13},{13,1},{2,6},{6,10},{... | collective-permute-start | bytes 1277960 | tf_op jit(solution)/shard_map/ppermute | solution.py:25
  32.7 42.9 %collective-permute-start.10 = (f32[384,256]{1,0:T(8,128)S(1)}, f32[384,256]{1,0:T(8,128)S(1)}, u32[]{:S(2)}, u32[]{:S(2)}) collective-permute-start(f32[384,256]{1,0:T(8,128)S(1)} %get-tuple-element.53), channel_id=1, source_target_pairs={{0,3},{1,2},{2,1},{3,0},{4,7},{5,6},{6,5},{7,4},{8,11},{9,10},{10,... | collective-permute-start | bytes 1179656 | tf_op jit(solution)/shard_map/ppermute | solution.py:39
  32.7 42.9 %collective-permute-start.8 = (f32[384,256]{1,0:T(8,128)S(1)}, f32[384,256]{1,0:T(8,128)S(1)}, u32[]{:S(2)}, u32[]{:S(2)}) collective-permute-start(f32[384,256]{1,0:T(8,128)S(1)} %get-tuple-element.51), channel_id=1, source_target_pairs={{0,1},{1,0},{2,3},{3,2},{4,5},{5,4},{6,7},{7,6},{8,9},{9,8},{10,11... | collective-permute-start | bytes 1179656 | tf_op jit(solution)/shard_map/ppermute | solution.py:39
  50.2 25.5 %collective-permute-start.9 = (f32[384,256]{1,0:T(8,128)S(1)}, f32[384,256]{1,0:T(8,128)S(1)}, u32[]{:S(2)}, u32[]{:S(2)}) collective-permute-start(f32[384,256]{1,0:T(8,128)S(1)} %get-tuple-element.52), channel_id=1, source_target_pairs={{0,2},{1,3},{2,0},{3,1},{4,6},{5,7},{6,4},{7,5},{8,10},{9,11},{10,... | collective-permute-start | bytes 1179656 | tf_op jit(solution)/shard_map/ppermute | solution.py:39
  51.7 14.6 %collective-permute-start.5 = (bf16[1664,128]{1,0:T(8,128)(2,1)S(1)}, bf16[1664,128]{1,0:T(8,128)(2,1)S(1)}, u32[]{:S(2)}, u32[]{:S(2)}) collective-permute-start(bf16[1664,128]{1,0:T(8,128)(2,1)S(1)} %collective-permute-done.4.refs_5_), channel_id=1, source_target_pairs={{0,4},{4,8},{8,12},{12,0},{1,5},{5,9},{9,13},{13,1},{2,6},{6,10},{... | collective-permute-start | bytes 1277960 | tf_op jit(solution)/shard_map/ppermute | solution.py:25
  51.7 21.8 %collective-permute-start.2 = (bf16[1792,128]{1,0:T(8,128)(2,1)S(1)}, bf16[1792,128]{1,0:T(8,128)(2,1)S(1)}, u32[]{:S(2)}, u32[]{:S(2)}) collective-permute-start(bf16[1792,128]{1,0:T(8,128)(2,1)S(1)} %collective-permute-done.1.refs_6_), channel_id=1, source_target_pairs={{0,4},{4,8},{8,12},{12,0},{1,5},{5,9},{9,13},{13,1},{2,6},{6,10},{... | collective-permute-start | bytes 1376264 | tf_op jit(solution)/shard_map/ppermute | solution.py:25
  59.6 13.9 %copy-start.3 = (s32[4]{0:T(128)S(1)}, s32[4]{0:T(128)}, u32[]{:S(2)}) copy-start(s32[4]{0:T(128)} %owner.3) | copy-start | bytes 52
  75.6 11.6 %collective-permute-start.7 = (f32[2,512,128]{2,1,0:T(8,128)S(1)}, f32[2,512,128]{2,1,0:T(8,128)S(1)}, u32[]{:S(2)}, u32[]{:S(2)}) collective-permute-start(f32[2,512,128]{2,1,0:T(8,128)S(1)} %get-tuple-element.48), channel_id=1, source_target_pairs={{0,1},{1,0},{2,3},{3,2},{4,5},{5,4},{6,7},{7,6},{8,9},{9,8},{10,11... | collective-permute-start | bytes 1572872 | tf_op jit(solution)/shard_map/ppermute | solution.py:25
  75.8 22.2 %copy-start.4 = (s32[2]{0:T(128)S(1)}, s32[2]{0:T(128)}, u32[]{:S(2)}) copy-start(s32[2]{0:T(128)} %counts.1) | copy-start | bytes 28
  75.8 22.2 %copy-start.5 = (s32[1,2]{1,0:T(1,128)S(1)}, s32[1,2]{1,0:T(1,128)}, u32[]{:S(2)}) copy-start(s32[1,2]{1,0:T(1,128)} %wanted.1) | copy-start | bytes 28
  75.8 2.0 %collective-permute-start.11 = (bf16[384,256]{1,0:T(8,128)(2,1)S(1)}, bf16[384,256]{1,0:T(8,128)(2,1)S(1)}, u32[]{:S(2)}, u32[]{:S(2)}) collective-permute-start(bf16[384,256]{1,0:T(8,128)(2,1)S(1)} %add_convert_fusion.refs_0_), channel_id=1, source_target_pairs={{0,1},{1,0},{2,3},{3,2},{4,5},{5,4},{6,7},{7,6},{8,9},{9,8},{10,11... | collective-permute-start | bytes 589832 | tf_op jit(solution)/shard_map/ppermute | solution.py:39
  76.4 7.8 %collective-permute-start.12 = (bf16[384,256]{1,0:T(8,128)(2,1)S(1)}, bf16[384,256]{1,0:T(8,128)(2,1)S(1)}, u32[]{:S(2)}, u32[]{:S(2)}) collective-permute-start(bf16[384,256]{1,0:T(8,128)(2,1)S(1)} %add_convert_fusion.refs_0_), channel_id=1, source_target_pairs={{0,2},{1,3},{2,0},{3,1},{4,6},{5,7},{6,4},{7,5},{8,10},{9,11},{10,... | collective-permute-start | bytes 589832 | tf_op jit(solution)/shard_map/ppermute | solution.py:39
  76.9 9.7 %collective-permute-start.13 = (bf16[384,256]{1,0:T(8,128)(2,1)S(1)}, bf16[384,256]{1,0:T(8,128)(2,1)S(1)}, u32[]{:S(2)}, u32[]{:S(2)}) collective-permute-start(bf16[384,256]{1,0:T(8,128)(2,1)S(1)} %add_convert_fusion.refs_0_), channel_id=1, source_target_pairs={{0,3},{1,2},{2,1},{3,0},{4,7},{5,6},{6,5},{7,4},{8,11},{9,10},{10,... | collective-permute-start | bytes 589832 | tf_op jit(solution)/shard_map/ppermute | solution.py:39
  87.9 6.2 %collective-permute-start.14 = (f32[256,128]{1,0:T(8,128)S(1)}, f32[256,128]{1,0:T(8,128)S(1)}, u32[]{:S(2)}, u32[]{:S(2)}) collective-permute-start(f32[256,128]{1,0:T(8,128)S(1)} %get-tuple-element.58), channel_id=1, source_target_pairs={{0,16},{2,18},{16,0},{18,2},{1,17},{3,19},{17,1},{19,3},{4,20},{6,... | collective-permute-start | bytes 393224 | tf_op jit(solution)/shard_map/ppermute | solution.py:310
  88.5 6.3 %collective-permute-start.15 = (f32[256,128]{1,0:T(8,128)S(1)}, f32[256,128]{1,0:T(8,128)S(1)}, u32[]{:S(2)}, u32[]{:S(2)}) collective-permute-start(f32[256,128]{1,0:T(8,128)S(1)} %get-tuple-element.59), channel_id=1, source_target_pairs={{0,2},{2,0},{16,18},{18,16},{1,3},{3,1},{17,19},{19,17},{4,6},{6,4... | collective-permute-start | bytes 393224 | tf_op jit(solution)/shard_map/ppermute | solution.py:310
  89.2 8.8 %collective-permute-start.16 = (f32[256,128]{1,0:T(8,128)S(1)}, f32[256,128]{1,0:T(8,128)S(1)}, u32[]{:S(2)}, u32[]{:S(2)}) collective-permute-start(f32[256,128]{1,0:T(8,128)S(1)} %get-tuple-element.60), channel_id=1, source_target_pairs={{0,18},{2,16},{16,2},{18,0},{1,19},{3,17},{17,3},{19,1},{4,22},{6,... | collective-permute-start | bytes 393224 | tf_op jit(solution)/shard_map/ppermute | solution.py:310
  98.9 6.9 %collective-permute-start.17 = (bf16[256,128]{1,0:T(8,128)(2,1)S(1)}, bf16[256,128]{1,0:T(8,128)(2,1)S(1)}, u32[]{:S(2)}, u32[]{:S(2)}) collective-permute-start(bf16[256,128]{1,0:T(8,128)(2,1)S(1)} %get-tuple-element.62), channel_id=1, source_target_pairs={{0,4},{4,8},{8,12},{12,0},{1,5},{5,9},{9,13},{13,1},{2,6},{6,10},{... | collective-permute-start | bytes 196616 | tf_op jit(solution)/shard_map/ppermute | solution.py:25
  99.0 8.1 %collective-permute-start.18 = (bf16[256,128]{1,0:T(8,128)(2,1)S(1)}, bf16[256,128]{1,0:T(8,128)(2,1)S(1)}, u32[]{:S(2)}, u32[]{:S(2)}) collective-permute-start(bf16[256,128]{1,0:T(8,128)(2,1)S(1)} %get-tuple-element.63), channel_id=1, source_target_pairs={{0,8},{4,12},{8,0},{12,4},{1,9},{5,13},{9,1},{13,5},{2,10},{6,14},... | collective-permute-start | bytes 196616 | tf_op jit(solution)/shard_map/ppermute | solution.py:25
  99.5 7.6 %collective-permute-start.19 = (bf16[256,128]{1,0:T(8,128)(2,1)S(1)}, bf16[256,128]{1,0:T(8,128)(2,1)S(1)}, u32[]{:S(2)}, u32[]{:S(2)}) collective-permute-start(bf16[256,128]{1,0:T(8,128)(2,1)S(1)} %get-tuple-element.64), channel_id=1, source_target_pairs={{0,12},{4,0},{8,4},{12,8},{1,13},{5,1},{9,5},{13,9},{2,14},{6,2},{... | collective-permute-start | bytes 196616 | tf_op jit(solution)/shard_map/ppermute | solution.py:25

commit v7 on v6

--- a/solution.py
+++ b/solution.py
@@ -282,19 +282,18 @@
                 to_neighbour(part, i // cores, i % cores) for i, part in enumerate(away_act, 1)
             ]
             rows = [[share(group)]] + others
-    act = after(act, second[2])
+    act = after(act, first[2], second[2])
     for part in away_act:
         act = act + part
     act_rot_t = gather_act(place, act.astype(BF16))
 
     pieces = [piece for pair in zip(first, second) for piece in pair]
     early = [early_products(part, pieces[:-2], shares) for part in rows]
-    pieces[-2], *early = lax.optimization_barrier((pieces[-2], *early))
     almost = [early_products(part, pieces[-2:-1], shares[:1]) for part in rows]
-    last, *almost = lax.optimization_barrier((pieces[-1], *almost))
+    last, act_rot_t, *done = lax.optimization_barrier((pieces[-1], act_rot_t, *almost, *early))
+    almost, early = done[: len(rows)], done[len(rows) :]
     last, *sends = pack(owner_slot, place, rows, last, cut, early, almost, blocks, cores)
     came = [shift(send, "cores", step) for step, send in enumerate(sends, 1)]
-    came[0], act_rot_t = lax.optimization_barrier((came[0], act_rot_t))
     parts = join(owner_slot, place, last, early, came, blocks, cores)
 
     parts = list(parts)

time: 108 us -> 96 us (0.89)
  waiting for transfers between devices: 62.8 us -> 54.7 us
  Pallas kernels: 15.6 us -> 12.6 us
  local copies, waits for them, and re-layouts: 8.43 us -> 7.25 us
    ppermute x11, waiting for transfers between devices: 47.4 us -> 42.6 us  [shift(): lax.ppermute(value, axis, [(i, (i + step) % size) for i in range(size)])]
    ppermute x6, waiting for transfers between devices: 8.8 us -> 6.02 us  [to_neighbour(): return lax.ppermute(value, ('block', 'cores'), pairs)]
    ppermute x11, starting transfers between devices: 11.4 us -> 13.6 us  [shift(): lax.ppermute(value, axis, [(i, (i + step) % size) for i in range(size)])]
    ppermute x6, starting transfers between devices: 5.07 us -> 3.04 us  [to_neighbour(): return lax.ppermute(value, ('block', 'cores'), pairs)]
    pallas_call x4, Pallas kernels: 8.68 us -> 6.7 us  [early_products(): pl.pallas_call(functools.partial(early_kernel, len(rows), shares), out_sh...]
    dynamic_slice x2, local copies, waits for them, and re-layouts: 1.43 us -> 0.24 us  [share(): lax.dynamic_slice_in_dim(flat_grads, index * part_features, part_features...]
  transfers between devices with their start and end apart: 20 -> 20, of which waited for: 12 -> 15; matrix products, arithmetic and copies ran while one was open for 0% -> 2% of each run, Pallas kernels for 13% -> 10%
where the time goes in v7:
time: 96 us; the launch traced here: 95.7 us
  waiting for transfers between devices  54.7 us (57%)
  starting transfers between devices  20.1 us (21%)
  Pallas kernels  12.6 us (13%)
  local copies, waits for them, and re-layouts  7.25 us (8%)
    ppermute x11, waiting for transfers between devices, shift(): lax.ppermute(value, axis, [(i, (i + step) % size) for i in range(size)])  42.6 us
    ppermute x11, starting transfers between devices, shift(): lax.ppermute(value, axis, [(i, (i + step) % size) for i in range(size)])  13.6 us
    pallas_call x4, Pallas kernels, early_products(): pl.pallas_call(functools.partial(early_kernel, len(rows), shares), out_sh...  6.7 us
    ppermute x3, waiting for transfers between devices, on_device(): parts[i] = lax.ppermute(parts[i], ('groups', 'block'), pairs)  6.04 us
    ppermute x6, waiting for transfers between devices, to_neighbour(): return lax.ppermute(value, ('block', 'cores'), pairs)  6.02 us
    dynamic_slice x2, local copies, waits for them, and re-layouts, on_device(): lax.dynamic_slice_in_dim(basis_store[0], group * part_features + start, s...  3.79 us
    ppermute x3, starting transfers between devices, on_device(): parts[i] = lax.ppermute(parts[i], ('groups', 'block'), pairs)  3.55 us
    unnamed x12, local copies, waits for them, and re-layouts  3.22 us
  transfers between devices with their start and end apart: 20, of which 15 were waited for; matrix products, arithmetic and copies ran while one was open for 2% of the time, Pallas kernels for 10%

profile of v7, /device:TPU:0, one launch (start us, length us, event | category | flops | bytes accessed | tf_op | source)
XLA Modules:
  0.0 95.7 jit_solution(8636373592881107005)
XLA Ops:
  0.0 0.0 copy-start
  0.0 2.0 %dynamic-slice_bitcast_fusion.1.refs_1_ = bf16[1664,128]{1,0:T(8,128)(2,1)} fusion(bf16[1,6912,128]{2,1,0:T(8,128)(2,1)} %param.11, s32[]{:T(128)S(6)} %select_n.18), kind=kLoop, calls=%fused_computation.1 | loop fusion | bytes 851972 | tf_op jit(solution)/shard_map/dynamic_slice | solution.py:261
  2.0 3.0 %collective-permute-start.3 = (bf16[1664,128]{1,0:T(8,128)(2,1)}, bf16[1664,128]{1,0:T(8,128)(2,1)}, u32[]{:S(2)}, u32[]{:S(2)}) collective-permute-start(bf16[1664,128]{1,0:T(8,128)(2,1)} %dynamic-slice_bitcast_fusion.1.refs_1_), channel_id=1, source_target_pairs={{0,4},{4,8},{8,12},{12,0},{1,5},{5,9},{9,13},{13,1},{2,6},{6,10},{... | collective-permute-start | bytes 1277960 | tf_op jit(solution)/shard_map/ppermute | solution.py:25
  5.0 1.8 %dynamic-slice_bitcast_fusion.refs_2_ = bf16[1792,128]{1,0:T(8,128)(2,1)} fusion(bf16[1,6912,128]{2,1,0:T(8,128)(2,1)} %param.11, s32[]{:T(128)S(6)} %select_n.17), kind=kLoop, calls=%fused_computation | loop fusion | bytes 917508 | tf_op jit(solution)/shard_map/dynamic_slice | solution.py:261
  6.8 1.6 %collective-permute-start = (bf16[1792,128]{1,0:T(8,128)(2,1)}, bf16[1792,128]{1,0:T(8,128)(2,1)}, u32[]{:S(2)}, u32[]{:S(2)}) collective-permute-start(bf16[1792,128]{1,0:T(8,128)(2,1)} %dynamic-slice_bitcast_fusion.refs_2_), channel_id=1, source_target_pairs={{0,4},{4,8},{8,12},{12,0},{1,5},{5,9},{9,13},{13,1},{2,6},{6,10},{... | collective-permute-start | bytes 1376264 | tf_op jit(solution)/shard_map/ppermute | solution.py:25
  8.4 0.0 copy-done
  8.4 0.1 pad_add_fusion.place
  8.5 2.1 %copy-done.1 = bf16[1280,1536]{1,0:T(8,128)(2,1)S(1)} copy-done((bf16[1280,1536]{1,0:T(8,128)(2,1)S(1)}, bf16[1280,1536]{1,0:T(8,128)(2,1)}, u32[]{:S(2)}) %copy-start.1) | copy-done | bytes 3932184
  10.6 1.1 %copy-done.2 = bf16[2,128,1280]{2,1,0:T(8,128)(2,1)S(1)} copy-done((bf16[2,128,1280]{2,1,0:T(8,128)(2,1)S(1)}, bf16[2,128,1280]{2,1,0:T(8,128)(2,1)}, u32[]{:S(2)}) %copy-start.2) | copy-done | bytes 655384
  11.7 2.6 %shard_map.73 = (f32[384,256]{1,0:T(8,128)S(1)}, f32[384,256]{1,0:T(8,128)S(1)}, f32[384,256]{1,0:T(8,128)S(1)}, f32[384,256]{1,0:T(8,128)S(1)}) custom-call(s32[3]{0:T(128)S(1)} %pad_add_fusion.place, bf16[256,1280]{1,0:T(8,128)(2,1)S(1)} %bitcast.11, bf16[1280,1536]{1,0:T(8,128)(2,1)S(1)} %copy-done.1), custom_call_target="tpu_custom_call" | custom-call | tf_op jit(solution)/shard_map/pallas_call | solution.py:84
  14.3 3.7 %collective-permute-done.3.refs_3_ = bf16[1664,128]{1,0:T(8,128)(2,1)} collective-permute-done((bf16[1664,128]{1,0:T(8,128)(2,1)}, bf16[1664,128]{1,0:T(8,128)(2,1)}, u32[]{:S(2)}, u32[]{:S(2)}) %collective-permute-start.3) | collective-permute-done | bytes 426016 | tf_op jit(solution)/shard_map/ppermute | solution.py:25
  18.0 0.0 collective-permute-start.4
  18.0 0.1 constant_dynamic-slice_fusion
  18.1 1.8 %collective-permute-start.12 = (bf16[256,3456]{1,0:T(8,128)(2,1)S(1)}, bf16[256,3456]{1,0:T(8,128)(2,1)S(1)}, u32[]{:S(2)}, u32[]{:S(2)}) collective-permute-start(bf16[256,3456]{1,0:T(8,128)(2,1)S(1)} %constant_dynamic-slice_fusion), channel_id=1, source_target_pairs={{0,16},{16,0},{1,17},{17,1},{2,18},{18,2},{3,19},{19,3},{4,20},{20... | collective-permute-start | bytes 5308424 | tf_op jit(solution)/shard_map/ppermute | solution.py:25
  19.9 7.9 %collective-permute-done.refs_4_ = bf16[1792,128]{1,0:T(8,128)(2,1)} collective-permute-done((bf16[1792,128]{1,0:T(8,128)(2,1)}, bf16[1792,128]{1,0:T(8,128)(2,1)}, u32[]{:S(2)}, u32[]{:S(2)}) %collective-permute-start) | collective-permute-done | bytes 458784 | tf_op jit(solution)/shard_map/ppermute | solution.py:25
  27.8 0.0 collective-permute-start.1
  27.8 0.0 collective-permute-start.5
  27.8 1.7 %collective-permute-start.6 = (f32[384,256]{1,0:T(8,128)S(1)}, f32[384,256]{1,0:T(8,128)S(1)}, u32[]{:S(2)}, u32[]{:S(2)}) collective-permute-start(f32[384,256]{1,0:T(8,128)S(1)} %get-tuple-element.42), channel_id=1, source_target_pairs={{0,2},{1,3},{2,0},{3,1},{4,6},{5,7},{6,4},{7,5},{8,10},{9,11},{10,... | collective-permute-start | bytes 1179656 | tf_op jit(solution)/shard_map/ppermute | solution.py:39
  29.6 7.3 %collective-permute-done.4.refs_5_ = bf16[1664,128]{1,0:T(8,128)(2,1)S(1)} collective-permute-done((bf16[1664,128]{1,0:T(8,128)(2,1)}, bf16[1664,128]{1,0:T(8,128)(2,1)S(1)}, u32[]{:S(2)}, u32[]{:S(2)}) %collective-permute-start.4) | collective-permute-done | bytes 426016 | tf_op jit(solution)/shard_map/ppermute | solution.py:25
  36.8 0.0 collective-permute-start.7
  36.8 9.0 %collective-permute-done.1.refs_6_ = bf16[1792,128]{1,0:T(8,128)(2,1)S(1)} collective-permute-done((bf16[1792,128]{1,0:T(8,128)(2,1)}, bf16[1792,128]{1,0:T(8,128)(2,1)S(1)}, u32[]{:S(2)}, u32[]{:S(2)}) %collective-permute-start.1) | collective-permute-done | bytes 458784 | tf_op jit(solution)/shard_map/ppermute | solution.py:25
  45.8 0.0 collective-permute-done.5
  45.8 0.0 collective-permute-done.6
  45.8 2.1 %collective-permute-done.7 = f32[384,256]{1,0:T(8,128)S(1)} collective-permute-done((f32[384,256]{1,0:T(8,128)S(1)}, f32[384,256]{1,0:T(8,128)S(1)}, u32[]{:S(2)}, u32[]{:S(2)}) %collective-permute-start.7) | collective-permute-done | bytes 393248 | tf_op jit(solution)/shard_map/ppermute | solution.py:39
  48.0 0.1 add_convert_fusion.refs_0_
  48.1 0.8 collective-permute-start.10
  48.9 1.9 %collective-permute-start.11 = (bf16[1664,128]{1,0:T(8,128)(2,1)S(1)}, bf16[1664,128]{1,0:T(8,128)(2,1)S(1)}, u32[]{:S(2)}, u32[]{:S(2)}) collective-permute-start(bf16[1664,128]{1,0:T(8,128)(2,1)S(1)} %collective-permute-done.4.refs_5_), channel_id=1, source_target_pairs={{0,4},{4,8},{8,12},{12,0},{1,5},{5,9},{9,13},{13,1},{2,6},{6,10},{... | collective-permute-start | bytes 1277960 | tf_op jit(solution)/shard_map/ppermute | solution.py:25
  50.8 0.0 collective-permute-start.8
  50.8 0.5 collective-permute-start.9
  51.3 3.5 %collective-permute-done.10.refs_3_ = bf16[384,256]{1,0:T(8,128)(2,1)S(1)} collective-permute-done((bf16[384,256]{1,0:T(8,128)(2,1)S(1)}, bf16[384,256]{1,0:T(8,128)(2,1)S(1)}, u32[]{:S(2)}, u32[]{:S(2)}) %collective-permute-start.10) | collective-permute-done | bytes 196640 | tf_op jit(solution)/shard_map/ppermute | solution.py:39
  54.8 1.2 %collective-permute-start.2 = (bf16[1792,128]{1,0:T(8,128)(2,1)S(1)}, bf16[1792,128]{1,0:T(8,128)(2,1)S(1)}, u32[]{:S(2)}, u32[]{:S(2)}) collective-permute-start(bf16[1792,128]{1,0:T(8,128)(2,1)S(1)} %collective-permute-done.1.refs_6_), channel_id=1, source_target_pairs={{0,4},{4,8},{8,12},{12,0},{1,5},{5,9},{9,13},{13,1},{2,6},{6,10},{... | collective-permute-start | bytes 1376264 | tf_op jit(solution)/shard_map/ppermute | solution.py:25
  56.0 0.1 constant_dynamic-slice_fusion.1.refs_0_
  56.1 3.0 %shard_map.77.refs_2_.refs_0_ = f32[3,256,128]{2,1,0:T(8,128)S(1)} custom-call(bf16[256,3456]{1,0:T(8,128)(2,1)S(1)} %constant_dynamic-slice_fusion.1.refs_0_, bf16[1664,128]{1,0:T(8,128)(2,1)} %dynamic-slice_bitcast_fusion.1.refs_1_, bf16[1792,128]{1,0:T(8,128)(2,1)} %dynamic-slice_bitcast_fusion.refs_2_, bf16[1664,128]{1,0:T(8,128)(2,1)} %collective-permute-done.3.refs_3_, ...), custom_call_target="tpu_custom_call" | custom-call | flops 679477248 | bytes 5308416 | tf_op jit(solution)/shard_map/pallas_call | solution.py:125
  59.1 0.0 collective-permute-done.8.refs_1_
  59.1 0.4 collective-permute-done.9.refs_2_
  59.5 0.6 shard_map.74.act
  60.2 3.7 %collective-permute-done.11.refs_1_ = bf16[1664,128]{1,0:T(8,128)(2,1)S(1)} collective-permute-done((bf16[1664,128]{1,0:T(8,128)(2,1)S(1)}, bf16[1664,128]{1,0:T(8,128)(2,1)S(1)}, u32[]{:S(2)}, u32[]{:S(2)}) %collective-permute-start.11) | collective-permute-done | bytes 426016 | tf_op jit(solution)/shard_map/ppermute | solution.py:25
  63.8 0.4 shard_map.75.refs_4_
  64.2 0.0 collective-permute-done.12.refs_0_.refs_1_
  64.2 0.4 shard_map.76.refs_5_
  64.6 0.0 copy-start.3
  64.6 3.0 %shard_map.78.refs_3_.refs_1_ = f32[3,256,128]{2,1,0:T(8,128)S(1)} custom-call(bf16[256,3456]{1,0:T(8,128)(2,1)S(1)} %collective-permute-done.12.refs_0_.refs_1_, bf16[1664,128]{1,0:T(8,128)(2,1)} %dynamic-slice_bitcast_fusion.1.refs_1_, bf16[1792,128]{1,0:T(8,128)(2,1)} %dynamic-slice_bitcast_fusion.refs_2_, ...), custom_call_target="tpu_custom_call" | custom-call | flops 679477248 | bytes 5308416 | tf_op jit(solution)/shard_map/pallas_call | solution.py:125
  67.6 0.0 copy-start.4
  67.6 0.0 copy-start.5
  67.6 5.5 %collective-permute-done.2.held = bf16[1792,128]{1,0:T(8,128)(2,1)S(1)} collective-permute-done((bf16[1792,128]{1,0:T(8,128)(2,1)S(1)}, bf16[1792,128]{1,0:T(8,128)(2,1)S(1)}, u32[]{:S(2)}, u32[]{:S(2)}) %collective-permute-start.2) | collective-permute-done | bytes 458784 | tf_op jit(solution)/shard_map/ppermute | solution.py:25
  73.2 1.2 %shard_map.79 = (f32[512,128]{1,0:T(8,128)S(1)}, f32[2,512,128]{2,1,0:T(8,128)S(1)}) custom-call(s32[4]{0:T(128)S(1)} %copy-done.3, s32[3]{0:T(128)S(1)} %pad_add_fusion.place, bf16[1792,128]{1,0:T(8,128)(2,1)S(1)} %collective-permute-done.2.held, bf16[256,3456]{1,0:T(8,128)(2,1)S(1)} %constant_dynamic-slice_fusion.1.refs_0_, ...), custom_call_target="tpu_custom_call" | custom-call | tf_op jit(solution)/shard_map/pallas_call | solution.py:169
  74.3 0.1 collective-permute-start.13
  74.4 1.9 %collective-permute-done.13.refs_2_ = f32[2,512,128]{2,1,0:T(8,128)S(1)} collective-permute-done((f32[2,512,128]{2,1,0:T(8,128)S(1)}, f32[2,512,128]{2,1,0:T(8,128)S(1)}, u32[]{:S(2)}, u32[]{:S(2)}) %collective-permute-start.13) | collective-permute-done | bytes 524320 | tf_op jit(solution)/shard_map/ppermute | solution.py:25
  76.3 0.6 shard_map.80
  77.0 1.6 %collective-permute-start.14 = (f32[256,128]{1,0:T(8,128)S(1)}, f32[256,128]{1,0:T(8,128)S(1)}, u32[]{:S(2)}, u32[]{:S(2)}) collective-permute-start(f32[256,128]{1,0:T(8,128)S(1)} %get-tuple-element.54), channel_id=1, source_target_pairs={{0,16},{2,18},{16,0},{18,2},{1,17},{3,19},{17,1},{19,3},{4,20},{6,... | collective-permute-start | bytes 393224 | tf_op jit(solution)/shard_map/ppermute | solution.py:309
  78.5 1.0 %collective-permute-start.15 = (f32[256,128]{1,0:T(8,128)S(1)}, f32[256,128]{1,0:T(8,128)S(1)}, u32[]{:S(2)}, u32[]{:S(2)}) collective-permute-start(f32[256,128]{1,0:T(8,128)S(1)} %get-tuple-element.55), channel_id=1, source_target_pairs={{0,2},{2,0},{16,18},{18,16},{1,3},{3,1},{17,19},{19,17},{4,6},{6,4... | collective-permute-start | bytes 393224 | tf_op jit(solution)/shard_map/ppermute | solution.py:309
  79.5 1.0 %collective-permute-start.16 = (f32[256,128]{1,0:T(8,128)S(1)}, f32[256,128]{1,0:T(8,128)S(1)}, u32[]{:S(2)}, u32[]{:S(2)}) collective-permute-start(f32[256,128]{1,0:T(8,128)S(1)} %get-tuple-element.56), channel_id=1, source_target_pairs={{0,18},{2,16},{16,2},{18,0},{1,19},{3,17},{17,3},{19,1},{4,22},{6,... | collective-permute-start | bytes 393224 | tf_op jit(solution)/shard_map/ppermute | solution.py:309
  80.5 2.0 %collective-permute-done.14.refs_1_ = f32[256,128]{1,0:T(8,128)S(1)} collective-permute-done((f32[256,128]{1,0:T(8,128)S(1)}, f32[256,128]{1,0:T(8,128)S(1)}, u32[]{:S(2)}, u32[]{:S(2)}) %collective-permute-start.14) | collective-permute-done | bytes 131104 | tf_op jit(solution)/shard_map/ppermute | solution.py:309
  82.6 2.4 %collective-permute-done.15.refs_2_ = f32[256,128]{1,0:T(8,128)S(1)} collective-permute-done((f32[256,128]{1,0:T(8,128)S(1)}, f32[256,128]{1,0:T(8,128)S(1)}, u32[]{:S(2)}, u32[]{:S(2)}) %collective-permute-start.15) | collective-permute-done | bytes 131104 | tf_op jit(solution)/shard_map/ppermute | solution.py:309
  84.9 1.6 %collective-permute-done.16.refs_3_ = f32[256,128]{1,0:T(8,128)S(1)} collective-permute-done((f32[256,128]{1,0:T(8,128)S(1)}, f32[256,128]{1,0:T(8,128)S(1)}, u32[]{:S(2)}, u32[]{:S(2)}) %collective-permute-start.16) | collective-permute-done | bytes 131104 | tf_op jit(solution)/shard_map/ppermute | solution.py:309
  86.5 0.0 copy-done.5
  86.6 0.9 shard_map.81
  87.4 0.1 collective-permute-start.17
  87.5 2.2 %collective-permute-start.18 = (bf16[256,128]{1,0:T(8,128)(2,1)S(1)}, bf16[256,128]{1,0:T(8,128)(2,1)S(1)}, u32[]{:S(2)}, u32[]{:S(2)}) collective-permute-start(bf16[256,128]{1,0:T(8,128)(2,1)S(1)} %get-tuple-element.59), channel_id=1, source_target_pairs={{0,8},{4,12},{8,0},{12,4},{1,9},{5,13},{9,1},{13,5},{2,10},{6,14},... | collective-permute-start | bytes 196616 | tf_op jit(solution)/shard_map/ppermute | solution.py:25
  89.7 1.6 %collective-permute-start.19 = (bf16[256,128]{1,0:T(8,128)(2,1)S(1)}, bf16[256,128]{1,0:T(8,128)(2,1)S(1)}, u32[]{:S(2)}, u32[]{:S(2)}) collective-permute-start(bf16[256,128]{1,0:T(8,128)(2,1)S(1)} %get-tuple-element.60), channel_id=1, source_target_pairs={{0,12},{4,0},{8,4},{12,8},{1,13},{5,1},{9,5},{13,9},{2,14},{6,2},{... | collective-permute-start | bytes 196616 | tf_op jit(solution)/shard_map/ppermute | solution.py:25
  91.3 2.5 %collective-permute-done.17 = bf16[256,128]{1,0:T(8,128)(2,1)S(1)} collective-permute-done((bf16[256,128]{1,0:T(8,128)(2,1)S(1)}, bf16[256,128]{1,0:T(8,128)(2,1)S(1)}, u32[]{:S(2)}, u32[]{:S(2)}) %collective-permute-start.17) | collective-permute-done | bytes 65568 | tf_op jit(solution)/shard_map/ppermute | solution.py:25
  93.8 1.2 %collective-permute-done.18 = bf16[256,128]{1,0:T(8,128)(2,1)S(1)} collective-permute-done((bf16[256,128]{1,0:T(8,128)(2,1)S(1)}, bf16[256,128]{1,0:T(8,128)(2,1)S(1)}, u32[]{:S(2)}, u32[]{:S(2)}) %collective-permute-start.18) | collective-permute-done | bytes 65568 | tf_op jit(solution)/shard_map/ppermute | solution.py:25
  95.0 0.0 collective-permute-done.19
  95.0 0.7 add_multiply_fusion
  (4 shorter events, 0.0 us)
Async XLA Ops:
  0.0 8.4 %copy-start = (bf16[2,128,6912]{2,1,0:T(8,128)(2,1)S(1)}, bf16[2,128,6912]{2,1,0:T(8,128)(2,1)}, u32[]{:S(2)}) copy-start(bf16[2,128,6912]{2,1,0:T(8,128)(2,1)} %param.8) | copy-start | bytes 10616836
  2.0 16.0 %collective-permute-start.3 = (bf16[1664,128]{1,0:T(8,128)(2,1)}, bf16[1664,128]{1,0:T(8,128)(2,1)}, u32[]{:S(2)}, u32[]{:S(2)}) collective-permute-start(bf16[1664,128]{1,0:T(8,128)(2,1)} %dynamic-slice_bitcast_fusion.1.refs_1_), channel_id=1, source_target_pairs={{0,4},{4,8},{8,12},{12,0},{1,5},{5,9},{9,13},{13,1},{2,6},{6,10},{... | collective-permute-start | bytes 1277960 | tf_op jit(solution)/shard_map/ppermute | solution.py:25
  6.8 21.0 %collective-permute-start = (bf16[1792,128]{1,0:T(8,128)(2,1)}, bf16[1792,128]{1,0:T(8,128)(2,1)}, u32[]{:S(2)}, u32[]{:S(2)}) collective-permute-start(bf16[1792,128]{1,0:T(8,128)(2,1)} %dynamic-slice_bitcast_fusion.refs_2_), channel_id=1, source_target_pairs={{0,4},{4,8},{8,12},{12,0},{1,5},{5,9},{9,13},{13,1},{2,6},{6,10},{... | collective-permute-start | bytes 1376264 | tf_op jit(solution)/shard_map/ppermute | solution.py:25
  8.5 2.1 %copy-start.1 = (bf16[1280,1536]{1,0:T(8,128)(2,1)S(1)}, bf16[1280,1536]{1,0:T(8,128)(2,1)}, u32[]{:S(2)}) copy-start(bf16[1280,1536]{1,0:T(8,128)(2,1)} %basis.1) | copy-start | bytes 11796484
  10.6 1.1 %copy-start.2 = (bf16[2,128,1280]{2,1,0:T(8,128)(2,1)S(1)}, bf16[2,128,1280]{2,1,0:T(8,128)(2,1)}, u32[]{:S(2)}) copy-start(bf16[2,128,1280]{2,1,0:T(8,128)(2,1)} %param.7) | copy-start | bytes 1966084
  18.0 18.9 %collective-permute-start.4 = (bf16[1664,128]{1,0:T(8,128)(2,1)}, bf16[1664,128]{1,0:T(8,128)(2,1)S(1)}, u32[]{:S(2)}, u32[]{:S(2)}) collective-permute-start(bf16[1664,128]{1,0:T(8,128)(2,1)} %collective-permute-done.3.refs_3_), channel_id=1, source_target_pairs={{0,4},{4,8},{8,12},{12,0},{1,5},{5,9},{9,13},{13,1},{2,6},{6,10},{... | collective-permute-start | bytes 1277960 | tf_op jit(solution)/shard_map/ppermute | solution.py:25
  18.1 46.1 %collective-permute-start.12 = (bf16[256,3456]{1,0:T(8,128)(2,1)S(1)}, bf16[256,3456]{1,0:T(8,128)(2,1)S(1)}, u32[]{:S(2)}, u32[]{:S(2)}) collective-permute-start(bf16[256,3456]{1,0:T(8,128)(2,1)S(1)} %constant_dynamic-slice_fusion), channel_id=1, source_target_pairs={{0,16},{16,0},{1,17},{17,1},{2,18},{18,2},{3,19},{19,3},{4,20},{20... | collective-permute-start | bytes 5308424 | tf_op jit(solution)/shard_map/ppermute | solution.py:25
  27.8 18.0 %collective-permute-start.1 = (bf16[1792,128]{1,0:T(8,128)(2,1)}, bf16[1792,128]{1,0:T(8,128)(2,1)S(1)}, u32[]{:S(2)}, u32[]{:S(2)}) collective-permute-start(bf16[1792,128]{1,0:T(8,128)(2,1)} %collective-permute-done.refs_4_), channel_id=1, source_target_pairs={{0,4},{4,8},{8,12},{12,0},{1,5},{5,9},{9,13},{13,1},{2,6},{6,10},{... | collective-permute-start | bytes 1376264 | tf_op jit(solution)/shard_map/ppermute | solution.py:25
  27.8 18.0 %collective-permute-start.5 = (f32[384,256]{1,0:T(8,128)S(1)}, f32[384,256]{1,0:T(8,128)S(1)}, u32[]{:S(2)}, u32[]{:S(2)}) collective-permute-start(f32[384,256]{1,0:T(8,128)S(1)} %get-tuple-element.41), channel_id=1, source_target_pairs={{0,1},{1,0},{2,3},{3,2},{4,5},{5,4},{6,7},{7,6},{8,9},{9,8},{10,11... | collective-permute-start | bytes 1179656 | tf_op jit(solution)/shard_map/ppermute | solution.py:39
  27.8 18.0 %collective-permute-start.6 = (f32[384,256]{1,0:T(8,128)S(1)}, f32[384,256]{1,0:T(8,128)S(1)}, u32[]{:S(2)}, u32[]{:S(2)}) collective-permute-start(f32[384,256]{1,0:T(8,128)S(1)} %get-tuple-element.42), channel_id=1, source_target_pairs={{0,2},{1,3},{2,0},{3,1},{4,6},{5,7},{6,4},{7,5},{8,10},{9,11},{10,... | collective-permute-start | bytes 1179656 | tf_op jit(solution)/shard_map/ppermute | solution.py:39
  36.8 11.1 %collective-permute-start.7 = (f32[384,256]{1,0:T(8,128)S(1)}, f32[384,256]{1,0:T(8,128)S(1)}, u32[]{:S(2)}, u32[]{:S(2)}) collective-permute-start(f32[384,256]{1,0:T(8,128)S(1)} %get-tuple-element.43), channel_id=1, source_target_pairs={{0,3},{1,2},{2,1},{3,0},{4,7},{5,6},{6,5},{7,4},{8,11},{9,10},{10,... | collective-permute-start | bytes 1179656 | tf_op jit(solution)/shard_map/ppermute | solution.py:39
  48.1 6.7 %collective-permute-start.10 = (bf16[384,256]{1,0:T(8,128)(2,1)S(1)}, bf16[384,256]{1,0:T(8,128)(2,1)S(1)}, u32[]{:S(2)}, u32[]{:S(2)}) collective-permute-start(bf16[384,256]{1,0:T(8,128)(2,1)S(1)} %add_convert_fusion.refs_0_), channel_id=1, source_target_pairs={{0,3},{1,2},{2,1},{3,0},{4,7},{5,6},{6,5},{7,4},{8,11},{9,10},{10,... | collective-permute-start | bytes 589832 | tf_op jit(solution)/shard_map/ppermute | solution.py:39
  48.9 15.0 %collective-permute-start.11 = (bf16[1664,128]{1,0:T(8,128)(2,1)S(1)}, bf16[1664,128]{1,0:T(8,128)(2,1)S(1)}, u32[]{:S(2)}, u32[]{:S(2)}) collective-permute-start(bf16[1664,128]{1,0:T(8,128)(2,1)S(1)} %collective-permute-done.4.refs_5_), channel_id=1, source_target_pairs={{0,4},{4,8},{8,12},{12,0},{1,5},{5,9},{9,13},{13,1},{2,6},{6,10},{... | collective-permute-start | bytes 1277960 | tf_op jit(solution)/shard_map/ppermute | solution.py:25
  50.8 8.4 %collective-permute-start.8 = (bf16[384,256]{1,0:T(8,128)(2,1)S(1)}, bf16[384,256]{1,0:T(8,128)(2,1)S(1)}, u32[]{:S(2)}, u32[]{:S(2)}) collective-permute-start(bf16[384,256]{1,0:T(8,128)(2,1)S(1)} %add_convert_fusion.refs_0_), channel_id=1, source_target_pairs={{0,1},{1,0},{2,3},{3,2},{4,5},{5,4},{6,7},{7,6},{8,9},{9,8},{10,11... | collective-permute-start | bytes 589832 | tf_op jit(solution)/shard_map/ppermute | solution.py:39
  50.8 8.8 %collective-permute-start.9 = (bf16[384,256]{1,0:T(8,128)(2,1)S(1)}, bf16[384,256]{1,0:T(8,128)(2,1)S(1)}, u32[]{:S(2)}, u32[]{:S(2)}) collective-permute-start(bf16[384,256]{1,0:T(8,128)(2,1)S(1)} %add_convert_fusion.refs_0_), channel_id=1, source_target_pairs={{0,2},{1,3},{2,0},{3,1},{4,6},{5,7},{6,4},{7,5},{8,10},{9,11},{10,... | collective-permute-start | bytes 589832 | tf_op jit(solution)/shard_map/ppermute | solution.py:39
  54.8 18.4 %collective-permute-start.2 = (bf16[1792,128]{1,0:T(8,128)(2,1)S(1)}, bf16[1792,128]{1,0:T(8,128)(2,1)S(1)}, u32[]{:S(2)}, u32[]{:S(2)}) collective-permute-start(bf16[1792,128]{1,0:T(8,128)(2,1)S(1)} %collective-permute-done.1.refs_6_), channel_id=1, source_target_pairs={{0,4},{4,8},{8,12},{12,0},{1,5},{5,9},{9,13},{13,1},{2,6},{6,10},{... | collective-permute-start | bytes 1376264 | tf_op jit(solution)/shard_map/ppermute | solution.py:25
  64.6 8.5 %copy-start.3 = (s32[4]{0:T(128)S(1)}, s32[4]{0:T(128)}, u32[]{:S(2)}) copy-start(s32[4]{0:T(128)} %owner.3) | copy-start | bytes 52
  67.6 19.0 %copy-start.4 = (s32[2]{0:T(128)S(1)}, s32[2]{0:T(128)}, u32[]{:S(2)}) copy-start(s32[2]{0:T(128)} %counts.1) | copy-start | bytes 28
  67.6 18.9 %copy-start.5 = (s32[1,2]{1,0:T(1,128)S(1)}, s32[1,2]{1,0:T(1,128)}, u32[]{:S(2)}) copy-start(s32[1,2]{1,0:T(1,128)} %wanted.1) | copy-start | bytes 28
  74.3 2.0 %collective-permute-start.13 = (f32[2,512,128]{2,1,0:T(8,128)S(1)}, f32[2,512,128]{2,1,0:T(8,128)S(1)}, u32[]{:S(2)}, u32[]{:S(2)}) collective-permute-start(f32[2,512,128]{2,1,0:T(8,128)S(1)} %get-tuple-element.52), channel_id=1, source_target_pairs={{0,1},{1,0},{2,3},{3,2},{4,5},{5,4},{6,7},{7,6},{8,9},{9,8},{10,11... | collective-permute-start | bytes 1572872 | tf_op jit(solution)/shard_map/ppermute | solution.py:25
  77.0 5.6 %collective-permute-start.14 = (f32[256,128]{1,0:T(8,128)S(1)}, f32[256,128]{1,0:T(8,128)S(1)}, u32[]{:S(2)}, u32[]{:S(2)}) collective-permute-start(f32[256,128]{1,0:T(8,128)S(1)} %get-tuple-element.54), channel_id=1, source_target_pairs={{0,16},{2,18},{16,0},{18,2},{1,17},{3,19},{17,1},{19,3},{4,20},{6,... | collective-permute-start | bytes 393224 | tf_op jit(solution)/shard_map/ppermute | solution.py:309
  78.5 6.4 %collective-permute-start.15 = (f32[256,128]{1,0:T(8,128)S(1)}, f32[256,128]{1,0:T(8,128)S(1)}, u32[]{:S(2)}, u32[]{:S(2)}) collective-permute-start(f32[256,128]{1,0:T(8,128)S(1)} %get-tuple-element.55), channel_id=1, source_target_pairs={{0,2},{2,0},{16,18},{18,16},{1,3},{3,1},{17,19},{19,17},{4,6},{6,4... | collective-permute-start | bytes 393224 | tf_op jit(solution)/shard_map/ppermute | solution.py:309
  79.5 7.0 %collective-permute-start.16 = (f32[256,128]{1,0:T(8,128)S(1)}, f32[256,128]{1,0:T(8,128)S(1)}, u32[]{:S(2)}, u32[]{:S(2)}) collective-permute-start(f32[256,128]{1,0:T(8,128)S(1)} %get-tuple-element.56), channel_id=1, source_target_pairs={{0,18},{2,16},{16,2},{18,0},{1,19},{3,17},{17,3},{19,1},{4,22},{6,... | collective-permute-start | bytes 393224 | tf_op jit(solution)/shard_map/ppermute | solution.py:309
  87.4 6.4 %collective-permute-start.17 = (bf16[256,128]{1,0:T(8,128)(2,1)S(1)}, bf16[256,128]{1,0:T(8,128)(2,1)S(1)}, u32[]{:S(2)}, u32[]{:S(2)}) collective-permute-start(bf16[256,128]{1,0:T(8,128)(2,1)S(1)} %get-tuple-element.58), channel_id=1, source_target_pairs={{0,4},{4,8},{8,12},{12,0},{1,5},{5,9},{9,13},{13,1},{2,6},{6,10},{... | collective-permute-start | bytes 196616 | tf_op jit(solution)/shard_map/ppermute | solution.py:25
  87.5 7.5 %collective-permute-start.18 = (bf16[256,128]{1,0:T(8,128)(2,1)S(1)}, bf16[256,128]{1,0:T(8,128)(2,1)S(1)}, u32[]{:S(2)}, u32[]{:S(2)}) collective-permute-start(bf16[256,128]{1,0:T(8,128)(2,1)S(1)} %get-tuple-element.59), channel_id=1, source_target_pairs={{0,8},{4,12},{8,0},{12,4},{1,9},{5,13},{9,1},{13,5},{2,10},{6,14},... | collective-permute-start | bytes 196616 | tf_op jit(solution)/shard_map/ppermute | solution.py:25
  89.7 5.3 %collective-permute-start.19 = (bf16[256,128]{1,0:T(8,128)(2,1)S(1)}, bf16[256,128]{1,0:T(8,128)(2,1)S(1)}, u32[]{:S(2)}, u32[]{:S(2)}) collective-permute-start(bf16[256,128]{1,0:T(8,128)(2,1)S(1)} %get-tuple-element.60), channel_id=1, source_target_pairs={{0,12},{4,0},{8,4},{12,8},{1,13},{5,1},{9,5},{13,9},{2,14},{6,2},{... | collective-permute-start | bytes 196616 | tf_op jit(solution)/shard_map/ppermute | solution.py:25

commit v8 on v7

--- a/solution.py
+++ b/solution.py
@@ -49,13 +49,18 @@
         out[pl.ds(start, height)] = part[...]
 
 
-def gather_act(place, act):
+def gather_act(act, gate):
     cores, blocks = lax.axis_size("cores"), lax.axis_size("block")
-    parts = [act] + [to_neighbour(act, i // cores, i % cores) for i in range(1, blocks * cores)]
-    shape = (len(parts) * act.shape[0], act.shape[1])
+    sent = [after(act, gate) if i == 1 else act for i in range(blocks * cores)]
+    parts = [act] + [to_neighbour(sent[i], i // cores, i % cores) for i in range(1, len(sent))]
+    return parts
+
+
+def assemble(place, parts, blocks, cores):
+    shape = (len(parts) * parts[0].shape[0], parts[0].shape[1])
     return pl.pallas_call(
         functools.partial(assemble_kernel, blocks, cores),
-        out_shape=jax.ShapeDtypeStruct(shape, act.dtype),
+        out_shape=jax.ShapeDtypeStruct(shape, BF16),
         in_specs=[SMEM] + [VMEM] * len(parts),
         out_specs=VMEM,
         compiler_params=pltpu.CompilerParams(vmem_limit_bytes=VMEM_LIMIT),
@@ -282,14 +287,15 @@
                 to_neighbour(part, i // cores, i % cores) for i, part in enumerate(away_act, 1)
             ]
             rows = [[share(group)]] + others
-    act = after(act, first[2], second[2])
-    for part in away_act:
-        act = act + part
-    act_rot_t = gather_act(place, act.astype(BF16))
+    act = after(act, first[2])
+    for i, part in enumerate(away_act):
+        act = act + (after(part, first[-1]) if i == 0 else part)
+    act_parts = gather_act(act.astype(BF16), first[-1])
 
     pieces = [piece for pair in zip(first, second) for piece in pair]
     early = [early_products(part, pieces[:-2], shares) for part in rows]
     almost = [early_products(part, pieces[-2:-1], shares[:1]) for part in rows]
+    act_rot_t = assemble(after(place, *early, *almost), act_parts, blocks, cores)
     last, act_rot_t, *done = lax.optimization_barrier((pieces[-1], act_rot_t, *almost, *early))
     almost, early = done[: len(rows)], done[len(rows) :]
     last, *sends = pack(owner_slot, place, rows, last, cut, early, almost, blocks, cores)

time: 96 us -> 91.7 us (0.955)
  waiting for transfers between devices: 54.7 us -> 47.7 us
  Pallas kernels: 12.6 us -> 15.6 us
  starting transfers between devices: 20.1 us -> 18.6 us
  local copies, waits for them, and re-layouts: 7.25 us -> 8.43 us
    ppermute x6, waiting for transfers between devices: 6.02 us -> 0.02 us  [to_neighbour(): return lax.ppermute(value, ('block', 'cores'), pairs)]
    ppermute x11, starting transfers between devices: 13.6 us -> 11.1 us  [shift(): lax.ppermute(value, axis, [(i, (i + step) % size) for i in range(size)])]
    pallas_call x4, Pallas kernels: 6.7 us -> 8.7 us  [early_products(): pl.pallas_call(functools.partial(early_kernel, len(rows), shares), out_sh...]
    dynamic_slice x2, local copies, waits for them, and re-layouts: 0.24 us -> 1.43 us  [share(): lax.dynamic_slice_in_dim(flat_grads, index * part_features, part_features...]
    ppermute x11, waiting for transfers between devices: 42.6 us -> 41.6 us  [shift(): lax.ppermute(value, axis, [(i, (i + step) % size) for i in range(size)])]
  transfers between devices with their start and end apart: 20 -> 20, of which waited for: 15 -> 11; matrix products, arithmetic and copies ran while one was open for 2% -> 4% of each run, Pallas kernels for 10% -> 13%
where the time goes in v8:
time: 91.7 us; the launch traced here: 91.4 us
  waiting for transfers between devices  47.7 us (52%)
  starting transfers between devices  18.6 us (20%)
  Pallas kernels  15.6 us (17%)
  local copies, waits for them, and re-layouts  8.43 us (9%)
    ppermute x11, waiting for transfers between devices, shift(): lax.ppermute(value, axis, [(i, (i + step) % size) for i in range(size)])  41.6 us
    ppermute x11, starting transfers between devices, shift(): lax.ppermute(value, axis, [(i, (i + step) % size) for i in range(size)])  11.1 us
    pallas_call x4, Pallas kernels, early_products(): pl.pallas_call(functools.partial(early_kernel, len(rows), shares), out_sh...  8.7 us
    ppermute x3, waiting for transfers between devices, on_device(): parts[i] = lax.ppermute(parts[i], ('groups', 'block'), pairs)  6.13 us
    ppermute x6, starting transfers between devices, to_neighbour(): return lax.ppermute(value, ('block', 'cores'), pairs)  3.92 us
    dynamic_slice x2, local copies, waits for them, and re-layouts, on_device(): lax.dynamic_slice_in_dim(basis_store[0], group * part_features + start, s...  3.77 us
    ppermute x3, starting transfers between devices, on_device(): parts[i] = lax.ppermute(parts[i], ('groups', 'block'), pairs)  3.55 us
    unnamed x12, local copies, waits for them, and re-layouts  3.22 us
  transfers between devices with their start and end apart: 20, of which 11 were waited for; matrix products, arithmetic and copies ran while one was open for 4% of the time, Pallas kernels for 13%

profile of v8, /device:TPU:0, one launch (start us, length us, event | category | flops | bytes accessed | tf_op | source)
XLA Modules:
  0.0 91.4 jit_solution(15537927932938329189)
XLA Ops:
  0.0 0.0 copy-start
  0.0 1.9 %dynamic-slice_bitcast_fusion.1.refs_1_ = bf16[1664,128]{1,0:T(8,128)(2,1)} fusion(bf16[1,6912,128]{2,1,0:T(8,128)(2,1)} %param.11, s32[]{:T(128)S(6)} %select_n.18), kind=kLoop, calls=%fused_computation.1 | loop fusion | bytes 851972 | tf_op jit(solution)/shard_map/dynamic_slice | solution.py:266
  1.9 3.0 %collective-permute-start.3 = (bf16[1664,128]{1,0:T(8,128)(2,1)}, bf16[1664,128]{1,0:T(8,128)(2,1)}, u32[]{:S(2)}, u32[]{:S(2)}) collective-permute-start(bf16[1664,128]{1,0:T(8,128)(2,1)} %dynamic-slice_bitcast_fusion.1.refs_1_), channel_id=1, source_target_pairs={{0,4},{4,8},{8,12},{12,0},{1,5},{5,9},{9,13},{13,1},{2,6},{6,10},{... | collective-permute-start | bytes 1277960 | tf_op jit(solution)/shard_map/ppermute | solution.py:25
  5.0 1.8 %dynamic-slice_bitcast_fusion.refs_2_ = bf16[1792,128]{1,0:T(8,128)(2,1)} fusion(bf16[1,6912,128]{2,1,0:T(8,128)(2,1)} %param.11, s32[]{:T(128)S(6)} %select_n.17), kind=kLoop, calls=%fused_computation | loop fusion | bytes 917508 | tf_op jit(solution)/shard_map/dynamic_slice | solution.py:266
  6.8 1.6 %collective-permute-start = (bf16[1792,128]{1,0:T(8,128)(2,1)}, bf16[1792,128]{1,0:T(8,128)(2,1)}, u32[]{:S(2)}, u32[]{:S(2)}) collective-permute-start(bf16[1792,128]{1,0:T(8,128)(2,1)} %dynamic-slice_bitcast_fusion.refs_2_), channel_id=1, source_target_pairs={{0,4},{4,8},{8,12},{12,0},{1,5},{5,9},{9,13},{13,1},{2,6},{6,10},{... | collective-permute-start | bytes 1376264 | tf_op jit(solution)/shard_map/ppermute | solution.py:25
  8.4 0.0 copy-done
  8.4 1.3 %constant_dynamic-slice_fusion = bf16[256,3456]{1,0:T(8,128)(2,1)} fusion(bf16[256,6912]{1,0:T(8,128)(2,1)S(1)} %bitcast.9, s32[]{:T(128)S(6)} %select_n.20), kind=kLoop, calls=%fused_computation.4 | loop fusion | bytes 3538948 | tf_op jit(solution)/shard_map/dynamic_slice | solution.py:272
  9.7 1.5 %collective-permute-start.5 = (bf16[256,3456]{1,0:T(8,128)(2,1)}, bf16[256,3456]{1,0:T(8,128)(2,1)}, u32[]{:S(2)}, u32[]{:S(2)}) collective-permute-start(bf16[256,3456]{1,0:T(8,128)(2,1)} %constant_dynamic-slice_fusion), channel_id=1, source_target_pairs={{0,16},{16,0},{1,17},{17,1},{2,18},{18,2},{3,19},{19,3},{4,20},{20... | collective-permute-start | bytes 5308424 | tf_op jit(solution)/shard_map/ppermute | solution.py:25
  11.2 0.1 pad_add_fusion.place
  11.3 2.1 %copy-done.1 = bf16[1280,1536]{1,0:T(8,128)(2,1)S(1)} copy-done((bf16[1280,1536]{1,0:T(8,128)(2,1)S(1)}, bf16[1280,1536]{1,0:T(8,128)(2,1)}, u32[]{:S(2)}) %copy-start.1) | copy-done | bytes 3932184
  13.4 1.1 %copy-done.2 = bf16[2,128,1280]{2,1,0:T(8,128)(2,1)S(1)} copy-done((bf16[2,128,1280]{2,1,0:T(8,128)(2,1)S(1)}, bf16[2,128,1280]{2,1,0:T(8,128)(2,1)}, u32[]{:S(2)}) %copy-start.2) | copy-done | bytes 655384
  14.5 2.6 %shard_map.73 = (f32[384,256]{1,0:T(8,128)S(1)}, f32[384,256]{1,0:T(8,128)S(1)}, f32[384,256]{1,0:T(8,128)S(1)}, f32[384,256]{1,0:T(8,128)S(1)}) custom-call(s32[3]{0:T(128)S(1)} %pad_add_fusion.place, bf16[256,1280]{1,0:T(8,128)(2,1)S(1)} %bitcast.11, bf16[1280,1536]{1,0:T(8,128)(2,1)S(1)} %copy-done.1), custom_call_target="tpu_custom_call" | custom-call | tf_op jit(solution)/shard_map/pallas_call | solution.py:89
  17.1 0.8 collective-permute-done.3.refs_3_
  18.0 0.8 collective-permute-start.4
  18.8 0.0 collective-permute-start.7
  18.8 9.0 %collective-permute-done.refs_4_ = bf16[1792,128]{1,0:T(8,128)(2,1)} collective-permute-done((bf16[1792,128]{1,0:T(8,128)(2,1)}, bf16[1792,128]{1,0:T(8,128)(2,1)}, u32[]{:S(2)}, u32[]{:S(2)}) %collective-permute-start) | collective-permute-done | bytes 458784 | tf_op jit(solution)/shard_map/ppermute | solution.py:25
  27.8 0.0 collective-permute-start.1
  27.8 9.0 %collective-permute-done.4.refs_5_ = bf16[1664,128]{1,0:T(8,128)(2,1)S(1)} collective-permute-done((bf16[1664,128]{1,0:T(8,128)(2,1)}, bf16[1664,128]{1,0:T(8,128)(2,1)S(1)}, u32[]{:S(2)}, u32[]{:S(2)}) %collective-permute-start.4) | collective-permute-done | bytes 426016 | tf_op jit(solution)/shard_map/ppermute | solution.py:25
  36.8 0.0 collective-permute-start.6
  36.8 1.7 %collective-permute-start.8 = (f32[384,256]{1,0:T(8,128)S(1)}, f32[384,256]{1,0:T(8,128)S(1)}, u32[]{:S(2)}, u32[]{:S(2)}) collective-permute-start(f32[384,256]{1,0:T(8,128)S(1)} %get-tuple-element.48), channel_id=1, source_target_pairs={{0,2},{1,3},{2,0},{3,1},{4,6},{5,7},{6,4},{7,5},{8,10},{9,11},{10,... | collective-permute-start | bytes 1179656 | tf_op jit(solution)/shard_map/ppermute | solution.py:39
  38.5 0.0 collective-permute-done.7
  38.6 0.0 collective-permute-start.9
  38.6 8.1 %collective-permute-done.1.refs_6_ = bf16[1792,128]{1,0:T(8,128)(2,1)S(1)} collective-permute-done((bf16[1792,128]{1,0:T(8,128)(2,1)}, bf16[1792,128]{1,0:T(8,128)(2,1)S(1)}, u32[]{:S(2)}, u32[]{:S(2)}) %collective-permute-start.1) | collective-permute-done | bytes 458784 | tf_op jit(solution)/shard_map/ppermute | solution.py:25
  46.6 0.0 collective-permute-start.2
  46.7 9.1 %collective-permute-done.6.refs_1_ = bf16[1664,128]{1,0:T(8,128)(2,1)S(1)} collective-permute-done((bf16[1664,128]{1,0:T(8,128)(2,1)S(1)}, bf16[1664,128]{1,0:T(8,128)(2,1)S(1)}, u32[]{:S(2)}, u32[]{:S(2)}) %collective-permute-start.6) | collective-permute-done | bytes 426016 | tf_op jit(solution)/shard_map/ppermute | solution.py:25
  55.8 0.0 collective-permute-done.8
  55.8 0.0 collective-permute-done.9
  55.8 0.1 add_convert_fusion.refs_0_
  55.9 1.8 %collective-permute-start.11 = (bf16[384,256]{1,0:T(8,128)(2,1)S(1)}, bf16[384,256]{1,0:T(8,128)(2,1)S(1)}, u32[]{:S(2)}, u32[]{:S(2)}) collective-permute-start(bf16[384,256]{1,0:T(8,128)(2,1)S(1)} %add_convert_fusion.refs_0_), channel_id=1, source_target_pairs={{0,2},{1,3},{2,0},{3,1},{4,6},{5,7},{6,4},{7,5},{8,10},{9,11},{10,... | collective-permute-start | bytes 589832 | tf_op jit(solution)/shard_map/ppermute | solution.py:39
  57.7 0.0 collective-permute-start.12
  57.7 0.4 collective-permute-start.10
  58.1 0.1 constant_dynamic-slice_fusion.1.refs_0_
  58.2 3.0 %shard_map.74.refs_2_.refs_0_ = f32[3,256,128]{2,1,0:T(8,128)S(1)} custom-call(bf16[256,3456]{1,0:T(8,128)(2,1)S(1)} %constant_dynamic-slice_fusion.1.refs_0_, bf16[1664,128]{1,0:T(8,128)(2,1)} %dynamic-slice_bitcast_fusion.1.refs_1_, bf16[1792,128]{1,0:T(8,128)(2,1)} %dynamic-slice_bitcast_fusion.refs_2_, bf16[1664,128]{1,0:T(8,128)(2,1)} %collective-permute-done.3.refs_3_, ...), custom_call_target="tpu_custom_call" | custom-call | flops 679477248 | bytes 5308416 | tf_op jit(solution)/shard_map/pallas_call | solution.py:130
  61.2 0.4 shard_map.76.refs_4_
  61.6 0.0 collective-permute-done.5.refs_0_.refs_1_
  61.6 1.9 %shard_map.77.refs_5_ = f32[1,256,128]{2,1,0:T(8,128)S(1)} custom-call(bf16[256,3456]{1,0:T(8,128)(2,1)} %collective-permute-done.5.refs_0_.refs_1_, bf16[1664,128]{1,0:T(8,128)(2,1)S(1)} %collective-permute-done.6.refs_1_), custom_call_target="tpu_custom_call" | custom-call | flops 109051904 | bytes 851968 | tf_op jit(solution)/shard_map/pallas_call | solution.py:130
  63.5 0.0 copy-start.3
  63.5 3.5 %shard_map.75.refs_3_.refs_1_ = f32[3,256,128]{2,1,0:T(8,128)S(1)} custom-call(bf16[256,3456]{1,0:T(8,128)(2,1)} %collective-permute-done.5.refs_0_.refs_1_, bf16[1664,128]{1,0:T(8,128)(2,1)} %dynamic-slice_bitcast_fusion.1.refs_1_, bf16[1792,128]{1,0:T(8,128)(2,1)} %dynamic-slice_bitcast_fusion.refs_2_, bf16[1664,128]{1,0:T(8,128)(2,1)} %collective-permute-done.3.refs_3_, ...), custom_call_target="tpu_custom_call" | custom-call | flops 679477248 | bytes 5308416 | tf_op jit(solution)/shard_map/pallas_call | solution.py:130
  67.0 0.0 collective-permute-done.10.refs_1_
  67.0 0.0 collective-permute-done.11.refs_2_
  67.0 0.0 collective-permute-done.12.refs_3_
  67.0 0.6 shard_map.78.act
  67.6 0.0 copy-start.4
  67.6 0.0 copy-start.5
  67.6 0.0 collective-permute-done.2.held
  67.7 2.1 %shard_map.79 = (f32[512,128]{1,0:T(8,128)S(1)}, f32[2,512,128]{2,1,0:T(8,128)S(1)}) custom-call(s32[4]{0:T(128)S(1)} %copy-done.3, s32[3]{0:T(128)S(1)} %pad_add_fusion.place, bf16[1792,128]{1,0:T(8,128)(2,1)S(1)} %collective-permute-done.2.held, bf16[256,3456]{1,0:T(8,128)(2,1)S(1)} %constant_dynamic-slice_fusion.1.refs_0_, ...), custom_call_target="tpu_custom_call" | custom-call | tf_op jit(solution)/shard_map/pallas_call | solution.py:174
  69.8 0.2 collective-permute-start.13
  70.0 1.8 %collective-permute-done.13.refs_2_ = f32[2,512,128]{2,1,0:T(8,128)S(1)} collective-permute-done((f32[2,512,128]{2,1,0:T(8,128)S(1)}, f32[2,512,128]{2,1,0:T(8,128)S(1)}, u32[]{:S(2)}, u32[]{:S(2)}) %collective-permute-start.13) | collective-permute-done | bytes 524320 | tf_op jit(solution)/shard_map/ppermute | solution.py:25
  71.8 0.6 shard_map.80
  72.4 1.8 %collective-permute-start.14 = (f32[256,128]{1,0:T(8,128)S(1)}, f32[256,128]{1,0:T(8,128)S(1)}, u32[]{:S(2)}, u32[]{:S(2)}) collective-permute-start(f32[256,128]{1,0:T(8,128)S(1)} %get-tuple-element.60), channel_id=1, source_target_pairs={{0,16},{2,18},{16,0},{18,2},{1,17},{3,19},{17,1},{19,3},{4,20},{6,... | collective-permute-start | bytes 393224 | tf_op jit(solution)/shard_map/ppermute | solution.py:315
  74.2 1.5 %collective-permute-start.15 = (f32[256,128]{1,0:T(8,128)S(1)}, f32[256,128]{1,0:T(8,128)S(1)}, u32[]{:S(2)}, u32[]{:S(2)}) collective-permute-start(f32[256,128]{1,0:T(8,128)S(1)} %get-tuple-element.61), channel_id=1, source_target_pairs={{0,2},{2,0},{16,18},{18,16},{1,3},{3,1},{17,19},{19,17},{4,6},{6,4... | collective-permute-start | bytes 393224 | tf_op jit(solution)/shard_map/ppermute | solution.py:315
  75.7 0.2 collective-permute-start.16
  76.0 2.1 %collective-permute-done.14.refs_1_ = f32[256,128]{1,0:T(8,128)S(1)} collective-permute-done((f32[256,128]{1,0:T(8,128)S(1)}, f32[256,128]{1,0:T(8,128)S(1)}, u32[]{:S(2)}, u32[]{:S(2)}) %collective-permute-start.14) | collective-permute-done | bytes 131104 | tf_op jit(solution)/shard_map/ppermute | solution.py:315
  78.0 2.6 %collective-permute-done.15.refs_2_ = f32[256,128]{1,0:T(8,128)S(1)} collective-permute-done((f32[256,128]{1,0:T(8,128)S(1)}, f32[256,128]{1,0:T(8,128)S(1)}, u32[]{:S(2)}, u32[]{:S(2)}) %collective-permute-start.15) | collective-permute-done | bytes 131104 | tf_op jit(solution)/shard_map/ppermute | solution.py:315
  80.6 1.5 %collective-permute-done.16.refs_3_ = f32[256,128]{1,0:T(8,128)S(1)} collective-permute-done((f32[256,128]{1,0:T(8,128)S(1)}, f32[256,128]{1,0:T(8,128)S(1)}, u32[]{:S(2)}, u32[]{:S(2)}) %collective-permute-start.16) | collective-permute-done | bytes 131104 | tf_op jit(solution)/shard_map/ppermute | solution.py:315
  82.1 0.0 copy-done.5
  82.1 0.9 shard_map.81
  83.0 0.1 collective-permute-start.17
  83.0 2.7 %collective-permute-start.18 = (bf16[256,128]{1,0:T(8,128)(2,1)S(1)}, bf16[256,128]{1,0:T(8,128)(2,1)S(1)}, u32[]{:S(2)}, u32[]{:S(2)}) collective-permute-start(bf16[256,128]{1,0:T(8,128)(2,1)S(1)} %get-tuple-element.65), channel_id=1, source_target_pairs={{0,8},{4,12},{8,0},{12,4},{1,9},{5,13},{9,1},{13,5},{2,10},{6,14},... | collective-permute-start | bytes 196616 | tf_op jit(solution)/shard_map/ppermute | solution.py:25
  85.7 1.2 %collective-permute-start.19 = (bf16[256,128]{1,0:T(8,128)(2,1)S(1)}, bf16[256,128]{1,0:T(8,128)(2,1)S(1)}, u32[]{:S(2)}, u32[]{:S(2)}) collective-permute-start(bf16[256,128]{1,0:T(8,128)(2,1)S(1)} %get-tuple-element.66), channel_id=1, source_target_pairs={{0,12},{4,0},{8,4},{12,8},{1,13},{5,1},{9,5},{13,9},{2,14},{6,2},{... | collective-permute-start | bytes 196616 | tf_op jit(solution)/shard_map/ppermute | solution.py:25
  86.9 2.6 %collective-permute-done.17 = bf16[256,128]{1,0:T(8,128)(2,1)S(1)} collective-permute-done((bf16[256,128]{1,0:T(8,128)(2,1)S(1)}, bf16[256,128]{1,0:T(8,128)(2,1)S(1)}, u32[]{:S(2)}, u32[]{:S(2)}) %collective-permute-start.17) | collective-permute-done | bytes 65568 | tf_op jit(solution)/shard_map/ppermute | solution.py:25
  89.5 1.2 %collective-permute-done.18 = bf16[256,128]{1,0:T(8,128)(2,1)S(1)} collective-permute-done((bf16[256,128]{1,0:T(8,128)(2,1)S(1)}, bf16[256,128]{1,0:T(8,128)(2,1)S(1)}, u32[]{:S(2)}, u32[]{:S(2)}) %collective-permute-start.18) | collective-permute-done | bytes 65568 | tf_op jit(solution)/shard_map/ppermute | solution.py:25
  90.7 0.0 collective-permute-done.19
  90.7 0.7 add_multiply_fusion
  (4 shorter events, 0.0 us)
Async XLA Ops:
  0.0 8.4 %copy-start = (bf16[2,128,6912]{2,1,0:T(8,128)(2,1)S(1)}, bf16[2,128,6912]{2,1,0:T(8,128)(2,1)}, u32[]{:S(2)}) copy-start(bf16[2,128,6912]{2,1,0:T(8,128)(2,1)} %param.8) | copy-start | bytes 10616836
  1.9 16.0 %collective-permute-start.3 = (bf16[1664,128]{1,0:T(8,128)(2,1)}, bf16[1664,128]{1,0:T(8,128)(2,1)}, u32[]{:S(2)}, u32[]{:S(2)}) collective-permute-start(bf16[1664,128]{1,0:T(8,128)(2,1)} %dynamic-slice_bitcast_fusion.1.refs_1_), channel_id=1, source_target_pairs={{0,4},{4,8},{8,12},{12,0},{1,5},{5,9},{9,13},{13,1},{2,6},{6,10},{... | collective-permute-start | bytes 1277960 | tf_op jit(solution)/shard_map/ppermute | solution.py:25
  6.8 21.0 %collective-permute-start = (bf16[1792,128]{1,0:T(8,128)(2,1)}, bf16[1792,128]{1,0:T(8,128)(2,1)}, u32[]{:S(2)}, u32[]{:S(2)}) collective-permute-start(bf16[1792,128]{1,0:T(8,128)(2,1)} %dynamic-slice_bitcast_fusion.refs_2_), channel_id=1, source_target_pairs={{0,4},{4,8},{8,12},{12,0},{1,5},{5,9},{9,13},{13,1},{2,6},{6,10},{... | collective-permute-start | bytes 1376264 | tf_op jit(solution)/shard_map/ppermute | solution.py:25
  9.7 51.9 %collective-permute-start.5 = (bf16[256,3456]{1,0:T(8,128)(2,1)}, bf16[256,3456]{1,0:T(8,128)(2,1)}, u32[]{:S(2)}, u32[]{:S(2)}) collective-permute-start(bf16[256,3456]{1,0:T(8,128)(2,1)} %constant_dynamic-slice_fusion), channel_id=1, source_target_pairs={{0,16},{16,0},{1,17},{17,1},{2,18},{18,2},{3,19},{19,3},{4,20},{20... | collective-permute-start | bytes 5308424 | tf_op jit(solution)/shard_map/ppermute | solution.py:25
  11.3 2.1 %copy-start.1 = (bf16[1280,1536]{1,0:T(8,128)(2,1)S(1)}, bf16[1280,1536]{1,0:T(8,128)(2,1)}, u32[]{:S(2)}) copy-start(bf16[1280,1536]{1,0:T(8,128)(2,1)} %basis.1) | copy-start | bytes 11796484
  13.4 1.1 %copy-start.2 = (bf16[2,128,1280]{2,1,0:T(8,128)(2,1)S(1)}, bf16[2,128,1280]{2,1,0:T(8,128)(2,1)}, u32[]{:S(2)}) copy-start(bf16[2,128,1280]{2,1,0:T(8,128)(2,1)} %param.7) | copy-start | bytes 1966084
  18.0 18.9 %collective-permute-start.4 = (bf16[1664,128]{1,0:T(8,128)(2,1)}, bf16[1664,128]{1,0:T(8,128)(2,1)S(1)}, u32[]{:S(2)}, u32[]{:S(2)}) collective-permute-start(bf16[1664,128]{1,0:T(8,128)(2,1)} %collective-permute-done.3.refs_3_), channel_id=1, source_target_pairs={{0,4},{4,8},{8,12},{12,0},{1,5},{5,9},{9,13},{13,1},{2,6},{6,10},{... | collective-permute-start | bytes 1277960 | tf_op jit(solution)/shard_map/ppermute | solution.py:25
  18.8 19.8 %collective-permute-start.7 = (f32[384,256]{1,0:T(8,128)S(1)}, f32[384,256]{1,0:T(8,128)S(1)}, u32[]{:S(2)}, u32[]{:S(2)}) collective-permute-start(f32[384,256]{1,0:T(8,128)S(1)} %get-tuple-element.46), channel_id=1, source_target_pairs={{0,1},{1,0},{2,3},{3,2},{4,5},{5,4},{6,7},{7,6},{8,9},{9,8},{10,11... | collective-permute-start | bytes 1179656 | tf_op jit(solution)/shard_map/ppermute | solution.py:39
  27.8 18.9 %collective-permute-start.1 = (bf16[1792,128]{1,0:T(8,128)(2,1)}, bf16[1792,128]{1,0:T(8,128)(2,1)S(1)}, u32[]{:S(2)}, u32[]{:S(2)}) collective-permute-start(bf16[1792,128]{1,0:T(8,128)(2,1)} %collective-permute-done.refs_4_), channel_id=1, source_target_pairs={{0,4},{4,8},{8,12},{12,0},{1,5},{5,9},{9,13},{13,1},{2,6},{6,10},{... | collective-permute-start | bytes 1376264 | tf_op jit(solution)/shard_map/ppermute | solution.py:25
  36.8 19.0 %collective-permute-start.6 = (bf16[1664,128]{1,0:T(8,128)(2,1)S(1)}, bf16[1664,128]{1,0:T(8,128)(2,1)S(1)}, u32[]{:S(2)}, u32[]{:S(2)}) collective-permute-start(bf16[1664,128]{1,0:T(8,128)(2,1)S(1)} %collective-permute-done.4.refs_5_), channel_id=1, source_target_pairs={{0,4},{4,8},{8,12},{12,0},{1,5},{5,9},{9,13},{13,1},{2,6},{6,10},{... | collective-permute-start | bytes 1277960 | tf_op jit(solution)/shard_map/ppermute | solution.py:25
  36.8 18.9 %collective-permute-start.8 = (f32[384,256]{1,0:T(8,128)S(1)}, f32[384,256]{1,0:T(8,128)S(1)}, u32[]{:S(2)}, u32[]{:S(2)}) collective-permute-start(f32[384,256]{1,0:T(8,128)S(1)} %get-tuple-element.48), channel_id=1, source_target_pairs={{0,2},{1,3},{2,0},{3,1},{4,6},{5,7},{6,4},{7,5},{8,10},{9,11},{10,... | collective-permute-start | bytes 1179656 | tf_op jit(solution)/shard_map/ppermute | solution.py:39
  38.6 17.2 %collective-permute-start.9 = (f32[384,256]{1,0:T(8,128)S(1)}, f32[384,256]{1,0:T(8,128)S(1)}, u32[]{:S(2)}, u32[]{:S(2)}) collective-permute-start(f32[384,256]{1,0:T(8,128)S(1)} %get-tuple-element.49), channel_id=1, source_target_pairs={{0,3},{1,2},{2,1},{3,0},{4,7},{5,6},{6,5},{7,4},{8,11},{9,10},{10,... | collective-permute-start | bytes 1179656 | tf_op jit(solution)/shard_map/ppermute | solution.py:39
  46.6 21.0 %collective-permute-start.2 = (bf16[1792,128]{1,0:T(8,128)(2,1)S(1)}, bf16[1792,128]{1,0:T(8,128)(2,1)S(1)}, u32[]{:S(2)}, u32[]{:S(2)}) collective-permute-start(bf16[1792,128]{1,0:T(8,128)(2,1)S(1)} %collective-permute-done.1.refs_6_), channel_id=1, source_target_pairs={{0,4},{4,8},{8,12},{12,0},{1,5},{5,9},{9,13},{13,1},{2,6},{6,10},{... | collective-permute-start | bytes 1376264 | tf_op jit(solution)/shard_map/ppermute | solution.py:25
  55.9 11.1 %collective-permute-start.11 = (bf16[384,256]{1,0:T(8,128)(2,1)S(1)}, bf16[384,256]{1,0:T(8,128)(2,1)S(1)}, u32[]{:S(2)}, u32[]{:S(2)}) collective-permute-start(bf16[384,256]{1,0:T(8,128)(2,1)S(1)} %add_convert_fusion.refs_0_), channel_id=1, source_target_pairs={{0,2},{1,3},{2,0},{3,1},{4,6},{5,7},{6,4},{7,5},{8,10},{9,11},{10,... | collective-permute-start | bytes 589832 | tf_op jit(solution)/shard_map/ppermute | solution.py:39
  57.7 9.3 %collective-permute-start.12 = (bf16[384,256]{1,0:T(8,128)(2,1)S(1)}, bf16[384,256]{1,0:T(8,128)(2,1)S(1)}, u32[]{:S(2)}, u32[]{:S(2)}) collective-permute-start(bf16[384,256]{1,0:T(8,128)(2,1)S(1)} %add_convert_fusion.refs_0_), channel_id=1, source_target_pairs={{0,3},{1,2},{2,1},{3,0},{4,7},{5,6},{6,5},{7,4},{8,11},{9,10},{10,... | collective-permute-start | bytes 589832 | tf_op jit(solution)/shard_map/ppermute | solution.py:39
  57.7 9.3 %collective-permute-start.10 = (bf16[384,256]{1,0:T(8,128)(2,1)S(1)}, bf16[384,256]{1,0:T(8,128)(2,1)S(1)}, u32[]{:S(2)}, u32[]{:S(2)}) collective-permute-start(bf16[384,256]{1,0:T(8,128)(2,1)S(1)} %add_convert_fusion.refs_0_), channel_id=1, source_target_pairs={{0,1},{1,0},{2,3},{3,2},{4,5},{5,4},{6,7},{7,6},{8,9},{9,8},{10,11... | collective-permute-start | bytes 589832 | tf_op jit(solution)/shard_map/ppermute | solution.py:39
  63.5 4.2 %copy-start.3 = (s32[4]{0:T(128)S(1)}, s32[4]{0:T(128)}, u32[]{:S(2)}) copy-start(s32[4]{0:T(128)} %owner.3) | copy-start | bytes 52
  67.6 14.5 %copy-start.4 = (s32[2]{0:T(128)S(1)}, s32[2]{0:T(128)}, u32[]{:S(2)}) copy-start(s32[2]{0:T(128)} %counts.1) | copy-start | bytes 28
  67.6 14.5 %copy-start.5 = (s32[1,2]{1,0:T(1,128)S(1)}, s32[1,2]{1,0:T(1,128)}, u32[]{:S(2)}) copy-start(s32[1,2]{1,0:T(1,128)} %wanted.1) | copy-start | bytes 28
  69.8 2.0 %collective-permute-start.13 = (f32[2,512,128]{2,1,0:T(8,128)S(1)}, f32[2,512,128]{2,1,0:T(8,128)S(1)}, u32[]{:S(2)}, u32[]{:S(2)}) collective-permute-start(f32[2,512,128]{2,1,0:T(8,128)S(1)} %get-tuple-element.58), channel_id=1, source_target_pairs={{0,1},{1,0},{2,3},{3,2},{4,5},{5,4},{6,7},{7,6},{8,9},{9,8},{10,11... | collective-permute-start | bytes 1572872 | tf_op jit(solution)/shard_map/ppermute | solution.py:25
  72.4 5.6 %collective-permute-start.14 = (f32[256,128]{1,0:T(8,128)S(1)}, f32[256,128]{1,0:T(8,128)S(1)}, u32[]{:S(2)}, u32[]{:S(2)}) collective-permute-start(f32[256,128]{1,0:T(8,128)S(1)} %get-tuple-element.60), channel_id=1, source_target_pairs={{0,16},{2,18},{16,0},{18,2},{1,17},{3,19},{17,1},{19,3},{4,20},{6,... | collective-permute-start | bytes 393224 | tf_op jit(solution)/shard_map/ppermute | solution.py:315
  74.2 6.4 %collective-permute-start.15 = (f32[256,128]{1,0:T(8,128)S(1)}, f32[256,128]{1,0:T(8,128)S(1)}, u32[]{:S(2)}, u32[]{:S(2)}) collective-permute-start(f32[256,128]{1,0:T(8,128)S(1)} %get-tuple-element.61), channel_id=1, source_target_pairs={{0,2},{2,0},{16,18},{18,16},{1,3},{3,1},{17,19},{19,17},{4,6},{6,4... | collective-permute-start | bytes 393224 | tf_op jit(solution)/shard_map/ppermute | solution.py:315
  75.7 6.4 %collective-permute-start.16 = (f32[256,128]{1,0:T(8,128)S(1)}, f32[256,128]{1,0:T(8,128)S(1)}, u32[]{:S(2)}, u32[]{:S(2)}) collective-permute-start(f32[256,128]{1,0:T(8,128)S(1)} %get-tuple-element.62), channel_id=1, source_target_pairs={{0,18},{2,16},{16,2},{18,0},{1,19},{3,17},{17,3},{19,1},{4,22},{6,... | collective-permute-start | bytes 393224 | tf_op jit(solution)/shard_map/ppermute | solution.py:315
  83.0 6.5 %collective-permute-start.17 = (bf16[256,128]{1,0:T(8,128)(2,1)S(1)}, bf16[256,128]{1,0:T(8,128)(2,1)S(1)}, u32[]{:S(2)}, u32[]{:S(2)}) collective-permute-start(bf16[256,128]{1,0:T(8,128)(2,1)S(1)} %get-tuple-element.64), channel_id=1, source_target_pairs={{0,4},{4,8},{8,12},{12,0},{1,5},{5,9},{9,13},{13,1},{2,6},{6,10},{... | collective-permute-start | bytes 196616 | tf_op jit(solution)/shard_map/ppermute | solution.py:25
  83.0 7.7 %collective-permute-start.18 = (bf16[256,128]{1,0:T(8,128)(2,1)S(1)}, bf16[256,128]{1,0:T(8,128)(2,1)S(1)}, u32[]{:S(2)}, u32[]{:S(2)}) collective-permute-start(bf16[256,128]{1,0:T(8,128)(2,1)S(1)} %get-tuple-element.65), channel_id=1, source_target_pairs={{0,8},{4,12},{8,0},{12,4},{1,9},{5,13},{9,1},{13,5},{2,10},{6,14},... | collective-permute-start | bytes 196616 | tf_op jit(solution)/shard_map/ppermute | solution.py:25
  85.7 5.0 %collective-permute-start.19 = (bf16[256,128]{1,0:T(8,128)(2,1)S(1)}, bf16[256,128]{1,0:T(8,128)(2,1)S(1)}, u32[]{:S(2)}, u32[]{:S(2)}) collective-permute-start(bf16[256,128]{1,0:T(8,128)(2,1)S(1)} %get-tuple-element.66), channel_id=1, source_target_pairs={{0,12},{4,0},{8,4},{12,8},{1,13},{5,1},{9,5},{13,9},{2,14},{6,2},{... | collective-permute-start | bytes 196616 | tf_op jit(solution)/shard_map/ppermute | solution.py:25

commit v9 on v8

--- a/solution.py
+++ b/solution.py
@@ -51,7 +51,7 @@
 
 def gather_act(act, gate):
     cores, blocks = lax.axis_size("cores"), lax.axis_size("block")
-    sent = [after(act, gate) if i == 1 else act for i in range(blocks * cores)]
+    sent = [after(act, *gate) if i == 1 else act for i in range(blocks * cores)]
     parts = [act] + [to_neighbour(sent[i], i // cores, i % cores) for i in range(1, len(sent))]
     return parts
 
@@ -139,12 +139,13 @@
     )(*rows, *pieces)
 
 
-def total_of(position, early, last, group):
+def total_of(position, early, rest, last, group):
     positions = early[0].shape[0]
     height = early[0].shape[1]
     at_last = last[pl.ds(group * height, height)]
     before = early[group][jnp.minimum(position, positions - 1)]
-    return jnp.where(position == positions, at_last, before)
+    late = jnp.where(position == positions, rest[group][0], at_last)
+    return jnp.where(position < positions, before, late)
 
 
 def pack_kernel(dp, cores, parts, start, owner, place, held, *refs):
@@ -152,59 +153,60 @@
     refs = list(refs)
     rows = [[refs.pop(0) for _ in range(cuts)] for cuts in parts]
     early = [refs.pop(0) for _ in parts]
-    almost = [refs.pop(0) for _ in parts]
+    rest = [refs.pop(0) for _ in parts]
     last, sends = refs[0], refs[1:]
     height = early[0].shape[1]
     for g in range(len(parts)):
-        last[g * height : (g + 1) * height] = almost[g][0] + product(rows[g], held, start)
+        last[g * height : (g + 1) * height] = rest[g][1] + product(rows[g], held, start)
     for step in range(1, cores):
         for block in range(sends[0].shape[0]):
             piece = block * cores + lax.rem(core + step, cores)
             position = lax.rem(row - owner[piece] + dp, dp)
             for g in range(len(parts)):
                 sends[step - 1][block, g * height : (g + 1) * height] = total_of(
-                    position, early, last, g
+                    position, early, rest, last, g
                 )
 
 
-def pack(owner_slot, place, rows, held, start, early, almost, blocks, cores):
+def pack(owner_slot, place, rows, held, start, early, rest, blocks, cores):
     positions, height, width = early[0].shape
     shape = (len(rows) * height, width)
     parts = tuple(len(part) for part in rows)
     return pl.pallas_call(
-        functools.partial(pack_kernel, positions + 1, cores, parts, start),
+        functools.partial(pack_kernel, positions + 2, cores, parts, start),
         out_shape=(jax.ShapeDtypeStruct(shape, F32),)
         + (jax.ShapeDtypeStruct((blocks,) + shape, F32),) * (cores - 1),
         in_specs=[SMEM, SMEM] + [VMEM] * (1 + sum(parts) + 2 * len(rows)),
         out_specs=(VMEM,) * cores,
         compiler_params=pltpu.CompilerParams(vmem_limit_bytes=VMEM_LIMIT),
-    )(owner_slot, place, held, *[cut for part in rows for cut in part], *early, *almost)
+    )(owner_slot, place, held, *[cut for part in rows for cut in part], *early, *rest)
 
 
 def join_kernel(dp, cores, groups, blocks, owner, place, last, *refs):
     row, core, me = place[0], place[1], place[2]
-    early, came, outs = refs[:groups], refs[groups : groups + cores - 1], refs[groups + cores - 1 :]
+    early, rest, refs = refs[:groups], refs[groups : 2 * groups], refs[2 * groups :]
+    came, outs = refs[: cores - 1], refs[cores - 1 :]
     height = early[0].shape[1]
     for far in range(blocks):
         block = lax.rem(me + far, blocks)
         position = lax.rem(row - owner[block * cores + core] + dp, dp)
         for g in range(groups):
-            total = total_of(position, early, last, g)
+            total = total_of(position, early, rest, last, g)
             for other in came:
                 total = total + other[block, g * height : (g + 1) * height]
             outs[far * groups + g][...] = total
 
 
-def join(owner_slot, place, last, early, came, blocks, cores):
+def join(owner_slot, place, last, early, rest, came, blocks, cores):
     positions, height, width = early[0].shape
     groups = len(early)
     return pl.pallas_call(
-        functools.partial(join_kernel, positions + 1, cores, groups, blocks),
+        functools.partial(join_kernel, positions + 2, cores, groups, blocks),
         out_shape=(jax.ShapeDtypeStruct((height, width), F32),) * (blocks * groups),
-        in_specs=[SMEM, SMEM] + [VMEM] * (1 + groups + len(came)),
+        in_specs=[SMEM, SMEM] + [VMEM] * (1 + 2 * groups + len(came)),
         out_specs=(VMEM,) * (blocks * groups),
         compiler_params=pltpu.CompilerParams(vmem_limit_bytes=VMEM_LIMIT),
-    )(owner_slot, place, last, *early, *came)
+    )(owner_slot, place, last, *early, *rest, *came)
 
 
 def square_kernel(dp, terms, counts, wanted, place, act, *refs):
@@ -290,17 +292,16 @@
     act = after(act, first[2])
     for i, part in enumerate(away_act):
         act = act + (after(part, first[-1]) if i == 0 else part)
-    act_parts = gather_act(act.astype(BF16), first[-1])
-
     pieces = [piece for pair in zip(first, second) for piece in pair]
-    early = [early_products(part, pieces[:-2], shares) for part in rows]
-    almost = [early_products(part, pieces[-2:-1], shares[:1]) for part in rows]
-    act_rot_t = assemble(after(place, *early, *almost), act_parts, blocks, cores)
-    last, act_rot_t, *done = lax.optimization_barrier((pieces[-1], act_rot_t, *almost, *early))
-    almost, early = done[: len(rows)], done[len(rows) :]
-    last, *sends = pack(owner_slot, place, rows, last, cut, early, almost, blocks, cores)
+    early = [early_products(part, pieces[:-4], shares) for part in rows]
+    act_parts = gather_act(act.astype(BF16), (first[-1], early[0]))
+    rest = [early_products(part, pieces[-4:-1], shares) for part in rows]
+    act_rot_t = assemble(after(place, *early, *rest), act_parts, blocks, cores)
+    last, act_rot_t, *done = lax.optimization_barrier((pieces[-1], act_rot_t, *early, *rest))
+    early, rest = done[: len(rows)], done[len(rows) :]
+    last, *sends = pack(owner_slot, place, rows, last, cut, early, rest, blocks, cores)
     came = [shift(send, "cores", step) for step, send in enumerate(sends, 1)]
-    parts = join(owner_slot, place, last, early, came, blocks, cores)
+    parts = join(owner_slot, place, last, early, rest, came, blocks, cores)
 
     parts = list(parts)
     for far in range(blocks):

time: 91.7 us -> 92.1 us (level)
    ppermute x6, waiting for transfers between devices: 0.02 us -> 2.98 us  [to_neighbour(): return lax.ppermute(value, ('block', 'cores'), pairs)]
    ppermute x11, waiting for transfers between devices: 41.6 us -> 39.2 us  [shift(): lax.ppermute(value, axis, [(i, (i + step) % size) for i in range(size)])]
  transfers between devices with their start and end apart: 20 -> 20, of which waited for: 11 -> 12; matrix products, arithmetic and copies ran while one was open for 4% -> 4% of each run, Pallas kernels for 13% -> 13%
where the time goes in v9:
time: 92.1 us; the launch traced here: 91.8 us
  waiting for transfers between devices  48.4 us (53%)
  starting transfers between devices  18.3 us (20%)
  Pallas kernels  15.6 us (17%)
  local copies, waits for them, and re-layouts  8.43 us (9%)
    ppermute x11, waiting for transfers between devices, shift(): lax.ppermute(value, axis, [(i, (i + step) % size) for i in range(size)])  39.2 us
    ppermute x11, starting transfers between devices, shift(): lax.ppermute(value, axis, [(i, (i + step) % size) for i in range(size)])  11.3 us
    pallas_call x4, Pallas kernels, early_products(): pl.pallas_call(functools.partial(early_kernel, len(rows), shares), out_sh...  8.68 us
    ppermute x3, waiting for transfers between devices, on_device(): parts[i] = lax.ppermute(parts[i], ('groups', 'block'), pairs)  6.28 us
    dynamic_slice x2, local copies, waits for them, and re-layouts, on_device(): lax.dynamic_slice_in_dim(basis_store[0], group * part_features + start, s...  3.77 us
    ppermute x3, starting transfers between devices, on_device(): parts[i] = lax.ppermute(parts[i], ('groups', 'block'), pairs)  3.55 us
    ppermute x6, starting transfers between devices, to_neighbour(): return lax.ppermute(value, ('block', 'cores'), pairs)  3.43 us
    unnamed x12, local copies, waits for them, and re-layouts  3.22 us
  transfers between devices with their start and end apart: 20, of which 12 were waited for; matrix products, arithmetic and copies ran while one was open for 4% of the time, Pallas kernels for 13%

profile of v9, /device:TPU:0, one launch (start us, length us, event | category | flops | bytes accessed | tf_op | source)
XLA Modules:
  0.0 91.8 jit_solution(9635368590873954912)
XLA Ops:
  0.0 0.0 copy-start
  0.0 1.9 %dynamic-slice_bitcast_fusion.1.refs_1_ = bf16[1664,128]{1,0:T(8,128)(2,1)} fusion(bf16[1,6912,128]{2,1,0:T(8,128)(2,1)} %param.11, s32[]{:T(128)S(6)} %select_n.18), kind=kLoop, calls=%fused_computation.1 | loop fusion | bytes 851972 | tf_op jit(solution)/shard_map/dynamic_slice | solution.py:268
  1.9 3.0 %collective-permute-start.3 = (bf16[1664,128]{1,0:T(8,128)(2,1)}, bf16[1664,128]{1,0:T(8,128)(2,1)}, u32[]{:S(2)}, u32[]{:S(2)}) collective-permute-start(bf16[1664,128]{1,0:T(8,128)(2,1)} %dynamic-slice_bitcast_fusion.1.refs_1_), channel_id=1, source_target_pairs={{0,4},{4,8},{8,12},{12,0},{1,5},{5,9},{9,13},{13,1},{2,6},{6,10},{... | collective-permute-start | bytes 1277960 | tf_op jit(solution)/shard_map/ppermute | solution.py:25
  5.0 1.8 %dynamic-slice_bitcast_fusion.refs_2_ = bf16[1792,128]{1,0:T(8,128)(2,1)} fusion(bf16[1,6912,128]{2,1,0:T(8,128)(2,1)} %param.11, s32[]{:T(128)S(6)} %select_n.17), kind=kLoop, calls=%fused_computation | loop fusion | bytes 917508 | tf_op jit(solution)/shard_map/dynamic_slice | solution.py:268
  6.8 0.0 copy-done
  6.8 1.3 %constant_dynamic-slice_fusion = bf16[256,3456]{1,0:T(8,128)(2,1)} fusion(bf16[256,6912]{1,0:T(8,128)(2,1)S(1)} %bitcast.9, s32[]{:T(128)S(6)} %select_n.20), kind=kLoop, calls=%fused_computation.4 | loop fusion | bytes 3538948 | tf_op jit(solution)/shard_map/dynamic_slice | solution.py:274
  8.1 1.5 %collective-permute-start.4 = (bf16[256,3456]{1,0:T(8,128)(2,1)}, bf16[256,3456]{1,0:T(8,128)(2,1)}, u32[]{:S(2)}, u32[]{:S(2)}) collective-permute-start(bf16[256,3456]{1,0:T(8,128)(2,1)} %constant_dynamic-slice_fusion), channel_id=1, source_target_pairs={{0,16},{16,0},{1,17},{17,1},{2,18},{18,2},{3,19},{19,3},{4,20},{20... | collective-permute-start | bytes 5308424 | tf_op jit(solution)/shard_map/ppermute | solution.py:25
  9.6 1.6 %collective-permute-start = (bf16[1792,128]{1,0:T(8,128)(2,1)}, bf16[1792,128]{1,0:T(8,128)(2,1)}, u32[]{:S(2)}, u32[]{:S(2)}) collective-permute-start(bf16[1792,128]{1,0:T(8,128)(2,1)} %dynamic-slice_bitcast_fusion.refs_2_), channel_id=1, source_target_pairs={{0,4},{4,8},{8,12},{12,0},{1,5},{5,9},{9,13},{13,1},{2,6},{6,10},{... | collective-permute-start | bytes 1376264 | tf_op jit(solution)/shard_map/ppermute | solution.py:25
  11.2 0.1 pad_add_fusion.place
  11.3 2.1 %copy-done.1 = bf16[1280,1536]{1,0:T(8,128)(2,1)S(1)} copy-done((bf16[1280,1536]{1,0:T(8,128)(2,1)S(1)}, bf16[1280,1536]{1,0:T(8,128)(2,1)}, u32[]{:S(2)}) %copy-start.1) | copy-done | bytes 3932184
  13.4 1.1 %copy-done.2 = bf16[2,128,1280]{2,1,0:T(8,128)(2,1)S(1)} copy-done((bf16[2,128,1280]{2,1,0:T(8,128)(2,1)S(1)}, bf16[2,128,1280]{2,1,0:T(8,128)(2,1)}, u32[]{:S(2)}) %copy-start.2) | copy-done | bytes 655384
  14.5 2.6 %shard_map.73 = (f32[384,256]{1,0:T(8,128)S(1)}, f32[384,256]{1,0:T(8,128)S(1)}, f32[384,256]{1,0:T(8,128)S(1)}, f32[384,256]{1,0:T(8,128)S(1)}) custom-call(s32[3]{0:T(128)S(1)} %pad_add_fusion.place, bf16[256,1280]{1,0:T(8,128)(2,1)S(1)} %bitcast.11, bf16[1280,1536]{1,0:T(8,128)(2,1)S(1)} %copy-done.1), custom_call_target="tpu_custom_call" | custom-call | tf_op jit(solution)/shard_map/pallas_call | solution.py:89
  17.1 0.8 collective-permute-done.3.refs_3_
  18.0 0.8 collective-permute-start.5
  18.8 0.0 collective-permute-start.7
  18.8 1.5 %collective-permute-start.8 = (f32[384,256]{1,0:T(8,128)S(1)}, f32[384,256]{1,0:T(8,128)S(1)}, u32[]{:S(2)}, u32[]{:S(2)}) collective-permute-start(f32[384,256]{1,0:T(8,128)S(1)} %get-tuple-element.48), channel_id=1, source_target_pairs={{0,2},{1,3},{2,0},{3,1},{4,6},{5,7},{6,4},{7,5},{8,10},{9,11},{10,... | collective-permute-start | bytes 1179656 | tf_op jit(solution)/shard_map/ppermute | solution.py:39
  20.3 7.5 %collective-permute-done.refs_4_ = bf16[1792,128]{1,0:T(8,128)(2,1)} collective-permute-done((bf16[1792,128]{1,0:T(8,128)(2,1)}, bf16[1792,128]{1,0:T(8,128)(2,1)}, u32[]{:S(2)}, u32[]{:S(2)}) %collective-permute-start) | collective-permute-done | bytes 458784 | tf_op jit(solution)/shard_map/ppermute | solution.py:25
  27.8 0.0 collective-permute-start.9
  27.8 0.0 collective-permute-done.7
  27.8 0.0 collective-permute-start.1
  27.8 9.0 %collective-permute-done.5.refs_1_ = bf16[1664,128]{1,0:T(8,128)(2,1)S(1)} collective-permute-done((bf16[1664,128]{1,0:T(8,128)(2,1)}, bf16[1664,128]{1,0:T(8,128)(2,1)S(1)}, u32[]{:S(2)}, u32[]{:S(2)}) %collective-permute-start.5) | collective-permute-done | bytes 426016 | tf_op jit(solution)/shard_map/ppermute | solution.py:25
  36.8 0.0 collective-permute-start.6
  36.8 0.1 constant_dynamic-slice_fusion.1.refs_0_
  37.0 2.5 %shard_map.74.refs_2_.refs_0_ = f32[2,256,128]{2,1,0:T(8,128)S(1)} custom-call(bf16[256,3456]{1,0:T(8,128)(2,1)S(1)} %constant_dynamic-slice_fusion.1.refs_0_, bf16[1664,128]{1,0:T(8,128)(2,1)} %dynamic-slice_bitcast_fusion.1.refs_1_, bf16[1792,128]{1,0:T(8,128)(2,1)} %dynamic-slice_bitcast_fusion.refs_2_, bf16[1664,128]{1,0:T(8,128)(2,1)} %collective-permute-done.3.refs_3_, ...), custom_call_target="tpu_custom_call" | custom-call | flops 452984832 | bytes 3538944 | tf_op jit(solution)/shard_map/pallas_call | solution.py:130
  39.5 7.2 %collective-permute-done.1.refs_2_ = bf16[1792,128]{1,0:T(8,128)(2,1)S(1)} collective-permute-done((bf16[1792,128]{1,0:T(8,128)(2,1)}, bf16[1792,128]{1,0:T(8,128)(2,1)S(1)}, u32[]{:S(2)}, u32[]{:S(2)}) %collective-permute-start.1) | collective-permute-done | bytes 458784 | tf_op jit(solution)/shard_map/ppermute | solution.py:25
  46.6 0.0 collective-permute-start.2
  46.7 9.1 %collective-permute-done.6.refs_3_ = bf16[1664,128]{1,0:T(8,128)(2,1)S(1)} collective-permute-done((bf16[1664,128]{1,0:T(8,128)(2,1)S(1)}, bf16[1664,128]{1,0:T(8,128)(2,1)S(1)}, u32[]{:S(2)}, u32[]{:S(2)}) %collective-permute-start.6) | collective-permute-done | bytes 426016 | tf_op jit(solution)/shard_map/ppermute | solution.py:25
  55.8 0.0 collective-permute-done.8
  55.8 0.0 collective-permute-done.9
  55.8 0.1 add_convert_fusion.refs_0_
  55.9 0.1 collective-permute-start.10
  56.0 1.8 %collective-permute-start.11 = (bf16[384,256]{1,0:T(8,128)(2,1)S(1)}, bf16[384,256]{1,0:T(8,128)(2,1)S(1)}, u32[]{:S(2)}, u32[]{:S(2)}) collective-permute-start(bf16[384,256]{1,0:T(8,128)(2,1)S(1)} %add_convert_fusion.refs_0_), channel_id=1, source_target_pairs={{0,2},{1,3},{2,0},{3,1},{4,6},{5,7},{6,4},{7,5},{8,10},{9,11},{10,... | collective-permute-start | bytes 589832 | tf_op jit(solution)/shard_map/ppermute | solution.py:39
  57.8 0.1 collective-permute-start.12
  57.8 0.8 shard_map.76.refs_4_.refs_2_
  58.7 0.0 collective-permute-done.4.refs_0_.refs_1_
  58.7 2.3 %shard_map.77.refs_5_.refs_3_ = f32[2,256,128]{2,1,0:T(8,128)S(1)} custom-call(bf16[256,3456]{1,0:T(8,128)(2,1)} %collective-permute-done.4.refs_0_.refs_1_, bf16[1664,128]{1,0:T(8,128)(2,1)S(1)} %collective-permute-done.5.refs_1_, bf16[1792,128]{1,0:T(8,128)(2,1)S(1)} %collective-permute-done.1.refs_2_, bf16[1664,128]{1,0:T(8,128)(2,1)S(1)} %collective-permute-done.6.refs_3_), custom_call_target="tpu_custom_call" | custom-call | flops 335544320 | bytes 2621440 | tf_op jit(solution)/shard_map/pallas_call | solution.py:130
  61.0 0.0 copy-start.3
  61.0 3.0 %shard_map.75.refs_3_.refs_1_ = f32[2,256,128]{2,1,0:T(8,128)S(1)} custom-call(bf16[256,3456]{1,0:T(8,128)(2,1)} %collective-permute-done.4.refs_0_.refs_1_, bf16[1664,128]{1,0:T(8,128)(2,1)} %dynamic-slice_bitcast_fusion.1.refs_1_, bf16[1792,128]{1,0:T(8,128)(2,1)} %dynamic-slice_bitcast_fusion.refs_2_, bf16[1664,128]{1,0:T(8,128)(2,1)} %collective-permute-done.3.refs_3_, ...), custom_call_target="tpu_custom_call" | custom-call | flops 452984832 | bytes 3538944 | tf_op jit(solution)/shard_map/pallas_call | solution.py:130
  64.1 0.0 collective-permute-done.10.refs_1_
  64.1 0.0 collective-permute-done.11.refs_2_
  64.1 3.0 %collective-permute-done.12.refs_3_ = bf16[384,256]{1,0:T(8,128)(2,1)S(1)} collective-permute-done((bf16[384,256]{1,0:T(8,128)(2,1)S(1)}, bf16[384,256]{1,0:T(8,128)(2,1)S(1)}, u32[]{:S(2)}, u32[]{:S(2)}) %collective-permute-start.12) | collective-permute-done | bytes 196640 | tf_op jit(solution)/shard_map/ppermute | solution.py:39
  67.0 0.6 shard_map.78.act
  67.6 0.0 collective-permute-done.2.held
  67.7 2.1 %shard_map.79 = (f32[512,128]{1,0:T(8,128)S(1)}, f32[2,512,128]{2,1,0:T(8,128)S(1)}) custom-call(s32[4]{0:T(128)S(1)} %copy-done.3, s32[3]{0:T(128)S(1)} %pad_add_fusion.place, bf16[1792,128]{1,0:T(8,128)(2,1)S(1)} %collective-permute-done.2.held, bf16[256,3456]{1,0:T(8,128)(2,1)S(1)} %constant_dynamic-slice_fusion.1.refs_0_, ...), custom_call_target="tpu_custom_call" | custom-call | tf_op jit(solution)/shard_map/pallas_call | solution.py:175
  69.8 0.0 copy-start.4
  69.8 0.0 copy-start.5
  69.8 0.3 collective-permute-start.13
  70.2 1.6 %collective-permute-done.13.refs_4_ = f32[2,512,128]{2,1,0:T(8,128)S(1)} collective-permute-done((f32[2,512,128]{2,1,0:T(8,128)S(1)}, f32[2,512,128]{2,1,0:T(8,128)S(1)}, u32[]{:S(2)}, u32[]{:S(2)}) %collective-permute-start.13) | collective-permute-done | bytes 524320 | tf_op jit(solution)/shard_map/ppermute | solution.py:25
  71.8 0.6 shard_map.80
  72.5 1.8 %collective-permute-start.14 = (f32[256,128]{1,0:T(8,128)S(1)}, f32[256,128]{1,0:T(8,128)S(1)}, u32[]{:S(2)}, u32[]{:S(2)}) collective-permute-start(f32[256,128]{1,0:T(8,128)S(1)} %get-tuple-element.60), channel_id=1, source_target_pairs={{0,16},{2,18},{16,0},{18,2},{1,17},{3,19},{17,1},{19,3},{4,20},{6,... | collective-permute-start | bytes 393224 | tf_op jit(solution)/shard_map/ppermute | solution.py:316
  74.3 1.5 %collective-permute-start.15 = (f32[256,128]{1,0:T(8,128)S(1)}, f32[256,128]{1,0:T(8,128)S(1)}, u32[]{:S(2)}, u32[]{:S(2)}) collective-permute-start(f32[256,128]{1,0:T(8,128)S(1)} %get-tuple-element.61), channel_id=1, source_target_pairs={{0,2},{2,0},{16,18},{18,16},{1,3},{3,1},{17,19},{19,17},{4,6},{6,4... | collective-permute-start | bytes 393224 | tf_op jit(solution)/shard_map/ppermute | solution.py:316
  75.8 0.2 collective-permute-start.16
  76.0 2.2 %collective-permute-done.14.refs_1_ = f32[256,128]{1,0:T(8,128)S(1)} collective-permute-done((f32[256,128]{1,0:T(8,128)S(1)}, f32[256,128]{1,0:T(8,128)S(1)}, u32[]{:S(2)}, u32[]{:S(2)}) %collective-permute-start.14) | collective-permute-done | bytes 131104 | tf_op jit(solution)/shard_map/ppermute | solution.py:316
  78.2 2.4 %collective-permute-done.15.refs_2_ = f32[256,128]{1,0:T(8,128)S(1)} collective-permute-done((f32[256,128]{1,0:T(8,128)S(1)}, f32[256,128]{1,0:T(8,128)S(1)}, u32[]{:S(2)}, u32[]{:S(2)}) %collective-permute-start.15) | collective-permute-done | bytes 131104 | tf_op jit(solution)/shard_map/ppermute | solution.py:316
  80.7 1.6 %collective-permute-done.16.refs_3_ = f32[256,128]{1,0:T(8,128)S(1)} collective-permute-done((f32[256,128]{1,0:T(8,128)S(1)}, f32[256,128]{1,0:T(8,128)S(1)}, u32[]{:S(2)}, u32[]{:S(2)}) %collective-permute-start.16) | collective-permute-done | bytes 131104 | tf_op jit(solution)/shard_map/ppermute | solution.py:316
  82.3 0.0 copy-done.5
  82.3 0.9 shard_map.81
  83.2 0.1 collective-permute-start.17
  83.2 2.5 %collective-permute-start.18 = (bf16[256,128]{1,0:T(8,128)(2,1)S(1)}, bf16[256,128]{1,0:T(8,128)(2,1)S(1)}, u32[]{:S(2)}, u32[]{:S(2)}) collective-permute-start(bf16[256,128]{1,0:T(8,128)(2,1)S(1)} %get-tuple-element.65), channel_id=1, source_target_pairs={{0,8},{4,12},{8,0},{12,4},{1,9},{5,13},{9,1},{13,5},{2,10},{6,14},... | collective-permute-start | bytes 196616 | tf_op jit(solution)/shard_map/ppermute | solution.py:25
  85.7 1.4 %collective-permute-start.19 = (bf16[256,128]{1,0:T(8,128)(2,1)S(1)}, bf16[256,128]{1,0:T(8,128)(2,1)S(1)}, u32[]{:S(2)}, u32[]{:S(2)}) collective-permute-start(bf16[256,128]{1,0:T(8,128)(2,1)S(1)} %get-tuple-element.66), channel_id=1, source_target_pairs={{0,12},{4,0},{8,4},{12,8},{1,13},{5,1},{9,5},{13,9},{2,14},{6,2},{... | collective-permute-start | bytes 196616 | tf_op jit(solution)/shard_map/ppermute | solution.py:25
  87.1 2.7 %collective-permute-done.17 = bf16[256,128]{1,0:T(8,128)(2,1)S(1)} collective-permute-done((bf16[256,128]{1,0:T(8,128)(2,1)S(1)}, bf16[256,128]{1,0:T(8,128)(2,1)S(1)}, u32[]{:S(2)}, u32[]{:S(2)}) %collective-permute-start.17) | collective-permute-done | bytes 65568 | tf_op jit(solution)/shard_map/ppermute | solution.py:25
  89.8 1.3 %collective-permute-done.18 = bf16[256,128]{1,0:T(8,128)(2,1)S(1)} collective-permute-done((bf16[256,128]{1,0:T(8,128)(2,1)S(1)}, bf16[256,128]{1,0:T(8,128)(2,1)S(1)}, u32[]{:S(2)}, u32[]{:S(2)}) %collective-permute-start.18) | collective-permute-done | bytes 65568 | tf_op jit(solution)/shard_map/ppermute | solution.py:25
  91.1 0.0 collective-permute-done.19
  91.1 0.7 add_multiply_fusion
  (4 shorter events, 0.0 us)
Async XLA Ops:
  0.0 6.8 %copy-start = (bf16[2,128,6912]{2,1,0:T(8,128)(2,1)S(1)}, bf16[2,128,6912]{2,1,0:T(8,128)(2,1)}, u32[]{:S(2)}) copy-start(bf16[2,128,6912]{2,1,0:T(8,128)(2,1)} %param.8) | copy-start | bytes 10616836
  1.9 16.0 %collective-permute-start.3 = (bf16[1664,128]{1,0:T(8,128)(2,1)}, bf16[1664,128]{1,0:T(8,128)(2,1)}, u32[]{:S(2)}, u32[]{:S(2)}) collective-permute-start(bf16[1664,128]{1,0:T(8,128)(2,1)} %dynamic-slice_bitcast_fusion.1.refs_1_), channel_id=1, source_target_pairs={{0,4},{4,8},{8,12},{12,0},{1,5},{5,9},{9,13},{13,1},{2,6},{6,10},{... | collective-permute-start | bytes 1277960 | tf_op jit(solution)/shard_map/ppermute | solution.py:25
  8.1 50.6 %collective-permute-start.4 = (bf16[256,3456]{1,0:T(8,128)(2,1)}, bf16[256,3456]{1,0:T(8,128)(2,1)}, u32[]{:S(2)}, u32[]{:S(2)}) collective-permute-start(bf16[256,3456]{1,0:T(8,128)(2,1)} %constant_dynamic-slice_fusion), channel_id=1, source_target_pairs={{0,16},{16,0},{1,17},{17,1},{2,18},{18,2},{3,19},{19,3},{4,20},{20... | collective-permute-start | bytes 5308424 | tf_op jit(solution)/shard_map/ppermute | solution.py:25
  9.6 18.2 %collective-permute-start = (bf16[1792,128]{1,0:T(8,128)(2,1)}, bf16[1792,128]{1,0:T(8,128)(2,1)}, u32[]{:S(2)}, u32[]{:S(2)}) collective-permute-start(bf16[1792,128]{1,0:T(8,128)(2,1)} %dynamic-slice_bitcast_fusion.refs_2_), channel_id=1, source_target_pairs={{0,4},{4,8},{8,12},{12,0},{1,5},{5,9},{9,13},{13,1},{2,6},{6,10},{... | collective-permute-start | bytes 1376264 | tf_op jit(solution)/shard_map/ppermute | solution.py:25
  11.3 2.1 %copy-start.1 = (bf16[1280,1536]{1,0:T(8,128)(2,1)S(1)}, bf16[1280,1536]{1,0:T(8,128)(2,1)}, u32[]{:S(2)}) copy-start(bf16[1280,1536]{1,0:T(8,128)(2,1)} %basis.1) | copy-start | bytes 11796484
  13.4 1.1 %copy-start.2 = (bf16[2,128,1280]{2,1,0:T(8,128)(2,1)S(1)}, bf16[2,128,1280]{2,1,0:T(8,128)(2,1)}, u32[]{:S(2)}) copy-start(bf16[2,128,1280]{2,1,0:T(8,128)(2,1)} %param.7) | copy-start | bytes 1966084
  18.0 18.9 %collective-permute-start.5 = (bf16[1664,128]{1,0:T(8,128)(2,1)}, bf16[1664,128]{1,0:T(8,128)(2,1)S(1)}, u32[]{:S(2)}, u32[]{:S(2)}) collective-permute-start(bf16[1664,128]{1,0:T(8,128)(2,1)} %collective-permute-done.3.refs_3_), channel_id=1, source_target_pairs={{0,4},{4,8},{8,12},{12,0},{1,5},{5,9},{9,13},{13,1},{2,6},{6,10},{... | collective-permute-start | bytes 1277960 | tf_op jit(solution)/shard_map/ppermute | solution.py:25
  18.8 9.0 %collective-permute-start.7 = (f32[384,256]{1,0:T(8,128)S(1)}, f32[384,256]{1,0:T(8,128)S(1)}, u32[]{:S(2)}, u32[]{:S(2)}) collective-permute-start(f32[384,256]{1,0:T(8,128)S(1)} %get-tuple-element.46), channel_id=1, source_target_pairs={{0,1},{1,0},{2,3},{3,2},{4,5},{5,4},{6,7},{7,6},{8,9},{9,8},{10,11... | collective-permute-start | bytes 1179656 | tf_op jit(solution)/shard_map/ppermute | solution.py:39
  18.8 37.0 %collective-permute-start.8 = (f32[384,256]{1,0:T(8,128)S(1)}, f32[384,256]{1,0:T(8,128)S(1)}, u32[]{:S(2)}, u32[]{:S(2)}) collective-permute-start(f32[384,256]{1,0:T(8,128)S(1)} %get-tuple-element.48), channel_id=1, source_target_pairs={{0,2},{1,3},{2,0},{3,1},{4,6},{5,7},{6,4},{7,5},{8,10},{9,11},{10,... | collective-permute-start | bytes 1179656 | tf_op jit(solution)/shard_map/ppermute | solution.py:39
  27.8 28.0 %collective-permute-start.9 = (f32[384,256]{1,0:T(8,128)S(1)}, f32[384,256]{1,0:T(8,128)S(1)}, u32[]{:S(2)}, u32[]{:S(2)}) collective-permute-start(f32[384,256]{1,0:T(8,128)S(1)} %get-tuple-element.49), channel_id=1, source_target_pairs={{0,3},{1,2},{2,1},{3,0},{4,7},{5,6},{6,5},{7,4},{8,11},{9,10},{10,... | collective-permute-start | bytes 1179656 | tf_op jit(solution)/shard_map/ppermute | solution.py:39
  27.8 18.8 %collective-permute-start.1 = (bf16[1792,128]{1,0:T(8,128)(2,1)}, bf16[1792,128]{1,0:T(8,128)(2,1)S(1)}, u32[]{:S(2)}, u32[]{:S(2)}) collective-permute-start(bf16[1792,128]{1,0:T(8,128)(2,1)} %collective-permute-done.refs_4_), channel_id=1, source_target_pairs={{0,4},{4,8},{8,12},{12,0},{1,5},{5,9},{9,13},{13,1},{2,6},{6,10},{... | collective-permute-start | bytes 1376264 | tf_op jit(solution)/shard_map/ppermute | solution.py:25
  36.8 19.0 %collective-permute-start.6 = (bf16[1664,128]{1,0:T(8,128)(2,1)S(1)}, bf16[1664,128]{1,0:T(8,128)(2,1)S(1)}, u32[]{:S(2)}, u32[]{:S(2)}) collective-permute-start(bf16[1664,128]{1,0:T(8,128)(2,1)S(1)} %collective-permute-done.5.refs_1_), channel_id=1, source_target_pairs={{0,4},{4,8},{8,12},{12,0},{1,5},{5,9},{9,13},{13,1},{2,6},{6,10},{... | collective-permute-start | bytes 1277960 | tf_op jit(solution)/shard_map/ppermute | solution.py:25
  46.6 21.0 %collective-permute-start.2 = (bf16[1792,128]{1,0:T(8,128)(2,1)S(1)}, bf16[1792,128]{1,0:T(8,128)(2,1)S(1)}, u32[]{:S(2)}, u32[]{:S(2)}) collective-permute-start(bf16[1792,128]{1,0:T(8,128)(2,1)S(1)} %collective-permute-done.1.refs_2_), channel_id=1, source_target_pairs={{0,4},{4,8},{8,12},{12,0},{1,5},{5,9},{9,13},{13,1},{2,6},{6,10},{... | collective-permute-start | bytes 1376264 | tf_op jit(solution)/shard_map/ppermute | solution.py:25
  55.9 8.2 %collective-permute-start.10 = (bf16[384,256]{1,0:T(8,128)(2,1)S(1)}, bf16[384,256]{1,0:T(8,128)(2,1)S(1)}, u32[]{:S(2)}, u32[]{:S(2)}) collective-permute-start(bf16[384,256]{1,0:T(8,128)(2,1)S(1)} %add_convert_fusion.refs_0_), channel_id=1, source_target_pairs={{0,1},{1,0},{2,3},{3,2},{4,5},{5,4},{6,7},{7,6},{8,9},{9,8},{10,11... | collective-permute-start | bytes 589832 | tf_op jit(solution)/shard_map/ppermute | solution.py:39
  56.0 8.1 %collective-permute-start.11 = (bf16[384,256]{1,0:T(8,128)(2,1)S(1)}, bf16[384,256]{1,0:T(8,128)(2,1)S(1)}, u32[]{:S(2)}, u32[]{:S(2)}) collective-permute-start(bf16[384,256]{1,0:T(8,128)(2,1)S(1)} %add_convert_fusion.refs_0_), channel_id=1, source_target_pairs={{0,2},{1,3},{2,0},{3,1},{4,6},{5,7},{6,4},{7,5},{8,10},{9,11},{10,... | collective-permute-start | bytes 589832 | tf_op jit(solution)/shard_map/ppermute | solution.py:39
  57.8 9.3 %collective-permute-start.12 = (bf16[384,256]{1,0:T(8,128)(2,1)S(1)}, bf16[384,256]{1,0:T(8,128)(2,1)S(1)}, u32[]{:S(2)}, u32[]{:S(2)}) collective-permute-start(bf16[384,256]{1,0:T(8,128)(2,1)S(1)} %add_convert_fusion.refs_0_), channel_id=1, source_target_pairs={{0,3},{1,2},{2,1},{3,0},{4,7},{5,6},{6,5},{7,4},{8,11},{9,10},{10,... | collective-permute-start | bytes 589832 | tf_op jit(solution)/shard_map/ppermute | solution.py:39
  61.0 6.6 %copy-start.3 = (s32[4]{0:T(128)S(1)}, s32[4]{0:T(128)}, u32[]{:S(2)}) copy-start(s32[4]{0:T(128)} %owner.3) | copy-start | bytes 52
  69.8 12.5 %copy-start.4 = (s32[2]{0:T(128)S(1)}, s32[2]{0:T(128)}, u32[]{:S(2)}) copy-start(s32[2]{0:T(128)} %counts.1) | copy-start | bytes 28
  69.8 12.5 %copy-start.5 = (s32[1,2]{1,0:T(1,128)S(1)}, s32[1,2]{1,0:T(1,128)}, u32[]{:S(2)}) copy-start(s32[1,2]{1,0:T(1,128)} %wanted.1) | copy-start | bytes 28
  69.8 2.0 %collective-permute-start.13 = (f32[2,512,128]{2,1,0:T(8,128)S(1)}, f32[2,512,128]{2,1,0:T(8,128)S(1)}, u32[]{:S(2)}, u32[]{:S(2)}) collective-permute-start(f32[2,512,128]{2,1,0:T(8,128)S(1)} %get-tuple-element.58), channel_id=1, source_target_pairs={{0,1},{1,0},{2,3},{3,2},{4,5},{5,4},{6,7},{7,6},{8,9},{9,8},{10,11... | collective-permute-start | bytes 1572872 | tf_op jit(solution)/shard_map/ppermute | solution.py:25
  72.5 5.8 %collective-permute-start.14 = (f32[256,128]{1,0:T(8,128)S(1)}, f32[256,128]{1,0:T(8,128)S(1)}, u32[]{:S(2)}, u32[]{:S(2)}) collective-permute-start(f32[256,128]{1,0:T(8,128)S(1)} %get-tuple-element.60), channel_id=1, source_target_pairs={{0,16},{2,18},{16,0},{18,2},{1,17},{3,19},{17,1},{19,3},{4,20},{6,... | collective-permute-start | bytes 393224 | tf_op jit(solution)/shard_map/ppermute | solution.py:316
  74.3 6.4 %collective-permute-start.15 = (f32[256,128]{1,0:T(8,128)S(1)}, f32[256,128]{1,0:T(8,128)S(1)}, u32[]{:S(2)}, u32[]{:S(2)}) collective-permute-start(f32[256,128]{1,0:T(8,128)S(1)} %get-tuple-element.61), channel_id=1, source_target_pairs={{0,2},{2,0},{16,18},{18,16},{1,3},{3,1},{17,19},{19,17},{4,6},{6,4... | collective-permute-start | bytes 393224 | tf_op jit(solution)/shard_map/ppermute | solution.py:316
  75.8 6.5 %collective-permute-start.16 = (f32[256,128]{1,0:T(8,128)S(1)}, f32[256,128]{1,0:T(8,128)S(1)}, u32[]{:S(2)}, u32[]{:S(2)}) collective-permute-start(f32[256,128]{1,0:T(8,128)S(1)} %get-tuple-element.62), channel_id=1, source_target_pairs={{0,18},{2,16},{16,2},{18,0},{1,19},{3,17},{17,3},{19,1},{4,22},{6,... | collective-permute-start | bytes 393224 | tf_op jit(solution)/shard_map/ppermute | solution.py:316
  83.2 6.6 %collective-permute-start.17 = (bf16[256,128]{1,0:T(8,128)(2,1)S(1)}, bf16[256,128]{1,0:T(8,128)(2,1)S(1)}, u32[]{:S(2)}, u32[]{:S(2)}) collective-permute-start(bf16[256,128]{1,0:T(8,128)(2,1)S(1)} %get-tuple-element.64), channel_id=1, source_target_pairs={{0,4},{4,8},{8,12},{12,0},{1,5},{5,9},{9,13},{13,1},{2,6},{6,10},{... | collective-permute-start | bytes 196616 | tf_op jit(solution)/shard_map/ppermute | solution.py:25
  83.2 7.8 %collective-permute-start.18 = (bf16[256,128]{1,0:T(8,128)(2,1)S(1)}, bf16[256,128]{1,0:T(8,128)(2,1)S(1)}, u32[]{:S(2)}, u32[]{:S(2)}) collective-permute-start(bf16[256,128]{1,0:T(8,128)(2,1)S(1)} %get-tuple-element.65), channel_id=1, source_target_pairs={{0,8},{4,12},{8,0},{12,4},{1,9},{5,13},{9,1},{13,5},{2,10},{6,14},... | collective-permute-start | bytes 196616 | tf_op jit(solution)/shard_map/ppermute | solution.py:25
  85.7 5.3 %collective-permute-start.19 = (bf16[256,128]{1,0:T(8,128)(2,1)S(1)}, bf16[256,128]{1,0:T(8,128)(2,1)S(1)}, u32[]{:S(2)}, u32[]{:S(2)}) collective-permute-start(bf16[256,128]{1,0:T(8,128)(2,1)S(1)} %get-tuple-element.66), channel_id=1, source_target_pairs={{0,12},{4,0},{8,4},{12,8},{1,13},{5,1},{9,5},{13,9},{2,14},{6,2},{... | collective-permute-start | bytes 196616 | tf_op jit(solution)/shard_map/ppermute | solution.py:25

commit v10 on v9

--- a/solution.py
+++ b/solution.py
@@ -290,8 +290,8 @@
             ]
             rows = [[share(group)]] + others
     act = after(act, first[2])
-    for i, part in enumerate(away_act):
-        act = act + (after(part, first[-1]) if i == 0 else part)
+    for part in away_act:
+        act = act + part
     pieces = [piece for pair in zip(first, second) for piece in pair]
     early = [early_products(part, pieces[:-4], shares) for part in rows]
     act_parts = gather_act(act.astype(BF16), (first[-1], early[0]))

time: 92.1 us -> 89 us (0.966)
  waiting for transfers between devices: 48.4 us -> 45.8 us
    ppermute x6, waiting for transfers between devices: 2.98 us -> 0.02 us  [to_neighbour(): return lax.ppermute(value, ('block', 'cores'), pairs)]
where the time goes in v10:
time: 89 us; the launch traced here: 88.6 us
  waiting for transfers between devices  45.8 us (51%)
  starting transfers between devices  17.8 us (20%)
  Pallas kernels  15.6 us (18%)
  local copies, waits for them, and re-layouts  8.43 us (9%)
    ppermute x11, waiting for transfers between devices, shift(): lax.ppermute(value, axis, [(i, (i + step) % size) for i in range(size)])  39.7 us
    ppermute x11, starting transfers between devices, shift(): lax.ppermute(value, axis, [(i, (i + step) % size) for i in range(size)])  11 us
    pallas_call x4, Pallas kernels, early_products(): pl.pallas_call(functools.partial(early_kernel, len(rows), shares), out_sh...  8.68 us
    ppermute x3, waiting for transfers between devices, on_device(): parts[i] = lax.ppermute(parts[i], ('groups', 'block'), pairs)  6.04 us
    dynamic_slice x2, local copies, waits for them, and re-layouts, on_device(): lax.dynamic_slice_in_dim(basis_store[0], group * part_features + start, s...  3.77 us
    ppermute x3, starting transfers between devices, on_device(): parts[i] = lax.ppermute(parts[i], ('groups', 'block'), pairs)  3.55 us
    ppermute x6, starting transfers between devices, to_neighbour(): return lax.ppermute(value, ('block', 'cores'), pairs)  3.27 us
    unnamed x12, local copies, waits for them, and re-layouts  3.22 us
  transfers between devices with their start and end apart: 20, of which 12 were waited for; matrix products, arithmetic and copies ran while one was open for 4% of the time, Pallas kernels for 13%

profile of v10, /device:TPU:0, one launch (start us, length us, event | category | flops | bytes accessed | tf_op | source)
XLA Modules:
  0.0 88.6 jit_solution(7103796257777976191)
XLA Ops:
  0.0 0.0 copy-start
  0.0 1.9 %dynamic-slice_bitcast_fusion.1.refs_1_ = bf16[1664,128]{1,0:T(8,128)(2,1)} fusion(bf16[1,6912,128]{2,1,0:T(8,128)(2,1)} %param.11, s32[]{:T(128)S(6)} %select_n.18), kind=kLoop, calls=%fused_computation.1 | loop fusion | bytes 851972 | tf_op jit(solution)/shard_map/dynamic_slice | solution.py:268
  1.9 3.0 %collective-permute-start.3 = (bf16[1664,128]{1,0:T(8,128)(2,1)}, bf16[1664,128]{1,0:T(8,128)(2,1)}, u32[]{:S(2)}, u32[]{:S(2)}) collective-permute-start(bf16[1664,128]{1,0:T(8,128)(2,1)} %dynamic-slice_bitcast_fusion.1.refs_1_), channel_id=1, source_target_pairs={{0,4},{4,8},{8,12},{12,0},{1,5},{5,9},{9,13},{13,1},{2,6},{6,10},{... | collective-permute-start | bytes 1277960 | tf_op jit(solution)/shard_map/ppermute | solution.py:25
  5.0 1.8 %dynamic-slice_bitcast_fusion.refs_2_ = bf16[1792,128]{1,0:T(8,128)(2,1)} fusion(bf16[1,6912,128]{2,1,0:T(8,128)(2,1)} %param.11, s32[]{:T(128)S(6)} %select_n.17), kind=kLoop, calls=%fused_computation | loop fusion | bytes 917508 | tf_op jit(solution)/shard_map/dynamic_slice | solution.py:268
  6.8 0.0 copy-done
  6.8 1.3 %constant_dynamic-slice_fusion = bf16[256,3456]{1,0:T(8,128)(2,1)} fusion(bf16[256,6912]{1,0:T(8,128)(2,1)S(1)} %bitcast.9, s32[]{:T(128)S(6)} %select_n.20), kind=kLoop, calls=%fused_computation.4 | loop fusion | bytes 3538948 | tf_op jit(solution)/shard_map/dynamic_slice | solution.py:274
  8.1 1.5 %collective-permute-start.4 = (bf16[256,3456]{1,0:T(8,128)(2,1)}, bf16[256,3456]{1,0:T(8,128)(2,1)}, u32[]{:S(2)}, u32[]{:S(2)}) collective-permute-start(bf16[256,3456]{1,0:T(8,128)(2,1)} %constant_dynamic-slice_fusion), channel_id=1, source_target_pairs={{0,16},{16,0},{1,17},{17,1},{2,18},{18,2},{3,19},{19,3},{4,20},{20... | collective-permute-start | bytes 5308424 | tf_op jit(solution)/shard_map/ppermute | solution.py:25
  9.6 1.6 %collective-permute-start = (bf16[1792,128]{1,0:T(8,128)(2,1)}, bf16[1792,128]{1,0:T(8,128)(2,1)}, u32[]{:S(2)}, u32[]{:S(2)}) collective-permute-start(bf16[1792,128]{1,0:T(8,128)(2,1)} %dynamic-slice_bitcast_fusion.refs_2_), channel_id=1, source_target_pairs={{0,4},{4,8},{8,12},{12,0},{1,5},{5,9},{9,13},{13,1},{2,6},{6,10},{... | collective-permute-start | bytes 1376264 | tf_op jit(solution)/shard_map/ppermute | solution.py:25
  11.2 0.1 pad_add_fusion.place
  11.3 2.1 %copy-done.1 = bf16[1280,1536]{1,0:T(8,128)(2,1)S(1)} copy-done((bf16[1280,1536]{1,0:T(8,128)(2,1)S(1)}, bf16[1280,1536]{1,0:T(8,128)(2,1)}, u32[]{:S(2)}) %copy-start.1) | copy-done | bytes 3932184
  13.4 1.1 %copy-done.2 = bf16[2,128,1280]{2,1,0:T(8,128)(2,1)S(1)} copy-done((bf16[2,128,1280]{2,1,0:T(8,128)(2,1)S(1)}, bf16[2,128,1280]{2,1,0:T(8,128)(2,1)}, u32[]{:S(2)}) %copy-start.2) | copy-done | bytes 655384
  14.5 2.6 %shard_map.73 = (f32[384,256]{1,0:T(8,128)S(1)}, f32[384,256]{1,0:T(8,128)S(1)}, f32[384,256]{1,0:T(8,128)S(1)}, f32[384,256]{1,0:T(8,128)S(1)}) custom-call(s32[3]{0:T(128)S(1)} %pad_add_fusion.place, bf16[256,1280]{1,0:T(8,128)(2,1)S(1)} %bitcast.11, bf16[1280,1536]{1,0:T(8,128)(2,1)S(1)} %copy-done.1), custom_call_target="tpu_custom_call" | custom-call | tf_op jit(solution)/shard_map/pallas_call | solution.py:89
  17.1 0.8 collective-permute-done.3.refs_3_
  18.0 0.8 collective-permute-start.5
  18.8 0.0 collective-permute-start.7
  18.8 1.5 %collective-permute-start.8 = (f32[384,256]{1,0:T(8,128)S(1)}, f32[384,256]{1,0:T(8,128)S(1)}, u32[]{:S(2)}, u32[]{:S(2)}) collective-permute-start(f32[384,256]{1,0:T(8,128)S(1)} %get-tuple-element.46), channel_id=1, source_target_pairs={{0,2},{1,3},{2,0},{3,1},{4,6},{5,7},{6,4},{7,5},{8,10},{9,11},{10,... | collective-permute-start | bytes 1179656 | tf_op jit(solution)/shard_map/ppermute | solution.py:39
  20.3 7.5 %collective-permute-done.refs_4_ = bf16[1792,128]{1,0:T(8,128)(2,1)} collective-permute-done((bf16[1792,128]{1,0:T(8,128)(2,1)}, bf16[1792,128]{1,0:T(8,128)(2,1)}, u32[]{:S(2)}, u32[]{:S(2)}) %collective-permute-start) | collective-permute-done | bytes 458784 | tf_op jit(solution)/shard_map/ppermute | solution.py:25
  27.8 0.0 collective-permute-start.9
  27.8 0.0 collective-permute-done.7
  27.8 0.0 collective-permute-start.1
  27.8 9.0 %collective-permute-done.5.refs_1_ = bf16[1664,128]{1,0:T(8,128)(2,1)S(1)} collective-permute-done((bf16[1664,128]{1,0:T(8,128)(2,1)}, bf16[1664,128]{1,0:T(8,128)(2,1)S(1)}, u32[]{:S(2)}, u32[]{:S(2)}) %collective-permute-start.5) | collective-permute-done | bytes 426016 | tf_op jit(solution)/shard_map/ppermute | solution.py:25
  36.8 0.0 collective-permute-start.6
  36.8 0.1 constant_dynamic-slice_fusion.1.refs_0_
  37.0 2.5 %shard_map.74.refs_2_.refs_0_ = f32[2,256,128]{2,1,0:T(8,128)S(1)} custom-call(bf16[256,3456]{1,0:T(8,128)(2,1)S(1)} %constant_dynamic-slice_fusion.1.refs_0_, bf16[1664,128]{1,0:T(8,128)(2,1)} %dynamic-slice_bitcast_fusion.1.refs_1_, bf16[1792,128]{1,0:T(8,128)(2,1)} %dynamic-slice_bitcast_fusion.refs_2_, bf16[1664,128]{1,0:T(8,128)(2,1)} %collective-permute-done.3.refs_3_, ...), custom_call_target="tpu_custom_call" | custom-call | flops 452984832 | bytes 3538944 | tf_op jit(solution)/shard_map/pallas_call | solution.py:130
  39.5 7.2 %collective-permute-done.1.refs_2_ = bf16[1792,128]{1,0:T(8,128)(2,1)S(1)} collective-permute-done((bf16[1792,128]{1,0:T(8,128)(2,1)}, bf16[1792,128]{1,0:T(8,128)(2,1)S(1)}, u32[]{:S(2)}, u32[]{:S(2)}) %collective-permute-start.1) | collective-permute-done | bytes 458784 | tf_op jit(solution)/shard_map/ppermute | solution.py:25
  46.6 0.0 collective-permute-start.2
  46.7 0.0 collective-permute-done.8
  46.7 0.0 collective-permute-done.9
  46.7 0.1 add_convert_fusion.refs_0_
  46.8 1.8 %collective-permute-start.11 = (bf16[384,256]{1,0:T(8,128)(2,1)S(1)}, bf16[384,256]{1,0:T(8,128)(2,1)S(1)}, u32[]{:S(2)}, u32[]{:S(2)}) collective-permute-start(bf16[384,256]{1,0:T(8,128)(2,1)S(1)} %add_convert_fusion.refs_0_), channel_id=1, source_target_pairs={{0,2},{1,3},{2,0},{3,1},{4,6},{5,7},{6,4},{7,5},{8,10},{9,11},{10,... | collective-permute-start | bytes 589832 | tf_op jit(solution)/shard_map/ppermute | solution.py:39
  48.6 0.0 collective-permute-start.12
  48.6 7.2 %collective-permute-done.6.refs_3_ = bf16[1664,128]{1,0:T(8,128)(2,1)S(1)} collective-permute-done((bf16[1664,128]{1,0:T(8,128)(2,1)S(1)}, bf16[1664,128]{1,0:T(8,128)(2,1)S(1)}, u32[]{:S(2)}, u32[]{:S(2)}) %collective-permute-start.6) | collective-permute-done | bytes 426016 | tf_op jit(solution)/shard_map/ppermute | solution.py:25
  55.8 0.0 collective-permute-start.10
  55.8 0.8 shard_map.76.refs_4_.refs_2_
  56.6 0.0 collective-permute-done.4.refs_0_.refs_1_
  56.6 2.3 %shard_map.77.refs_5_.refs_3_ = f32[2,256,128]{2,1,0:T(8,128)S(1)} custom-call(bf16[256,3456]{1,0:T(8,128)(2,1)} %collective-permute-done.4.refs_0_.refs_1_, bf16[1664,128]{1,0:T(8,128)(2,1)S(1)} %collective-permute-done.5.refs_1_, bf16[1792,128]{1,0:T(8,128)(2,1)S(1)} %collective-permute-done.1.refs_2_, bf16[1664,128]{1,0:T(8,128)(2,1)S(1)} %collective-permute-done.6.refs_3_), custom_call_target="tpu_custom_call" | custom-call | flops 335544320 | bytes 2621440 | tf_op jit(solution)/shard_map/pallas_call | solution.py:130
  59.0 0.0 copy-start.3
  59.0 3.0 %shard_map.75.refs_3_.refs_1_ = f32[2,256,128]{2,1,0:T(8,128)S(1)} custom-call(bf16[256,3456]{1,0:T(8,128)(2,1)} %collective-permute-done.4.refs_0_.refs_1_, bf16[1664,128]{1,0:T(8,128)(2,1)} %dynamic-slice_bitcast_fusion.1.refs_1_, bf16[1792,128]{1,0:T(8,128)(2,1)} %dynamic-slice_bitcast_fusion.refs_2_, bf16[1664,128]{1,0:T(8,128)(2,1)} %collective-permute-done.3.refs_3_, ...), custom_call_target="tpu_custom_call" | custom-call | flops 452984832 | bytes 3538944 | tf_op jit(solution)/shard_map/pallas_call | solution.py:130
  62.0 0.0 collective-permute-done.11.refs_2_
  62.0 0.0 collective-permute-done.12.refs_3_
  62.0 0.0 collective-permute-done.10.refs_1_
  62.0 0.6 shard_map.78.act
  62.6 2.1 %collective-permute-done.2.held = bf16[1792,128]{1,0:T(8,128)(2,1)S(1)} collective-permute-done((bf16[1792,128]{1,0:T(8,128)(2,1)S(1)}, bf16[1792,128]{1,0:T(8,128)(2,1)S(1)}, u32[]{:S(2)}, u32[]{:S(2)}) %collective-permute-start.2) | collective-permute-done | bytes 458784 | tf_op jit(solution)/shard_map/ppermute | solution.py:25
  64.8 0.0 copy-done.3
  64.8 2.1 %shard_map.79 = (f32[512,128]{1,0:T(8,128)S(1)}, f32[2,512,128]{2,1,0:T(8,128)S(1)}) custom-call(s32[4]{0:T(128)S(1)} %copy-done.3, s32[3]{0:T(128)S(1)} %pad_add_fusion.place, bf16[1792,128]{1,0:T(8,128)(2,1)S(1)} %collective-permute-done.2.held, bf16[256,3456]{1,0:T(8,128)(2,1)S(1)} %constant_dynamic-slice_fusion.1.refs_0_, ...), custom_call_target="tpu_custom_call" | custom-call | tf_op jit(solution)/shard_map/pallas_call | solution.py:175
  66.9 0.0 copy-start.4
  66.9 0.0 copy-start.5
  66.9 0.1 collective-permute-start.13
  67.0 1.9 %collective-permute-done.13.refs_4_ = f32[2,512,128]{2,1,0:T(8,128)S(1)} collective-permute-done((f32[2,512,128]{2,1,0:T(8,128)S(1)}, f32[2,512,128]{2,1,0:T(8,128)S(1)}, u32[]{:S(2)}, u32[]{:S(2)}) %collective-permute-start.13) | collective-permute-done | bytes 524320 | tf_op jit(solution)/shard_map/ppermute | solution.py:25
  68.9 0.6 shard_map.80
  69.6 1.6 %collective-permute-start.14 = (f32[256,128]{1,0:T(8,128)S(1)}, f32[256,128]{1,0:T(8,128)S(1)}, u32[]{:S(2)}, u32[]{:S(2)}) collective-permute-start(f32[256,128]{1,0:T(8,128)S(1)} %get-tuple-element.58), channel_id=1, source_target_pairs={{0,16},{2,18},{16,0},{18,2},{1,17},{3,19},{17,1},{19,3},{4,20},{6,... | collective-permute-start | bytes 393224 | tf_op jit(solution)/shard_map/ppermute | solution.py:316
  71.1 1.5 %collective-permute-start.15 = (f32[256,128]{1,0:T(8,128)S(1)}, f32[256,128]{1,0:T(8,128)S(1)}, u32[]{:S(2)}, u32[]{:S(2)}) collective-permute-start(f32[256,128]{1,0:T(8,128)S(1)} %get-tuple-element.59), channel_id=1, source_target_pairs={{0,2},{2,0},{16,18},{18,16},{1,3},{3,1},{17,19},{19,17},{4,6},{6,4... | collective-permute-start | bytes 393224 | tf_op jit(solution)/shard_map/ppermute | solution.py:316
  72.6 0.5 collective-permute-start.16
  73.1 2.0 %collective-permute-done.14.refs_1_ = f32[256,128]{1,0:T(8,128)S(1)} collective-permute-done((f32[256,128]{1,0:T(8,128)S(1)}, f32[256,128]{1,0:T(8,128)S(1)}, u32[]{:S(2)}, u32[]{:S(2)}) %collective-permute-start.14) | collective-permute-done | bytes 131104 | tf_op jit(solution)/shard_map/ppermute | solution.py:316
  75.2 2.4 %collective-permute-done.15.refs_2_ = f32[256,128]{1,0:T(8,128)S(1)} collective-permute-done((f32[256,128]{1,0:T(8,128)S(1)}, f32[256,128]{1,0:T(8,128)S(1)}, u32[]{:S(2)}, u32[]{:S(2)}) %collective-permute-start.15) | collective-permute-done | bytes 131104 | tf_op jit(solution)/shard_map/ppermute | solution.py:316
  77.5 1.6 %collective-permute-done.16.refs_3_ = f32[256,128]{1,0:T(8,128)S(1)} collective-permute-done((f32[256,128]{1,0:T(8,128)S(1)}, f32[256,128]{1,0:T(8,128)S(1)}, u32[]{:S(2)}, u32[]{:S(2)}) %collective-permute-start.16) | collective-permute-done | bytes 131104 | tf_op jit(solution)/shard_map/ppermute | solution.py:316
  79.2 0.9 shard_map.81
  80.0 0.1 collective-permute-start.17
  80.1 2.3 %collective-permute-start.18 = (bf16[256,128]{1,0:T(8,128)(2,1)S(1)}, bf16[256,128]{1,0:T(8,128)(2,1)S(1)}, u32[]{:S(2)}, u32[]{:S(2)}) collective-permute-start(bf16[256,128]{1,0:T(8,128)(2,1)S(1)} %get-tuple-element.63), channel_id=1, source_target_pairs={{0,8},{4,12},{8,0},{12,4},{1,9},{5,13},{9,1},{13,5},{2,10},{6,14},... | collective-permute-start | bytes 196616 | tf_op jit(solution)/shard_map/ppermute | solution.py:25
  82.4 1.5 %collective-permute-start.19 = (bf16[256,128]{1,0:T(8,128)(2,1)S(1)}, bf16[256,128]{1,0:T(8,128)(2,1)S(1)}, u32[]{:S(2)}, u32[]{:S(2)}) collective-permute-start(bf16[256,128]{1,0:T(8,128)(2,1)S(1)} %get-tuple-element.64), channel_id=1, source_target_pairs={{0,12},{4,0},{8,4},{12,8},{1,13},{5,1},{9,5},{13,9},{2,14},{6,2},{... | collective-permute-start | bytes 196616 | tf_op jit(solution)/shard_map/ppermute | solution.py:25
  83.9 2.7 %collective-permute-done.17 = bf16[256,128]{1,0:T(8,128)(2,1)S(1)} collective-permute-done((bf16[256,128]{1,0:T(8,128)(2,1)S(1)}, bf16[256,128]{1,0:T(8,128)(2,1)S(1)}, u32[]{:S(2)}, u32[]{:S(2)}) %collective-permute-start.17) | collective-permute-done | bytes 65568 | tf_op jit(solution)/shard_map/ppermute | solution.py:25
  86.6 1.3 %collective-permute-done.18 = bf16[256,128]{1,0:T(8,128)(2,1)S(1)} collective-permute-done((bf16[256,128]{1,0:T(8,128)(2,1)S(1)}, bf16[256,128]{1,0:T(8,128)(2,1)S(1)}, u32[]{:S(2)}, u32[]{:S(2)}) %collective-permute-start.18) | collective-permute-done | bytes 65568 | tf_op jit(solution)/shard_map/ppermute | solution.py:25
  87.9 0.0 collective-permute-done.19
  87.9 0.7 add_multiply_fusion
  (4 shorter events, 0.0 us)
Async XLA Ops:
  0.0 6.8 %copy-start = (bf16[2,128,6912]{2,1,0:T(8,128)(2,1)S(1)}, bf16[2,128,6912]{2,1,0:T(8,128)(2,1)}, u32[]{:S(2)}) copy-start(bf16[2,128,6912]{2,1,0:T(8,128)(2,1)} %param.8) | copy-start | bytes 10616836
  1.9 16.0 %collective-permute-start.3 = (bf16[1664,128]{1,0:T(8,128)(2,1)}, bf16[1664,128]{1,0:T(8,128)(2,1)}, u32[]{:S(2)}, u32[]{:S(2)}) collective-permute-start(bf16[1664,128]{1,0:T(8,128)(2,1)} %dynamic-slice_bitcast_fusion.1.refs_1_), channel_id=1, source_target_pairs={{0,4},{4,8},{8,12},{12,0},{1,5},{5,9},{9,13},{13,1},{2,6},{6,10},{... | collective-permute-start | bytes 1277960 | tf_op jit(solution)/shard_map/ppermute | solution.py:25
  8.1 48.5 %collective-permute-start.4 = (bf16[256,3456]{1,0:T(8,128)(2,1)}, bf16[256,3456]{1,0:T(8,128)(2,1)}, u32[]{:S(2)}, u32[]{:S(2)}) collective-permute-start(bf16[256,3456]{1,0:T(8,128)(2,1)} %constant_dynamic-slice_fusion), channel_id=1, source_target_pairs={{0,16},{16,0},{1,17},{17,1},{2,18},{18,2},{3,19},{19,3},{4,20},{20... | collective-permute-start | bytes 5308424 | tf_op jit(solution)/shard_map/ppermute | solution.py:25
  9.6 18.2 %collective-permute-start = (bf16[1792,128]{1,0:T(8,128)(2,1)}, bf16[1792,128]{1,0:T(8,128)(2,1)}, u32[]{:S(2)}, u32[]{:S(2)}) collective-permute-start(bf16[1792,128]{1,0:T(8,128)(2,1)} %dynamic-slice_bitcast_fusion.refs_2_), channel_id=1, source_target_pairs={{0,4},{4,8},{8,12},{12,0},{1,5},{5,9},{9,13},{13,1},{2,6},{6,10},{... | collective-permute-start | bytes 1376264 | tf_op jit(solution)/shard_map/ppermute | solution.py:25
  11.3 2.1 %copy-start.1 = (bf16[1280,1536]{1,0:T(8,128)(2,1)S(1)}, bf16[1280,1536]{1,0:T(8,128)(2,1)}, u32[]{:S(2)}) copy-start(bf16[1280,1536]{1,0:T(8,128)(2,1)} %basis.1) | copy-start | bytes 11796484
  13.4 1.1 %copy-start.2 = (bf16[2,128,1280]{2,1,0:T(8,128)(2,1)S(1)}, bf16[2,128,1280]{2,1,0:T(8,128)(2,1)}, u32[]{:S(2)}) copy-start(bf16[2,128,1280]{2,1,0:T(8,128)(2,1)} %param.7) | copy-start | bytes 1966084
  18.0 18.9 %collective-permute-start.5 = (bf16[1664,128]{1,0:T(8,128)(2,1)}, bf16[1664,128]{1,0:T(8,128)(2,1)S(1)}, u32[]{:S(2)}, u32[]{:S(2)}) collective-permute-start(bf16[1664,128]{1,0:T(8,128)(2,1)} %collective-permute-done.3.refs_3_), channel_id=1, source_target_pairs={{0,4},{4,8},{8,12},{12,0},{1,5},{5,9},{9,13},{13,1},{2,6},{6,10},{... | collective-permute-start | bytes 1277960 | tf_op jit(solution)/shard_map/ppermute | solution.py:25
  18.8 9.0 %collective-permute-start.7 = (f32[384,256]{1,0:T(8,128)S(1)}, f32[384,256]{1,0:T(8,128)S(1)}, u32[]{:S(2)}, u32[]{:S(2)}) collective-permute-start(f32[384,256]{1,0:T(8,128)S(1)} %get-tuple-element.45), channel_id=1, source_target_pairs={{0,1},{1,0},{2,3},{3,2},{4,5},{5,4},{6,7},{7,6},{8,9},{9,8},{10,11... | collective-permute-start | bytes 1179656 | tf_op jit(solution)/shard_map/ppermute | solution.py:39
  18.8 27.9 %collective-permute-start.8 = (f32[384,256]{1,0:T(8,128)S(1)}, f32[384,256]{1,0:T(8,128)S(1)}, u32[]{:S(2)}, u32[]{:S(2)}) collective-permute-start(f32[384,256]{1,0:T(8,128)S(1)} %get-tuple-element.46), channel_id=1, source_target_pairs={{0,2},{1,3},{2,0},{3,1},{4,6},{5,7},{6,4},{7,5},{8,10},{9,11},{10,... | collective-permute-start | bytes 1179656 | tf_op jit(solution)/shard_map/ppermute | solution.py:39
  27.8 18.9 %collective-permute-start.9 = (f32[384,256]{1,0:T(8,128)S(1)}, f32[384,256]{1,0:T(8,128)S(1)}, u32[]{:S(2)}, u32[]{:S(2)}) collective-permute-start(f32[384,256]{1,0:T(8,128)S(1)} %get-tuple-element.47), channel_id=1, source_target_pairs={{0,3},{1,2},{2,1},{3,0},{4,7},{5,6},{6,5},{7,4},{8,11},{9,10},{10,... | collective-permute-start | bytes 1179656 | tf_op jit(solution)/shard_map/ppermute | solution.py:39
  27.8 18.8 %collective-permute-start.1 = (bf16[1792,128]{1,0:T(8,128)(2,1)}, bf16[1792,128]{1,0:T(8,128)(2,1)S(1)}, u32[]{:S(2)}, u32[]{:S(2)}) collective-permute-start(bf16[1792,128]{1,0:T(8,128)(2,1)} %collective-permute-done.refs_4_), channel_id=1, source_target_pairs={{0,4},{4,8},{8,12},{12,0},{1,5},{5,9},{9,13},{13,1},{2,6},{6,10},{... | collective-permute-start | bytes 1376264 | tf_op jit(solution)/shard_map/ppermute | solution.py:25
  36.8 19.0 %collective-permute-start.6 = (bf16[1664,128]{1,0:T(8,128)(2,1)S(1)}, bf16[1664,128]{1,0:T(8,128)(2,1)S(1)}, u32[]{:S(2)}, u32[]{:S(2)}) collective-permute-start(bf16[1664,128]{1,0:T(8,128)(2,1)S(1)} %collective-permute-done.5.refs_1_), channel_id=1, source_target_pairs={{0,4},{4,8},{8,12},{12,0},{1,5},{5,9},{9,13},{13,1},{2,6},{6,10},{... | collective-permute-start | bytes 1277960 | tf_op jit(solution)/shard_map/ppermute | solution.py:25
  46.6 18.1 %collective-permute-start.2 = (bf16[1792,128]{1,0:T(8,128)(2,1)S(1)}, bf16[1792,128]{1,0:T(8,128)(2,1)S(1)}, u32[]{:S(2)}, u32[]{:S(2)}) collective-permute-start(bf16[1792,128]{1,0:T(8,128)(2,1)S(1)} %collective-permute-done.1.refs_2_), channel_id=1, source_target_pairs={{0,4},{4,8},{8,12},{12,0},{1,5},{5,9},{9,13},{13,1},{2,6},{6,10},{... | collective-permute-start | bytes 1376264 | tf_op jit(solution)/shard_map/ppermute | solution.py:25
  46.8 15.2 %collective-permute-start.11 = (bf16[384,256]{1,0:T(8,128)(2,1)S(1)}, bf16[384,256]{1,0:T(8,128)(2,1)S(1)}, u32[]{:S(2)}, u32[]{:S(2)}) collective-permute-start(bf16[384,256]{1,0:T(8,128)(2,1)S(1)} %add_convert_fusion.refs_0_), channel_id=1, source_target_pairs={{0,2},{1,3},{2,0},{3,1},{4,6},{5,7},{6,4},{7,5},{8,10},{9,11},{10,... | collective-permute-start | bytes 589832 | tf_op jit(solution)/shard_map/ppermute | solution.py:39
  48.6 13.4 %collective-permute-start.12 = (bf16[384,256]{1,0:T(8,128)(2,1)S(1)}, bf16[384,256]{1,0:T(8,128)(2,1)S(1)}, u32[]{:S(2)}, u32[]{:S(2)}) collective-permute-start(bf16[384,256]{1,0:T(8,128)(2,1)S(1)} %add_convert_fusion.refs_0_), channel_id=1, source_target_pairs={{0,3},{1,2},{2,1},{3,0},{4,7},{5,6},{6,5},{7,4},{8,11},{9,10},{10,... | collective-permute-start | bytes 589832 | tf_op jit(solution)/shard_map/ppermute | solution.py:39
  55.8 6.2 %collective-permute-start.10 = (bf16[384,256]{1,0:T(8,128)(2,1)S(1)}, bf16[384,256]{1,0:T(8,128)(2,1)S(1)}, u32[]{:S(2)}, u32[]{:S(2)}) collective-permute-start(bf16[384,256]{1,0:T(8,128)(2,1)S(1)} %add_convert_fusion.refs_0_), channel_id=1, source_target_pairs={{0,1},{1,0},{2,3},{3,2},{4,5},{5,4},{6,7},{7,6},{8,9},{9,8},{10,11... | collective-permute-start | bytes 589832 | tf_op jit(solution)/shard_map/ppermute | solution.py:39
  59.0 5.8 %copy-start.3 = (s32[4]{0:T(128)S(1)}, s32[4]{0:T(128)}, u32[]{:S(2)}) copy-start(s32[4]{0:T(128)} %owner.3) | copy-start | bytes 52
  66.9 12.3 %copy-start.4 = (s32[2]{0:T(128)S(1)}, s32[2]{0:T(128)}, u32[]{:S(2)}) copy-start(s32[2]{0:T(128)} %counts.1) | copy-start | bytes 28
  66.9 12.2 %copy-start.5 = (s32[1,2]{1,0:T(1,128)S(1)}, s32[1,2]{1,0:T(1,128)}, u32[]{:S(2)}) copy-start(s32[1,2]{1,0:T(1,128)} %wanted.1) | copy-start | bytes 28
  66.9 2.0 %collective-permute-start.13 = (f32[2,512,128]{2,1,0:T(8,128)S(1)}, f32[2,512,128]{2,1,0:T(8,128)S(1)}, u32[]{:S(2)}, u32[]{:S(2)}) collective-permute-start(f32[2,512,128]{2,1,0:T(8,128)S(1)} %get-tuple-element.56), channel_id=1, source_target_pairs={{0,1},{1,0},{2,3},{3,2},{4,5},{5,4},{6,7},{7,6},{8,9},{9,8},{10,11... | collective-permute-start | bytes 1572872 | tf_op jit(solution)/shard_map/ppermute | solution.py:25
  69.6 5.6 %collective-permute-start.14 = (f32[256,128]{1,0:T(8,128)S(1)}, f32[256,128]{1,0:T(8,128)S(1)}, u32[]{:S(2)}, u32[]{:S(2)}) collective-permute-start(f32[256,128]{1,0:T(8,128)S(1)} %get-tuple-element.58), channel_id=1, source_target_pairs={{0,16},{2,18},{16,0},{18,2},{1,17},{3,19},{17,1},{19,3},{4,20},{6,... | collective-permute-start | bytes 393224 | tf_op jit(solution)/shard_map/ppermute | solution.py:316
  71.1 6.4 %collective-permute-start.15 = (f32[256,128]{1,0:T(8,128)S(1)}, f32[256,128]{1,0:T(8,128)S(1)}, u32[]{:S(2)}, u32[]{:S(2)}) collective-permute-start(f32[256,128]{1,0:T(8,128)S(1)} %get-tuple-element.59), channel_id=1, source_target_pairs={{0,2},{2,0},{16,18},{18,16},{1,3},{3,1},{17,19},{19,17},{4,6},{6,4... | collective-permute-start | bytes 393224 | tf_op jit(solution)/shard_map/ppermute | solution.py:316
  72.6 6.5 %collective-permute-start.16 = (f32[256,128]{1,0:T(8,128)S(1)}, f32[256,128]{1,0:T(8,128)S(1)}, u32[]{:S(2)}, u32[]{:S(2)}) collective-permute-start(f32[256,128]{1,0:T(8,128)S(1)} %get-tuple-element.60), channel_id=1, source_target_pairs={{0,18},{2,16},{16,2},{18,0},{1,19},{3,17},{17,3},{19,1},{4,22},{6,... | collective-permute-start | bytes 393224 | tf_op jit(solution)/shard_map/ppermute | solution.py:316
  80.0 6.6 %collective-permute-start.17 = (bf16[256,128]{1,0:T(8,128)(2,1)S(1)}, bf16[256,128]{1,0:T(8,128)(2,1)S(1)}, u32[]{:S(2)}, u32[]{:S(2)}) collective-permute-start(bf16[256,128]{1,0:T(8,128)(2,1)S(1)} %get-tuple-element.62), channel_id=1, source_target_pairs={{0,4},{4,8},{8,12},{12,0},{1,5},{5,9},{9,13},{13,1},{2,6},{6,10},{... | collective-permute-start | bytes 196616 | tf_op jit(solution)/shard_map/ppermute | solution.py:25
  80.1 7.8 %collective-permute-start.18 = (bf16[256,128]{1,0:T(8,128)(2,1)S(1)}, bf16[256,128]{1,0:T(8,128)(2,1)S(1)}, u32[]{:S(2)}, u32[]{:S(2)}) collective-permute-start(bf16[256,128]{1,0:T(8,128)(2,1)S(1)} %get-tuple-element.63), channel_id=1, source_target_pairs={{0,8},{4,12},{8,0},{12,4},{1,9},{5,13},{9,1},{13,5},{2,10},{6,14},... | collective-permute-start | bytes 196616 | tf_op jit(solution)/shard_map/ppermute | solution.py:25
  82.4 5.5 %collective-permute-start.19 = (bf16[256,128]{1,0:T(8,128)(2,1)S(1)}, bf16[256,128]{1,0:T(8,128)(2,1)S(1)}, u32[]{:S(2)}, u32[]{:S(2)}) collective-permute-start(bf16[256,128]{1,0:T(8,128)(2,1)S(1)} %get-tuple-element.64), channel_id=1, source_target_pairs={{0,12},{4,0},{8,4},{12,8},{1,13},{5,1},{9,5},{13,9},{2,14},{6,2},{... | collective-permute-start | bytes 196616 | tf_op jit(solution)/shard_map/ppermute | solution.py:25

commit v11 on v10

--- a/solution.py
+++ b/solution.py
@@ -65,6 +65,32 @@
         out_specs=VMEM,
         compiler_params=pltpu.CompilerParams(vmem_limit_bytes=VMEM_LIMIT),
     )(place, *parts)
+
+
+def split_kernel(store, first, second, sems):
+    size = first.shape[0] + second.shape[0]
+    start = lax.axis_index("groups") * size
+    copies = []
+    for i, out in enumerate((first, second)):
+        rows = pl.ds(pl.multiple_of(start + i * first.shape[0], 16), out.shape[0])
+        copies.append(pltpu.make_async_copy(store.at[rows], out, sems.at[i]))
+    for copy in copies:
+        copy.start()
+    for copy in copies:
+        copy.wait()
+
+
+def split(store, cut, size):
+    return pl.pallas_call(
+        split_kernel,
+        out_shape=tuple(
+            jax.ShapeDtypeStruct((rows, store.shape[1]), store.dtype) for rows in (cut, size - cut)
+        ),
+        in_specs=[pl.BlockSpec(memory_space=pltpu.HBM)],
+        out_specs=(VMEM, VMEM),
+        scratch_shapes=[pltpu.SemaphoreType.DMA((2,))],
+        compiler_params=pltpu.CompilerParams(vmem_limit_bytes=VMEM_LIMIT),
+    )(store)
 
 
 def rotate_kernel(blocks, cores, place, acts, basis, *outs):
@@ -264,10 +290,7 @@
 
     cut = part_features // 256 * 128
     shares = (0, cut)
-    first, second = [
-        [lax.dynamic_slice_in_dim(basis_store[0], group * part_features + start, size, 0)]
-        for start, size in zip(shares, (cut, part_features - cut))
-    ]
+    first, second = [[part] for part in split(basis_store[0], cut, part_features)]
     flat_grads = after(gradients.reshape(slots, features), first[0], second[0])
 
     def share(index):

time: 89 us -> 90.2 us (1.013)
  waiting for transfers between devices: 45.8 us -> 41.8 us
  Pallas kernels: 15.6 us -> 18.9 us
  other arithmetic: 0.87 us -> 1.85 us
    ppermute x11, waiting for transfers between devices: 39.7 us -> 35.7 us  [shift(): lax.ppermute(value, axis, [(i, (i + step) % size) for i in range(size)])]
    unnamed x12 -> x22, local copies, waits for them, and re-layouts: 3.22 us -> 7.12 us
    dynamic_slice x2 -> x0, local copies, waits for them, and re-layouts: 3.77 us -> none  [on_device(): lax.dynamic_slice_in_dim(basis_store[0], group * part_features + start, s...]
    pallas_call x0 -> x1, Pallas kernels: none -> 1.46 us  [split(): pl.pallas_call(split_kernel, out_shape=tuple((jax.ShapeDtypeStruct((rows,...]
    pallas_call x4, Pallas kernels: 8.68 us -> 9.76 us  [early_products(): pl.pallas_call(functools.partial(early_kernel, len(rows), shares), out_sh...]
    convert_element_type x1, other arithmetic: 0.1 us -> 1.08 us  [on_device(): act_parts = gather_act(act.astype(BF16), (first[-1], early[0]))]
  transfers between devices with their start and end apart: 20 -> 20, of which waited for: 12 -> 11; matrix products, arithmetic and copies ran while one was open for 4% -> 3% of each run, Pallas kernels for 13% -> 15%
where the time goes in v11:
time: 90.2 us; the launch traced here: 89.9 us
  waiting for transfers between devices  41.8 us (46%)
  Pallas kernels  18.9 us (21%)
  starting transfers between devices  18.6 us (21%)
  local copies, waits for them, and re-layouts  8.55 us (9%)
  other arithmetic  1.85 us (2%)
    ppermute x11, waiting for transfers between devices, shift(): lax.ppermute(value, axis, [(i, (i + step) % size) for i in range(size)])  35.7 us
    ppermute x11, starting transfers between devices, shift(): lax.ppermute(value, axis, [(i, (i + step) % size) for i in range(size)])  11.8 us
    pallas_call x4, Pallas kernels, early_products(): pl.pallas_call(functools.partial(early_kernel, len(rows), shares), out_sh...  9.76 us
    unnamed x22, local copies, waits for them, and re-layouts  7.12 us
    ppermute x3, waiting for transfers between devices, on_device(): parts[i] = lax.ppermute(parts[i], ('groups', 'block'), pairs)  6.04 us
    ppermute x3, starting transfers between devices, on_device(): parts[i] = lax.ppermute(parts[i], ('groups', 'block'), pairs)  3.55 us
    pallas_call x1, Pallas kernels, rotate(): pl.pallas_call(functools.partial(rotate_kernel, blocks, cores), out_shape...  3.4 us
    ppermute x6, starting transfers between devices, to_neighbour(): return lax.ppermute(value, ('block', 'cores'), pairs)  3.28 us
  transfers between devices with their start and end apart: 20, of which 11 were waited for; matrix products, arithmetic and copies ran while one was open for 3% of the time, Pallas kernels for 15%

profile of v11, /device:TPU:0, one launch (start us, length us, event | category | flops | bytes accessed | tf_op | source)
XLA Modules:
  0.0 89.9 jit_solution(3971647572291043844)
XLA Ops:
  0.0 1.6 %copy-done.2 = bf16[1,6912,128]{2,1,0:T(8,128)(2,1)S(1)} copy-done((bf16[1,6912,128]{2,1,0:T(8,128)(2,1)S(1)}, bf16[1,6912,128]{2,1,0:T(8,128)(2,1)}, u32[]{:S(2)}) %copy-start.2) | copy-done | bytes 1769496
  1.6 1.5 %shard_map.73 = (bf16[1664,128]{1,0:T(8,128)(2,1)}, bf16[1792,128]{1,0:T(8,128)(2,1)}) custom-call(bf16[6912,128]{1,0:T(8,128)(2,1)S(1)} %bitcast.8), custom_call_target="tpu_custom_call" | custom-call | tf_op jit(solution)/shard_map/pallas_call | solution.py:84
  3.1 3.1 %collective-permute-start.3 = (bf16[1664,128]{1,0:T(8,128)(2,1)}, bf16[1664,128]{1,0:T(8,128)(2,1)}, u32[]{:S(2)}, u32[]{:S(2)}) collective-permute-start(bf16[1664,128]{1,0:T(8,128)(2,1)} %get-tuple-element.38.refs_1_), channel_id=1, source_target_pairs={{0,4},{4,8},{8,12},{12,0},{1,5},{5,9},{9,13},{13,1},{2,6},{6,10},{... | collective-permute-start | bytes 1277960 | tf_op jit(solution)/shard_map/ppermute | solution.py:25
  6.2 1.3 %constant_dynamic-slice_fusion = bf16[256,3456]{1,0:T(8,128)(2,1)} fusion(bf16[256,6912]{1,0:T(8,128)(2,1)S(1)} %bitcast.6, s32[]{:T(128)S(6)} %select_n.15), kind=kLoop, calls=%fused_computation.3 | loop fusion | bytes 3538948 | tf_op jit(solution)/shard_map/dynamic_slice | solution.py:297
  7.5 1.5 %collective-permute-start.4 = (bf16[256,3456]{1,0:T(8,128)(2,1)}, bf16[256,3456]{1,0:T(8,128)(2,1)}, u32[]{:S(2)}, u32[]{:S(2)}) collective-permute-start(bf16[256,3456]{1,0:T(8,128)(2,1)} %constant_dynamic-slice_fusion), channel_id=1, source_target_pairs={{0,16},{16,0},{1,17},{17,1},{2,18},{18,2},{3,19},{19,3},{4,20},{20... | collective-permute-start | bytes 5308424 | tf_op jit(solution)/shard_map/ppermute | solution.py:25
  9.0 1.6 %collective-permute-start = (bf16[1792,128]{1,0:T(8,128)(2,1)}, bf16[1792,128]{1,0:T(8,128)(2,1)}, u32[]{:S(2)}, u32[]{:S(2)}) collective-permute-start(bf16[1792,128]{1,0:T(8,128)(2,1)} %get-tuple-element.37.refs_2_), channel_id=1, source_target_pairs={{0,4},{4,8},{8,12},{12,0},{1,5},{5,9},{9,13},{13,1},{2,6},{6,10},{... | collective-permute-start | bytes 1376264 | tf_op jit(solution)/shard_map/ppermute | solution.py:25
  10.6 0.1 pad_add_fusion.place
  10.7 2.1 %copy-done.1 = bf16[1280,1536]{1,0:T(8,128)(2,1)S(1)} copy-done((bf16[1280,1536]{1,0:T(8,128)(2,1)S(1)}, bf16[1280,1536]{1,0:T(8,128)(2,1)}, u32[]{:S(2)}) %copy-start.1) | copy-done | bytes 3932184
  12.8 1.1 %copy-done.3 = bf16[2,128,1280]{2,1,0:T(8,128)(2,1)S(1)} copy-done((bf16[2,128,1280]{2,1,0:T(8,128)(2,1)S(1)}, bf16[2,128,1280]{2,1,0:T(8,128)(2,1)}, u32[]{:S(2)}) %copy-start.3) | copy-done | bytes 655384
  13.9 3.4 %shard_map.74 = (f32[384,256]{1,0:T(8,128)S(1)}, f32[384,256]{1,0:T(8,128)}, f32[384,256]{1,0:T(8,128)S(1)}, f32[384,256]{1,0:T(8,128)S(1)}) custom-call(s32[3]{0:T(128)S(1)} %pad_add_fusion.place, bf16[256,1280]{1,0:T(8,128)(2,1)S(1)} %bitcast.9, bf16[1280,1536]{1,0:T(8,128)(2,1)S(1)} %copy-done.1), custom_call_target="tpu_custom_call" | custom-call | tf_op jit(solution)/shard_map/pallas_call | solution.py:115
  17.3 0.8 copy-done.4
  18.0 0.8 copy-done.9
  18.8 0.7 copy-done.10
  19.5 0.0 collective-permute-done.3.refs_3_
  19.5 1.6 %collective-permute-start.5 = (bf16[1664,128]{1,0:T(8,128)(2,1)}, bf16[1664,128]{1,0:T(8,128)(2,1)}, u32[]{:S(2)}, u32[]{:S(2)}) collective-permute-start(bf16[1664,128]{1,0:T(8,128)(2,1)} %collective-permute-done.3.refs_3_), channel_id=1, source_target_pairs={{0,4},{4,8},{8,12},{12,0},{1,5},{5,9},{9,13},{13,1},{2,6},{6,10},{... | collective-permute-start | bytes 1277960 | tf_op jit(solution)/shard_map/ppermute | solution.py:25
  21.1 0.0 collective-permute-start.7
  21.1 1.5 %collective-permute-start.8 = (f32[384,256]{1,0:T(8,128)}, f32[384,256]{1,0:T(8,128)S(1)}, u32[]{:S(2)}, u32[]{:S(2)}) collective-permute-start(f32[384,256]{1,0:T(8,128)} %copy-done.10), channel_id=1, source_target_pairs={{0,2},{1,3},{2,0},{3,1},{4,6},{5,7},{6,4},{7,5},{8,10},{9,11},{10,... | collective-permute-start | bytes 1179656 | tf_op jit(solution)/shard_map/ppermute | solution.py:39
  22.6 6.4 %collective-permute-done.refs_4_ = bf16[1792,128]{1,0:T(8,128)(2,1)} collective-permute-done((bf16[1792,128]{1,0:T(8,128)(2,1)}, bf16[1792,128]{1,0:T(8,128)(2,1)}, u32[]{:S(2)}, u32[]{:S(2)}) %collective-permute-start) | collective-permute-done | bytes 458784 | tf_op jit(solution)/shard_map/ppermute | solution.py:25
  29.0 0.0 collective-permute-start.9
  29.0 0.0 collective-permute-done.7
  29.0 0.0 collective-permute-start.1
  29.0 9.1 %collective-permute-done.5.refs_1_ = bf16[1664,128]{1,0:T(8,128)(2,1)} collective-permute-done((bf16[1664,128]{1,0:T(8,128)(2,1)}, bf16[1664,128]{1,0:T(8,128)(2,1)}, u32[]{:S(2)}, u32[]{:S(2)}) %collective-permute-start.5) | collective-permute-done | bytes 426016 | tf_op jit(solution)/shard_map/ppermute | solution.py:25
  38.1 0.0 collective-permute-start.6
  38.2 0.1 constant_dynamic-slice_fusion.1.refs_0_
  38.3 2.5 %shard_map.75.refs_2_.refs_0_ = f32[2,256,128]{2,1,0:T(8,128)S(1)} custom-call(bf16[256,3456]{1,0:T(8,128)(2,1)S(1)} %constant_dynamic-slice_fusion.1.refs_0_, bf16[1664,128]{1,0:T(8,128)(2,1)} %get-tuple-element.38.refs_1_, bf16[1792,128]{1,0:T(8,128)(2,1)} %get-tuple-element.37.refs_2_, bf16[1664,128]{1,0:T(8,128)(2,1)} %collective-permute-done.3.refs_3_, ...), custom_call_target="tpu_custom_call" | custom-call | flops 452984832 | bytes 3538944 | tf_op jit(solution)/shard_map/pallas_call | solution.py:156
  40.8 7.0 %collective-permute-done.1.refs_2_ = bf16[1792,128]{1,0:T(8,128)(2,1)S(1)} collective-permute-done((bf16[1792,128]{1,0:T(8,128)(2,1)}, bf16[1792,128]{1,0:T(8,128)(2,1)S(1)}, u32[]{:S(2)}, u32[]{:S(2)}) %collective-permute-start.1) | collective-permute-done | bytes 458784 | tf_op jit(solution)/shard_map/ppermute | solution.py:25
  47.9 0.0 collective-permute-start.2
  47.9 0.0 collective-permute-done.8
  47.9 0.0 collective-permute-done.9
  47.9 1.1 %add_convert_fusion.refs_0_ = bf16[384,256]{1,0:T(8,128)(2,1)S(1)} fusion(f32[384,256]{1,0:T(8,128)S(1)} %collective-permute-done.9, f32[384,256]{1,0:T(8,128)S(1)} %collective-permute-done.8, f32[384,256]{1,0:T(8,128)S(1)} %copy-done.5, f32[384,256]{1,0:T(8,128)} %collective-permute-done.7), kind=kLoop, calls=%fused_computation | loop fusion | flops 393216 | bytes 1769472 | tf_op jit(solution)/shard_map/convert_element_type | solution.py:320
  49.0 1.8 %collective-permute-start.11 = (bf16[384,256]{1,0:T(8,128)(2,1)S(1)}, bf16[384,256]{1,0:T(8,128)(2,1)S(1)}, u32[]{:S(2)}, u32[]{:S(2)}) collective-permute-start(bf16[384,256]{1,0:T(8,128)(2,1)S(1)} %add_convert_fusion.refs_0_), channel_id=1, source_target_pairs={{0,2},{1,3},{2,0},{3,1},{4,6},{5,7},{6,4},{7,5},{8,10},{9,11},{10,... | collective-permute-start | bytes 589832 | tf_op jit(solution)/shard_map/ppermute | solution.py:39
  50.8 0.0 collective-permute-start.12
  50.8 6.2 %collective-permute-done.6.refs_3_ = bf16[1664,128]{1,0:T(8,128)(2,1)S(1)} collective-permute-done((bf16[1664,128]{1,0:T(8,128)(2,1)}, bf16[1664,128]{1,0:T(8,128)(2,1)S(1)}, u32[]{:S(2)}, u32[]{:S(2)}) %collective-permute-start.6) | collective-permute-done | bytes 426016 | tf_op jit(solution)/shard_map/ppermute | solution.py:25
  57.0 0.0 collective-permute-start.10
  57.0 1.8 %shard_map.77.refs_4_.refs_2_ = f32[2,256,128]{2,1,0:T(8,128)S(1)} custom-call(bf16[256,3456]{1,0:T(8,128)(2,1)S(1)} %constant_dynamic-slice_fusion.1.refs_0_, bf16[1664,128]{1,0:T(8,128)(2,1)} %collective-permute-done.5.refs_1_, bf16[1792,128]{1,0:T(8,128)(2,1)S(1)} %collective-permute-done.1.refs_2_, bf16[1664,128]{1,0:T(8,128)(2,1)S(1)} %collective-permute-done.6.refs_3_), custom_call_target="tpu_custom_call" | custom-call | flops 335544320 | bytes 2621440 | tf_op jit(solution)/shard_map/pallas_call | solution.py:156
  58.8 0.0 collective-permute-done.4.refs_0_.refs_1_
  58.8 2.4 %shard_map.78.refs_5_.refs_3_ = f32[2,256,128]{2,1,0:T(8,128)S(1)} custom-call(bf16[256,3456]{1,0:T(8,128)(2,1)} %collective-permute-done.4.refs_0_.refs_1_, bf16[1664,128]{1,0:T(8,128)(2,1)} %collective-permute-done.5.refs_1_, bf16[1792,128]{1,0:T(8,128)(2,1)S(1)} %collective-permute-done.1.refs_2_, bf16[1664,128]{1,0:T(8,128)(2,1)S(1)} %collective-permute-done.6.refs_3_), custom_call_target="tpu_custom_call" | custom-call | flops 335544320 | bytes 2621440 | tf_op jit(solution)/shard_map/pallas_call | solution.py:156
  61.2 0.0 copy-start.6
  61.2 3.0 %shard_map.76.refs_3_.refs_1_ = f32[2,256,128]{2,1,0:T(8,128)S(1)} custom-call(bf16[256,3456]{1,0:T(8,128)(2,1)} %collective-permute-done.4.refs_0_.refs_1_, bf16[1664,128]{1,0:T(8,128)(2,1)} %get-tuple-element.38.refs_1_, bf16[1792,128]{1,0:T(8,128)(2,1)} %get-tuple-element.37.refs_2_, bf16[1664,128]{1,0:T(8,128)(2,1)} %collective-permute-done.3.refs_3_, ...), custom_call_target="tpu_custom_call" | custom-call | flops 452984832 | bytes 3538944 | tf_op jit(solution)/shard_map/pallas_call | solution.py:156
  64.3 0.0 collective-permute-done.11.refs_2_
  64.3 0.0 collective-permute-done.12.refs_3_
  64.3 0.0 collective-permute-done.10.refs_1_
  64.3 0.6 shard_map.79.act
  64.9 1.1 %collective-permute-done.2.held = bf16[1792,128]{1,0:T(8,128)(2,1)S(1)} collective-permute-done((bf16[1792,128]{1,0:T(8,128)(2,1)S(1)}, bf16[1792,128]{1,0:T(8,128)(2,1)S(1)}, u32[]{:S(2)}, u32[]{:S(2)}) %collective-permute-start.2) | collective-permute-done | bytes 458784 | tf_op jit(solution)/shard_map/ppermute | solution.py:25
  66.0 2.1 %shard_map.80 = (f32[512,128]{1,0:T(8,128)S(1)}, f32[2,512,128]{2,1,0:T(8,128)S(1)}) custom-call(s32[4]{0:T(128)S(1)} %copy-done.6, s32[3]{0:T(128)S(1)} %pad_add_fusion.place, bf16[1792,128]{1,0:T(8,128)(2,1)S(1)} %collective-permute-done.2.held, bf16[256,3456]{1,0:T(8,128)(2,1)S(1)} %constant_dynamic-slice_fusion.1.refs_0_, ...), custom_call_target="tpu_custom_call" | custom-call | tf_op jit(solution)/shard_map/pallas_call | solution.py:201
  68.1 0.0 copy-start.7
  68.1 0.0 copy-start.8
  68.1 0.1 collective-permute-start.13
  68.2 1.9 %collective-permute-done.13.refs_4_ = f32[2,512,128]{2,1,0:T(8,128)S(1)} collective-permute-done((f32[2,512,128]{2,1,0:T(8,128)S(1)}, f32[2,512,128]{2,1,0:T(8,128)S(1)}, u32[]{:S(2)}, u32[]{:S(2)}) %collective-permute-start.13) | collective-permute-done | bytes 524320 | tf_op jit(solution)/shard_map/ppermute | solution.py:25
  70.1 0.7 shard_map.81
  70.8 1.6 %collective-permute-start.14 = (f32[256,128]{1,0:T(8,128)S(1)}, f32[256,128]{1,0:T(8,128)S(1)}, u32[]{:S(2)}, u32[]{:S(2)}) collective-permute-start(f32[256,128]{1,0:T(8,128)S(1)} %get-tuple-element.62), channel_id=1, source_target_pairs={{0,16},{2,18},{16,0},{18,2},{1,17},{3,19},{17,1},{19,3},{4,20},{6,... | collective-permute-start | bytes 393224 | tf_op jit(solution)/shard_map/ppermute | solution.py:339
  72.4 1.5 %collective-permute-start.15 = (f32[256,128]{1,0:T(8,128)S(1)}, f32[256,128]{1,0:T(8,128)S(1)}, u32[]{:S(2)}, u32[]{:S(2)}) collective-permute-start(f32[256,128]{1,0:T(8,128)S(1)} %get-tuple-element.63), channel_id=1, source_target_pairs={{0,2},{2,0},{16,18},{18,16},{1,3},{3,1},{17,19},{19,17},{4,6},{6,4... | collective-permute-start | bytes 393224 | tf_op jit(solution)/shard_map/ppermute | solution.py:339
  73.9 0.5 collective-permute-start.16
  74.3 2.0 %collective-permute-done.14.refs_1_ = f32[256,128]{1,0:T(8,128)S(1)} collective-permute-done((f32[256,128]{1,0:T(8,128)S(1)}, f32[256,128]{1,0:T(8,128)S(1)}, u32[]{:S(2)}, u32[]{:S(2)}) %collective-permute-start.14) | collective-permute-done | bytes 131104 | tf_op jit(solution)/shard_map/ppermute | solution.py:339
  76.4 2.4 %collective-permute-done.15.refs_2_ = f32[256,128]{1,0:T(8,128)S(1)} collective-permute-done((f32[256,128]{1,0:T(8,128)S(1)}, f32[256,128]{1,0:T(8,128)S(1)}, u32[]{:S(2)}, u32[]{:S(2)}) %collective-permute-start.15) | collective-permute-done | bytes 131104 | tf_op jit(solution)/shard_map/ppermute | solution.py:339
  78.8 1.6 %collective-permute-done.16.refs_3_ = f32[256,128]{1,0:T(8,128)S(1)} collective-permute-done((f32[256,128]{1,0:T(8,128)S(1)}, f32[256,128]{1,0:T(8,128)S(1)}, u32[]{:S(2)}, u32[]{:S(2)}) %collective-permute-start.16) | collective-permute-done | bytes 131104 | tf_op jit(solution)/shard_map/ppermute | solution.py:339
  80.4 0.9 shard_map.82
  81.3 0.1 collective-permute-start.17
  81.3 2.3 %collective-permute-start.18 = (bf16[256,128]{1,0:T(8,128)(2,1)S(1)}, bf16[256,128]{1,0:T(8,128)(2,1)S(1)}, u32[]{:S(2)}, u32[]{:S(2)}) collective-permute-start(bf16[256,128]{1,0:T(8,128)(2,1)S(1)} %get-tuple-element.67), channel_id=1, source_target_pairs={{0,8},{4,12},{8,0},{12,4},{1,9},{5,13},{9,1},{13,5},{2,10},{6,14},... | collective-permute-start | bytes 196616 | tf_op jit(solution)/shard_map/ppermute | solution.py:25
  83.6 1.5 %collective-permute-start.19 = (bf16[256,128]{1,0:T(8,128)(2,1)S(1)}, bf16[256,128]{1,0:T(8,128)(2,1)S(1)}, u32[]{:S(2)}, u32[]{:S(2)}) collective-permute-start(bf16[256,128]{1,0:T(8,128)(2,1)S(1)} %get-tuple-element.68), channel_id=1, source_target_pairs={{0,12},{4,0},{8,4},{12,8},{1,13},{5,1},{9,5},{13,9},{2,14},{6,2},{... | collective-permute-start | bytes 196616 | tf_op jit(solution)/shard_map/ppermute | solution.py:25
  85.1 2.7 %collective-permute-done.17 = bf16[256,128]{1,0:T(8,128)(2,1)S(1)} collective-permute-done((bf16[256,128]{1,0:T(8,128)(2,1)S(1)}, bf16[256,128]{1,0:T(8,128)(2,1)S(1)}, u32[]{:S(2)}, u32[]{:S(2)}) %collective-permute-start.17) | collective-permute-done | bytes 65568 | tf_op jit(solution)/shard_map/ppermute | solution.py:25
  87.9 1.3 %collective-permute-done.18 = bf16[256,128]{1,0:T(8,128)(2,1)S(1)} collective-permute-done((bf16[256,128]{1,0:T(8,128)(2,1)S(1)}, bf16[256,128]{1,0:T(8,128)(2,1)S(1)}, u32[]{:S(2)}, u32[]{:S(2)}) %collective-permute-start.18) | collective-permute-done | bytes 65568 | tf_op jit(solution)/shard_map/ppermute | solution.py:25
  89.2 0.0 collective-permute-done.19
  89.2 0.7 add_multiply_fusion
  (13 shorter events, 0.0 us)
Async XLA Ops:
  0.0 6.2 %copy-start = (bf16[2,128,6912]{2,1,0:T(8,128)(2,1)S(1)}, bf16[2,128,6912]{2,1,0:T(8,128)(2,1)}, u32[]{:S(2)}) copy-start(bf16[2,128,6912]{2,1,0:T(8,128)(2,1)} %param.8) | copy-start | bytes 10616836
  0.0 1.6 %copy-start.2 = (bf16[1,6912,128]{2,1,0:T(8,128)(2,1)S(1)}, bf16[1,6912,128]{2,1,0:T(8,128)(2,1)}, u32[]{:S(2)}) copy-start(bf16[1,6912,128]{2,1,0:T(8,128)(2,1)} %param.11) | copy-start | bytes 5308420
  3.1 16.4 %collective-permute-start.3 = (bf16[1664,128]{1,0:T(8,128)(2,1)}, bf16[1664,128]{1,0:T(8,128)(2,1)}, u32[]{:S(2)}, u32[]{:S(2)}) collective-permute-start(bf16[1664,128]{1,0:T(8,128)(2,1)} %get-tuple-element.38.refs_1_), channel_id=1, source_target_pairs={{0,4},{4,8},{8,12},{12,0},{1,5},{5,9},{9,13},{13,1},{2,6},{6,10},{... | collective-permute-start | bytes 1277960 | tf_op jit(solution)/shard_map/ppermute | solution.py:25
  7.5 51.3 %collective-permute-start.4 = (bf16[256,3456]{1,0:T(8,128)(2,1)}, bf16[256,3456]{1,0:T(8,128)(2,1)}, u32[]{:S(2)}, u32[]{:S(2)}) collective-permute-start(bf16[256,3456]{1,0:T(8,128)(2,1)} %constant_dynamic-slice_fusion), channel_id=1, source_target_pairs={{0,16},{16,0},{1,17},{17,1},{2,18},{18,2},{3,19},{19,3},{4,20},{20... | collective-permute-start | bytes 5308424 | tf_op jit(solution)/shard_map/ppermute | solution.py:25
  9.0 20.0 %collective-permute-start = (bf16[1792,128]{1,0:T(8,128)(2,1)}, bf16[1792,128]{1,0:T(8,128)(2,1)}, u32[]{:S(2)}, u32[]{:S(2)}) collective-permute-start(bf16[1792,128]{1,0:T(8,128)(2,1)} %get-tuple-element.37.refs_2_), channel_id=1, source_target_pairs={{0,4},{4,8},{8,12},{12,0},{1,5},{5,9},{9,13},{13,1},{2,6},{6,10},{... | collective-permute-start | bytes 1376264 | tf_op jit(solution)/shard_map/ppermute | solution.py:25
  10.7 2.1 %copy-start.1 = (bf16[1280,1536]{1,0:T(8,128)(2,1)S(1)}, bf16[1280,1536]{1,0:T(8,128)(2,1)}, u32[]{:S(2)}) copy-start(bf16[1280,1536]{1,0:T(8,128)(2,1)} %basis.1) | copy-start | bytes 11796484
  12.8 1.1 %copy-start.3 = (bf16[2,128,1280]{2,1,0:T(8,128)(2,1)S(1)}, bf16[2,128,1280]{2,1,0:T(8,128)(2,1)}, u32[]{:S(2)}) copy-start(bf16[2,128,1280]{2,1,0:T(8,128)(2,1)} %param.7) | copy-start | bytes 1966084
  17.3 0.8 copy-start.4
  18.0 0.8 copy-start.9
  18.8 0.7 copy-start.10
  19.5 18.6 %collective-permute-start.5 = (bf16[1664,128]{1,0:T(8,128)(2,1)}, bf16[1664,128]{1,0:T(8,128)(2,1)}, u32[]{:S(2)}, u32[]{:S(2)}) collective-permute-start(bf16[1664,128]{1,0:T(8,128)(2,1)} %collective-permute-done.3.refs_3_), channel_id=1, source_target_pairs={{0,4},{4,8},{8,12},{12,0},{1,5},{5,9},{9,13},{13,1},{2,6},{6,10},{... | collective-permute-start | bytes 1277960 | tf_op jit(solution)/shard_map/ppermute | solution.py:25
  21.1 7.9 %collective-permute-start.7 = (f32[384,256]{1,0:T(8,128)}, f32[384,256]{1,0:T(8,128)}, u32[]{:S(2)}, u32[]{:S(2)}) collective-permute-start(f32[384,256]{1,0:T(8,128)} %get-tuple-element.49), channel_id=1, source_target_pairs={{0,1},{1,0},{2,3},{3,2},{4,5},{5,4},{6,7},{7,6},{8,9},{9,8},{10,11... | collective-permute-start | bytes 1179656 | tf_op jit(solution)/shard_map/ppermute | solution.py:39
  21.1 26.8 %collective-permute-start.8 = (f32[384,256]{1,0:T(8,128)}, f32[384,256]{1,0:T(8,128)S(1)}, u32[]{:S(2)}, u32[]{:S(2)}) collective-permute-start(f32[384,256]{1,0:T(8,128)} %copy-done.10), channel_id=1, source_target_pairs={{0,2},{1,3},{2,0},{3,1},{4,6},{5,7},{6,4},{7,5},{8,10},{9,11},{10,... | collective-permute-start | bytes 1179656 | tf_op jit(solution)/shard_map/ppermute | solution.py:39
  29.0 18.9 %collective-permute-start.9 = (f32[384,256]{1,0:T(8,128)}, f32[384,256]{1,0:T(8,128)S(1)}, u32[]{:S(2)}, u32[]{:S(2)}) collective-permute-start(f32[384,256]{1,0:T(8,128)} %copy-done.9), channel_id=1, source_target_pairs={{0,3},{1,2},{2,1},{3,0},{4,7},{5,6},{6,5},{7,4},{8,11},{9,10},{10,... | collective-permute-start | bytes 1179656 | tf_op jit(solution)/shard_map/ppermute | solution.py:39
  29.0 18.8 %collective-permute-start.1 = (bf16[1792,128]{1,0:T(8,128)(2,1)}, bf16[1792,128]{1,0:T(8,128)(2,1)S(1)}, u32[]{:S(2)}, u32[]{:S(2)}) collective-permute-start(bf16[1792,128]{1,0:T(8,128)(2,1)} %collective-permute-done.refs_4_), channel_id=1, source_target_pairs={{0,4},{4,8},{8,12},{12,0},{1,5},{5,9},{9,13},{13,1},{2,6},{6,10},{... | collective-permute-start | bytes 1376264 | tf_op jit(solution)/shard_map/ppermute | solution.py:25
  38.1 18.9 %collective-permute-start.6 = (bf16[1664,128]{1,0:T(8,128)(2,1)}, bf16[1664,128]{1,0:T(8,128)(2,1)S(1)}, u32[]{:S(2)}, u32[]{:S(2)}) collective-permute-start(bf16[1664,128]{1,0:T(8,128)(2,1)} %collective-permute-done.5.refs_1_), channel_id=1, source_target_pairs={{0,4},{4,8},{8,12},{12,0},{1,5},{5,9},{9,13},{13,1},{2,6},{6,10},{... | collective-permute-start | bytes 1277960 | tf_op jit(solution)/shard_map/ppermute | solution.py:25
  38.3 9.6 %copy-start.5 = (f32[384,256]{1,0:T(8,128)S(1)}, f32[384,256]{1,0:T(8,128)}, u32[]{:S(2)}) copy-start(f32[384,256]{1,0:T(8,128)} %copy-done.4) | copy-start | bytes 1179652
  47.9 18.1 %collective-permute-start.2 = (bf16[1792,128]{1,0:T(8,128)(2,1)S(1)}, bf16[1792,128]{1,0:T(8,128)(2,1)S(1)}, u32[]{:S(2)}, u32[]{:S(2)}) collective-permute-start(bf16[1792,128]{1,0:T(8,128)(2,1)S(1)} %collective-permute-done.1.refs_2_), channel_id=1, source_target_pairs={{0,4},{4,8},{8,12},{12,0},{1,5},{5,9},{9,13},{13,1},{2,6},{6,10},{... | collective-permute-start | bytes 1376264 | tf_op jit(solution)/shard_map/ppermute | solution.py:25
  49.0 15.3 %collective-permute-start.11 = (bf16[384,256]{1,0:T(8,128)(2,1)S(1)}, bf16[384,256]{1,0:T(8,128)(2,1)S(1)}, u32[]{:S(2)}, u32[]{:S(2)}) collective-permute-start(bf16[384,256]{1,0:T(8,128)(2,1)S(1)} %add_convert_fusion.refs_0_), channel_id=1, source_target_pairs={{0,2},{1,3},{2,0},{3,1},{4,6},{5,7},{6,4},{7,5},{8,10},{9,11},{10,... | collective-permute-start | bytes 589832 | tf_op jit(solution)/shard_map/ppermute | solution.py:39
  50.8 13.5 %collective-permute-start.12 = (bf16[384,256]{1,0:T(8,128)(2,1)S(1)}, bf16[384,256]{1,0:T(8,128)(2,1)S(1)}, u32[]{:S(2)}, u32[]{:S(2)}) collective-permute-start(bf16[384,256]{1,0:T(8,128)(2,1)S(1)} %add_convert_fusion.refs_0_), channel_id=1, source_target_pairs={{0,3},{1,2},{2,1},{3,0},{4,7},{5,6},{6,5},{7,4},{8,11},{9,10},{10,... | collective-permute-start | bytes 589832 | tf_op jit(solution)/shard_map/ppermute | solution.py:39
  57.0 7.3 %collective-permute-start.10 = (bf16[384,256]{1,0:T(8,128)(2,1)S(1)}, bf16[384,256]{1,0:T(8,128)(2,1)S(1)}, u32[]{:S(2)}, u32[]{:S(2)}) collective-permute-start(bf16[384,256]{1,0:T(8,128)(2,1)S(1)} %add_convert_fusion.refs_0_), channel_id=1, source_target_pairs={{0,1},{1,0},{2,3},{3,2},{4,5},{5,4},{6,7},{7,6},{8,9},{9,8},{10,11... | collective-permute-start | bytes 589832 | tf_op jit(solution)/shard_map/ppermute | solution.py:39
  61.2 4.8 %copy-start.6 = (s32[4]{0:T(128)S(1)}, s32[4]{0:T(128)}, u32[]{:S(2)}) copy-start(s32[4]{0:T(128)} %owner.3) | copy-start | bytes 52
  68.1 12.3 %copy-start.7 = (s32[2]{0:T(128)S(1)}, s32[2]{0:T(128)}, u32[]{:S(2)}) copy-start(s32[2]{0:T(128)} %counts.1) | copy-start | bytes 28
  68.1 12.3 %copy-start.8 = (s32[1,2]{1,0:T(1,128)S(1)}, s32[1,2]{1,0:T(1,128)}, u32[]{:S(2)}) copy-start(s32[1,2]{1,0:T(1,128)} %wanted.1) | copy-start | bytes 28
  68.1 2.0 %collective-permute-start.13 = (f32[2,512,128]{2,1,0:T(8,128)S(1)}, f32[2,512,128]{2,1,0:T(8,128)S(1)}, u32[]{:S(2)}, u32[]{:S(2)}) collective-permute-start(f32[2,512,128]{2,1,0:T(8,128)S(1)} %get-tuple-element.60), channel_id=1, source_target_pairs={{0,1},{1,0},{2,3},{3,2},{4,5},{5,4},{6,7},{7,6},{8,9},{9,8},{10,11... | collective-permute-start | bytes 1572872 | tf_op jit(solution)/shard_map/ppermute | solution.py:25
  70.8 5.6 %collective-permute-start.14 = (f32[256,128]{1,0:T(8,128)S(1)}, f32[256,128]{1,0:T(8,128)S(1)}, u32[]{:S(2)}, u32[]{:S(2)}) collective-permute-start(f32[256,128]{1,0:T(8,128)S(1)} %get-tuple-element.62), channel_id=1, source_target_pairs={{0,16},{2,18},{16,0},{18,2},{1,17},{3,19},{17,1},{19,3},{4,20},{6,... | collective-permute-start | bytes 393224 | tf_op jit(solution)/shard_map/ppermute | solution.py:339
  72.4 6.4 %collective-permute-start.15 = (f32[256,128]{1,0:T(8,128)S(1)}, f32[256,128]{1,0:T(8,128)S(1)}, u32[]{:S(2)}, u32[]{:S(2)}) collective-permute-start(f32[256,128]{1,0:T(8,128)S(1)} %get-tuple-element.63), channel_id=1, source_target_pairs={{0,2},{2,0},{16,18},{18,16},{1,3},{3,1},{17,19},{19,17},{4,6},{6,4... | collective-permute-start | bytes 393224 | tf_op jit(solution)/shard_map/ppermute | solution.py:339
  73.9 6.5 %collective-permute-start.16 = (f32[256,128]{1,0:T(8,128)S(1)}, f32[256,128]{1,0:T(8,128)S(1)}, u32[]{:S(2)}, u32[]{:S(2)}) collective-permute-start(f32[256,128]{1,0:T(8,128)S(1)} %get-tuple-element.64), channel_id=1, source_target_pairs={{0,18},{2,16},{16,2},{18,0},{1,19},{3,17},{17,3},{19,1},{4,22},{6,... | collective-permute-start | bytes 393224 | tf_op jit(solution)/shard_map/ppermute | solution.py:339
  81.3 6.6 %collective-permute-start.17 = (bf16[256,128]{1,0:T(8,128)(2,1)S(1)}, bf16[256,128]{1,0:T(8,128)(2,1)S(1)}, u32[]{:S(2)}, u32[]{:S(2)}) collective-permute-start(bf16[256,128]{1,0:T(8,128)(2,1)S(1)} %get-tuple-element.66), channel_id=1, source_target_pairs={{0,4},{4,8},{8,12},{12,0},{1,5},{5,9},{9,13},{13,1},{2,6},{6,10},{... | collective-permute-start | bytes 196616 | tf_op jit(solution)/shard_map/ppermute | solution.py:25
  81.3 7.8 %collective-permute-start.18 = (bf16[256,128]{1,0:T(8,128)(2,1)S(1)}, bf16[256,128]{1,0:T(8,128)(2,1)S(1)}, u32[]{:S(2)}, u32[]{:S(2)}) collective-permute-start(bf16[256,128]{1,0:T(8,128)(2,1)S(1)} %get-tuple-element.67), channel_id=1, source_target_pairs={{0,8},{4,12},{8,0},{12,4},{1,9},{5,13},{9,1},{13,5},{2,10},{6,14},... | collective-permute-start | bytes 196616 | tf_op jit(solution)/shard_map/ppermute | solution.py:25
  83.6 5.5 %collective-permute-start.19 = (bf16[256,128]{1,0:T(8,128)(2,1)S(1)}, bf16[256,128]{1,0:T(8,128)(2,1)S(1)}, u32[]{:S(2)}, u32[]{:S(2)}) collective-permute-start(bf16[256,128]{1,0:T(8,128)(2,1)S(1)} %get-tuple-element.68), channel_id=1, source_target_pairs={{0,12},{4,0},{8,4},{12,8},{1,13},{5,1},{9,5},{13,9},{2,14},{6,2},{... | collective-permute-start | bytes 196616 | tf_op jit(solution)/shard_map/ppermute | solution.py:25

commit v12 on v11

--- a/solution.py
+++ b/solution.py
@@ -89,7 +89,6 @@
         in_specs=[pl.BlockSpec(memory_space=pltpu.HBM)],
         out_specs=(VMEM, VMEM),
         scratch_shapes=[pltpu.SemaphoreType.DMA((2,))],
-        compiler_params=pltpu.CompilerParams(vmem_limit_bytes=VMEM_LIMIT),
     )(store)
 
 

time: 90.2 us -> 89.4 us (level)
  local copies, waits for them, and re-layouts: 8.55 us -> 6.93 us
    unnamed x22, local copies, waits for them, and re-layouts: 7.12 us -> 5.5 us
where the time goes in v12:
time: 89.4 us; the launch traced here: 89 us
  waiting for transfers between devices  42 us (47%)
  Pallas kernels  19.4 us (22%)
  starting transfers between devices  18.6 us (21%)
  local copies, waits for them, and re-layouts  6.93 us (8%)
  other arithmetic  1.85 us (2%)
    ppermute x11, waiting for transfers between devices, shift(): lax.ppermute(value, axis, [(i, (i + step) % size) for i in range(size)])  36 us
    ppermute x11, starting transfers between devices, shift(): lax.ppermute(value, axis, [(i, (i + step) % size) for i in range(size)])  11.8 us
    pallas_call x4, Pallas kernels, early_products(): pl.pallas_call(functools.partial(early_kernel, len(rows), shares), out_sh...  9.5 us
    ppermute x3, waiting for transfers between devices, on_device(): parts[i] = lax.ppermute(parts[i], ('groups', 'block'), pairs)  6.04 us
    unnamed x22, local copies, waits for them, and re-layouts  5.5 us
    ppermute x3, starting transfers between devices, on_device(): parts[i] = lax.ppermute(parts[i], ('groups', 'block'), pairs)  3.55 us
    pallas_call x1, Pallas kernels, rotate(): pl.pallas_call(functools.partial(rotate_kernel, blocks, cores), out_shape...  3.4 us
    ppermute x6, starting transfers between devices, to_neighbour(): return lax.ppermute(value, ('block', 'cores'), pairs)  3.28 us
  transfers between devices with their start and end apart: 20, of which 11 were waited for; matrix products, arithmetic and copies ran while one was open for 3% of the time, Pallas kernels for 15%

profile of v12, /device:TPU:0, one launch (start us, length us, event | category | flops | bytes accessed | tf_op | source)
XLA Modules:
  0.0 89.0 jit_solution(15009104425438589601)
XLA Ops:
  0.0 0.0 copy-start
  0.0 2.2 %shard_map.73 = (bf16[1664,128]{1,0:T(8,128)(2,1)}, bf16[1792,128]{1,0:T(8,128)(2,1)}) custom-call(bf16[6912,128]{1,0:T(8,128)(2,1)} %bitcast.9), custom_call_target="tpu_custom_call" | custom-call | tf_op jit(solution)/shard_map/pallas_call | solution.py:84
  2.2 3.1 %collective-permute-start.3 = (bf16[1664,128]{1,0:T(8,128)(2,1)}, bf16[1664,128]{1,0:T(8,128)(2,1)}, u32[]{:S(2)}, u32[]{:S(2)}) collective-permute-start(bf16[1664,128]{1,0:T(8,128)(2,1)} %get-tuple-element.38.refs_1_), channel_id=1, source_target_pairs={{0,4},{4,8},{8,12},{12,0},{1,5},{5,9},{9,13},{13,1},{2,6},{6,10},{... | collective-permute-start | bytes 1277960 | tf_op jit(solution)/shard_map/ppermute | solution.py:25
  5.3 1.3 %constant_dynamic-slice_fusion = bf16[256,3456]{1,0:T(8,128)(2,1)} fusion(bf16[256,6912]{1,0:T(8,128)(2,1)S(1)} %bitcast.6, s32[]{:T(128)S(6)} %select_n.15), kind=kLoop, calls=%fused_computation.3 | loop fusion | bytes 3538948 | tf_op jit(solution)/shard_map/dynamic_slice | solution.py:296
  6.6 1.5 %collective-permute-start.4 = (bf16[256,3456]{1,0:T(8,128)(2,1)}, bf16[256,3456]{1,0:T(8,128)(2,1)}, u32[]{:S(2)}, u32[]{:S(2)}) collective-permute-start(bf16[256,3456]{1,0:T(8,128)(2,1)} %constant_dynamic-slice_fusion), channel_id=1, source_target_pairs={{0,16},{16,0},{1,17},{17,1},{2,18},{18,2},{3,19},{19,3},{4,20},{20... | collective-permute-start | bytes 5308424 | tf_op jit(solution)/shard_map/ppermute | solution.py:25
  8.1 1.6 %collective-permute-start = (bf16[1792,128]{1,0:T(8,128)(2,1)}, bf16[1792,128]{1,0:T(8,128)(2,1)}, u32[]{:S(2)}, u32[]{:S(2)}) collective-permute-start(bf16[1792,128]{1,0:T(8,128)(2,1)} %get-tuple-element.37.refs_2_), channel_id=1, source_target_pairs={{0,4},{4,8},{8,12},{12,0},{1,5},{5,9},{9,13},{13,1},{2,6},{6,10},{... | collective-permute-start | bytes 1376264 | tf_op jit(solution)/shard_map/ppermute | solution.py:25
  9.7 0.1 pad_add_fusion.place
  9.8 2.1 %copy-done.1 = bf16[1280,1536]{1,0:T(8,128)(2,1)S(1)} copy-done((bf16[1280,1536]{1,0:T(8,128)(2,1)S(1)}, bf16[1280,1536]{1,0:T(8,128)(2,1)}, u32[]{:S(2)}) %copy-start.1) | copy-done | bytes 3932184
  11.9 1.1 %copy-done.3 = bf16[2,128,1280]{2,1,0:T(8,128)(2,1)S(1)} copy-done((bf16[2,128,1280]{2,1,0:T(8,128)(2,1)S(1)}, bf16[2,128,1280]{2,1,0:T(8,128)(2,1)}, u32[]{:S(2)}) %copy-start.3) | copy-done | bytes 655384
  13.0 3.4 %shard_map.74 = (f32[384,256]{1,0:T(8,128)S(1)}, f32[384,256]{1,0:T(8,128)}, f32[384,256]{1,0:T(8,128)S(1)}, f32[384,256]{1,0:T(8,128)S(1)}) custom-call(s32[3]{0:T(128)S(1)} %pad_add_fusion.place, bf16[256,1280]{1,0:T(8,128)(2,1)S(1)} %bitcast.8, bf16[1280,1536]{1,0:T(8,128)(2,1)S(1)} %copy-done.1), custom_call_target="tpu_custom_call" | custom-call | tf_op jit(solution)/shard_map/pallas_call | solution.py:114
  16.4 0.8 copy-done.4
  17.2 0.8 copy-done.9
  17.9 0.7 copy-done.10
  18.7 0.0 collective-permute-done.3.refs_3_
  18.7 1.6 %collective-permute-start.5 = (bf16[1664,128]{1,0:T(8,128)(2,1)}, bf16[1664,128]{1,0:T(8,128)(2,1)}, u32[]{:S(2)}, u32[]{:S(2)}) collective-permute-start(bf16[1664,128]{1,0:T(8,128)(2,1)} %collective-permute-done.3.refs_3_), channel_id=1, source_target_pairs={{0,4},{4,8},{8,12},{12,0},{1,5},{5,9},{9,13},{13,1},{2,6},{6,10},{... | collective-permute-start | bytes 1277960 | tf_op jit(solution)/shard_map/ppermute | solution.py:25
  20.2 0.0 collective-permute-start.7
  20.3 1.5 %collective-permute-start.8 = (f32[384,256]{1,0:T(8,128)}, f32[384,256]{1,0:T(8,128)S(1)}, u32[]{:S(2)}, u32[]{:S(2)}) collective-permute-start(f32[384,256]{1,0:T(8,128)} %copy-done.10), channel_id=1, source_target_pairs={{0,2},{1,3},{2,0},{3,1},{4,6},{5,7},{6,4},{7,5},{8,10},{9,11},{10,... | collective-permute-start | bytes 1179656 | tf_op jit(solution)/shard_map/ppermute | solution.py:39
  21.7 6.4 %collective-permute-done.refs_4_ = bf16[1792,128]{1,0:T(8,128)(2,1)} collective-permute-done((bf16[1792,128]{1,0:T(8,128)(2,1)}, bf16[1792,128]{1,0:T(8,128)(2,1)}, u32[]{:S(2)}, u32[]{:S(2)}) %collective-permute-start) | collective-permute-done | bytes 458784 | tf_op jit(solution)/shard_map/ppermute | solution.py:25
  28.1 0.0 collective-permute-start.9
  28.1 0.0 collective-permute-done.7
  28.1 0.0 collective-permute-start.1
  28.2 9.1 %collective-permute-done.5.refs_1_ = bf16[1664,128]{1,0:T(8,128)(2,1)} collective-permute-done((bf16[1664,128]{1,0:T(8,128)(2,1)}, bf16[1664,128]{1,0:T(8,128)(2,1)}, u32[]{:S(2)}, u32[]{:S(2)}) %collective-permute-start.5) | collective-permute-done | bytes 426016 | tf_op jit(solution)/shard_map/ppermute | solution.py:25
  37.3 0.0 collective-permute-start.6
  37.3 0.1 constant_dynamic-slice_fusion.1.refs_0_
  37.4 2.4 %shard_map.75.refs_2_.refs_0_ = f32[2,256,128]{2,1,0:T(8,128)S(1)} custom-call(bf16[256,3456]{1,0:T(8,128)(2,1)S(1)} %constant_dynamic-slice_fusion.1.refs_0_, bf16[1664,128]{1,0:T(8,128)(2,1)S(1)} %copy-done.2, bf16[1792,128]{1,0:T(8,128)(2,1)} %get-tuple-element.37.refs_2_, bf16[1664,128]{1,0:T(8,128)(2,1)} %collective-permute-done.3.refs_3_, ...), custom_call_target="tpu_custom_call" | custom-call | flops 452984832 | bytes 3538944 | tf_op jit(solution)/shard_map/pallas_call | solution.py:155
  39.8 7.1 %collective-permute-done.1.refs_2_ = bf16[1792,128]{1,0:T(8,128)(2,1)S(1)} collective-permute-done((bf16[1792,128]{1,0:T(8,128)(2,1)}, bf16[1792,128]{1,0:T(8,128)(2,1)S(1)}, u32[]{:S(2)}, u32[]{:S(2)}) %collective-permute-start.1) | collective-permute-done | bytes 458784 | tf_op jit(solution)/shard_map/ppermute | solution.py:25
  47.0 0.0 collective-permute-start.2
  47.0 0.0 collective-permute-done.8
  47.0 0.0 collective-permute-done.9
  47.0 1.1 %add_convert_fusion.refs_0_ = bf16[384,256]{1,0:T(8,128)(2,1)S(1)} fusion(f32[384,256]{1,0:T(8,128)S(1)} %collective-permute-done.9, f32[384,256]{1,0:T(8,128)S(1)} %collective-permute-done.8, f32[384,256]{1,0:T(8,128)S(1)} %copy-done.5, f32[384,256]{1,0:T(8,128)} %collective-permute-done.7), kind=kLoop, calls=%fused_computation | loop fusion | flops 393216 | bytes 1769472 | tf_op jit(solution)/shard_map/convert_element_type | solution.py:319
  48.1 1.8 %collective-permute-start.11 = (bf16[384,256]{1,0:T(8,128)(2,1)S(1)}, bf16[384,256]{1,0:T(8,128)(2,1)S(1)}, u32[]{:S(2)}, u32[]{:S(2)}) collective-permute-start(bf16[384,256]{1,0:T(8,128)(2,1)S(1)} %add_convert_fusion.refs_0_), channel_id=1, source_target_pairs={{0,2},{1,3},{2,0},{3,1},{4,6},{5,7},{6,4},{7,5},{8,10},{9,11},{10,... | collective-permute-start | bytes 589832 | tf_op jit(solution)/shard_map/ppermute | solution.py:39
  49.9 0.0 collective-permute-start.12
  49.9 6.2 %collective-permute-done.6.refs_3_ = bf16[1664,128]{1,0:T(8,128)(2,1)S(1)} collective-permute-done((bf16[1664,128]{1,0:T(8,128)(2,1)}, bf16[1664,128]{1,0:T(8,128)(2,1)S(1)}, u32[]{:S(2)}, u32[]{:S(2)}) %collective-permute-start.6) | collective-permute-done | bytes 426016 | tf_op jit(solution)/shard_map/ppermute | solution.py:25
  56.1 0.0 collective-permute-start.10
  56.1 1.8 %shard_map.77.refs_4_.refs_2_ = f32[2,256,128]{2,1,0:T(8,128)S(1)} custom-call(bf16[256,3456]{1,0:T(8,128)(2,1)S(1)} %constant_dynamic-slice_fusion.1.refs_0_, bf16[1664,128]{1,0:T(8,128)(2,1)} %collective-permute-done.5.refs_1_, bf16[1792,128]{1,0:T(8,128)(2,1)S(1)} %collective-permute-done.1.refs_2_, bf16[1664,128]{1,0:T(8,128)(2,1)S(1)} %collective-permute-done.6.refs_3_), custom_call_target="tpu_custom_call" | custom-call | flops 335544320 | bytes 2621440 | tf_op jit(solution)/shard_map/pallas_call | solution.py:155
  58.0 0.0 collective-permute-done.4.refs_0_.refs_1_
  58.0 2.4 %shard_map.78.refs_5_.refs_3_ = f32[2,256,128]{2,1,0:T(8,128)S(1)} custom-call(bf16[256,3456]{1,0:T(8,128)(2,1)} %collective-permute-done.4.refs_0_.refs_1_, bf16[1664,128]{1,0:T(8,128)(2,1)} %collective-permute-done.5.refs_1_, bf16[1792,128]{1,0:T(8,128)(2,1)S(1)} %collective-permute-done.1.refs_2_, bf16[1664,128]{1,0:T(8,128)(2,1)S(1)} %collective-permute-done.6.refs_3_), custom_call_target="tpu_custom_call" | custom-call | flops 335544320 | bytes 2621440 | tf_op jit(solution)/shard_map/pallas_call | solution.py:155
  60.3 0.0 copy-start.6
  60.4 2.9 %shard_map.76.refs_3_.refs_1_ = f32[2,256,128]{2,1,0:T(8,128)S(1)} custom-call(bf16[256,3456]{1,0:T(8,128)(2,1)} %collective-permute-done.4.refs_0_.refs_1_, bf16[1664,128]{1,0:T(8,128)(2,1)S(1)} %copy-done.2, bf16[1792,128]{1,0:T(8,128)(2,1)} %get-tuple-element.37.refs_2_, bf16[1664,128]{1,0:T(8,128)(2,1)} %collective-permute-done.3.refs_3_, ...), custom_call_target="tpu_custom_call" | custom-call | flops 452984832 | bytes 3538944 | tf_op jit(solution)/shard_map/pallas_call | solution.py:155
  63.3 0.0 collective-permute-done.11.refs_2_
  63.3 0.0 collective-permute-done.12.refs_3_
  63.3 0.0 collective-permute-done.10.refs_1_
  63.3 0.6 shard_map.79.act
  63.9 1.2 %collective-permute-done.2.held = bf16[1792,128]{1,0:T(8,128)(2,1)S(1)} collective-permute-done((bf16[1792,128]{1,0:T(8,128)(2,1)S(1)}, bf16[1792,128]{1,0:T(8,128)(2,1)S(1)}, u32[]{:S(2)}, u32[]{:S(2)}) %collective-permute-start.2) | collective-permute-done | bytes 458784 | tf_op jit(solution)/shard_map/ppermute | solution.py:25
  65.1 2.1 %shard_map.80 = (f32[512,128]{1,0:T(8,128)S(1)}, f32[2,512,128]{2,1,0:T(8,128)S(1)}) custom-call(s32[4]{0:T(128)S(1)} %copy-done.6, s32[3]{0:T(128)S(1)} %pad_add_fusion.place, bf16[1792,128]{1,0:T(8,128)(2,1)S(1)} %collective-permute-done.2.held, bf16[256,3456]{1,0:T(8,128)(2,1)S(1)} %constant_dynamic-slice_fusion.1.refs_0_, ...), custom_call_target="tpu_custom_call" | custom-call | tf_op jit(solution)/shard_map/pallas_call | solution.py:200
  67.2 0.0 copy-start.7
  67.3 0.0 copy-start.8
  67.3 0.1 collective-permute-start.13
  67.3 1.9 %collective-permute-done.13.refs_4_ = f32[2,512,128]{2,1,0:T(8,128)S(1)} collective-permute-done((f32[2,512,128]{2,1,0:T(8,128)S(1)}, f32[2,512,128]{2,1,0:T(8,128)S(1)}, u32[]{:S(2)}, u32[]{:S(2)}) %collective-permute-start.13) | collective-permute-done | bytes 524320 | tf_op jit(solution)/shard_map/ppermute | solution.py:25
  69.2 0.7 shard_map.81
  69.9 1.6 %collective-permute-start.14 = (f32[256,128]{1,0:T(8,128)S(1)}, f32[256,128]{1,0:T(8,128)S(1)}, u32[]{:S(2)}, u32[]{:S(2)}) collective-permute-start(f32[256,128]{1,0:T(8,128)S(1)} %get-tuple-element.62), channel_id=1, source_target_pairs={{0,16},{2,18},{16,0},{18,2},{1,17},{3,19},{17,1},{19,3},{4,20},{6,... | collective-permute-start | bytes 393224 | tf_op jit(solution)/shard_map/ppermute | solution.py:338
  71.5 1.5 %collective-permute-start.15 = (f32[256,128]{1,0:T(8,128)S(1)}, f32[256,128]{1,0:T(8,128)S(1)}, u32[]{:S(2)}, u32[]{:S(2)}) collective-permute-start(f32[256,128]{1,0:T(8,128)S(1)} %get-tuple-element.63), channel_id=1, source_target_pairs={{0,2},{2,0},{16,18},{18,16},{1,3},{3,1},{17,19},{19,17},{4,6},{6,4... | collective-permute-start | bytes 393224 | tf_op jit(solution)/shard_map/ppermute | solution.py:338
  73.0 0.5 collective-permute-start.16
  73.5 2.0 %collective-permute-done.14.refs_1_ = f32[256,128]{1,0:T(8,128)S(1)} collective-permute-done((f32[256,128]{1,0:T(8,128)S(1)}, f32[256,128]{1,0:T(8,128)S(1)}, u32[]{:S(2)}, u32[]{:S(2)}) %collective-permute-start.14) | collective-permute-done | bytes 131104 | tf_op jit(solution)/shard_map/ppermute | solution.py:338
  75.5 2.4 %collective-permute-done.15.refs_2_ = f32[256,128]{1,0:T(8,128)S(1)} collective-permute-done((f32[256,128]{1,0:T(8,128)S(1)}, f32[256,128]{1,0:T(8,128)S(1)}, u32[]{:S(2)}, u32[]{:S(2)}) %collective-permute-start.15) | collective-permute-done | bytes 131104 | tf_op jit(solution)/shard_map/ppermute | solution.py:338
  77.9 1.6 %collective-permute-done.16.refs_3_ = f32[256,128]{1,0:T(8,128)S(1)} collective-permute-done((f32[256,128]{1,0:T(8,128)S(1)}, f32[256,128]{1,0:T(8,128)S(1)}, u32[]{:S(2)}, u32[]{:S(2)}) %collective-permute-start.16) | collective-permute-done | bytes 131104 | tf_op jit(solution)/shard_map/ppermute | solution.py:338
  79.5 0.9 shard_map.82
  80.4 0.1 collective-permute-start.17
  80.5 2.3 %collective-permute-start.18 = (bf16[256,128]{1,0:T(8,128)(2,1)S(1)}, bf16[256,128]{1,0:T(8,128)(2,1)S(1)}, u32[]{:S(2)}, u32[]{:S(2)}) collective-permute-start(bf16[256,128]{1,0:T(8,128)(2,1)S(1)} %get-tuple-element.67), channel_id=1, source_target_pairs={{0,8},{4,12},{8,0},{12,4},{1,9},{5,13},{9,1},{13,5},{2,10},{6,14},... | collective-permute-start | bytes 196616 | tf_op jit(solution)/shard_map/ppermute | solution.py:25
  82.7 1.5 %collective-permute-start.19 = (bf16[256,128]{1,0:T(8,128)(2,1)S(1)}, bf16[256,128]{1,0:T(8,128)(2,1)S(1)}, u32[]{:S(2)}, u32[]{:S(2)}) collective-permute-start(bf16[256,128]{1,0:T(8,128)(2,1)S(1)} %get-tuple-element.68), channel_id=1, source_target_pairs={{0,12},{4,0},{8,4},{12,8},{1,13},{5,1},{9,5},{13,9},{2,14},{6,2},{... | collective-permute-start | bytes 196616 | tf_op jit(solution)/shard_map/ppermute | solution.py:25
  84.3 2.7 %collective-permute-done.17 = bf16[256,128]{1,0:T(8,128)(2,1)S(1)} collective-permute-done((bf16[256,128]{1,0:T(8,128)(2,1)S(1)}, bf16[256,128]{1,0:T(8,128)(2,1)S(1)}, u32[]{:S(2)}, u32[]{:S(2)}) %collective-permute-start.17) | collective-permute-done | bytes 65568 | tf_op jit(solution)/shard_map/ppermute | solution.py:25
  87.0 1.3 %collective-permute-done.18 = bf16[256,128]{1,0:T(8,128)(2,1)S(1)} collective-permute-done((bf16[256,128]{1,0:T(8,128)(2,1)S(1)}, bf16[256,128]{1,0:T(8,128)(2,1)S(1)}, u32[]{:S(2)}, u32[]{:S(2)}) %collective-permute-start.18) | collective-permute-done | bytes 65568 | tf_op jit(solution)/shard_map/ppermute | solution.py:25
  88.3 0.0 collective-permute-done.19
  88.3 0.7 add_multiply_fusion
  (13 shorter events, 0.0 us)
Async XLA Ops:
  0.0 5.3 %copy-start = (bf16[2,128,6912]{2,1,0:T(8,128)(2,1)S(1)}, bf16[2,128,6912]{2,1,0:T(8,128)(2,1)}, u32[]{:S(2)}) copy-start(bf16[2,128,6912]{2,1,0:T(8,128)(2,1)} %param.8) | copy-start | bytes 10616836
  2.2 16.4 %collective-permute-start.3 = (bf16[1664,128]{1,0:T(8,128)(2,1)}, bf16[1664,128]{1,0:T(8,128)(2,1)}, u32[]{:S(2)}, u32[]{:S(2)}) collective-permute-start(bf16[1664,128]{1,0:T(8,128)(2,1)} %get-tuple-element.38.refs_1_), channel_id=1, source_target_pairs={{0,4},{4,8},{8,12},{12,0},{1,5},{5,9},{9,13},{13,1},{2,6},{6,10},{... | collective-permute-start | bytes 1277960 | tf_op jit(solution)/shard_map/ppermute | solution.py:25
  6.6 51.3 %collective-permute-start.4 = (bf16[256,3456]{1,0:T(8,128)(2,1)}, bf16[256,3456]{1,0:T(8,128)(2,1)}, u32[]{:S(2)}, u32[]{:S(2)}) collective-permute-start(bf16[256,3456]{1,0:T(8,128)(2,1)} %constant_dynamic-slice_fusion), channel_id=1, source_target_pairs={{0,16},{16,0},{1,17},{17,1},{2,18},{18,2},{3,19},{19,3},{4,20},{20... | collective-permute-start | bytes 5308424 | tf_op jit(solution)/shard_map/ppermute | solution.py:25
  8.1 20.0 %collective-permute-start = (bf16[1792,128]{1,0:T(8,128)(2,1)}, bf16[1792,128]{1,0:T(8,128)(2,1)}, u32[]{:S(2)}, u32[]{:S(2)}) collective-permute-start(bf16[1792,128]{1,0:T(8,128)(2,1)} %get-tuple-element.37.refs_2_), channel_id=1, source_target_pairs={{0,4},{4,8},{8,12},{12,0},{1,5},{5,9},{9,13},{13,1},{2,6},{6,10},{... | collective-permute-start | bytes 1376264 | tf_op jit(solution)/shard_map/ppermute | solution.py:25
  9.8 2.1 %copy-start.1 = (bf16[1280,1536]{1,0:T(8,128)(2,1)S(1)}, bf16[1280,1536]{1,0:T(8,128)(2,1)}, u32[]{:S(2)}) copy-start(bf16[1280,1536]{1,0:T(8,128)(2,1)} %basis.1) | copy-start | bytes 11796484
  11.9 1.1 %copy-start.3 = (bf16[2,128,1280]{2,1,0:T(8,128)(2,1)S(1)}, bf16[2,128,1280]{2,1,0:T(8,128)(2,1)}, u32[]{:S(2)}) copy-start(bf16[2,128,1280]{2,1,0:T(8,128)(2,1)} %param.7) | copy-start | bytes 1966084
  16.4 0.8 copy-start.4
  17.2 0.8 copy-start.9
  17.9 0.7 copy-start.10
  18.7 18.6 %collective-permute-start.5 = (bf16[1664,128]{1,0:T(8,128)(2,1)}, bf16[1664,128]{1,0:T(8,128)(2,1)}, u32[]{:S(2)}, u32[]{:S(2)}) collective-permute-start(bf16[1664,128]{1,0:T(8,128)(2,1)} %collective-permute-done.3.refs_3_), channel_id=1, source_target_pairs={{0,4},{4,8},{8,12},{12,0},{1,5},{5,9},{9,13},{13,1},{2,6},{6,10},{... | collective-permute-start | bytes 1277960 | tf_op jit(solution)/shard_map/ppermute | solution.py:25
  20.2 7.9 %collective-permute-start.7 = (f32[384,256]{1,0:T(8,128)}, f32[384,256]{1,0:T(8,128)}, u32[]{:S(2)}, u32[]{:S(2)}) collective-permute-start(f32[384,256]{1,0:T(8,128)} %get-tuple-element.49), channel_id=1, source_target_pairs={{0,1},{1,0},{2,3},{3,2},{4,5},{5,4},{6,7},{7,6},{8,9},{9,8},{10,11... | collective-permute-start | bytes 1179656 | tf_op jit(solution)/shard_map/ppermute | solution.py:39
  20.3 17.2 %copy-start.2 = (bf16[1664,128]{1,0:T(8,128)(2,1)S(1)}, bf16[1664,128]{1,0:T(8,128)(2,1)}, u32[]{:S(2)}) copy-start(bf16[1664,128]{1,0:T(8,128)(2,1)} %get-tuple-element.38.refs_1_) | copy-start | bytes 1277956
  20.3 26.8 %collective-permute-start.8 = (f32[384,256]{1,0:T(8,128)}, f32[384,256]{1,0:T(8,128)S(1)}, u32[]{:S(2)}, u32[]{:S(2)}) collective-permute-start(f32[384,256]{1,0:T(8,128)} %copy-done.10), channel_id=1, source_target_pairs={{0,2},{1,3},{2,0},{3,1},{4,6},{5,7},{6,4},{7,5},{8,10},{9,11},{10,... | collective-permute-start | bytes 1179656 | tf_op jit(solution)/shard_map/ppermute | solution.py:39
  28.1 18.9 %collective-permute-start.9 = (f32[384,256]{1,0:T(8,128)}, f32[384,256]{1,0:T(8,128)S(1)}, u32[]{:S(2)}, u32[]{:S(2)}) collective-permute-start(f32[384,256]{1,0:T(8,128)} %copy-done.9), channel_id=1, source_target_pairs={{0,3},{1,2},{2,1},{3,0},{4,7},{5,6},{6,5},{7,4},{8,11},{9,10},{10,... | collective-permute-start | bytes 1179656 | tf_op jit(solution)/shard_map/ppermute | solution.py:39
  28.1 18.8 %collective-permute-start.1 = (bf16[1792,128]{1,0:T(8,128)(2,1)}, bf16[1792,128]{1,0:T(8,128)(2,1)S(1)}, u32[]{:S(2)}, u32[]{:S(2)}) collective-permute-start(bf16[1792,128]{1,0:T(8,128)(2,1)} %collective-permute-done.refs_4_), channel_id=1, source_target_pairs={{0,4},{4,8},{8,12},{12,0},{1,5},{5,9},{9,13},{13,1},{2,6},{6,10},{... | collective-permute-start | bytes 1376264 | tf_op jit(solution)/shard_map/ppermute | solution.py:25
  37.3 18.9 %collective-permute-start.6 = (bf16[1664,128]{1,0:T(8,128)(2,1)}, bf16[1664,128]{1,0:T(8,128)(2,1)S(1)}, u32[]{:S(2)}, u32[]{:S(2)}) collective-permute-start(bf16[1664,128]{1,0:T(8,128)(2,1)} %collective-permute-done.5.refs_1_), channel_id=1, source_target_pairs={{0,4},{4,8},{8,12},{12,0},{1,5},{5,9},{9,13},{13,1},{2,6},{6,10},{... | collective-permute-start | bytes 1277960 | tf_op jit(solution)/shard_map/ppermute | solution.py:25
  37.4 9.6 %copy-start.5 = (f32[384,256]{1,0:T(8,128)S(1)}, f32[384,256]{1,0:T(8,128)}, u32[]{:S(2)}) copy-start(f32[384,256]{1,0:T(8,128)} %copy-done.4) | copy-start | bytes 1179652
  47.0 18.1 %collective-permute-start.2 = (bf16[1792,128]{1,0:T(8,128)(2,1)S(1)}, bf16[1792,128]{1,0:T(8,128)(2,1)S(1)}, u32[]{:S(2)}, u32[]{:S(2)}) collective-permute-start(bf16[1792,128]{1,0:T(8,128)(2,1)S(1)} %collective-permute-done.1.refs_2_), channel_id=1, source_target_pairs={{0,4},{4,8},{8,12},{12,0},{1,5},{5,9},{9,13},{13,1},{2,6},{6,10},{... | collective-permute-start | bytes 1376264 | tf_op jit(solution)/shard_map/ppermute | solution.py:25
  48.1 15.1 %collective-permute-start.11 = (bf16[384,256]{1,0:T(8,128)(2,1)S(1)}, bf16[384,256]{1,0:T(8,128)(2,1)S(1)}, u32[]{:S(2)}, u32[]{:S(2)}) collective-permute-start(bf16[384,256]{1,0:T(8,128)(2,1)S(1)} %add_convert_fusion.refs_0_), channel_id=1, source_target_pairs={{0,2},{1,3},{2,0},{3,1},{4,6},{5,7},{6,4},{7,5},{8,10},{9,11},{10,... | collective-permute-start | bytes 589832 | tf_op jit(solution)/shard_map/ppermute | solution.py:39
  49.9 13.4 %collective-permute-start.12 = (bf16[384,256]{1,0:T(8,128)(2,1)S(1)}, bf16[384,256]{1,0:T(8,128)(2,1)S(1)}, u32[]{:S(2)}, u32[]{:S(2)}) collective-permute-start(bf16[384,256]{1,0:T(8,128)(2,1)S(1)} %add_convert_fusion.refs_0_), channel_id=1, source_target_pairs={{0,3},{1,2},{2,1},{3,0},{4,7},{5,6},{6,5},{7,4},{8,11},{9,10},{10,... | collective-permute-start | bytes 589832 | tf_op jit(solution)/shard_map/ppermute | solution.py:39
  56.1 7.2 %collective-permute-start.10 = (bf16[384,256]{1,0:T(8,128)(2,1)S(1)}, bf16[384,256]{1,0:T(8,128)(2,1)S(1)}, u32[]{:S(2)}, u32[]{:S(2)}) collective-permute-start(bf16[384,256]{1,0:T(8,128)(2,1)S(1)} %add_convert_fusion.refs_0_), channel_id=1, source_target_pairs={{0,1},{1,0},{2,3},{3,2},{4,5},{5,4},{6,7},{7,6},{8,9},{9,8},{10,11... | collective-permute-start | bytes 589832 | tf_op jit(solution)/shard_map/ppermute | solution.py:39
  60.3 4.8 %copy-start.6 = (s32[4]{0:T(128)S(1)}, s32[4]{0:T(128)}, u32[]{:S(2)}) copy-start(s32[4]{0:T(128)} %owner.3) | copy-start | bytes 52
  67.2 12.3 %copy-start.7 = (s32[2]{0:T(128)S(1)}, s32[2]{0:T(128)}, u32[]{:S(2)}) copy-start(s32[2]{0:T(128)} %counts.1) | copy-start | bytes 28
  67.3 12.3 %copy-start.8 = (s32[1,2]{1,0:T(1,128)S(1)}, s32[1,2]{1,0:T(1,128)}, u32[]{:S(2)}) copy-start(s32[1,2]{1,0:T(1,128)} %wanted.1) | copy-start | bytes 28
  67.3 2.0 %collective-permute-start.13 = (f32[2,512,128]{2,1,0:T(8,128)S(1)}, f32[2,512,128]{2,1,0:T(8,128)S(1)}, u32[]{:S(2)}, u32[]{:S(2)}) collective-permute-start(f32[2,512,128]{2,1,0:T(8,128)S(1)} %get-tuple-element.60), channel_id=1, source_target_pairs={{0,1},{1,0},{2,3},{3,2},{4,5},{5,4},{6,7},{7,6},{8,9},{9,8},{10,11... | collective-permute-start | bytes 1572872 | tf_op jit(solution)/shard_map/ppermute | solution.py:25
  69.9 5.6 %collective-permute-start.14 = (f32[256,128]{1,0:T(8,128)S(1)}, f32[256,128]{1,0:T(8,128)S(1)}, u32[]{:S(2)}, u32[]{:S(2)}) collective-permute-start(f32[256,128]{1,0:T(8,128)S(1)} %get-tuple-element.62), channel_id=1, source_target_pairs={{0,16},{2,18},{16,0},{18,2},{1,17},{3,19},{17,1},{19,3},{4,20},{6,... | collective-permute-start | bytes 393224 | tf_op jit(solution)/shard_map/ppermute | solution.py:338
  71.5 6.4 %collective-permute-start.15 = (f32[256,128]{1,0:T(8,128)S(1)}, f32[256,128]{1,0:T(8,128)S(1)}, u32[]{:S(2)}, u32[]{:S(2)}) collective-permute-start(f32[256,128]{1,0:T(8,128)S(1)} %get-tuple-element.63), channel_id=1, source_target_pairs={{0,2},{2,0},{16,18},{18,16},{1,3},{3,1},{17,19},{19,17},{4,6},{6,4... | collective-permute-start | bytes 393224 | tf_op jit(solution)/shard_map/ppermute | solution.py:338
  73.0 6.5 %collective-permute-start.16 = (f32[256,128]{1,0:T(8,128)S(1)}, f32[256,128]{1,0:T(8,128)S(1)}, u32[]{:S(2)}, u32[]{:S(2)}) collective-permute-start(f32[256,128]{1,0:T(8,128)S(1)} %get-tuple-element.64), channel_id=1, source_target_pairs={{0,18},{2,16},{16,2},{18,0},{1,19},{3,17},{17,3},{19,1},{4,22},{6,... | collective-permute-start | bytes 393224 | tf_op jit(solution)/shard_map/ppermute | solution.py:338
  80.4 6.6 %collective-permute-start.17 = (bf16[256,128]{1,0:T(8,128)(2,1)S(1)}, bf16[256,128]{1,0:T(8,128)(2,1)S(1)}, u32[]{:S(2)}, u32[]{:S(2)}) collective-permute-start(bf16[256,128]{1,0:T(8,128)(2,1)S(1)} %get-tuple-element.66), channel_id=1, source_target_pairs={{0,4},{4,8},{8,12},{12,0},{1,5},{5,9},{9,13},{13,1},{2,6},{6,10},{... | collective-permute-start | bytes 196616 | tf_op jit(solution)/shard_map/ppermute | solution.py:25
  80.5 7.8 %collective-permute-start.18 = (bf16[256,128]{1,0:T(8,128)(2,1)S(1)}, bf16[256,128]{1,0:T(8,128)(2,1)S(1)}, u32[]{:S(2)}, u32[]{:S(2)}) collective-permute-start(bf16[256,128]{1,0:T(8,128)(2,1)S(1)} %get-tuple-element.67), channel_id=1, source_target_pairs={{0,8},{4,12},{8,0},{12,4},{1,9},{5,13},{9,1},{13,5},{2,10},{6,14},... | collective-permute-start | bytes 196616 | tf_op jit(solution)/shard_map/ppermute | solution.py:25
  82.7 5.6 %collective-permute-start.19 = (bf16[256,128]{1,0:T(8,128)(2,1)S(1)}, bf16[256,128]{1,0:T(8,128)(2,1)S(1)}, u32[]{:S(2)}, u32[]{:S(2)}) collective-permute-start(bf16[256,128]{1,0:T(8,128)(2,1)S(1)} %get-tuple-element.68), channel_id=1, source_target_pairs={{0,12},{4,0},{8,4},{12,8},{1,13},{5,1},{9,5},{13,9},{2,14},{6,2},{... | collective-permute-start | bytes 196616 | tf_op jit(solution)/shard_map/ppermute | solution.py:25

commit v13 on v10

--- a/solution.py
+++ b/solution.py
@@ -297,9 +297,13 @@
     act_parts = gather_act(act.astype(BF16), (first[-1], early[0]))
     rest = [early_products(part, pieces[-4:-1], shares) for part in rows]
     act_rot_t = assemble(after(place, *early, *rest), act_parts, blocks, cores)
-    last, act_rot_t, *done = lax.optimization_barrier((pieces[-1], act_rot_t, *early, *rest))
-    early, rest = done[: len(rows)], done[len(rows) :]
-    last, *sends = pack(owner_slot, place, rows, last, cut, early, rest, blocks, cores)
+    ends = [part[0][:, cut:] for part in rows]
+    last, act_rot_t, *done = lax.optimization_barrier(
+        (pieces[-1], act_rot_t, *early, *rest, *ends)
+    )
+    early, rest, ends = (done[i * len(rows) : (i + 1) * len(rows)] for i in range(3))
+    ends = [[part] for part in ends]
+    last, *sends = pack(owner_slot, place, ends, last, 0, early, rest, blocks, cores)
     came = [shift(send, "cores", step) for step, send in enumerate(sends, 1)]
     parts = join(owner_slot, place, last, early, rest, came, blocks, cores)
 

time: 89 us -> 89 us (level)
  waiting for transfers between devices: 45.8 us -> 38.8 us
  local copies, waits for them, and re-layouts: 8.43 us -> 12 us
  starting transfers between devices: 17.8 us -> 19.1 us
  other arithmetic: 0.87 us -> 1.88 us
  Pallas kernels: 15.6 us -> 16.5 us
    ppermute x11, waiting for transfers between devices: 39.7 us -> 32.5 us  [shift(): lax.ppermute(value, axis, [(i, (i + step) % size) for i in range(size)])]
    unnamed x12 -> x20, local copies, waits for them, and re-layouts: 3.22 us -> 5.49 us
    slice x0 -> x2, local copies, waits for them, and re-layouts: none -> 1.3 us  [on_device(): ends = [part[0][:, cut:] for part in rows]]
    ppermute x11, starting transfers between devices: 11 us -> 12.3 us  [shift(): lax.ppermute(value, axis, [(i, (i + step) % size) for i in range(size)])]
    pallas_call x4, Pallas kernels: 8.68 us -> 9.79 us  [early_products(): pl.pallas_call(functools.partial(early_kernel, len(rows), shares), out_sh...]
    convert_element_type x1, other arithmetic: 0.1 us -> 1.11 us  [on_device(): act_parts = gather_act(act.astype(BF16), (first[-1], early[0]))]
    pallas_call x1, Pallas kernels: 2.13 us -> 1.2 us  [pack(): pl.pallas_call(functools.partial(pack_kernel, positions + 2, cores, parts...]
  transfers between devices with their start and end apart: 20 -> 20, of which waited for: 12 -> 10; matrix products, arithmetic and copies ran while one was open for 4% -> 6% of each run, Pallas kernels for 13% -> 16%
where the time goes in v13:
time: 89 us; the launch traced here: 88.5 us
  waiting for transfers between devices  38.8 us (44%)
  starting transfers between devices  19.1 us (21%)
  Pallas kernels  16.5 us (19%)
  local copies, waits for them, and re-layouts  12 us (13%)
  other arithmetic  1.88 us (2%)
    ppermute x11, waiting for transfers between devices, shift(): lax.ppermute(value, axis, [(i, (i + step) % size) for i in range(size)])  32.5 us
    ppermute x11, starting transfers between devices, shift(): lax.ppermute(value, axis, [(i, (i + step) % size) for i in range(size)])  12.3 us
    pallas_call x4, Pallas kernels, early_products(): pl.pallas_call(functools.partial(early_kernel, len(rows), shares), out_sh...  9.79 us
    ppermute x3, waiting for transfers between devices, on_device(): parts[i] = lax.ppermute(parts[i], ('groups', 'block'), pairs)  6.36 us
    unnamed x20, local copies, waits for them, and re-layouts  5.49 us
    dynamic_slice x2, local copies, waits for them, and re-layouts, on_device(): lax.dynamic_slice_in_dim(basis_store[0], group * part_features + start, s...  3.75 us
    ppermute x3, starting transfers between devices, on_device(): parts[i] = lax.ppermute(parts[i], ('groups', 'block'), pairs)  3.57 us
    pallas_call x1, Pallas kernels, rotate(): pl.pallas_call(functools.partial(rotate_kernel, blocks, cores), out_shape...  3.4 us
  transfers between devices with their start and end apart: 20, of which 10 were waited for; matrix products, arithmetic and copies ran while one was open for 6% of the time, Pallas kernels for 16%

profile of v13, /device:TPU:0, one launch (start us, length us, event | category | flops | bytes accessed | tf_op | source)
XLA Modules:
  0.0 88.5 jit_solution(7340188817140760665)
XLA Ops:
  0.0 1.9 %dynamic-slice_bitcast_fusion.1.refs_1_ = bf16[1664,128]{1,0:T(8,128)(2,1)} fusion(bf16[1,6912,128]{2,1,0:T(8,128)(2,1)} %param.11, s32[]{:T(128)S(6)} %select_n.18), kind=kLoop, calls=%fused_computation.1 | loop fusion | bytes 851972 | tf_op jit(solution)/shard_map/dynamic_slice | solution.py:268
  1.9 3.0 %collective-permute-start.3 = (bf16[1664,128]{1,0:T(8,128)(2,1)}, bf16[1664,128]{1,0:T(8,128)(2,1)}, u32[]{:S(2)}, u32[]{:S(2)}) collective-permute-start(bf16[1664,128]{1,0:T(8,128)(2,1)} %dynamic-slice_bitcast_fusion.1.refs_1_), channel_id=1, source_target_pairs={{0,4},{4,8},{8,12},{12,0},{1,5},{5,9},{9,13},{13,1},{2,6},{6,10},{... | collective-permute-start | bytes 1277960 | tf_op jit(solution)/shard_map/ppermute | solution.py:25
  5.0 1.8 %dynamic-slice_bitcast_fusion.refs_2_ = bf16[1792,128]{1,0:T(8,128)(2,1)} fusion(bf16[1,6912,128]{2,1,0:T(8,128)(2,1)} %param.11, s32[]{:T(128)S(6)} %select_n.17), kind=kLoop, calls=%fused_computation | loop fusion | bytes 917508 | tf_op jit(solution)/shard_map/dynamic_slice | solution.py:268
  6.8 1.3 %constant_dynamic-slice_fusion.1 = bf16[256,3456]{1,0:T(8,128)(2,1)} fusion(bf16[256,6912]{1,0:T(8,128)(2,1)S(1)} %bitcast.9, s32[]{:T(128)S(6)} %select_n.20), kind=kLoop, calls=%fused_computation.5 | loop fusion | bytes 3538948 | tf_op jit(solution)/shard_map/dynamic_slice | solution.py:274
  8.1 1.5 %collective-permute-start.4 = (bf16[256,3456]{1,0:T(8,128)(2,1)}, bf16[256,3456]{1,0:T(8,128)(2,1)}, u32[]{:S(2)}, u32[]{:S(2)}) collective-permute-start(bf16[256,3456]{1,0:T(8,128)(2,1)} %constant_dynamic-slice_fusion.1), channel_id=1, source_target_pairs={{0,16},{16,0},{1,17},{17,1},{2,18},{18,2},{3,19},{19,3},{4,20},{20... | collective-permute-start | bytes 5308424 | tf_op jit(solution)/shard_map/ppermute | solution.py:25
  9.6 1.6 %collective-permute-start = (bf16[1792,128]{1,0:T(8,128)(2,1)}, bf16[1792,128]{1,0:T(8,128)(2,1)}, u32[]{:S(2)}, u32[]{:S(2)}) collective-permute-start(bf16[1792,128]{1,0:T(8,128)(2,1)} %dynamic-slice_bitcast_fusion.refs_2_), channel_id=1, source_target_pairs={{0,4},{4,8},{8,12},{12,0},{1,5},{5,9},{9,13},{13,1},{2,6},{6,10},{... | collective-permute-start | bytes 1376264 | tf_op jit(solution)/shard_map/ppermute | solution.py:25
  11.2 0.1 pad_add_fusion.place
  11.3 2.1 %copy-done.1 = bf16[1280,1536]{1,0:T(8,128)(2,1)S(1)} copy-done((bf16[1280,1536]{1,0:T(8,128)(2,1)S(1)}, bf16[1280,1536]{1,0:T(8,128)(2,1)}, u32[]{:S(2)}) %copy-start.1) | copy-done | bytes 3932184
  13.4 1.1 %copy-done.2 = bf16[2,128,1280]{2,1,0:T(8,128)(2,1)S(1)} copy-done((bf16[2,128,1280]{2,1,0:T(8,128)(2,1)S(1)}, bf16[2,128,1280]{2,1,0:T(8,128)(2,1)}, u32[]{:S(2)}) %copy-start.2) | copy-done | bytes 655384
  14.5 3.4 %shard_map.73 = (f32[384,256]{1,0:T(8,128)S(1)}, f32[384,256]{1,0:T(8,128)}, f32[384,256]{1,0:T(8,128)S(1)}, f32[384,256]{1,0:T(8,128)S(1)}) custom-call(s32[3]{0:T(128)S(1)} %pad_add_fusion.place, bf16[256,1280]{1,0:T(8,128)(2,1)S(1)} %bitcast.12, bf16[1280,1536]{1,0:T(8,128)(2,1)S(1)} %copy-done.1), custom_call_target="tpu_custom_call" | custom-call | tf_op jit(solution)/shard_map/pallas_call | solution.py:89
  17.9 0.8 copy-done.3
  18.6 0.7 copy-done.8
  19.4 0.7 copy-done.9
  20.1 0.0 collective-permute-done.3.refs_3_
  20.1 1.6 %collective-permute-start.5 = (bf16[1664,128]{1,0:T(8,128)(2,1)}, bf16[1664,128]{1,0:T(8,128)(2,1)}, u32[]{:S(2)}, u32[]{:S(2)}) collective-permute-start(bf16[1664,128]{1,0:T(8,128)(2,1)} %collective-permute-done.3.refs_3_), channel_id=1, source_target_pairs={{0,4},{4,8},{8,12},{12,0},{1,5},{5,9},{9,13},{13,1},{2,6},{6,10},{... | collective-permute-start | bytes 1277960 | tf_op jit(solution)/shard_map/ppermute | solution.py:25
  21.7 0.0 collective-permute-start.7
  21.7 1.5 %collective-permute-start.8 = (f32[384,256]{1,0:T(8,128)}, f32[384,256]{1,0:T(8,128)S(1)}, u32[]{:S(2)}, u32[]{:S(2)}) collective-permute-start(f32[384,256]{1,0:T(8,128)} %copy-done.9), channel_id=1, source_target_pairs={{0,2},{1,3},{2,0},{3,1},{4,6},{5,7},{6,4},{7,5},{8,10},{9,11},{10,... | collective-permute-start | bytes 1179656 | tf_op jit(solution)/shard_map/ppermute | solution.py:39
  23.2 4.6 %collective-permute-done.refs_4_ = bf16[1792,128]{1,0:T(8,128)(2,1)} collective-permute-done((bf16[1792,128]{1,0:T(8,128)(2,1)}, bf16[1792,128]{1,0:T(8,128)(2,1)}, u32[]{:S(2)}, u32[]{:S(2)}) %collective-permute-start) | collective-permute-done | bytes 458784 | tf_op jit(solution)/shard_map/ppermute | solution.py:25
  27.8 0.0 collective-permute-start.9
  27.8 0.0 collective-permute-done.7
  27.8 0.0 collective-permute-start.1
  27.8 9.1 %collective-permute-done.5.refs_1_ = bf16[1664,128]{1,0:T(8,128)(2,1)} collective-permute-done((bf16[1664,128]{1,0:T(8,128)(2,1)}, bf16[1664,128]{1,0:T(8,128)(2,1)}, u32[]{:S(2)}, u32[]{:S(2)}) %collective-permute-start.5) | collective-permute-done | bytes 426016 | tf_op jit(solution)/shard_map/ppermute | solution.py:25
  36.9 0.0 collective-permute-start.6
  36.9 0.1 constant_dynamic-slice_fusion.2.refs_0_
  37.1 2.6 %shard_map.74.refs_2_.refs_0_ = f32[2,256,128]{2,1,0:T(8,128)S(1)} custom-call(bf16[256,3456]{1,0:T(8,128)(2,1)S(1)} %constant_dynamic-slice_fusion.2.refs_0_, bf16[1664,128]{1,0:T(8,128)(2,1)} %dynamic-slice_bitcast_fusion.1.refs_1_, bf16[1792,128]{1,0:T(8,128)(2,1)} %dynamic-slice_bitcast_fusion.refs_2_, bf16[1664,128]{1,0:T(8,128)(2,1)} %collective-permute-done.3.refs_3_, ...), custom_call_target="tpu_custom_call" | custom-call | flops 452984832 | bytes 3538944 | tf_op jit(solution)/shard_map/pallas_call | solution.py:130
  39.6 7.0 %collective-permute-done.1.refs_2_ = bf16[1792,128]{1,0:T(8,128)(2,1)S(1)} collective-permute-done((bf16[1792,128]{1,0:T(8,128)(2,1)}, bf16[1792,128]{1,0:T(8,128)(2,1)S(1)}, u32[]{:S(2)}, u32[]{:S(2)}) %collective-permute-start.1) | collective-permute-done | bytes 458784 | tf_op jit(solution)/shard_map/ppermute | solution.py:25
  46.6 0.0 collective-permute-start.2
  46.7 0.0 collective-permute-done.8
  46.7 0.0 collective-permute-done.9
  46.7 1.1 %add_convert_fusion.refs_0_ = bf16[384,256]{1,0:T(8,128)(2,1)S(1)} fusion(f32[384,256]{1,0:T(8,128)S(1)} %collective-permute-done.9, f32[384,256]{1,0:T(8,128)S(1)} %collective-permute-done.8, f32[384,256]{1,0:T(8,128)S(1)} %copy-done.4, f32[384,256]{1,0:T(8,128)} %collective-permute-done.7), kind=kLoop, calls=%fused_computation.2 | loop fusion | flops 393216 | bytes 1769472 | tf_op jit(solution)/shard_map/convert_element_type | solution.py:297
  47.8 1.8 %collective-permute-start.11 = (bf16[384,256]{1,0:T(8,128)(2,1)S(1)}, bf16[384,256]{1,0:T(8,128)(2,1)S(1)}, u32[]{:S(2)}, u32[]{:S(2)}) collective-permute-start(bf16[384,256]{1,0:T(8,128)(2,1)S(1)} %add_convert_fusion.refs_0_), channel_id=1, source_target_pairs={{0,2},{1,3},{2,0},{3,1},{4,6},{5,7},{6,4},{7,5},{8,10},{9,11},{10,... | collective-permute-start | bytes 589832 | tf_op jit(solution)/shard_map/ppermute | solution.py:39
  49.6 0.0 collective-permute-start.12
  49.6 6.2 %collective-permute-done.6.refs_3_ = bf16[1664,128]{1,0:T(8,128)(2,1)S(1)} collective-permute-done((bf16[1664,128]{1,0:T(8,128)(2,1)}, bf16[1664,128]{1,0:T(8,128)(2,1)S(1)}, u32[]{:S(2)}, u32[]{:S(2)}) %collective-permute-start.6) | collective-permute-done | bytes 426016 | tf_op jit(solution)/shard_map/ppermute | solution.py:25
  55.8 0.0 collective-permute-start.10
  55.8 0.1 constant_dynamic-slice_fusion.refs_0_
  55.8 1.9 %shard_map.76.refs_4_.refs_2_ = f32[2,256,128]{2,1,0:T(8,128)S(1)} custom-call(bf16[256,3456]{1,0:T(8,128)(2,1)S(1)} %constant_dynamic-slice_fusion.2.refs_0_, bf16[1664,128]{1,0:T(8,128)(2,1)} %collective-permute-done.5.refs_1_, bf16[1792,128]{1,0:T(8,128)(2,1)S(1)} %collective-permute-done.1.refs_2_, bf16[1664,128]{1,0:T(8,128)(2,1)S(1)} %collective-permute-done.6.refs_3_), custom_call_target="tpu_custom_call" | custom-call | flops 335544320 | bytes 2621440 | tf_op jit(solution)/shard_map/pallas_call | solution.py:130
  57.7 0.0 collective-permute-done.4.refs_0_
  57.7 2.4 %shard_map.77.refs_5_.refs_3_ = f32[2,256,128]{2,1,0:T(8,128)S(1)} custom-call(bf16[256,3456]{1,0:T(8,128)(2,1)} %collective-permute-done.4.refs_0_, bf16[1664,128]{1,0:T(8,128)(2,1)} %collective-permute-done.5.refs_1_, bf16[1792,128]{1,0:T(8,128)(2,1)S(1)} %collective-permute-done.1.refs_2_, bf16[1664,128]{1,0:T(8,128)(2,1)S(1)} %collective-permute-done.6.refs_3_), custom_call_target="tpu_custom_call" | custom-call | flops 335544320 | bytes 2621440 | tf_op jit(solution)/shard_map/pallas_call | solution.py:130
  60.1 3.0 %shard_map.75.refs_3_.refs_1_ = f32[2,256,128]{2,1,0:T(8,128)S(1)} custom-call(bf16[256,3456]{1,0:T(8,128)(2,1)} %collective-permute-done.4.refs_0_, bf16[1664,128]{1,0:T(8,128)(2,1)} %dynamic-slice_bitcast_fusion.1.refs_1_, bf16[1792,128]{1,0:T(8,128)(2,1)} %dynamic-slice_bitcast_fusion.refs_2_, bf16[1664,128]{1,0:T(8,128)(2,1)} %collective-permute-done.3.refs_3_, ...), custom_call_target="tpu_custom_call" | custom-call | flops 452984832 | bytes 3538944 | tf_op jit(solution)/shard_map/pallas_call | solution.py:130
  63.1 0.0 copy-start.5
  63.1 1.2 %slice.8.refs_1_ = bf16[256,1792]{1,0:T(8,128)(2,1)S(1)} slice(bf16[256,3456]{1,0:T(8,128)(2,1)} %collective-permute-done.4.refs_0_), slice={[0:256], [1664:3456]} | slice | bytes 1835008 | tf_op jit(solution)/shard_map/slice | solution.py:300
  64.4 0.0 collective-permute-done.11.refs_2_
  64.4 0.0 collective-permute-done.10.refs_1_
  64.4 0.6 shard_map.78.act
  65.0 0.0 copy-start.6
  65.0 0.0 copy-start.7
  65.1 1.2 %shard_map.79 = (f32[512,128]{1,0:T(8,128)S(1)}, f32[2,512,128]{2,1,0:T(8,128)S(1)}) custom-call(s32[4]{0:T(128)S(1)} %copy-done.5, s32[3]{0:T(128)S(1)} %pad_add_fusion.place, bf16[1792,128]{1,0:T(8,128)(2,1)S(1)} %collective-permute-done.2.held, bf16[256,1792]{1,0:T(8,128)(2,1)S(1)} %constant_dynamic-slice_fusion.refs_0_, ...), custom_call_target="tpu_custom_call" | custom-call | tf_op jit(solution)/shard_map/pallas_call | solution.py:175
  66.3 0.6 collective-permute-start.13
  66.8 1.5 %collective-permute-done.13.refs_4_ = f32[2,512,128]{2,1,0:T(8,128)S(1)} collective-permute-done((f32[2,512,128]{2,1,0:T(8,128)S(1)}, f32[2,512,128]{2,1,0:T(8,128)S(1)}, u32[]{:S(2)}, u32[]{:S(2)}) %collective-permute-start.13) | collective-permute-done | bytes 524320 | tf_op jit(solution)/shard_map/ppermute | solution.py:25
  68.4 0.7 shard_map.80
  69.0 1.8 %collective-permute-start.14 = (f32[256,128]{1,0:T(8,128)S(1)}, f32[256,128]{1,0:T(8,128)S(1)}, u32[]{:S(2)}, u32[]{:S(2)}) collective-permute-start(f32[256,128]{1,0:T(8,128)S(1)} %get-tuple-element.62), channel_id=1, source_target_pairs={{0,16},{2,18},{16,0},{18,2},{1,17},{3,19},{17,1},{19,3},{4,20},{6,... | collective-permute-start | bytes 393224 | tf_op jit(solution)/shard_map/ppermute | solution.py:320
  70.9 1.5 %collective-permute-start.15 = (f32[256,128]{1,0:T(8,128)S(1)}, f32[256,128]{1,0:T(8,128)S(1)}, u32[]{:S(2)}, u32[]{:S(2)}) collective-permute-start(f32[256,128]{1,0:T(8,128)S(1)} %get-tuple-element.63), channel_id=1, source_target_pairs={{0,2},{2,0},{16,18},{18,16},{1,3},{3,1},{17,19},{19,17},{4,6},{6,4... | collective-permute-start | bytes 393224 | tf_op jit(solution)/shard_map/ppermute | solution.py:320
  72.4 0.2 collective-permute-start.16
  72.6 2.3 %collective-permute-done.14.refs_1_ = f32[256,128]{1,0:T(8,128)S(1)} collective-permute-done((f32[256,128]{1,0:T(8,128)S(1)}, f32[256,128]{1,0:T(8,128)S(1)}, u32[]{:S(2)}, u32[]{:S(2)}) %collective-permute-start.14) | collective-permute-done | bytes 131104 | tf_op jit(solution)/shard_map/ppermute | solution.py:320
  74.9 2.3 %collective-permute-done.15.refs_2_ = f32[256,128]{1,0:T(8,128)S(1)} collective-permute-done((f32[256,128]{1,0:T(8,128)S(1)}, f32[256,128]{1,0:T(8,128)S(1)}, u32[]{:S(2)}, u32[]{:S(2)}) %collective-permute-start.15) | collective-permute-done | bytes 131104 | tf_op jit(solution)/shard_map/ppermute | solution.py:320
  77.2 1.7 %collective-permute-done.16.refs_3_ = f32[256,128]{1,0:T(8,128)S(1)} collective-permute-done((f32[256,128]{1,0:T(8,128)S(1)}, f32[256,128]{1,0:T(8,128)S(1)}, u32[]{:S(2)}, u32[]{:S(2)}) %collective-permute-start.16) | collective-permute-done | bytes 131104 | tf_op jit(solution)/shard_map/ppermute | solution.py:320
  79.0 0.9 shard_map.81
  79.9 0.1 collective-permute-start.17
  79.9 2.5 %collective-permute-start.18 = (bf16[256,128]{1,0:T(8,128)(2,1)S(1)}, bf16[256,128]{1,0:T(8,128)(2,1)S(1)}, u32[]{:S(2)}, u32[]{:S(2)}) collective-permute-start(bf16[256,128]{1,0:T(8,128)(2,1)S(1)} %get-tuple-element.67), channel_id=1, source_target_pairs={{0,8},{4,12},{8,0},{12,4},{1,9},{5,13},{9,1},{13,5},{2,10},{6,14},... | collective-permute-start | bytes 196616 | tf_op jit(solution)/shard_map/ppermute | solution.py:25
  82.4 1.4 %collective-permute-start.19 = (bf16[256,128]{1,0:T(8,128)(2,1)S(1)}, bf16[256,128]{1,0:T(8,128)(2,1)S(1)}, u32[]{:S(2)}, u32[]{:S(2)}) collective-permute-start(bf16[256,128]{1,0:T(8,128)(2,1)S(1)} %get-tuple-element.68), channel_id=1, source_target_pairs={{0,12},{4,0},{8,4},{12,8},{1,13},{5,1},{9,5},{13,9},{2,14},{6,2},{... | collective-permute-start | bytes 196616 | tf_op jit(solution)/shard_map/ppermute | solution.py:25
  83.8 2.8 %collective-permute-done.17 = bf16[256,128]{1,0:T(8,128)(2,1)S(1)} collective-permute-done((bf16[256,128]{1,0:T(8,128)(2,1)S(1)}, bf16[256,128]{1,0:T(8,128)(2,1)S(1)}, u32[]{:S(2)}, u32[]{:S(2)}) %collective-permute-start.17) | collective-permute-done | bytes 65568 | tf_op jit(solution)/shard_map/ppermute | solution.py:25
  86.5 1.3 %collective-permute-done.18 = bf16[256,128]{1,0:T(8,128)(2,1)S(1)} collective-permute-done((bf16[256,128]{1,0:T(8,128)(2,1)S(1)}, bf16[256,128]{1,0:T(8,128)(2,1)S(1)}, u32[]{:S(2)}, u32[]{:S(2)}) %collective-permute-start.18) | collective-permute-done | bytes 65568 | tf_op jit(solution)/shard_map/ppermute | solution.py:25
  87.9 0.0 collective-permute-done.19
  87.9 0.7 add_multiply_fusion
  (14 shorter events, 0.0 us)
Async XLA Ops:
  0.0 6.8 %copy-start = (bf16[2,128,6912]{2,1,0:T(8,128)(2,1)S(1)}, bf16[2,128,6912]{2,1,0:T(8,128)(2,1)}, u32[]{:S(2)}) copy-start(bf16[2,128,6912]{2,1,0:T(8,128)(2,1)} %param.8) | copy-start | bytes 10616836
  1.9 18.2 %collective-permute-start.3 = (bf16[1664,128]{1,0:T(8,128)(2,1)}, bf16[1664,128]{1,0:T(8,128)(2,1)}, u32[]{:S(2)}, u32[]{:S(2)}) collective-permute-start(bf16[1664,128]{1,0:T(8,128)(2,1)} %dynamic-slice_bitcast_fusion.1.refs_1_), channel_id=1, source_target_pairs={{0,4},{4,8},{8,12},{12,0},{1,5},{5,9},{9,13},{13,1},{2,6},{6,10},{... | collective-permute-start | bytes 1277960 | tf_op jit(solution)/shard_map/ppermute | solution.py:25
  8.1 49.6 %collective-permute-start.4 = (bf16[256,3456]{1,0:T(8,128)(2,1)}, bf16[256,3456]{1,0:T(8,128)(2,1)}, u32[]{:S(2)}, u32[]{:S(2)}) collective-permute-start(bf16[256,3456]{1,0:T(8,128)(2,1)} %constant_dynamic-slice_fusion.1), channel_id=1, source_target_pairs={{0,16},{16,0},{1,17},{17,1},{2,18},{18,2},{3,19},{19,3},{4,20},{20... | collective-permute-start | bytes 5308424 | tf_op jit(solution)/shard_map/ppermute | solution.py:25
  9.6 18.2 %collective-permute-start = (bf16[1792,128]{1,0:T(8,128)(2,1)}, bf16[1792,128]{1,0:T(8,128)(2,1)}, u32[]{:S(2)}, u32[]{:S(2)}) collective-permute-start(bf16[1792,128]{1,0:T(8,128)(2,1)} %dynamic-slice_bitcast_fusion.refs_2_), channel_id=1, source_target_pairs={{0,4},{4,8},{8,12},{12,0},{1,5},{5,9},{9,13},{13,1},{2,6},{6,10},{... | collective-permute-start | bytes 1376264 | tf_op jit(solution)/shard_map/ppermute | solution.py:25
  11.3 2.1 %copy-start.1 = (bf16[1280,1536]{1,0:T(8,128)(2,1)S(1)}, bf16[1280,1536]{1,0:T(8,128)(2,1)}, u32[]{:S(2)}) copy-start(bf16[1280,1536]{1,0:T(8,128)(2,1)} %basis.1) | copy-start | bytes 11796484
  13.4 1.1 %copy-start.2 = (bf16[2,128,1280]{2,1,0:T(8,128)(2,1)S(1)}, bf16[2,128,1280]{2,1,0:T(8,128)(2,1)}, u32[]{:S(2)}) copy-start(bf16[2,128,1280]{2,1,0:T(8,128)(2,1)} %param.7) | copy-start | bytes 1966084
  17.9 0.8 copy-start.3
  18.6 0.8 copy-start.8
  19.4 0.7 copy-start.9
  20.1 16.8 %collective-permute-start.5 = (bf16[1664,128]{1,0:T(8,128)(2,1)}, bf16[1664,128]{1,0:T(8,128)(2,1)}, u32[]{:S(2)}, u32[]{:S(2)}) collective-permute-start(bf16[1664,128]{1,0:T(8,128)(2,1)} %collective-permute-done.3.refs_3_), channel_id=1, source_target_pairs={{0,4},{4,8},{8,12},{12,0},{1,5},{5,9},{9,13},{13,1},{2,6},{6,10},{... | collective-permute-start | bytes 1277960 | tf_op jit(solution)/shard_map/ppermute | solution.py:25
  21.7 6.1 %collective-permute-start.7 = (f32[384,256]{1,0:T(8,128)}, f32[384,256]{1,0:T(8,128)}, u32[]{:S(2)}, u32[]{:S(2)}) collective-permute-start(f32[384,256]{1,0:T(8,128)} %get-tuple-element.47), channel_id=1, source_target_pairs={{0,1},{1,0},{2,3},{3,2},{4,5},{5,4},{6,7},{7,6},{8,9},{9,8},{10,11... | collective-permute-start | bytes 1179656 | tf_op jit(solution)/shard_map/ppermute | solution.py:39
  21.7 24.9 %collective-permute-start.8 = (f32[384,256]{1,0:T(8,128)}, f32[384,256]{1,0:T(8,128)S(1)}, u32[]{:S(2)}, u32[]{:S(2)}) collective-permute-start(f32[384,256]{1,0:T(8,128)} %copy-done.9), channel_id=1, source_target_pairs={{0,2},{1,3},{2,0},{3,1},{4,6},{5,7},{6,4},{7,5},{8,10},{9,11},{10,... | collective-permute-start | bytes 1179656 | tf_op jit(solution)/shard_map/ppermute | solution.py:39
  27.8 18.9 %collective-permute-start.9 = (f32[384,256]{1,0:T(8,128)}, f32[384,256]{1,0:T(8,128)S(1)}, u32[]{:S(2)}, u32[]{:S(2)}) collective-permute-start(f32[384,256]{1,0:T(8,128)} %copy-done.8), channel_id=1, source_target_pairs={{0,3},{1,2},{2,1},{3,0},{4,7},{5,6},{6,5},{7,4},{8,11},{9,10},{10,... | collective-permute-start | bytes 1179656 | tf_op jit(solution)/shard_map/ppermute | solution.py:39
  27.8 18.8 %collective-permute-start.1 = (bf16[1792,128]{1,0:T(8,128)(2,1)}, bf16[1792,128]{1,0:T(8,128)(2,1)S(1)}, u32[]{:S(2)}, u32[]{:S(2)}) collective-permute-start(bf16[1792,128]{1,0:T(8,128)(2,1)} %collective-permute-done.refs_4_), channel_id=1, source_target_pairs={{0,4},{4,8},{8,12},{12,0},{1,5},{5,9},{9,13},{13,1},{2,6},{6,10},{... | collective-permute-start | bytes 1376264 | tf_op jit(solution)/shard_map/ppermute | solution.py:25
  36.9 18.9 %collective-permute-start.6 = (bf16[1664,128]{1,0:T(8,128)(2,1)}, bf16[1664,128]{1,0:T(8,128)(2,1)S(1)}, u32[]{:S(2)}, u32[]{:S(2)}) collective-permute-start(bf16[1664,128]{1,0:T(8,128)(2,1)} %collective-permute-done.5.refs_1_), channel_id=1, source_target_pairs={{0,4},{4,8},{8,12},{12,0},{1,5},{5,9},{9,13},{13,1},{2,6},{6,10},{... | collective-permute-start | bytes 1277960 | tf_op jit(solution)/shard_map/ppermute | solution.py:25
  37.1 9.6 %copy-start.4 = (f32[384,256]{1,0:T(8,128)S(1)}, f32[384,256]{1,0:T(8,128)}, u32[]{:S(2)}) copy-start(f32[384,256]{1,0:T(8,128)} %copy-done.3) | copy-start | bytes 1179652
  46.6 18.4 %collective-permute-start.2 = (bf16[1792,128]{1,0:T(8,128)(2,1)S(1)}, bf16[1792,128]{1,0:T(8,128)(2,1)S(1)}, u32[]{:S(2)}, u32[]{:S(2)}) collective-permute-start(bf16[1792,128]{1,0:T(8,128)(2,1)S(1)} %collective-permute-done.1.refs_2_), channel_id=1, source_target_pairs={{0,4},{4,8},{8,12},{12,0},{1,5},{5,9},{9,13},{13,1},{2,6},{6,10},{... | collective-permute-start | bytes 1376264 | tf_op jit(solution)/shard_map/ppermute | solution.py:25
  47.8 16.6 %collective-permute-start.11 = (bf16[384,256]{1,0:T(8,128)(2,1)S(1)}, bf16[384,256]{1,0:T(8,128)(2,1)S(1)}, u32[]{:S(2)}, u32[]{:S(2)}) collective-permute-start(bf16[384,256]{1,0:T(8,128)(2,1)S(1)} %add_convert_fusion.refs_0_), channel_id=1, source_target_pairs={{0,2},{1,3},{2,0},{3,1},{4,6},{5,7},{6,4},{7,5},{8,10},{9,11},{10,... | collective-permute-start | bytes 589832 | tf_op jit(solution)/shard_map/ppermute | solution.py:39
  49.6 14.8 %collective-permute-start.12 = (bf16[384,256]{1,0:T(8,128)(2,1)S(1)}, bf16[384,256]{1,0:T(8,128)(2,1)S(1)}, u32[]{:S(2)}, u32[]{:S(2)}) collective-permute-start(bf16[384,256]{1,0:T(8,128)(2,1)S(1)} %add_convert_fusion.refs_0_), channel_id=1, source_target_pairs={{0,3},{1,2},{2,1},{3,0},{4,7},{5,6},{6,5},{7,4},{8,11},{9,10},{10,... | collective-permute-start | bytes 589832 | tf_op jit(solution)/shard_map/ppermute | solution.py:39
  55.8 8.6 %collective-permute-start.10 = (bf16[384,256]{1,0:T(8,128)(2,1)S(1)}, bf16[384,256]{1,0:T(8,128)(2,1)S(1)}, u32[]{:S(2)}, u32[]{:S(2)}) collective-permute-start(bf16[384,256]{1,0:T(8,128)(2,1)S(1)} %add_convert_fusion.refs_0_), channel_id=1, source_target_pairs={{0,1},{1,0},{2,3},{3,2},{4,5},{5,4},{6,7},{7,6},{8,9},{9,8},{10,11... | collective-permute-start | bytes 589832 | tf_op jit(solution)/shard_map/ppermute | solution.py:39
  63.1 1.9 %copy-start.5 = (s32[4]{0:T(128)S(1)}, s32[4]{0:T(128)}, u32[]{:S(2)}) copy-start(s32[4]{0:T(128)} %owner.3) | copy-start | bytes 52
  65.0 14.0 %copy-start.6 = (s32[2]{0:T(128)S(1)}, s32[2]{0:T(128)}, u32[]{:S(2)}) copy-start(s32[2]{0:T(128)} %counts.1) | copy-start | bytes 28
  65.0 14.0 %copy-start.7 = (s32[1,2]{1,0:T(1,128)S(1)}, s32[1,2]{1,0:T(1,128)}, u32[]{:S(2)}) copy-start(s32[1,2]{1,0:T(1,128)} %wanted.1) | copy-start | bytes 28
  66.3 2.1 %collective-permute-start.13 = (f32[2,512,128]{2,1,0:T(8,128)S(1)}, f32[2,512,128]{2,1,0:T(8,128)S(1)}, u32[]{:S(2)}, u32[]{:S(2)}) collective-permute-start(f32[2,512,128]{2,1,0:T(8,128)S(1)} %get-tuple-element.60), channel_id=1, source_target_pairs={{0,1},{1,0},{2,3},{3,2},{4,5},{5,4},{6,7},{7,6},{8,9},{9,8},{10,11... | collective-permute-start | bytes 1572872 | tf_op jit(solution)/shard_map/ppermute | solution.py:25
  69.0 5.9 %collective-permute-start.14 = (f32[256,128]{1,0:T(8,128)S(1)}, f32[256,128]{1,0:T(8,128)S(1)}, u32[]{:S(2)}, u32[]{:S(2)}) collective-permute-start(f32[256,128]{1,0:T(8,128)S(1)} %get-tuple-element.62), channel_id=1, source_target_pairs={{0,16},{2,18},{16,0},{18,2},{1,17},{3,19},{17,1},{19,3},{4,20},{6,... | collective-permute-start | bytes 393224 | tf_op jit(solution)/shard_map/ppermute | solution.py:320
  70.9 6.4 %collective-permute-start.15 = (f32[256,128]{1,0:T(8,128)S(1)}, f32[256,128]{1,0:T(8,128)S(1)}, u32[]{:S(2)}, u32[]{:S(2)}) collective-permute-start(f32[256,128]{1,0:T(8,128)S(1)} %get-tuple-element.63), channel_id=1, source_target_pairs={{0,2},{2,0},{16,18},{18,16},{1,3},{3,1},{17,19},{19,17},{4,6},{6,4... | collective-permute-start | bytes 393224 | tf_op jit(solution)/shard_map/ppermute | solution.py:320
  72.4 6.6 %collective-permute-start.16 = (f32[256,128]{1,0:T(8,128)S(1)}, f32[256,128]{1,0:T(8,128)S(1)}, u32[]{:S(2)}, u32[]{:S(2)}) collective-permute-start(f32[256,128]{1,0:T(8,128)S(1)} %get-tuple-element.64), channel_id=1, source_target_pairs={{0,18},{2,16},{16,2},{18,0},{1,19},{3,17},{17,3},{19,1},{4,22},{6,... | collective-permute-start | bytes 393224 | tf_op jit(solution)/shard_map/ppermute | solution.py:320
  79.9 6.7 %collective-permute-start.17 = (bf16[256,128]{1,0:T(8,128)(2,1)S(1)}, bf16[256,128]{1,0:T(8,128)(2,1)S(1)}, u32[]{:S(2)}, u32[]{:S(2)}) collective-permute-start(bf16[256,128]{1,0:T(8,128)(2,1)S(1)} %get-tuple-element.66), channel_id=1, source_target_pairs={{0,4},{4,8},{8,12},{12,0},{1,5},{5,9},{9,13},{13,1},{2,6},{6,10},{... | collective-permute-start | bytes 196616 | tf_op jit(solution)/shard_map/ppermute | solution.py:25
  79.9 7.9 %collective-permute-start.18 = (bf16[256,128]{1,0:T(8,128)(2,1)S(1)}, bf16[256,128]{1,0:T(8,128)(2,1)S(1)}, u32[]{:S(2)}, u32[]{:S(2)}) collective-permute-start(bf16[256,128]{1,0:T(8,128)(2,1)S(1)} %get-tuple-element.67), channel_id=1, source_target_pairs={{0,8},{4,12},{8,0},{12,4},{1,9},{5,13},{9,1},{13,5},{2,10},{6,14},... | collective-permute-start | bytes 196616 | tf_op jit(solution)/shard_map/ppermute | solution.py:25
  82.4 5.4 %collective-permute-start.19 = (bf16[256,128]{1,0:T(8,128)(2,1)S(1)}, bf16[256,128]{1,0:T(8,128)(2,1)S(1)}, u32[]{:S(2)}, u32[]{:S(2)}) collective-permute-start(bf16[256,128]{1,0:T(8,128)(2,1)S(1)} %get-tuple-element.68), channel_id=1, source_target_pairs={{0,12},{4,0},{8,4},{12,8},{1,13},{5,1},{9,5},{13,9},{2,14},{6,2},{... | collective-permute-start | bytes 196616 | tf_op jit(solution)/shard_map/ppermute | solution.py:25

commit v14 on v13

--- a/solution.py
+++ b/solution.py
@@ -157,7 +157,7 @@
     last, sends = refs[0], refs[1:]
     height = early[0].shape[1]
     for g in range(len(parts)):
-        last[g * height : (g + 1) * height] = rest[g][1] + product(rows[g], held, start)
+        last[g * height : (g + 1) * height] = rest[g][1] + product(rows[g], held, start if g == 0 else 0)
     for step in range(1, cores):
         for block in range(sends[0].shape[0]):
             piece = block * cores + lax.rem(core + step, cores)
@@ -297,13 +297,13 @@
     act_parts = gather_act(act.astype(BF16), (first[-1], early[0]))
     rest = [early_products(part, pieces[-4:-1], shares) for part in rows]
     act_rot_t = assemble(after(place, *early, *rest), act_parts, blocks, cores)
-    ends = [part[0][:, cut:] for part in rows]
+    ends = [rows[0][0]] + [part[0][:, cut:] for part in rows[1:]]
     last, act_rot_t, *done = lax.optimization_barrier(
         (pieces[-1], act_rot_t, *early, *rest, *ends)
     )
     early, rest, ends = (done[i * len(rows) : (i + 1) * len(rows)] for i in range(3))
     ends = [[part] for part in ends]
-    last, *sends = pack(owner_slot, place, ends, last, 0, early, rest, blocks, cores)
+    last, *sends = pack(owner_slot, place, ends, last, cut, early, rest, blocks, cores)
     came = [shift(send, "cores", step) for step, send in enumerate(sends, 1)]
     parts = join(owner_slot, place, last, early, rest, came, blocks, cores)
 

time: 89 us -> 88 us (0.989)
  waiting for transfers between devices: 38.8 us -> 44.5 us
  local copies, waits for them, and re-layouts: 12 us -> 9.67 us
  Pallas kernels: 16.5 us -> 14.6 us
  starting transfers between devices: 19.1 us -> 17.8 us
  other arithmetic: 1.88 us -> 0.87 us
    ppermute x11, waiting for transfers between devices: 32.5 us -> 38.5 us  [shift(): lax.ppermute(value, axis, [(i, (i + step) % size) for i in range(size)])]
    unnamed x20 -> x12, local copies, waits for them, and re-layouts: 5.49 us -> 3.22 us
    ppermute x11, starting transfers between devices: 12.3 us -> 11 us  [shift(): lax.ppermute(value, axis, [(i, (i + step) % size) for i in range(size)])]
    pallas_call x4, Pallas kernels: 9.79 us -> 8.68 us  [early_products(): pl.pallas_call(functools.partial(early_kernel, len(rows), shares), out_sh...]
    convert_element_type x1, other arithmetic: 1.11 us -> 0.1 us  [on_device(): act_parts = gather_act(act.astype(BF16), (first[-1], early[0]))]
  transfers between devices with their start and end apart: 20 -> 20, of which waited for: 10 -> 12; matrix products, arithmetic and copies ran while one was open for 6% -> 5% of each run, Pallas kernels for 16% -> 14%
where the time goes in v14:
time: 88 us; the launch traced here: 87.7 us
  waiting for transfers between devices  44.5 us (51%)
  starting transfers between devices  17.8 us (20%)
  Pallas kernels  14.6 us (17%)
  local copies, waits for them, and re-layouts  9.67 us (11%)
    ppermute x11, waiting for transfers between devices, shift(): lax.ppermute(value, axis, [(i, (i + step) % size) for i in range(size)])  38.5 us
    ppermute x11, starting transfers between devices, shift(): lax.ppermute(value, axis, [(i, (i + step) % size) for i in range(size)])  11 us
    pallas_call x4, Pallas kernels, early_products(): pl.pallas_call(functools.partial(early_kernel, len(rows), shares), out_sh...  8.68 us
    ppermute x3, waiting for transfers between devices, on_device(): parts[i] = lax.ppermute(parts[i], ('groups', 'block'), pairs)  6.04 us
    dynamic_slice x2, local copies, waits for them, and re-layouts, on_device(): lax.dynamic_slice_in_dim(basis_store[0], group * part_features + start, s...  3.77 us
    ppermute x3, starting transfers between devices, on_device(): parts[i] = lax.ppermute(parts[i], ('groups', 'block'), pairs)  3.55 us
    ppermute x6, starting transfers between devices, to_neighbour(): return lax.ppermute(value, ('block', 'cores'), pairs)  3.27 us
    unnamed x12, local copies, waits for them, and re-layouts  3.22 us
  transfers between devices with their start and end apart: 20, of which 12 were waited for; matrix products, arithmetic and copies ran while one was open for 5% of the time, Pallas kernels for 14%

profile of v14, /device:TPU:0, one launch (start us, length us, event | category | flops | bytes accessed | tf_op | source)
XLA Modules:
  0.0 87.7 jit_solution(14338655056920813251)
XLA Ops:
  0.0 1.9 %dynamic-slice_bitcast_fusion.1.refs_1_ = bf16[1664,128]{1,0:T(8,128)(2,1)} fusion(bf16[1,6912,128]{2,1,0:T(8,128)(2,1)} %param.11, s32[]{:T(128)S(6)} %select_n.18), kind=kLoop, calls=%fused_computation.1 | loop fusion | bytes 851972 | tf_op jit(solution)/shard_map/dynamic_slice | solution.py:268
  1.9 3.0 %collective-permute-start.3 = (bf16[1664,128]{1,0:T(8,128)(2,1)}, bf16[1664,128]{1,0:T(8,128)(2,1)}, u32[]{:S(2)}, u32[]{:S(2)}) collective-permute-start(bf16[1664,128]{1,0:T(8,128)(2,1)} %dynamic-slice_bitcast_fusion.1.refs_1_), channel_id=1, source_target_pairs={{0,4},{4,8},{8,12},{12,0},{1,5},{5,9},{9,13},{13,1},{2,6},{6,10},{... | collective-permute-start | bytes 1277960 | tf_op jit(solution)/shard_map/ppermute | solution.py:25
  5.0 1.8 %dynamic-slice_bitcast_fusion.refs_2_ = bf16[1792,128]{1,0:T(8,128)(2,1)} fusion(bf16[1,6912,128]{2,1,0:T(8,128)(2,1)} %param.11, s32[]{:T(128)S(6)} %select_n.17), kind=kLoop, calls=%fused_computation | loop fusion | bytes 917508 | tf_op jit(solution)/shard_map/dynamic_slice | solution.py:268
  6.8 0.0 copy-done
  6.8 1.3 %constant_dynamic-slice_fusion = bf16[256,3456]{1,0:T(8,128)(2,1)} fusion(bf16[256,6912]{1,0:T(8,128)(2,1)S(1)} %bitcast.9, s32[]{:T(128)S(6)} %select_n.20), kind=kLoop, calls=%fused_computation.4 | loop fusion | bytes 3538948 | tf_op jit(solution)/shard_map/dynamic_slice | solution.py:274
  8.1 1.5 %collective-permute-start.4 = (bf16[256,3456]{1,0:T(8,128)(2,1)}, bf16[256,3456]{1,0:T(8,128)(2,1)}, u32[]{:S(2)}, u32[]{:S(2)}) collective-permute-start(bf16[256,3456]{1,0:T(8,128)(2,1)} %constant_dynamic-slice_fusion), channel_id=1, source_target_pairs={{0,16},{16,0},{1,17},{17,1},{2,18},{18,2},{3,19},{19,3},{4,20},{20... | collective-permute-start | bytes 5308424 | tf_op jit(solution)/shard_map/ppermute | solution.py:25
  9.6 1.6 %collective-permute-start = (bf16[1792,128]{1,0:T(8,128)(2,1)}, bf16[1792,128]{1,0:T(8,128)(2,1)}, u32[]{:S(2)}, u32[]{:S(2)}) collective-permute-start(bf16[1792,128]{1,0:T(8,128)(2,1)} %dynamic-slice_bitcast_fusion.refs_2_), channel_id=1, source_target_pairs={{0,4},{4,8},{8,12},{12,0},{1,5},{5,9},{9,13},{13,1},{2,6},{6,10},{... | collective-permute-start | bytes 1376264 | tf_op jit(solution)/shard_map/ppermute | solution.py:25
  11.2 0.1 pad_add_fusion.place
  11.3 2.1 %copy-done.1 = bf16[1280,1536]{1,0:T(8,128)(2,1)S(1)} copy-done((bf16[1280,1536]{1,0:T(8,128)(2,1)S(1)}, bf16[1280,1536]{1,0:T(8,128)(2,1)}, u32[]{:S(2)}) %copy-start.1) | copy-done | bytes 3932184
  13.4 1.1 %copy-done.2 = bf16[2,128,1280]{2,1,0:T(8,128)(2,1)S(1)} copy-done((bf16[2,128,1280]{2,1,0:T(8,128)(2,1)S(1)}, bf16[2,128,1280]{2,1,0:T(8,128)(2,1)}, u32[]{:S(2)}) %copy-start.2) | copy-done | bytes 655384
  14.5 2.6 %shard_map.73 = (f32[384,256]{1,0:T(8,128)S(1)}, f32[384,256]{1,0:T(8,128)S(1)}, f32[384,256]{1,0:T(8,128)S(1)}, f32[384,256]{1,0:T(8,128)S(1)}) custom-call(s32[3]{0:T(128)S(1)} %pad_add_fusion.place, bf16[256,1280]{1,0:T(8,128)(2,1)S(1)} %bitcast.11, bf16[1280,1536]{1,0:T(8,128)(2,1)S(1)} %copy-done.1), custom_call_target="tpu_custom_call" | custom-call | tf_op jit(solution)/shard_map/pallas_call | solution.py:89
  17.1 0.8 collective-permute-done.3.refs_3_
  18.0 0.8 collective-permute-start.5
  18.8 0.0 collective-permute-start.7
  18.8 1.5 %collective-permute-start.8 = (f32[384,256]{1,0:T(8,128)S(1)}, f32[384,256]{1,0:T(8,128)S(1)}, u32[]{:S(2)}, u32[]{:S(2)}) collective-permute-start(f32[384,256]{1,0:T(8,128)S(1)} %get-tuple-element.48), channel_id=1, source_target_pairs={{0,2},{1,3},{2,0},{3,1},{4,6},{5,7},{6,4},{7,5},{8,10},{9,11},{10,... | collective-permute-start | bytes 1179656 | tf_op jit(solution)/shard_map/ppermute | solution.py:39
  20.3 7.5 %collective-permute-done.refs_4_ = bf16[1792,128]{1,0:T(8,128)(2,1)} collective-permute-done((bf16[1792,128]{1,0:T(8,128)(2,1)}, bf16[1792,128]{1,0:T(8,128)(2,1)}, u32[]{:S(2)}, u32[]{:S(2)}) %collective-permute-start) | collective-permute-done | bytes 458784 | tf_op jit(solution)/shard_map/ppermute | solution.py:25
  27.8 0.0 collective-permute-start.9
  27.8 0.0 collective-permute-done.7
  27.8 0.0 collective-permute-start.1
  27.8 9.0 %collective-permute-done.5.refs_1_ = bf16[1664,128]{1,0:T(8,128)(2,1)S(1)} collective-permute-done((bf16[1664,128]{1,0:T(8,128)(2,1)}, bf16[1664,128]{1,0:T(8,128)(2,1)S(1)}, u32[]{:S(2)}, u32[]{:S(2)}) %collective-permute-start.5) | collective-permute-done | bytes 426016 | tf_op jit(solution)/shard_map/ppermute | solution.py:25
  36.8 0.0 collective-permute-start.6
  36.8 0.1 constant_dynamic-slice_fusion.1.refs_0_
  37.0 2.5 %shard_map.74.refs_2_.refs_0_ = f32[2,256,128]{2,1,0:T(8,128)S(1)} custom-call(bf16[256,3456]{1,0:T(8,128)(2,1)S(1)} %constant_dynamic-slice_fusion.1.refs_0_, bf16[1664,128]{1,0:T(8,128)(2,1)} %dynamic-slice_bitcast_fusion.1.refs_1_, bf16[1792,128]{1,0:T(8,128)(2,1)} %dynamic-slice_bitcast_fusion.refs_2_, bf16[1664,128]{1,0:T(8,128)(2,1)} %collective-permute-done.3.refs_3_, ...), custom_call_target="tpu_custom_call" | custom-call | flops 452984832 | bytes 3538944 | tf_op jit(solution)/shard_map/pallas_call | solution.py:130
  39.5 7.2 %collective-permute-done.1.refs_2_ = bf16[1792,128]{1,0:T(8,128)(2,1)S(1)} collective-permute-done((bf16[1792,128]{1,0:T(8,128)(2,1)}, bf16[1792,128]{1,0:T(8,128)(2,1)S(1)}, u32[]{:S(2)}, u32[]{:S(2)}) %collective-permute-start.1) | collective-permute-done | bytes 458784 | tf_op jit(solution)/shard_map/ppermute | solution.py:25
  46.6 0.0 collective-permute-start.2
  46.7 0.0 collective-permute-done.8
  46.7 0.0 collective-permute-done.9
  46.7 0.1 add_convert_fusion.refs_0_
  46.8 1.8 %collective-permute-start.11 = (bf16[384,256]{1,0:T(8,128)(2,1)S(1)}, bf16[384,256]{1,0:T(8,128)(2,1)S(1)}, u32[]{:S(2)}, u32[]{:S(2)}) collective-permute-start(bf16[384,256]{1,0:T(8,128)(2,1)S(1)} %add_convert_fusion.refs_0_), channel_id=1, source_target_pairs={{0,2},{1,3},{2,0},{3,1},{4,6},{5,7},{6,4},{7,5},{8,10},{9,11},{10,... | collective-permute-start | bytes 589832 | tf_op jit(solution)/shard_map/ppermute | solution.py:39
  48.6 0.0 collective-permute-start.12
  48.6 7.2 %collective-permute-done.6.refs_3_ = bf16[1664,128]{1,0:T(8,128)(2,1)S(1)} collective-permute-done((bf16[1664,128]{1,0:T(8,128)(2,1)S(1)}, bf16[1664,128]{1,0:T(8,128)(2,1)S(1)}, u32[]{:S(2)}, u32[]{:S(2)}) %collective-permute-start.6) | collective-permute-done | bytes 426016 | tf_op jit(solution)/shard_map/ppermute | solution.py:25
  55.8 0.0 collective-permute-start.10
  55.8 0.8 shard_map.76.refs_4_.refs_2_
  56.6 0.0 collective-permute-done.4.refs_0_
  56.6 2.3 %shard_map.77.refs_5_.refs_3_ = f32[2,256,128]{2,1,0:T(8,128)S(1)} custom-call(bf16[256,3456]{1,0:T(8,128)(2,1)} %collective-permute-done.4.refs_0_, bf16[1664,128]{1,0:T(8,128)(2,1)S(1)} %collective-permute-done.5.refs_1_, bf16[1792,128]{1,0:T(8,128)(2,1)S(1)} %collective-permute-done.1.refs_2_, bf16[1664,128]{1,0:T(8,128)(2,1)S(1)} %collective-permute-done.6.refs_3_), custom_call_target="tpu_custom_call" | custom-call | flops 335544320 | bytes 2621440 | tf_op jit(solution)/shard_map/pallas_call | solution.py:130
  59.0 3.0 %shard_map.75.refs_3_.refs_1_ = f32[2,256,128]{2,1,0:T(8,128)S(1)} custom-call(bf16[256,3456]{1,0:T(8,128)(2,1)} %collective-permute-done.4.refs_0_, bf16[1664,128]{1,0:T(8,128)(2,1)} %dynamic-slice_bitcast_fusion.1.refs_1_, bf16[1792,128]{1,0:T(8,128)(2,1)} %dynamic-slice_bitcast_fusion.refs_2_, bf16[1664,128]{1,0:T(8,128)(2,1)} %collective-permute-done.3.refs_3_, ...), custom_call_target="tpu_custom_call" | custom-call | flops 452984832 | bytes 3538944 | tf_op jit(solution)/shard_map/pallas_call | solution.py:130
  62.0 0.0 copy-start.3
  62.0 1.2 %slice.4.refs_1_ = bf16[256,1792]{1,0:T(8,128)(2,1)S(1)} slice(bf16[256,3456]{1,0:T(8,128)(2,1)} %collective-permute-done.4.refs_0_), slice={[0:256], [1664:3456]} | slice | bytes 1835008 | tf_op jit(solution)/shard_map/slice | solution.py:300
  63.2 0.0 collective-permute-done.11.refs_2_
  63.2 0.0 collective-permute-done.12.refs_3_
  63.3 0.0 collective-permute-done.10.refs_1_
  63.3 0.6 shard_map.78.act
  63.9 0.9 %collective-permute-done.2.held = bf16[1792,128]{1,0:T(8,128)(2,1)S(1)} collective-permute-done((bf16[1792,128]{1,0:T(8,128)(2,1)S(1)}, bf16[1792,128]{1,0:T(8,128)(2,1)S(1)}, u32[]{:S(2)}, u32[]{:S(2)}) %collective-permute-start.2) | collective-permute-done | bytes 458784 | tf_op jit(solution)/shard_map/ppermute | solution.py:25
  64.8 0.0 copy-done.3
  64.8 1.2 %shard_map.79 = (f32[512,128]{1,0:T(8,128)S(1)}, f32[2,512,128]{2,1,0:T(8,128)S(1)}) custom-call(s32[4]{0:T(128)S(1)} %copy-done.3, s32[3]{0:T(128)S(1)} %pad_add_fusion.place, bf16[1792,128]{1,0:T(8,128)(2,1)S(1)} %collective-permute-done.2.held, bf16[256,3456]{1,0:T(8,128)(2,1)S(1)} %constant_dynamic-slice_fusion.1.refs_0_, ...), custom_call_target="tpu_custom_call" | custom-call | tf_op jit(solution)/shard_map/pallas_call | solution.py:175
  65.9 0.0 copy-start.4
  66.0 0.0 copy-start.5
  66.0 0.1 collective-permute-start.13
  66.1 1.9 %collective-permute-done.13.refs_4_ = f32[2,512,128]{2,1,0:T(8,128)S(1)} collective-permute-done((f32[2,512,128]{2,1,0:T(8,128)S(1)}, f32[2,512,128]{2,1,0:T(8,128)S(1)}, u32[]{:S(2)}, u32[]{:S(2)}) %collective-permute-start.13) | collective-permute-done | bytes 524320 | tf_op jit(solution)/shard_map/ppermute | solution.py:25
  68.0 0.6 shard_map.80
  68.6 1.6 %collective-permute-start.14 = (f32[256,128]{1,0:T(8,128)S(1)}, f32[256,128]{1,0:T(8,128)S(1)}, u32[]{:S(2)}, u32[]{:S(2)}) collective-permute-start(f32[256,128]{1,0:T(8,128)S(1)} %get-tuple-element.62), channel_id=1, source_target_pairs={{0,16},{2,18},{16,0},{18,2},{1,17},{3,19},{17,1},{19,3},{4,20},{6,... | collective-permute-start | bytes 393224 | tf_op jit(solution)/shard_map/ppermute | solution.py:320
  70.2 1.5 %collective-permute-start.15 = (f32[256,128]{1,0:T(8,128)S(1)}, f32[256,128]{1,0:T(8,128)S(1)}, u32[]{:S(2)}, u32[]{:S(2)}) collective-permute-start(f32[256,128]{1,0:T(8,128)S(1)} %get-tuple-element.63), channel_id=1, source_target_pairs={{0,2},{2,0},{16,18},{18,16},{1,3},{3,1},{17,19},{19,17},{4,6},{6,4... | collective-permute-start | bytes 393224 | tf_op jit(solution)/shard_map/ppermute | solution.py:320
  71.7 0.5 collective-permute-start.16
  72.2 2.0 %collective-permute-done.14.refs_1_ = f32[256,128]{1,0:T(8,128)S(1)} collective-permute-done((f32[256,128]{1,0:T(8,128)S(1)}, f32[256,128]{1,0:T(8,128)S(1)}, u32[]{:S(2)}, u32[]{:S(2)}) %collective-permute-start.14) | collective-permute-done | bytes 131104 | tf_op jit(solution)/shard_map/ppermute | solution.py:320
  74.2 2.4 %collective-permute-done.15.refs_2_ = f32[256,128]{1,0:T(8,128)S(1)} collective-permute-done((f32[256,128]{1,0:T(8,128)S(1)}, f32[256,128]{1,0:T(8,128)S(1)}, u32[]{:S(2)}, u32[]{:S(2)}) %collective-permute-start.15) | collective-permute-done | bytes 131104 | tf_op jit(solution)/shard_map/ppermute | solution.py:320
  76.6 1.6 %collective-permute-done.16.refs_3_ = f32[256,128]{1,0:T(8,128)S(1)} collective-permute-done((f32[256,128]{1,0:T(8,128)S(1)}, f32[256,128]{1,0:T(8,128)S(1)}, u32[]{:S(2)}, u32[]{:S(2)}) %collective-permute-start.16) | collective-permute-done | bytes 131104 | tf_op jit(solution)/shard_map/ppermute | solution.py:320
  78.2 0.9 shard_map.81
  79.1 0.1 collective-permute-start.17
  79.1 2.3 %collective-permute-start.18 = (bf16[256,128]{1,0:T(8,128)(2,1)S(1)}, bf16[256,128]{1,0:T(8,128)(2,1)S(1)}, u32[]{:S(2)}, u32[]{:S(2)}) collective-permute-start(bf16[256,128]{1,0:T(8,128)(2,1)S(1)} %get-tuple-element.67), channel_id=1, source_target_pairs={{0,8},{4,12},{8,0},{12,4},{1,9},{5,13},{9,1},{13,5},{2,10},{6,14},... | collective-permute-start | bytes 196616 | tf_op jit(solution)/shard_map/ppermute | solution.py:25
  81.4 1.5 %collective-permute-start.19 = (bf16[256,128]{1,0:T(8,128)(2,1)S(1)}, bf16[256,128]{1,0:T(8,128)(2,1)S(1)}, u32[]{:S(2)}, u32[]{:S(2)}) collective-permute-start(bf16[256,128]{1,0:T(8,128)(2,1)S(1)} %get-tuple-element.68), channel_id=1, source_target_pairs={{0,12},{4,0},{8,4},{12,8},{1,13},{5,1},{9,5},{13,9},{2,14},{6,2},{... | collective-permute-start | bytes 196616 | tf_op jit(solution)/shard_map/ppermute | solution.py:25
  83.0 2.7 %collective-permute-done.17 = bf16[256,128]{1,0:T(8,128)(2,1)S(1)} collective-permute-done((bf16[256,128]{1,0:T(8,128)(2,1)S(1)}, bf16[256,128]{1,0:T(8,128)(2,1)S(1)}, u32[]{:S(2)}, u32[]{:S(2)}) %collective-permute-start.17) | collective-permute-done | bytes 65568 | tf_op jit(solution)/shard_map/ppermute | solution.py:25
  85.7 1.3 %collective-permute-done.18 = bf16[256,128]{1,0:T(8,128)(2,1)S(1)} collective-permute-done((bf16[256,128]{1,0:T(8,128)(2,1)S(1)}, bf16[256,128]{1,0:T(8,128)(2,1)S(1)}, u32[]{:S(2)}, u32[]{:S(2)}) %collective-permute-start.18) | collective-permute-done | bytes 65568 | tf_op jit(solution)/shard_map/ppermute | solution.py:25
  87.0 0.0 collective-permute-done.19
  87.0 0.7 add_multiply_fusion
  (5 shorter events, 0.0 us)
Async XLA Ops:
  0.0 6.8 %copy-start = (bf16[2,128,6912]{2,1,0:T(8,128)(2,1)S(1)}, bf16[2,128,6912]{2,1,0:T(8,128)(2,1)}, u32[]{:S(2)}) copy-start(bf16[2,128,6912]{2,1,0:T(8,128)(2,1)} %param.8) | copy-start | bytes 10616836
  1.9 16.0 %collective-permute-start.3 = (bf16[1664,128]{1,0:T(8,128)(2,1)}, bf16[1664,128]{1,0:T(8,128)(2,1)}, u32[]{:S(2)}, u32[]{:S(2)}) collective-permute-start(bf16[1664,128]{1,0:T(8,128)(2,1)} %dynamic-slice_bitcast_fusion.1.refs_1_), channel_id=1, source_target_pairs={{0,4},{4,8},{8,12},{12,0},{1,5},{5,9},{9,13},{13,1},{2,6},{6,10},{... | collective-permute-start | bytes 1277960 | tf_op jit(solution)/shard_map/ppermute | solution.py:25
  8.1 48.5 %collective-permute-start.4 = (bf16[256,3456]{1,0:T(8,128)(2,1)}, bf16[256,3456]{1,0:T(8,128)(2,1)}, u32[]{:S(2)}, u32[]{:S(2)}) collective-permute-start(bf16[256,3456]{1,0:T(8,128)(2,1)} %constant_dynamic-slice_fusion), channel_id=1, source_target_pairs={{0,16},{16,0},{1,17},{17,1},{2,18},{18,2},{3,19},{19,3},{4,20},{20... | collective-permute-start | bytes 5308424 | tf_op jit(solution)/shard_map/ppermute | solution.py:25
  9.6 18.2 %collective-permute-start = (bf16[1792,128]{1,0:T(8,128)(2,1)}, bf16[1792,128]{1,0:T(8,128)(2,1)}, u32[]{:S(2)}, u32[]{:S(2)}) collective-permute-start(bf16[1792,128]{1,0:T(8,128)(2,1)} %dynamic-slice_bitcast_fusion.refs_2_), channel_id=1, source_target_pairs={{0,4},{4,8},{8,12},{12,0},{1,5},{5,9},{9,13},{13,1},{2,6},{6,10},{... | collective-permute-start | bytes 1376264 | tf_op jit(solution)/shard_map/ppermute | solution.py:25
  11.3 2.1 %copy-start.1 = (bf16[1280,1536]{1,0:T(8,128)(2,1)S(1)}, bf16[1280,1536]{1,0:T(8,128)(2,1)}, u32[]{:S(2)}) copy-start(bf16[1280,1536]{1,0:T(8,128)(2,1)} %basis.1) | copy-start | bytes 11796484
  13.4 1.1 %copy-start.2 = (bf16[2,128,1280]{2,1,0:T(8,128)(2,1)S(1)}, bf16[2,128,1280]{2,1,0:T(8,128)(2,1)}, u32[]{:S(2)}) copy-start(bf16[2,128,1280]{2,1,0:T(8,128)(2,1)} %param.7) | copy-start | bytes 1966084
  18.0 18.9 %collective-permute-start.5 = (bf16[1664,128]{1,0:T(8,128)(2,1)}, bf16[1664,128]{1,0:T(8,128)(2,1)S(1)}, u32[]{:S(2)}, u32[]{:S(2)}) collective-permute-start(bf16[1664,128]{1,0:T(8,128)(2,1)} %collective-permute-done.3.refs_3_), channel_id=1, source_target_pairs={{0,4},{4,8},{8,12},{12,0},{1,5},{5,9},{9,13},{13,1},{2,6},{6,10},{... | collective-permute-start | bytes 1277960 | tf_op jit(solution)/shard_map/ppermute | solution.py:25
  18.8 9.0 %collective-permute-start.7 = (f32[384,256]{1,0:T(8,128)S(1)}, f32[384,256]{1,0:T(8,128)S(1)}, u32[]{:S(2)}, u32[]{:S(2)}) collective-permute-start(f32[384,256]{1,0:T(8,128)S(1)} %get-tuple-element.47), channel_id=1, source_target_pairs={{0,1},{1,0},{2,3},{3,2},{4,5},{5,4},{6,7},{7,6},{8,9},{9,8},{10,11... | collective-permute-start | bytes 1179656 | tf_op jit(solution)/shard_map/ppermute | solution.py:39
  18.8 27.9 %collective-permute-start.8 = (f32[384,256]{1,0:T(8,128)S(1)}, f32[384,256]{1,0:T(8,128)S(1)}, u32[]{:S(2)}, u32[]{:S(2)}) collective-permute-start(f32[384,256]{1,0:T(8,128)S(1)} %get-tuple-element.48), channel_id=1, source_target_pairs={{0,2},{1,3},{2,0},{3,1},{4,6},{5,7},{6,4},{7,5},{8,10},{9,11},{10,... | collective-permute-start | bytes 1179656 | tf_op jit(solution)/shard_map/ppermute | solution.py:39
  27.8 18.9 %collective-permute-start.9 = (f32[384,256]{1,0:T(8,128)S(1)}, f32[384,256]{1,0:T(8,128)S(1)}, u32[]{:S(2)}, u32[]{:S(2)}) collective-permute-start(f32[384,256]{1,0:T(8,128)S(1)} %get-tuple-element.49), channel_id=1, source_target_pairs={{0,3},{1,2},{2,1},{3,0},{4,7},{5,6},{6,5},{7,4},{8,11},{9,10},{10,... | collective-permute-start | bytes 1179656 | tf_op jit(solution)/shard_map/ppermute | solution.py:39
  27.8 18.8 %collective-permute-start.1 = (bf16[1792,128]{1,0:T(8,128)(2,1)}, bf16[1792,128]{1,0:T(8,128)(2,1)S(1)}, u32[]{:S(2)}, u32[]{:S(2)}) collective-permute-start(bf16[1792,128]{1,0:T(8,128)(2,1)} %collective-permute-done.refs_4_), channel_id=1, source_target_pairs={{0,4},{4,8},{8,12},{12,0},{1,5},{5,9},{9,13},{13,1},{2,6},{6,10},{... | collective-permute-start | bytes 1376264 | tf_op jit(solution)/shard_map/ppermute | solution.py:25
  36.8 19.0 %collective-permute-start.6 = (bf16[1664,128]{1,0:T(8,128)(2,1)S(1)}, bf16[1664,128]{1,0:T(8,128)(2,1)S(1)}, u32[]{:S(2)}, u32[]{:S(2)}) collective-permute-start(bf16[1664,128]{1,0:T(8,128)(2,1)S(1)} %collective-permute-done.5.refs_1_), channel_id=1, source_target_pairs={{0,4},{4,8},{8,12},{12,0},{1,5},{5,9},{9,13},{13,1},{2,6},{6,10},{... | collective-permute-start | bytes 1277960 | tf_op jit(solution)/shard_map/ppermute | solution.py:25
  46.6 18.1 %collective-permute-start.2 = (bf16[1792,128]{1,0:T(8,128)(2,1)S(1)}, bf16[1792,128]{1,0:T(8,128)(2,1)S(1)}, u32[]{:S(2)}, u32[]{:S(2)}) collective-permute-start(bf16[1792,128]{1,0:T(8,128)(2,1)S(1)} %collective-permute-done.1.refs_2_), channel_id=1, source_target_pairs={{0,4},{4,8},{8,12},{12,0},{1,5},{5,9},{9,13},{13,1},{2,6},{6,10},{... | collective-permute-start | bytes 1376264 | tf_op jit(solution)/shard_map/ppermute | solution.py:25
  46.8 16.4 %collective-permute-start.11 = (bf16[384,256]{1,0:T(8,128)(2,1)S(1)}, bf16[384,256]{1,0:T(8,128)(2,1)S(1)}, u32[]{:S(2)}, u32[]{:S(2)}) collective-permute-start(bf16[384,256]{1,0:T(8,128)(2,1)S(1)} %add_convert_fusion.refs_0_), channel_id=1, source_target_pairs={{0,2},{1,3},{2,0},{3,1},{4,6},{5,7},{6,4},{7,5},{8,10},{9,11},{10,... | collective-permute-start | bytes 589832 | tf_op jit(solution)/shard_map/ppermute | solution.py:39
  48.6 14.7 %collective-permute-start.12 = (bf16[384,256]{1,0:T(8,128)(2,1)S(1)}, bf16[384,256]{1,0:T(8,128)(2,1)S(1)}, u32[]{:S(2)}, u32[]{:S(2)}) collective-permute-start(bf16[384,256]{1,0:T(8,128)(2,1)S(1)} %add_convert_fusion.refs_0_), channel_id=1, source_target_pairs={{0,3},{1,2},{2,1},{3,0},{4,7},{5,6},{6,5},{7,4},{8,11},{9,10},{10,... | collective-permute-start | bytes 589832 | tf_op jit(solution)/shard_map/ppermute | solution.py:39
  55.8 7.5 %collective-permute-start.10 = (bf16[384,256]{1,0:T(8,128)(2,1)S(1)}, bf16[384,256]{1,0:T(8,128)(2,1)S(1)}, u32[]{:S(2)}, u32[]{:S(2)}) collective-permute-start(bf16[384,256]{1,0:T(8,128)(2,1)S(1)} %add_convert_fusion.refs_0_), channel_id=1, source_target_pairs={{0,1},{1,0},{2,3},{3,2},{4,5},{5,4},{6,7},{7,6},{8,9},{9,8},{10,11... | collective-permute-start | bytes 589832 | tf_op jit(solution)/shard_map/ppermute | solution.py:39
  62.0 2.8 %copy-start.3 = (s32[4]{0:T(128)S(1)}, s32[4]{0:T(128)}, u32[]{:S(2)}) copy-start(s32[4]{0:T(128)} %owner.3) | copy-start | bytes 52
  65.9 12.3 %copy-start.4 = (s32[2]{0:T(128)S(1)}, s32[2]{0:T(128)}, u32[]{:S(2)}) copy-start(s32[2]{0:T(128)} %counts.1) | copy-start | bytes 28
  66.0 12.2 %copy-start.5 = (s32[1,2]{1,0:T(1,128)S(1)}, s32[1,2]{1,0:T(1,128)}, u32[]{:S(2)}) copy-start(s32[1,2]{1,0:T(1,128)} %wanted.1) | copy-start | bytes 28
  66.0 2.0 %collective-permute-start.13 = (f32[2,512,128]{2,1,0:T(8,128)S(1)}, f32[2,512,128]{2,1,0:T(8,128)S(1)}, u32[]{:S(2)}, u32[]{:S(2)}) collective-permute-start(f32[2,512,128]{2,1,0:T(8,128)S(1)} %get-tuple-element.60), channel_id=1, source_target_pairs={{0,1},{1,0},{2,3},{3,2},{4,5},{5,4},{6,7},{7,6},{8,9},{9,8},{10,11... | collective-permute-start | bytes 1572872 | tf_op jit(solution)/shard_map/ppermute | solution.py:25
  68.6 5.6 %collective-permute-start.14 = (f32[256,128]{1,0:T(8,128)S(1)}, f32[256,128]{1,0:T(8,128)S(1)}, u32[]{:S(2)}, u32[]{:S(2)}) collective-permute-start(f32[256,128]{1,0:T(8,128)S(1)} %get-tuple-element.62), channel_id=1, source_target_pairs={{0,16},{2,18},{16,0},{18,2},{1,17},{3,19},{17,1},{19,3},{4,20},{6,... | collective-permute-start | bytes 393224 | tf_op jit(solution)/shard_map/ppermute | solution.py:320
  70.2 6.4 %collective-permute-start.15 = (f32[256,128]{1,0:T(8,128)S(1)}, f32[256,128]{1,0:T(8,128)S(1)}, u32[]{:S(2)}, u32[]{:S(2)}) collective-permute-start(f32[256,128]{1,0:T(8,128)S(1)} %get-tuple-element.63), channel_id=1, source_target_pairs={{0,2},{2,0},{16,18},{18,16},{1,3},{3,1},{17,19},{19,17},{4,6},{6,4... | collective-permute-start | bytes 393224 | tf_op jit(solution)/shard_map/ppermute | solution.py:320
  71.7 6.5 %collective-permute-start.16 = (f32[256,128]{1,0:T(8,128)S(1)}, f32[256,128]{1,0:T(8,128)S(1)}, u32[]{:S(2)}, u32[]{:S(2)}) collective-permute-start(f32[256,128]{1,0:T(8,128)S(1)} %get-tuple-element.64), channel_id=1, source_target_pairs={{0,18},{2,16},{16,2},{18,0},{1,19},{3,17},{17,3},{19,1},{4,22},{6,... | collective-permute-start | bytes 393224 | tf_op jit(solution)/shard_map/ppermute | solution.py:320
  79.1 6.6 %collective-permute-start.17 = (bf16[256,128]{1,0:T(8,128)(2,1)S(1)}, bf16[256,128]{1,0:T(8,128)(2,1)S(1)}, u32[]{:S(2)}, u32[]{:S(2)}) collective-permute-start(bf16[256,128]{1,0:T(8,128)(2,1)S(1)} %get-tuple-element.66), channel_id=1, source_target_pairs={{0,4},{4,8},{8,12},{12,0},{1,5},{5,9},{9,13},{13,1},{2,6},{6,10},{... | collective-permute-start | bytes 196616 | tf_op jit(solution)/shard_map/ppermute | solution.py:25
  79.1 7.8 %collective-permute-start.18 = (bf16[256,128]{1,0:T(8,128)(2,1)S(1)}, bf16[256,128]{1,0:T(8,128)(2,1)S(1)}, u32[]{:S(2)}, u32[]{:S(2)}) collective-permute-start(bf16[256,128]{1,0:T(8,128)(2,1)S(1)} %get-tuple-element.67), channel_id=1, source_target_pairs={{0,8},{4,12},{8,0},{12,4},{1,9},{5,13},{9,1},{13,5},{2,10},{6,14},... | collective-permute-start | bytes 196616 | tf_op jit(solution)/shard_map/ppermute | solution.py:25
  81.4 5.5 %collective-permute-start.19 = (bf16[256,128]{1,0:T(8,128)(2,1)S(1)}, bf16[256,128]{1,0:T(8,128)(2,1)S(1)}, u32[]{:S(2)}, u32[]{:S(2)}) collective-permute-start(bf16[256,128]{1,0:T(8,128)(2,1)S(1)} %get-tuple-element.68), channel_id=1, source_target_pairs={{0,12},{4,0},{8,4},{12,8},{1,13},{5,1},{9,5},{13,9},{2,14},{6,2},{... | collective-permute-start | bytes 196616 | tf_op jit(solution)/shard_map/ppermute | solution.py:25
